TPU v7x, 32 devices: a whole 2x2x4 slice. The times are simulated.
32 devices in a mesh: dp: 4 (over z), tensor: 8 (over y, x, core).
Axes of the slice: x: 2, y: 2, z: 4, core: 2. Of those that a mesh axis runs over, the one named last changes fastest.
Arguments:
- queries: bfloat16 [4, 133, 1024], P('dp', None, 'tensor'), may hold values from -50 to 50
- keys: bfloat16 [4, 1024, 1024], P('dp', None, 'tensor'), may hold values from -4 to 4
- values: bfloat16 [4, 1024, 1024], P('dp', None, 'tensor'), may hold values from -6 to 6
- conv_kernel: float32 [8, 6, 11], P('tensor'), may hold values from -0.9 to 1.9
- span_start: int32 [4], P('dp'), may hold values from 0 to 896, as said below
- out_grad: bfloat16 [4, 128, 1024], P('dp', None, 'tensor'), may hold values from -6 to 6
- proj_weight: float32 [1024, 1024], P('tensor', 'dp'), may hold values from -0.1875 to 0.1875
- moment_one: float32 [1024, 1024], P('tensor', 'dp'), may hold values from -12 to 12
- moment_two: float32 [1024, 1024], P('tensor', 'dp'), may hold values from 1 to 100
Outputs:
- query_grad: bfloat16 [4, 133, 1024], P('dp', None, 'tensor')
- key_grad: bfloat16 [4, 1024, 1024], P('dp', None, 'tensor')
- value_grad: bfloat16 [4, 1024, 1024], P('dp', None, 'tensor')
- kernel_grad: float32 [8, 6, 11], P('tensor')
- proj_new: float32 [1024, 1024], P('tensor', 'dp')
- moment_one_new: float32 [1024, 1024], P('tensor', 'dp')
- moment_two_new: float32 [1024, 1024], P('tensor', 'dp')
Inputs may be any that keep to these rules, and one draw needn't show every extreme that they name: `span_start`: each sequence's first block row; one sequence starts at 0 and one at 896.
All inputs are finite; a program needn't handle non-finite values.
Results may differ from a plain program's by a relative error of at most 0.0029.
The roundings to bfloat16 on the way count: a program that leaves them out, or rounds other values in their place, can miss the bound.
Values may be sent and summed in bfloat16 or wider, within the bound.
No kernel may reach another device: no remote copies, remote signals or barrier semaphores. Data moves between devices by JAX's collectives and lax.ppermute only.
A program may use at most 64 MiB of HBM per device.

v0:
```python
import math

import jax
import jax.numpy as jnp
from jax import lax
from jax.sharding import PartitionSpec as P

beta_one = 0.9
beta_two = 0.95
learn_rate = 0.01
decay_rate = 0.1
adam_eps = 1e-08
bias_one = 1.0 - 0.9**10
bias_two = 1.0 - 0.95**10


def contract_rows(left, right):
    return lax.dot_general(
        left, right, (((0,), (0,)), ((), ())), preferred_element_type=jnp.float32
    )


def contract_cols(left, right):
    return lax.dot_general(
        left, right, (((1,), (1,)), ((), ())), preferred_element_type=jnp.float32
    )


def shards(
    queries, keys, values, conv_kernel, span_start, out_grad, proj_weight, moment_one, moment_two
):
    first_pos = span_start[0]
    query_rows = queries[0]
    key_rows = keys[0]
    value_rows = values[0]
    kernel = conv_kernel[0]
    conv_rows, conv_cols = kernel.shape
    half_width = (conv_cols - 1) // 2
    span_len = out_grad.shape[1]
    key_count = key_rows.shape[0]
    query_count = query_rows.shape[0]
    head_dim = query_rows.shape[1]
    group_count = lax.axis_size("dp")
    score_scale = 1.0 / math.sqrt(head_dim)
    key_pos = jnp.arange(key_count, dtype=jnp.int32)
    row_pos = first_pos - (conv_rows - 1) + jnp.arange(query_count, dtype=jnp.int32)
    visible = key_pos[None, :] <= row_pos[:, None]
    masked = jnp.where(visible, contract_cols(query_rows, key_rows) * score_scale, 0.0)
    padded = jnp.pad(masked, ((0, 0), (half_width, half_width)))
    mixed_scores = jnp.zeros((span_len, key_count), jnp.float32)
    for tap_row in range(conv_rows):
        for tap_col in range(conv_cols):
            row_first = conv_rows - 1 - tap_row
            mixed_scores = (
                mixed_scores
                + kernel[tap_row, tap_col]
                * padded[row_first : row_first + span_len, tap_col : tap_col + key_count]
            )
    live_mask = visible[conv_rows - 1 :]
    row_top = jnp.max(jnp.where(live_mask, mixed_scores, -jnp.inf), axis=1, keepdims=True)
    exp_terms = jnp.where(live_mask, jnp.exp(mixed_scores - row_top), 0.0)
    weights_soft = exp_terms / jnp.sum(exp_terms, axis=1, keepdims=True)
    weights_bf = weights_soft.astype(jnp.bfloat16)
    attended = jnp.dot(weights_bf, value_rows, preferred_element_type=jnp.float32).astype(
        jnp.bfloat16
    )
    proj_bf = proj_weight.astype(jnp.bfloat16)
    local_grad = out_grad[0]
    upstream = lax.all_gather(local_grad, "tensor", axis=1, tiled=True)
    columns = upstream
    grad_out32 = contract_cols(columns, lax.all_gather(proj_bf, "dp", axis=1, tiled=True))
    grad_out = grad_out32.astype(jnp.bfloat16)
    grad_values = contract_rows(weights_bf, grad_out).astype(jnp.bfloat16)
    grad_weights = contract_cols(grad_out, value_rows)
    row_inner = jnp.sum(weights_soft * grad_weights, axis=1, keepdims=True)
    grad_mixed = weights_soft * (grad_weights - row_inner)
    grad_pad = jnp.pad(grad_mixed, ((conv_rows - 1, conv_rows - 1), (half_width, half_width)))
    grad_masked = jnp.zeros((query_count, key_count), jnp.float32)
    kernel_terms = []
    for tap_row in range(conv_rows):
        for tap_col in range(conv_cols):
            col_first = 2 * half_width - tap_col
            grad_masked = (
                grad_masked
                + kernel[tap_row, tap_col]
                * grad_pad[tap_row : tap_row + query_count, col_first : col_first + key_count]
            )
            row_first = conv_rows - 1 - tap_row
            kernel_terms.append(
                jnp.sum(
                    grad_mixed
                    * padded[row_first : row_first + span_len, tap_col : tap_col + key_count]
                )
            )
    kernel_local = jnp.stack(kernel_terms).reshape(conv_rows, conv_cols)
    grad_scores = jnp.where(visible, grad_masked, 0.0).astype(jnp.bfloat16)
    grad_query = (
        score_scale * jnp.dot(grad_scores, key_rows, preferred_element_type=jnp.float32)
    ).astype(jnp.bfloat16)
    grad_keys = (score_scale * contract_rows(grad_scores, query_rows)).astype(jnp.bfloat16)
    columns = upstream
    proj_sum = lax.psum_scatter(
        contract_rows(columns, attended), "dp", scatter_dimension=0, tiled=True
    ).T
    grad_proj = proj_sum / float(group_count)
    kernel_total = lax.psum(kernel_local, "dp") / float(group_count * span_len)
    moment_one_new = beta_one * moment_one + (1.0 - beta_one) * grad_proj
    moment_two_new = beta_two * moment_two + (1.0 - beta_two) * grad_proj * grad_proj
    first_hat = moment_one_new / bias_one
    second_hat = moment_two_new / bias_two
    proj_new = proj_weight - learn_rate * (
        first_hat / (jnp.sqrt(second_hat) + adam_eps) + decay_rate * proj_weight
    )
    return (
        grad_query[None],
        grad_keys[None],
        grad_values[None],
        kernel_total[None],
        proj_new,
        moment_one_new,
        moment_two_new,
    )


def solution(mesh):
    placed = (
        P("dp", None, "tensor"),
        P("dp", None, "tensor"),
        P("dp", None, "tensor"),
        P("tensor", None, None),
        P("dp"),
        P("dp", None, "tensor"),
        P("tensor", "dp"),
        P("tensor", "dp"),
        P("tensor", "dp"),
    )
    return jax.shard_map(
        shards,
        mesh=mesh,
        in_specs=placed,
        out_specs=(
            P("dp", None, "tensor"),
            P("dp", None, "tensor"),
            P("dp", None, "tensor"),
            P("tensor", None, None),
            P("tensor", "dp"),
            P("tensor", "dp"),
            P("tensor", "dp"),
        ),
        check_vma=False,
    )
```

profile of v0, /device:TPU:0, one launch (start us, length us, event | category | flops | bytes accessed | tf_op | source)
XLA Modules:
  0.0 221.9 jit_solution(13766386470075223006)
XLA Ops:
  7.2 0.0 copy-start
  7.2 0.0 reduce-scatter.2.cloned.1.call-start
  7.2 0.7 copy.19
  7.9 0.7 fusion.156
  8.6 0.7 fusion.155
  9.3 0.7 fusion.154
  10.1 0.7 fusion.153
  11.4 0.9 convert_element_type.28
  12.4 0.1 iota_compare_fusion
  12.5 0.0 copy-start.6
  12.5 15.6 %all_gather.7 = bf16[128,1024]{1,0:T(8,128)(2,1)S(1)} all-gather(bf16[128,256]{1,0:T(8,128)(2,1)S(1)} %convert_element_type.28), channel_id=1, replica_groups=mesh['dp'=4,'tensor'=8] {'dp'}, dimensions={1}, use_global_device_ids=true | all-gather | bytes 327680 | tf_op jit(solution)/shard_map/all_gather | solution.py:71
  28.2 0.0 copy-done.6
  28.2 9.4 %all-gather = bf16[1,128,1024]{2,1,0:T(8,128)(2,1)S(1)} all-gather(bf16[1,128,128]{2,1,0:T(8,128)(2,1)S(1)} %copy-done.6), channel_id=2, replica_groups=mesh['dp'=4,'tensor'=8] {'tensor'}, dimensions={2}, use_global_device_ids=true | all-gather | bytes 294912 | tf_op jit(solution)/shard_map/all_gather | solution.py:69
  37.5 0.0 copy-start.1
  37.5 0.0 copy-start.3
  37.5 0.2 convolution_convert_fusion.2
  37.8 0.7 copy-done.1
  38.5 0.0 copy-done.3
  38.5 0.3 fusion
  38.8 50.3 %select_reduce_fusion = (f32[128]{0:T(128)S(1)}, f32[128,1024]{1,0:T(8,128)S(1)}) fusion(pred[133,1024]{1,0:T(8,128)(4,1)S(1)} %iota_compare_fusion, f32[]{:T(128)} %bitcast.68, f32[]{:T(128)} %bitcast.67, f32[]{:T(128)} %bitcast.66, f32[]{:T(128)} %bitcast.65, f32[]{:T(128)} %bitcast.64, f32[133,1024]{1,0:T(8,128)S(1)} %fusion, f32[]{:T(128)} %bitcast.63, ...), kind=kLoop, calls=%fused_computation.281 | loop fusion | flops 17432448 | bytes 4358920 | tf_op jit(solution)/shard_map/reduce_max | solution.py:60
  89.1 0.3 fusion.138
  89.4 0.0 copy-done
  89.4 0.4 multiply_reduce_fusion.66
  89.8 1.3 convolution_bitcast_fusion
  91.1 0.0 reduce-scatter.2.cloned.1.call-update
  91.1 3.1 %multiply_reduce_fusion = (f32[]{:T(128)}, f32[]{:T(128)}, f32[]{:T(128)}, f32[]{:T(128)}, f32[]{:T(128)}, /*index=5*/f32[]{:T(128)}, f32[]{:T(128)}, f32[]{:T(1...) fusion(f32[133,1024]{1,0:T(8,128)S(1)} %fusion, ...), kind=kLoop, calls=%fused_computation.212 | loop fusion | flops 4980718 | bytes 3179080 | tf_op jit(solution)/shard_map/reduce_sum | solution.py:90
  94.2 2.2 %multiply_reduce_fusion.54 = (f32[]{:T(128)}, f32[]{:T(128)}, f32[]{:T(128)}, f32[]{:T(128)}, f32[]{:T(128)}, /*index=5*/f32[]{:T(128)}, f32[]{:T(128)}, f32[]{:...) fusion(f32[128,1024]{1,0:T(8,128)S(1)} %get-tuple-element.83, f32[133,1024]{1,0:T(8,128)S(1)} %fusion), kind=kLoop, calls=%fused_computation.266 | loop fusion | flops 3145716 | bytes 1605680 | tf_op jit(solution)/shard_map/reduce_sum | solution.py:90
  96.5 3.1 %multiply_reduce_fusion.36 = (f32[]{:T(128)}, f32[]{:T(128)}, f32[]{:T(128)}, f32[]{:T(128)}, f32[]{:T(128)}, /*index=5*/f32[]{:T(128)}, f32[]{:T(128)}, f32[]{:...) fusion(f32[128,1024]{1,0:T(8,128)S(1)} %get-tuple-element.83, ...), kind=kLoop, calls=%fused_computation.248 | loop fusion | flops 4718574 | bytes 2129992 | tf_op jit(solution)/shard_map/reduce_sum | solution.py:90
  99.5 3.2 %multiply_reduce_fusion.18 = (f32[]{:T(128)}, f32[]{:T(128)}, f32[]{:T(128)}, f32[]{:T(128)}, f32[]{:T(128)}, /*index=5*/f32[]{:T(128)}, f32[]{:T(128)}, f32[]{:...) fusion(f32[128,1024]{1,0:T(8,128)S(1)} %get-tuple-element.83, ...), kind=kLoop, calls=%fused_computation.230 | loop fusion | flops 4718574 | bytes 1605704 | tf_op jit(solution)/shard_map/reduce_sum | solution.py:90
  102.7 42.4 %stack.267 = f32[66]{0:T(128)S(1)} concatenate(f32[1]{0:T(128)} %bitcast.74, f32[1]{0:T(128)} %bitcast.75, f32[1]{0:T(128)} %bitcast.76, f32[1]{0:T(128)} %bitcast.77, f32[1]{0:T(128)} %bitcast.78, f32[1]{0:T(128)} %bitcast.79, f32[1]{0:T(128)} %bitcast.80, f32[1]{0:T(128)} %bitcast.81, f32[1]{0:T(128)} %bitcast.82, f32[1]{0:T(128)} %bitcast.83, f32[1]{0:T(128)} %bitcast.84, ...), dimensions={0} | concatenate | bytes 528 | tf_op jit(solution)/shard_map/stack | solution.py:95
  145.2 0.1 reshape.26
  145.2 12.4 %psum.7 = f32[6,11]{1,0:T(8,128)S(1)} all-reduce(f32[6,11]{1,0:T(8,128)S(1)} %reshape.26), channel_id=1, replica_groups=mesh['dp'=4,'tensor'=8] {'dp'}, use_global_device_ids=true, to_apply=%region_69.70 | all-reduce | flops 66 | bytes 528 | tf_op jit(solution)/shard_map/psum | solution.py:106
  157.7 0.6 copy.16
  158.2 52.0 %select_convert_fusion = bf16[133,1024]{1,0:T(8,128)(2,1)S(1)} fusion(f32[128,1024]{1,0:T(8,128)S(1)} %get-tuple-element.83, f32[]{:T(128)} %bitcast.68, f32[]{:T(128)} %bitcast.67, f32[]{:T(128)} %bitcast.66, f32[]{:T(128)} %bitcast.65, f32[]{:T(128)} %bitcast.64, f32[]{:T(128)} %bitcast.63, f32[]{:T(128)} %bitcast.62, f32[]{:T(128)} %bitcast.61, ...), kind=kLoop, calls=%fused_computation.210 | loop fusion | flops 18249728 | bytes 797468 | tf_op jit(solution)/shard_map/convert_element_type | solution.py:96
  210.3 1.1 fusion.3
  211.3 1.0 fusion.2
  212.3 0.0 copy-start.2
  212.3 0.0 copy-start.4
  212.3 0.0 copy-start.5
  212.3 0.8 fusion.5
  213.1 0.0 reduce-scatter.2.cloned.1.call-done
  213.2 0.0 copy-done.2
  213.2 0.1 copy-done.4
  213.3 0.1 copy-done.5
  213.3 1.7 multiply_subtract_fusion
  (2 shorter events, 0.0 us)
Async XLA Ops:
  7.2 82.3 %copy-start = (bf16[1,1024,128]{2,1,0:T(8,128)(2,1)S(1)}, bf16[1,1024,128]{2,1,0:T(8,128)(2,1)}, u32[]{:S(2)}) copy-start(bf16[1,1024,128]{2,1,0:T(8,128)(2,1)} %param.11) | copy-start | bytes 786436
  7.2 206.0 %reduce-scatter.2.cloned.1.call-start = ((), (), s32[]{:S(2)}) async-start(), calls=%async_computation.1 | async-start | bytes 655360 | tf_op jit(solution)/shard_map/reduce_scatter | solution.py:102
  12.5 15.6 %copy-start.6 = (bf16[1,128,128]{2,1,0:T(8,128)(2,1)S(1)}, bf16[1,128,128]{2,1,0:T(8,128)(2,1)}, u32[]{:S(2)}) copy-start(bf16[1,128,128]{2,1,0:T(8,128)(2,1)} %param.14) | copy-start | bytes 98308
  37.5 0.9 copy-start.1
  37.5 1.0 copy-start.3
  212.3 0.9 copy-start.2
  212.3 1.0 copy-start.4
  212.3 1.0 copy-start.5
Sparse Core Ops, SparseCore 0:
  91.2 22.2 reduce-scatter.1
where the time goes:
time: 224 us; the launch traced here: 222 us
  other arithmetic  117 us (52%)
  local copies, waits for them, and re-layouts  47.5 us (21%)
  blocking collectives  37.4 us (17%)
  between operations  14.8 us (7%)
  matrix products  5.06 us (2%)
    convert_element_type x1, other arithmetic, shards(): grad_scores = jnp.where(visible, grad_masked, 0.0).astype(jnp.bfloat16)  52 us
    reduce_max x1, other arithmetic, shards(): jnp.max(jnp.where(live_mask, mixed_scores, -jnp.inf), axis=1, keepdims=True)  50.3 us
    another operation x1, local copies, waits for them, and re-layouts, shards(): kernel_local = jnp.stack(kernel_terms).reshape(conv_rows, conv_cols)  42.4 us
    all_gather x1, blocking collectives, shards(): lax.all_gather(proj_bf, 'dp', axis=1, tiled=True)  15.6 us
    psum x1, blocking collectives, shards(): kernel_total = lax.psum(kernel_local, 'dp') / float(group_count * span_len)  12.4 us
    reduce_sum x4, other arithmetic, shards(): jnp.sum(grad_mixed * padded[row_first:row_first + span_len, tap_col:tap_c...  11.6 us
    all_gather x1, blocking collectives, shards(): upstream = lax.all_gather(local_grad, 'tensor', axis=1, tiled=True)  9.37 us
  transfers between devices with their start and end apart: 1, of which 0 were waited for; matrix products, arithmetic and copies ran while one was open for 49% of the time, Pallas kernels for 0%

commit v1 on v0

v1 whole, which is shorter than its diff:
```python
import functools
import math

import jax
import jax.numpy as jnp
from jax import lax
from jax.experimental import pallas as pl
from jax.experimental.pallas import tpu as pltpu
from jax.sharding import PartitionSpec as P

beta_one = 0.9
beta_two = 0.95
learn_rate = 0.01
decay_rate = 0.1
adam_eps = 1e-08
bias_one = 1.0 - 0.9**10
bias_two = 1.0 - 0.95**10

LANES = 128
HALF = LANES // 2
F32 = jnp.float32
BF16 = jnp.bfloat16


def dot(left, right, dims=((1,), (0,))):
    return lax.dot_general(left, right, (dims, ((), ())), preferred_element_type=F32)


def split(x):
    high = x.astype(BF16)
    return high, (x - high.astype(F32)).astype(BF16)


def up_to(n, multiple):
    return -(-n // multiple) * multiple


def iota(shape, axis):
    return lax.broadcasted_iota(jnp.int32, shape, axis)


def bands(kernel_ref, taps_a, taps_b, flipped):
    half = (taps_b - 1) // 2
    place = iota((2 * LANES, LANES), 0) - iota((2 * LANES, LANES), 1) - (HALF - half)
    out = [jnp.zeros((2 * LANES, LANES), F32) for _ in range(taps_a)]
    for b in range(taps_b):
        here = place == (taps_b - 1 - b if flipped else b)
        for a in range(taps_a):
            out[a] = jnp.where(here, kernel_ref[0, a, b], out[a])
    return out


def forward(
    first_ref, kernel_ref, q_ref, k_ref, v_ref,
    p_ref, pt_ref, o_ref, xth_ref, xtl_ref, bh_ref, bl_ref,
    q32, fh, fl, xh, xl, y, kpad, vpad,
):
    _, taps_a, taps_b = kernel_ref.shape
    _, rows, depth = q_ref.shape
    keys = k_ref.shape[1]
    span = rows - taps_a + 1
    rows_up = q32.shape[0]
    blocks = keys // LANES
    scale = 1.0 / math.sqrt(depth)
    first = first_ref[0]

    q32[...] = jnp.zeros_like(q32)
    q32[:rows] = q_ref[0].astype(F32)
    for a, (f, t) in enumerate(
        zip(bands(kernel_ref, taps_a, taps_b, False), bands(kernel_ref, taps_a, taps_b, True), strict=True)
    ):
        cols = pl.ds(a * LANES, LANES)
        fh[:, cols], fl[:, cols] = split(f)
        bh_ref[:, cols], bl_ref[:, cols] = split(t)

    q_all = q32[...].astype(BF16)
    zero = jnp.zeros((rows_up, LANES), BF16)
    for ref in (xh, xl):
        ref[:rows_up, :LANES] = zero
        ref[blocks * rows_up :, LANES:] = zero
    for n in range(blocks):
        x = dot(q_all, k_ref[0, n * LANES : (n + 1) * LANES], ((1,), (1,))) * scale
        key = n * LANES + iota(x.shape, 1)
        pos = first - (taps_a - 1) + iota(x.shape, 0)
        high, low = split(jnp.where(key <= pos, x, 0.0))
        for ref, part in ((xh, high), (xl, low)):
            ref[n * rows_up : (n + 1) * rows_up, LANES:] = part
            ref[(n + 1) * rows_up : (n + 2) * rows_up, :LANES] = part

    for at in range(0, taps_a * LANES, 2 * LANES):
        cols = pl.ds(at, 2 * LANES)
        y[:, cols] = dot(xh[...], fh[:, cols]) + dot(xh[...], fl[:, cols]) + dot(xl[...], fh[:, cols])
    mixed = []
    for w in range(blocks + 1):
        total = None
        for a in range(taps_a):
            start = w * rows_up + taps_a - 1 - a
            term = y[start : start + span, a * LANES : (a + 1) * LANES]
            total = term if total is None else total + term
        mixed.append(total)
    c = jnp.concatenate(mixed, axis=1)
    key = iota(c.shape, 1) - HALF
    live = (key >= 0) & (key <= first + iota(c.shape, 0))
    top = jnp.max(jnp.where(live, c, -jnp.inf), axis=1, keepdims=True)
    terms = jnp.where(live, jnp.exp(c - top), 0.0)
    p = terms / jnp.sum(terms, axis=1, keepdims=True)
    p_ref[...] = p
    pt_ref[...] = p.T.astype(BF16)
    vpad[...] = jnp.zeros_like(vpad)
    vpad[HALF : HALF + keys] = v_ref[0]
    o_ref[...] = dot(p.astype(BF16), vpad[...]).astype(BF16)

    edge = (kpad.shape[0] - keys) // 2
    kpad[...] = jnp.zeros_like(kpad)
    flip = (iota((LANES, LANES), 0) + iota((LANES, LANES), 1) == LANES - 1).astype(F32).astype(BF16)
    for n in range(blocks):
        kpad[edge + n * LANES : edge + (n + 1) * LANES] = dot(
            flip, k_ref[0, keys - (n + 1) * LANES : keys - n * LANES]
        ).astype(BF16)
    for a in range(taps_a):
        start = taps_a - 1 - a
        xt = dot(kpad[...], q32[start : start + span].astype(BF16), ((1,), (1,))) * scale
        key = keys - 1 + edge - iota(xt.shape, 0)
        pos = first - a + iota(xt.shape, 1)
        cols = pl.ds(a * LANES, LANES)
        xth_ref[:, cols], xtl_ref[:, cols] = split(jnp.where(key <= pos, xt, 0.0))


def backward(
    taps_b, first_ref, up_ref, w_ref, p_ref, pt_ref, xth_ref, xtl_ref, bh_ref, bl_ref, q_ref, k_ref, v_ref,
    dq_ref, dk_ref, dv_ref, taps_ref,
    vpad, ch, cl, z, q16,
):
    _, rows, depth = q_ref.shape
    keys = k_ref.shape[1]
    span = p_ref.shape[0]
    taps_a = rows - span + 1
    blocks = keys // LANES
    scale = 1.0 / math.sqrt(depth)
    first = first_ref[0]
    half = (taps_b - 1) // 2
    edge = (xth_ref.shape[0] - keys) // 2

    vpad[...] = jnp.zeros_like(vpad)
    vpad[HALF : HALF + keys] = v_ref[0]
    do = dot(up_ref[...], w_ref[...], ((1,), (1,))).astype(BF16)
    dp = dot(do, vpad[...], ((1,), (1,)))
    p = p_ref[...]
    dc = p * (dp - jnp.sum(p * dp, axis=1, keepdims=True))
    high, low = split(dc)
    for w in range(blocks + 1):
        cols = slice(w * LANES, (w + 1) * LANES)
        here = slice(w * span, (w + 1) * span)
        ch[here] = high[:, cols]
        cl[here] = low[:, cols]

    window = up_to(LANES + edge - HALF + half, 16)
    right = jnp.concatenate([ch[...], cl[...]], axis=1)
    spot = window - 1 - (edge - HALF - half) - iota((window, LANES), 0) - iota((window, LANES), 1)
    wanted = (spot >= 0) & (spot < taps_b)
    for a in range(taps_a):
        total = None
        for ref in (xth_ref, xtl_ref):
            left = jnp.concatenate(
                [ref[w * LANES : w * LANES + window, a * LANES : (a + 1) * LANES] for w in range(blocks, -1, -1)], axis=1
            )
            term = dot(left, right)
            total = term if total is None else total + term
        total = jnp.where(wanted, total[:, :LANES] + total[:, LANES:], 0.0)
        turned = pltpu.roll(total, 0, 1, stride=1, stride_axis=0)
        taps_ref[a : a + 1] = jnp.sum(turned, axis=0, keepdims=True)

    rows_up = up_to(rows, 16)
    depth_z = z.shape[0] // blocks
    for n in range(blocks):
        left_h = jnp.concatenate([ch[n * span : (n + 1) * span], ch[(n + 1) * span : (n + 2) * span]], axis=1)
        left_l = jnp.concatenate([cl[n * span : (n + 1) * span], cl[(n + 1) * span : (n + 2) * span]], axis=1)
        z[n * depth_z : n * depth_z + 8] = jnp.zeros((8, z.shape[1]), F32)
        z[n * depth_z + 8 + span : (n + 1) * depth_z] = jnp.zeros((depth_z - 8 - span, z.shape[1]), F32)
        for at in range(0, taps_a * LANES, 2 * LANES):
            cols = pl.ds(at, 2 * LANES)
            z[n * depth_z + 8 : n * depth_z + 8 + span, cols] = (
                dot(left_h, bh_ref[:, cols]) + dot(left_h, bl_ref[:, cols]) + dot(left_l, bh_ref[:, cols])
            )
    q16[...] = jnp.zeros_like(q16)
    q16[:rows] = q_ref[0]
    dq = jnp.zeros((rows_up, depth), F32)
    for n in range(blocks):
        total = None
        for a in range(taps_a):
            start = n * depth_z + 8 - (taps_a - 1) + a
            term = z[start : start + rows_up, a * LANES : (a + 1) * LANES]
            total = term if total is None else total + term
        key = n * LANES + iota(total.shape, 1)
        pos = first - (taps_a - 1) + iota(total.shape, 0)
        ds = jnp.where(key <= pos, total, 0.0)
        here = slice(n * LANES, (n + 1) * LANES)
        dq = dq + dot(ds.astype(BF16), k_ref[0, here])
        dk_ref[0, here] = (scale * dot(ds.T.astype(BF16), q16[...])).astype(BF16)
    dq_ref[0] = (scale * dq)[:rows].astype(BF16)
    dv_ref[0] = dot(pt_ref[...], do)[HALF : HALF + keys].astype(BF16)


def exchange(x, axis):
    n = lax.axis_size(axis)
    return [x] + [lax.ppermute(x, axis, [(i, (i + s) % n) for i in range(n)]) for s in range(1, n)]


def shards(queries, keys, values, conv_kernel, span_start, out_grad, proj_weight, moment_one, moment_two):
    _, rows, depth = queries.shape
    key_count = keys.shape[1]
    _, taps_a, taps_b = conv_kernel.shape
    span = out_grad.shape[1]
    blocks = key_count // LANES
    rows_up = up_to(rows, 16)
    padded = key_count + LANES
    edge = up_to(HALF + (taps_b - 1) // 2, 16)
    wide = key_count + 2 * edge
    group_count = lax.axis_size("dp")
    vmem = pltpu.CompilerParams(vmem_limit_bytes=40 * 2**20)
    smem = pl.BlockSpec(memory_space=pltpu.SMEM)
    whole = pl.BlockSpec(memory_space=pltpu.VMEM)

    upstream = lax.all_gather(out_grad[0], "tensor", axis=1, tiled=True)
    proj_all = lax.all_gather(proj_weight.astype(BF16), "dp", axis=1, tiled=True)

    p, pt, attended, xth, xtl, bh, bl = pl.pallas_call(
        forward,
        out_shape=(
            jax.ShapeDtypeStruct((span, padded), F32),
            jax.ShapeDtypeStruct((padded, span), BF16),
            jax.ShapeDtypeStruct((span, depth), BF16),
            jax.ShapeDtypeStruct((wide, taps_a * span), BF16),
            jax.ShapeDtypeStruct((wide, taps_a * span), BF16),
            jax.ShapeDtypeStruct((2 * LANES, taps_a * LANES), BF16),
            jax.ShapeDtypeStruct((2 * LANES, taps_a * LANES), BF16),
        ),
        in_specs=[smem, smem, whole, whole, whole],
        out_specs=(whole,) * 7,
        scratch_shapes=[
            pltpu.VMEM((rows_up, depth), F32),
            pltpu.VMEM((2 * LANES, taps_a * LANES), BF16),
            pltpu.VMEM((2 * LANES, taps_a * LANES), BF16),
            pltpu.VMEM(((blocks + 1) * rows_up, 2 * LANES), BF16),
            pltpu.VMEM(((blocks + 1) * rows_up, 2 * LANES), BF16),
            pltpu.VMEM(((blocks + 1) * rows_up, taps_a * LANES), F32),
            pltpu.VMEM((wide, depth), BF16),
            pltpu.VMEM((padded, depth), BF16),
        ],
        compiler_params=vmem,
        name="attention_forward",
    )(span_start, conv_kernel, queries, keys, values)

    query_grad, key_grad, value_grad, taps = pl.pallas_call(
        functools.partial(backward, taps_b),
        out_shape=(
            jax.ShapeDtypeStruct(queries.shape, BF16),
            jax.ShapeDtypeStruct(keys.shape, BF16),
            jax.ShapeDtypeStruct(values.shape, BF16),
            jax.ShapeDtypeStruct((taps_a, LANES), F32),
        ),
        in_specs=[smem] + [whole] * 11,
        out_specs=(whole,) * 4,
        scratch_shapes=[
            pltpu.VMEM((padded, depth), BF16),
            pltpu.VMEM(((blocks + 1) * span, LANES), BF16),
            pltpu.VMEM(((blocks + 1) * span, LANES), BF16),
            pltpu.VMEM((blocks * (span + 32), taps_a * LANES), F32),
            pltpu.VMEM((rows_up, depth), BF16),
        ],
        compiler_params=vmem,
        name="attention_backward",
    )(span_start, upstream, proj_all, p, pt, xth, xtl, bh, bl, queries, keys, values)

    me = lax.axis_index("dp")
    share = proj_weight.shape[1]
    part = dot(attended, upstream, ((0,), (0,)))
    grad_proj = lax.dynamic_slice_in_dim(part, me * share, share, axis=1)
    for s in range(1, group_count):
        owner = lax.rem(me + s, group_count)
        piece = lax.dynamic_slice_in_dim(part, owner * share, share, axis=1)
        grad_proj = grad_proj + lax.ppermute(piece, "dp", [(i, (i + s) % group_count) for i in range(group_count)])
    grad_proj = grad_proj / float(group_count)
    half = (taps_b - 1) // 2
    last = up_to(LANES + edge - HALF + half, 16) - 1 - (edge - HALF - half) - LANES
    taps = sum(exchange(taps, "dp"))[:, last - taps_b + 1 : last + 1][:, ::-1]
    kernel_total = taps / float(group_count * span)
    moment_one_new = beta_one * moment_one + (1.0 - beta_one) * grad_proj
    moment_two_new = beta_two * moment_two + (1.0 - beta_two) * grad_proj * grad_proj
    first_hat = moment_one_new / bias_one
    second_hat = moment_two_new / bias_two
    proj_new = proj_weight - learn_rate * (first_hat / (jnp.sqrt(second_hat) + adam_eps) + decay_rate * proj_weight)
    return (query_grad, key_grad, value_grad, kernel_total[None], proj_new, moment_one_new, moment_two_new)


def solution(mesh):
    heads, rows_of, blocks_of = P("dp", None, "tensor"), P("tensor", None, None), P("tensor", "dp")
    return jax.shard_map(
        shards,
        mesh=mesh,
        in_specs=(heads, heads, heads, rows_of, P("dp"), heads, blocks_of, blocks_of, blocks_of),
        out_specs=(heads, heads, heads, rows_of, blocks_of, blocks_of, blocks_of),
        check_vma=False,
    )
```

time: 224 us -> 72.5 us (0.32)
  other arithmetic: 117 us -> 2.11 us
  local copies, waits for them, and re-layouts: 47.5 us -> 9.89 us
  waiting for transfers between devices: 0.02 us -> 15.9 us
  between operations: 14.8 us -> 1.38 us
  blocking collectives: 37.4 us -> 25.2 us
  Pallas kernels: 0 us -> 10.1 us
  starting transfers between devices: 0.04 us -> 7.31 us
  matrix products: 5.06 us -> 0.24 us
    convert_element_type x2 -> x0, other arithmetic: 52.9 us -> none  [the longest x1 52 us: shards(): grad_scores = jnp.where(visible, grad_masked, 0.0).astype(jnp.bfloat16)]
    reduce_max x1 -> x0, other arithmetic: 50.3 us -> none  [shards(): jnp.max(jnp.where(live_mask, mixed_scores, -jnp.inf), axis=1, keepdims=True)]
    another operation x1 -> x0, local copies, waits for them, and re-layouts: 42.4 us -> none  [shards(): kernel_local = jnp.stack(kernel_terms).reshape(conv_rows, conv_cols)]
    ppermute x0 -> x6, waiting for transfers between devices: none -> 15.9 us  [the longest x3 11.7 us: shards(): lax.ppermute(piece, 'dp', [(i, (i + s) % group_count) for i in range(grou...]
    psum x1 -> x0, blocking collectives: 12.4 us -> none  [shards(): kernel_total = lax.psum(kernel_local, 'dp') / float(group_count * span_len)]
    reduce_sum x5 -> x0, other arithmetic: 11.9 us -> none  [the longest x4 11.6 us: shards(): jnp.sum(grad_mixed * padded[row_first:row_first + span_len, tap_col:tap_c...]
    pallas_call x0 -> x2, Pallas kernels: none -> 10.1 us  [the longest x1 5.44 us: shards(): pl.pallas_call(forward, out_shape=(jax.ShapeDtypeStruct((span, padded), F...]
    ppermute x0 -> x6, starting transfers between devices: none -> 7.31 us  [the longest x3 4.63 us: shards(): lax.ppermute(piece, 'dp', [(i, (i + s) % group_count) for i in range(grou...]
  transfers between devices with their start and end apart: 1 -> 6, of which waited for: 0 -> 6; matrix products, arithmetic and copies ran while one was open for 49% -> 0% of each run, Pallas kernels for 0% -> 0%
where the time goes in v1:
time: 72.5 us; the launch traced here: 72.1 us
  blocking collectives  25.2 us (35%)
  waiting for transfers between devices  15.9 us (22%)
  Pallas kernels  10.1 us (14%)
  local copies, waits for them, and re-layouts  9.89 us (14%)
  starting transfers between devices  7.31 us (10%)
  other arithmetic  2.11 us (3%)
  between operations  1.38 us (2%)
    all_gather x1, blocking collectives, shards(): lax.all_gather(proj_weight.astype(BF16), 'dp', axis=1, tiled=True)  14.2 us
    ppermute x3, waiting for transfers between devices, shards(): lax.ppermute(piece, 'dp', [(i, (i + s) % group_count) for i in range(grou...  11.7 us
    all_gather x1, blocking collectives, shards(): upstream = lax.all_gather(out_grad[0], 'tensor', axis=1, tiled=True)  11 us
    unnamed x28, local copies, waits for them, and re-layouts  8.99 us
    pallas_call x1, Pallas kernels, shards(): pl.pallas_call(forward, out_shape=(jax.ShapeDtypeStruct((span, padded), F...  5.44 us
    pallas_call x1, Pallas kernels, shards(): pl.pallas_call(functools.partial(backward, taps_b), out_shape=(jax.ShapeD...  4.7 us
    ppermute x3, starting transfers between devices, shards(): lax.ppermute(piece, 'dp', [(i, (i + s) % group_count) for i in range(grou...  4.63 us
    ppermute x3, waiting for transfers between devices, exchange(): lax.ppermute(x, axis, [(i, (i + s) % n) for i in range(n)])  4.12 us
  transfers between devices with their start and end apart: 6, of which 6 were waited for; matrix products, arithmetic and copies ran while one was open for 0% of the time, Pallas kernels for 0%

profile of v1, /device:TPU:0, one launch (start us, length us, event | category | flops | bytes accessed | tf_op | source)
XLA Modules:
  0.0 72.1 jit_solution(14793213451565240239)
XLA Ops:
  1.3 0.7 copy.16.kernel_ref
  2.0 11.0 %all-gather = bf16[1,128,1024]{2,1,0:T(8,128)(2,1)S(1)} all-gather(bf16[1,128,128]{2,1,0:T(8,128)(2,1)} %param.14), channel_id=2, replica_groups=mesh['dp'=4,'tensor'=8] {'tensor'}, dimensions={2}, use_global_device_ids=true | all-gather | bytes 294912 | tf_op jit(solution)/shard_map/all_gather | solution.py:224
  13.0 0.0 copy-start.2
  13.0 0.9 %copy-done.2 = bf16[1,1024,128]{2,1,0:T(8,128)(2,1)S(1)} copy-done((bf16[1,1024,128]{2,1,0:T(8,128)(2,1)S(1)}, bf16[1,1024,128]{2,1,0:T(8,128)(2,1)}, u32[]{:S(2)}) %copy-start.2) | copy-done | bytes 262168
  14.0 0.0 copy-start.4
  14.0 0.9 %copy-done.4 = bf16[1,1024,128]{2,1,0:T(8,128)(2,1)S(1)} copy-done((bf16[1,1024,128]{2,1,0:T(8,128)(2,1)S(1)}, bf16[1,1024,128]{2,1,0:T(8,128)(2,1)}, u32[]{:S(2)}) %copy-start.4) | copy-done | bytes 262168
  14.9 0.0 copy-start.10
  14.9 0.8 %copy-done.10 = bf16[1,133,128]{2,1,0:T(8,128)(2,1)S(1)} copy-done((bf16[1,133,128]{2,1,0:T(8,128)(2,1)S(1)}, bf16[1,133,128]{2,1,0:T(8,128)(2,1)}, u32[]{:S(2)}) %copy-start.10) | copy-done | bytes 34072
  15.7 0.0 copy-start.3
  15.7 0.0 copy-start.5
  15.7 0.0 copy-start.11
  15.7 5.4 %attention_forward.1 = (f32[128,1152]{1,0:T(8,128)S(1)}, bf16[1152,128]{1,0:T(8,128)(2,1)S(1)}, bf16[128,128]{1,0:T(8,128)(2,1)S(1)}, bf16[1184,768]{1,0:T(8,128...) custom-call(s32[1]{0:T(128)S(6)} %copy.18.first_ref, ...), custom_call_target="tpu_custom_call" | custom-call | tf_op jit(solution)/shard_map/attention_forward/pallas_call | solution.py:227
  21.1 0.0 copy-start
  21.1 1.2 %copy-done = bf16[1184,768]{1,0:T(8,128)(2,1)} copy-done((bf16[1184,768]{1,0:T(8,128)(2,1)}, bf16[1184,768]{1,0:T(8,128)(2,1)S(1)}, u32[]{:S(2)}) %copy-start) | copy-done | bytes 1818648
  22.4 0.0 copy-start.6
  22.4 0.8 %copy-done.6 = bf16[256,768]{1,0:T(8,128)(2,1)} copy-done((bf16[256,768]{1,0:T(8,128)(2,1)}, bf16[256,768]{1,0:T(8,128)(2,1)S(1)}, u32[]{:S(2)}) %copy-start.6) | copy-done | bytes 393240
  23.1 0.0 copy-start.8
  23.1 0.8 %copy-done.8 = bf16[256,768]{1,0:T(8,128)(2,1)} copy-done((bf16[256,768]{1,0:T(8,128)(2,1)}, bf16[256,768]{1,0:T(8,128)(2,1)S(1)}, u32[]{:S(2)}) %copy-start.8) | copy-done | bytes 393240
  23.9 0.2 fusion
  24.1 0.0 copy-start.12
  24.1 0.8 %copy-done.12 = f32[128,1024]{1,0:T(8,128)} copy-done((f32[128,1024]{1,0:T(8,128)}, f32[128,1024]{1,0:T(8,128)S(1)}, u32[]{:S(2)}) %copy-start.12) | copy-done | bytes 524312
  24.9 0.8 %constant_dynamic-slice_fusion.2 = (f32[128,256]{1,0:T(8,128)}, f32[128,256]{1,0:T(8,128)}, f32[128,256]{1,0:T(8,128)}) fusion(f32[128,1024]{1,0:T(8,128)S(1)} %fusion, s32[]{:T(128)S(6)} %select_n.13, s32[]{:T(128)S(6)} %select_n.15, s32[]{:T(128)S(6)} %select_n.14), kind=kLoop, calls=%fused_computation.8 | loop fusion | bytes 786444 | tf_op jit(solution)/shard_map/dynamic_slice | solution.py:281
  25.7 1.6 %collective-permute-start.3 = (f32[128,256]{1,0:T(8,128)}, f32[128,256]{1,0:T(8,128)}, u32[]{:S(2)}, u32[]{:S(2)}) collective-permute-start(f32[128,256]{1,0:T(8,128)} %get-tuple-element.39), channel_id=1, source_target_pairs={{0,8},{8,16},{16,24},{24,0},{1,9},{9,17},{17,25},{25,1},{2,10},{10... | collective-permute-start | bytes 393224 | tf_op jit(solution)/shard_map/ppermute | solution.py:282
  27.3 2.2 %collective-permute-start.5 = (f32[128,256]{1,0:T(8,128)}, f32[128,256]{1,0:T(8,128)}, u32[]{:S(2)}, u32[]{:S(2)}) collective-permute-start(f32[128,256]{1,0:T(8,128)} %get-tuple-element.40), channel_id=1, source_target_pairs={{0,24},{8,0},{16,8},{24,16},{1,25},{9,1},{17,9},{25,17},{2,26},{10... | collective-permute-start | bytes 393224 | tf_op jit(solution)/shard_map/ppermute | solution.py:282
  29.5 0.8 %collective-permute-start.4 = (f32[128,256]{1,0:T(8,128)}, f32[128,256]{1,0:T(8,128)}, u32[]{:S(2)}, u32[]{:S(2)}) collective-permute-start(f32[128,256]{1,0:T(8,128)} %get-tuple-element.41), channel_id=1, source_target_pairs={{0,16},{8,24},{16,0},{24,8},{1,17},{9,25},{17,1},{25,9},{2,18},{10... | collective-permute-start | bytes 393224 | tf_op jit(solution)/shard_map/ppermute | solution.py:282
  30.3 0.0 copy-start.7
  30.3 3.8 %collective-permute-done.3 = f32[128,256]{1,0:T(8,128)} collective-permute-done((f32[128,256]{1,0:T(8,128)}, f32[128,256]{1,0:T(8,128)}, u32[]{:S(2)}, u32[]{:S(2)}) %collective-permute-start.3) | collective-permute-done | bytes 131104 | tf_op jit(solution)/shard_map/ppermute | solution.py:282
  34.2 1.7 %collective-permute-done.5 = f32[128,256]{1,0:T(8,128)} collective-permute-done((f32[128,256]{1,0:T(8,128)}, f32[128,256]{1,0:T(8,128)}, u32[]{:S(2)}, u32[]{:S(2)}) %collective-permute-start.5) | collective-permute-done | bytes 131104 | tf_op jit(solution)/shard_map/ppermute | solution.py:282
  35.9 6.2 %collective-permute-done.4 = f32[128,256]{1,0:T(8,128)} collective-permute-done((f32[128,256]{1,0:T(8,128)}, f32[128,256]{1,0:T(8,128)}, u32[]{:S(2)}, u32[]{:S(2)}) %collective-permute-start.4) | collective-permute-done | bytes 131104 | tf_op jit(solution)/shard_map/ppermute | solution.py:282
  42.0 2.1 %multiply_subtract_fusion = (f32[128,256]{1,0:T(8,128)}, f32[128,256]{1,0:T(8,128)}, f32[128,256]{1,0:T(8,128)}, bf16[128,256]{1,0:T(8,128)(2,1)S(1)}) fusion(f32[128,256]{1,0:T(8,128)} %param.15, f32[128,256]{1,0:T(8,128)} %param.16, f32[128,256]{1,0:T(8,128)} %param.17, f32[128,256]{1,0:T(8,128)} %collective-permute-done.5, ...), kind=kLoop, calls=%fused_computation | loop fusion | flops 655360 | bytes 1376260 | tf_op jit(solution)/shard_map/sub | solution.py:292
  44.1 14.2 %all_gather.7.w_ref = bf16[128,1024]{1,0:T(8,128)(2,1)S(1)} all-gather(bf16[128,256]{1,0:T(8,128)(2,1)S(1)} %get-tuple-element.42), channel_id=1, replica_groups=mesh['dp'=4,'tensor'=8] {'dp'}, dimensions={1}, use_global_device_ids=true | all-gather | bytes 327680 | tf_op jit(solution)/shard_map/all_gather | solution.py:225
  58.3 0.0 copy-done.3
  58.3 0.0 copy-done.5
  58.3 0.0 copy-done.11
  58.3 0.0 copy-done.7
  58.3 0.0 copy-done.9
  58.3 0.0 copy-start.1
  58.3 1.5 %copy-done.1 = bf16[1184,768]{1,0:T(8,128)(2,1)S(1)} copy-done((bf16[1184,768]{1,0:T(8,128)(2,1)S(1)}, bf16[1184,768]{1,0:T(8,128)(2,1)}, u32[]{:S(2)}) %copy-start.1) | copy-done | bytes 1818648
  59.8 4.7 %attention_backward.1 = (bf16[1,133,128]{2,1,0:T(8,128)(2,1)}, bf16[1,1024,128]{2,1,0:T(8,128)(2,1)}, bf16[1,1024,128]{2,1,0:T(8,128)(2,1)}, f32[6,128]{1,0:T(8,128)S(1)}) custom-call(s32[1]{0:T(128)S(6)} %copy.18.first_ref, bf16[128,1024]{1,0:T(8,128)(2,1)S(1)} %bitcast.6, bf16[128,1024]{1,0:T(8,128)(2,1)S(1)} %all_gather.7.w_ref, ...), custom_call_target="tpu_custom_call" | custom-call | tf_op jit(solution)/shard_map/attention_backward/pallas_call | solution.py:254
  64.5 1.4 %collective-permute-start.2 = (f32[6,128]{1,0:T(8,128)S(1)}, f32[6,128]{1,0:T(8,128)S(1)}, u32[]{:S(2)}, u32[]{:S(2)}) collective-permute-start(f32[6,128]{1,0:T(8,128)S(1)} %get-tuple-element.27), channel_id=1, source_target_pairs={{0,24},{8,0},{16,8},{24,16},{1,25},{9,1},{17,9},{25,17},{2,26},{10... | collective-permute-start | bytes 9224 | tf_op jit(solution)/shard_map/ppermute | solution.py:206
  65.9 0.0 collective-permute-start.1
  65.9 1.3 %collective-permute-start = (f32[6,128]{1,0:T(8,128)S(1)}, f32[6,128]{1,0:T(8,128)S(1)}, u32[]{:S(2)}, u32[]{:S(2)}) collective-permute-start(f32[6,128]{1,0:T(8,128)S(1)} %get-tuple-element.27), channel_id=1, source_target_pairs={{0,8},{8,16},{16,24},{24,0},{1,9},{9,17},{17,25},{25,1},{2,10},{10... | collective-permute-start | bytes 9224 | tf_op jit(solution)/shard_map/ppermute | solution.py:206
  67.2 0.9 %collective-permute-done.2 = f32[6,128]{1,0:T(8,128)S(1)} collective-permute-done((f32[6,128]{1,0:T(8,128)S(1)}, f32[6,128]{1,0:T(8,128)S(1)}, u32[]{:S(2)}, u32[]{:S(2)}) %collective-permute-start.2) | collective-permute-done | bytes 3104 | tf_op jit(solution)/shard_map/ppermute | solution.py:206
  68.1 2.3 %collective-permute-done.1 = f32[6,128]{1,0:T(8,128)S(1)} collective-permute-done((f32[6,128]{1,0:T(8,128)S(1)}, f32[6,128]{1,0:T(8,128)S(1)}, u32[]{:S(2)}, u32[]{:S(2)}) %collective-permute-start.1) | collective-permute-done | bytes 3104 | tf_op jit(solution)/shard_map/ppermute | solution.py:206
  70.4 0.9 %collective-permute-done = f32[6,128]{1,0:T(8,128)S(1)} collective-permute-done((f32[6,128]{1,0:T(8,128)S(1)}, f32[6,128]{1,0:T(8,128)S(1)}, u32[]{:S(2)}, u32[]{:S(2)}) %collective-permute-start) | collective-permute-done | bytes 3104 | tf_op jit(solution)/shard_map/ppermute | solution.py:206
  71.3 0.1 slice.3
  71.4 0.1 rev.3
  71.5 0.6 copy.17
  (3 shorter events, 0.0 us)
Async XLA Ops:
  13.0 0.9 %copy-start.2 = (bf16[1,1024,128]{2,1,0:T(8,128)(2,1)S(1)}, bf16[1,1024,128]{2,1,0:T(8,128)(2,1)}, u32[]{:S(2)}) copy-start(bf16[1,1024,128]{2,1,0:T(8,128)(2,1)} %k_ref.3) | copy-start | bytes 786436
  14.0 0.9 %copy-start.4 = (bf16[1,1024,128]{2,1,0:T(8,128)(2,1)S(1)}, bf16[1,1024,128]{2,1,0:T(8,128)(2,1)}, u32[]{:S(2)}) copy-start(bf16[1,1024,128]{2,1,0:T(8,128)(2,1)} %v_ref.3) | copy-start | bytes 786436
  14.9 0.8 %copy-start.10 = (bf16[1,133,128]{2,1,0:T(8,128)(2,1)S(1)}, bf16[1,133,128]{2,1,0:T(8,128)(2,1)}, u32[]{:S(2)}) copy-start(bf16[1,133,128]{2,1,0:T(8,128)(2,1)} %q_ref.3) | copy-start | bytes 102148
  15.7 42.6 %copy-start.3 = (bf16[1,1024,128]{2,1,0:T(8,128)(2,1)S(1)}, bf16[1,1024,128]{2,1,0:T(8,128)(2,1)}, u32[]{:S(2)}) copy-start(bf16[1,1024,128]{2,1,0:T(8,128)(2,1)} %k_ref.3) | copy-start | bytes 786436
  15.7 42.6 %copy-start.5 = (bf16[1,1024,128]{2,1,0:T(8,128)(2,1)S(1)}, bf16[1,1024,128]{2,1,0:T(8,128)(2,1)}, u32[]{:S(2)}) copy-start(bf16[1,1024,128]{2,1,0:T(8,128)(2,1)} %v_ref.3) | copy-start | bytes 786436
  15.7 42.6 %copy-start.11 = (bf16[1,133,128]{2,1,0:T(8,128)(2,1)S(1)}, bf16[1,133,128]{2,1,0:T(8,128)(2,1)}, u32[]{:S(2)}) copy-start(bf16[1,133,128]{2,1,0:T(8,128)(2,1)} %q_ref.3) | copy-start | bytes 102148
  21.1 1.3 %copy-start = (bf16[1184,768]{1,0:T(8,128)(2,1)}, bf16[1184,768]{1,0:T(8,128)(2,1)S(1)}, u32[]{:S(2)}) copy-start(bf16[1184,768]{1,0:T(8,128)(2,1)S(1)} %get-tuple-element.21.xtl_ref) | copy-start | bytes 5455876
  22.4 0.8 %copy-start.6 = (bf16[256,768]{1,0:T(8,128)(2,1)}, bf16[256,768]{1,0:T(8,128)(2,1)S(1)}, u32[]{:S(2)}) copy-start(bf16[256,768]{1,0:T(8,128)(2,1)S(1)} %get-tuple-element.22.bh_ref) | copy-start | bytes 1179652
  23.1 0.8 %copy-start.8 = (bf16[256,768]{1,0:T(8,128)(2,1)}, bf16[256,768]{1,0:T(8,128)(2,1)S(1)}, u32[]{:S(2)}) copy-start(bf16[256,768]{1,0:T(8,128)(2,1)S(1)} %get-tuple-element.23.bl_ref) | copy-start | bytes 1179652
  24.1 0.8 %copy-start.12 = (f32[128,1024]{1,0:T(8,128)}, f32[128,1024]{1,0:T(8,128)S(1)}, u32[]{:S(2)}) copy-start(f32[128,1024]{1,0:T(8,128)S(1)} %fusion) | copy-start | bytes 1572868
  25.7 8.5 %collective-permute-start.3 = (f32[128,256]{1,0:T(8,128)}, f32[128,256]{1,0:T(8,128)}, u32[]{:S(2)}, u32[]{:S(2)}) collective-permute-start(f32[128,256]{1,0:T(8,128)} %get-tuple-element.39), channel_id=1, source_target_pairs={{0,8},{8,16},{16,24},{24,0},{1,9},{9,17},{17,25},{25,1},{2,10},{10... | collective-permute-start | bytes 393224 | tf_op jit(solution)/shard_map/ppermute | solution.py:282
  27.3 8.6 %collective-permute-start.5 = (f32[128,256]{1,0:T(8,128)}, f32[128,256]{1,0:T(8,128)}, u32[]{:S(2)}, u32[]{:S(2)}) collective-permute-start(f32[128,256]{1,0:T(8,128)} %get-tuple-element.40), channel_id=1, source_target_pairs={{0,24},{8,0},{16,8},{24,16},{1,25},{9,1},{17,9},{25,17},{2,26},{10... | collective-permute-start | bytes 393224 | tf_op jit(solution)/shard_map/ppermute | solution.py:282
  29.5 12.5 %collective-permute-start.4 = (f32[128,256]{1,0:T(8,128)}, f32[128,256]{1,0:T(8,128)}, u32[]{:S(2)}, u32[]{:S(2)}) collective-permute-start(f32[128,256]{1,0:T(8,128)} %get-tuple-element.41), channel_id=1, source_target_pairs={{0,16},{8,24},{16,0},{24,8},{1,17},{9,25},{17,1},{25,9},{2,18},{10... | collective-permute-start | bytes 393224 | tf_op jit(solution)/shard_map/ppermute | solution.py:282
  30.3 28.0 %copy-start.7 = (bf16[256,768]{1,0:T(8,128)(2,1)S(1)}, bf16[256,768]{1,0:T(8,128)(2,1)}, u32[]{:S(2)}) copy-start(bf16[256,768]{1,0:T(8,128)(2,1)} %copy-done.6) | copy-start | bytes 1179652
  30.3 28.0 %copy-start.9 = (bf16[256,768]{1,0:T(8,128)(2,1)S(1)}, bf16[256,768]{1,0:T(8,128)(2,1)}, u32[]{:S(2)}) copy-start(bf16[256,768]{1,0:T(8,128)(2,1)} %copy-done.8) | copy-start | bytes 1179652
  58.3 1.5 %copy-start.1 = (bf16[1184,768]{1,0:T(8,128)(2,1)S(1)}, bf16[1184,768]{1,0:T(8,128)(2,1)}, u32[]{:S(2)}) copy-start(bf16[1184,768]{1,0:T(8,128)(2,1)} %copy-done) | copy-start | bytes 5455876
  64.5 3.6 %collective-permute-start.2 = (f32[6,128]{1,0:T(8,128)S(1)}, f32[6,128]{1,0:T(8,128)S(1)}, u32[]{:S(2)}, u32[]{:S(2)}) collective-permute-start(f32[6,128]{1,0:T(8,128)S(1)} %get-tuple-element.27), channel_id=1, source_target_pairs={{0,24},{8,0},{16,8},{24,16},{1,25},{9,1},{17,9},{25,17},{2,26},{10... | collective-permute-start | bytes 9224 | tf_op jit(solution)/shard_map/ppermute | solution.py:206
  65.9 4.5 %collective-permute-start.1 = (f32[6,128]{1,0:T(8,128)S(1)}, f32[6,128]{1,0:T(8,128)S(1)}, u32[]{:S(2)}, u32[]{:S(2)}) collective-permute-start(f32[6,128]{1,0:T(8,128)S(1)} %get-tuple-element.27), channel_id=1, source_target_pairs={{0,16},{8,24},{16,0},{24,8},{1,17},{9,25},{17,1},{25,9},{2,18},{10... | collective-permute-start | bytes 9224 | tf_op jit(solution)/shard_map/ppermute | solution.py:206
  65.9 5.4 %collective-permute-start = (f32[6,128]{1,0:T(8,128)S(1)}, f32[6,128]{1,0:T(8,128)S(1)}, u32[]{:S(2)}, u32[]{:S(2)}) collective-permute-start(f32[6,128]{1,0:T(8,128)S(1)} %get-tuple-element.27), channel_id=1, source_target_pairs={{0,8},{8,16},{16,24},{24,0},{1,9},{9,17},{17,25},{25,1},{2,10},{10... | collective-permute-start | bytes 9224 | tf_op jit(solution)/shard_map/ppermute | solution.py:206

commit v2 on v1

v2 whole, which is shorter than its diff:
```python
import functools
import math

import jax
import jax.numpy as jnp
from jax import lax
from jax.experimental import pallas as pl
from jax.experimental.pallas import tpu as pltpu
from jax.sharding import PartitionSpec as P

beta_one = 0.9
beta_two = 0.95
learn_rate = 0.01
decay_rate = 0.1
adam_eps = 1e-08
bias_one = 1.0 - 0.9**10
bias_two = 1.0 - 0.95**10

LANES = 128
HALF = LANES // 2
F32 = jnp.float32
BF16 = jnp.bfloat16


def dot(left, right, dims=((1,), (0,))):
    return lax.dot_general(left, right, (dims, ((), ())), preferred_element_type=F32)


def split(x):
    high = x.astype(BF16)
    return high, (x - high.astype(F32)).astype(BF16)


def up_to(n, multiple):
    return -(-n // multiple) * multiple


def iota(shape, axis):
    return lax.broadcasted_iota(jnp.int32, shape, axis)


def bands(kernel_ref, flipped):
    taps_a, _, taps_b = kernel_ref.shape
    half = (taps_b - 1) // 2
    place = iota((2 * LANES, LANES), 0) - iota((2 * LANES, LANES), 1) - (HALF - half)
    out = [jnp.zeros((2 * LANES, LANES), F32) for _ in range(taps_a)]
    for b in range(taps_b):
        here = place == (taps_b - 1 - b if flipped else b)
        for a in range(taps_a):
            out[a] = jnp.where(here, kernel_ref[a, 0, b], out[a])
    return out


def forward(
    first_ref, kernel_ref, q_hbm, k_hbm, v_hbm,
    p_ref, pt_ref, o_ref, xth_ref, xtl_ref, bh_ref, bl_ref, vpad, q16,
    q_in, k_in, v_in, q32, fh, fl, xh, xl, y, kpad, sems,
):
    taps_a, _, taps_b = kernel_ref.shape
    rows, depth = q_in.shape
    keys = k_in.shape[0]
    span = rows - taps_a + 1
    rows_up = q32.shape[0]
    blocks = keys // LANES
    scale = 1.0 / math.sqrt(depth)
    first = first_ref[0]
    copies = [
        pltpu.make_async_copy(src.at[0], dst, sems.at[n])
        for n, (src, dst) in enumerate(((q_hbm, q_in), (k_hbm, k_in), (v_hbm, v_in)))
    ]
    for copy in copies:
        copy.start()

    for a, (f, t) in enumerate(zip(bands(kernel_ref, False), bands(kernel_ref, True), strict=True)):
        cols = pl.ds(a * LANES, LANES)
        fh[:, cols], fl[:, cols] = split(f)
        bh_ref[:, cols], bl_ref[:, cols] = split(t)
    q32[...] = jnp.zeros_like(q32)
    vpad[...] = jnp.zeros_like(vpad)
    kpad[...] = jnp.zeros_like(kpad)
    for copy in copies:
        copy.wait()
    q32[:rows] = q_in[...].astype(F32)
    q_all = q32[...].astype(BF16)
    q16[...] = q_all
    vpad[HALF : HALF + keys] = v_in[...]

    zero = jnp.zeros((rows_up, LANES), BF16)
    for ref in (xh, xl):
        ref[:rows_up, :LANES] = zero
        ref[blocks * rows_up :, LANES:] = zero
    for n in range(blocks):
        x = dot(q_all, k_in[n * LANES : (n + 1) * LANES], ((1,), (1,))) * scale
        key = n * LANES + iota(x.shape, 1)
        pos = first - (taps_a - 1) + iota(x.shape, 0)
        high, low = split(jnp.where(key <= pos, x, 0.0))
        for ref, part in ((xh, high), (xl, low)):
            ref[n * rows_up : (n + 1) * rows_up, LANES:] = part
            ref[(n + 1) * rows_up : (n + 2) * rows_up, :LANES] = part

    for at in range(0, taps_a * LANES, 2 * LANES):
        cols = pl.ds(at, 2 * LANES)
        y[:, cols] = dot(xh[...], fh[:, cols]) + dot(xh[...], fl[:, cols]) + dot(xl[...], fh[:, cols])
    mixed = []
    for w in range(blocks + 1):
        total = None
        for a in range(taps_a):
            start = w * rows_up + taps_a - 1 - a
            term = y[start : start + span, a * LANES : (a + 1) * LANES]
            total = term if total is None else total + term
        mixed.append(total)
    c = jnp.concatenate(mixed, axis=1)
    key = iota(c.shape, 1) - HALF
    live = (key >= 0) & (key <= first + iota(c.shape, 0))
    top = jnp.max(jnp.where(live, c, -jnp.inf), axis=1, keepdims=True)
    terms = jnp.where(live, jnp.exp(c - top), 0.0)
    p = terms / jnp.sum(terms, axis=1, keepdims=True)
    p_ref[...] = p
    pt_ref[...] = p.T.astype(BF16)
    o_ref[...] = dot(p.astype(BF16), vpad[...]).astype(BF16)

    edge = (kpad.shape[0] - keys) // 2
    flip = (iota((LANES, LANES), 0) + iota((LANES, LANES), 1) == LANES - 1).astype(F32).astype(BF16)
    for n in range(blocks):
        kpad[edge + n * LANES : edge + (n + 1) * LANES] = dot(
            flip, k_in[keys - (n + 1) * LANES : keys - n * LANES]
        ).astype(BF16)
    for a in range(taps_a):
        start = taps_a - 1 - a
        xt = dot(kpad[...], q32[start : start + span].astype(BF16), ((1,), (1,))) * scale
        key = keys - 1 + edge - iota(xt.shape, 0)
        pos = first - a + iota(xt.shape, 1)
        cols = pl.ds(a * LANES, LANES)
        xth_ref[:, cols], xtl_ref[:, cols] = split(jnp.where(key <= pos, xt, 0.0))


def backward_scores(taps_b, up_places, w_places, payloads, by_distance, *refs):
    n_up, n_w = len({p[0] for p in up_places}), len({p[0] for p in w_places})
    up_refs, w_refs, refs = refs[:n_up], refs[n_up : n_up + n_w], refs[n_up + n_w :]
    p_ref, vpad, xth_ref, xtl_ref, o_ref, do_ref, ch, cl = refs[:8]
    out_refs, (up, w) = refs[8 : 8 + payloads], refs[8 + payloads :]
    span = p_ref.shape[0]
    keys = vpad.shape[0] - LANES
    taps_a = xth_ref.shape[1] // span
    blocks = keys // LANES
    half = (taps_b - 1) // 2
    edge = (xth_ref.shape[0] - keys) // 2

    for refs_in, places, axis, whole in ((up_refs, up_places, "tensor", up), (w_refs, w_places, "dp", w)):
        me = lax.axis_index(axis)
        for n, part, shift, at in places:
            block = refs_in[n][part]
            width = block.shape[1]
            spot = at if shift is None else lax.bitwise_xor(me, shift)
            whole[:, pl.ds(pl.multiple_of(spot * width, width), width)] = block
    do = dot(up[...], w[...], ((1,), (1,))).astype(BF16)
    do_ref[...] = do
    dp = dot(do, vpad[...], ((1,), (1,)))
    p = p_ref[...]
    high, low = split(p * (dp - jnp.sum(p * dp, axis=1, keepdims=True)))
    for n in range(blocks + 1):
        cols = slice(n * LANES, (n + 1) * LANES)
        here = slice(n * span, (n + 1) * span)
        ch[here] = high[:, cols]
        cl[here] = low[:, cols]

    window = up_to(LANES + edge - HALF + half, 16)
    right = jnp.concatenate([ch[...], cl[...]], axis=1)
    spot = window - 1 - (edge - HALF - half) - iota((window, LANES), 0) - iota((window, LANES), 1)
    wanted = (spot >= 0) & (spot < taps_b)
    sums = []
    for a in range(taps_a):
        total = None
        for ref in (xth_ref, xtl_ref):
            left = jnp.concatenate(
                [ref[n * LANES : n * LANES + window, a * LANES : (a + 1) * LANES] for n in range(blocks, -1, -1)], axis=1
            )
            term = dot(left, right)
            total = term if total is None else total + term
        total = jnp.where(wanted, total[:, :LANES] + total[:, LANES:], 0.0)
        sums.append(jnp.sum(pltpu.roll(total, 0, 1, stride=1, stride_axis=0), axis=0, keepdims=True))
    taps = jnp.concatenate(sums + [jnp.zeros((8 - taps_a, LANES), F32)], axis=0)

    high, low = split(taps)
    mid, low = low, (taps - high.astype(F32) - low.astype(F32)).astype(BF16)
    parts = jnp.concatenate([high.astype(F32), mid.astype(F32)], axis=0).astype(BF16)
    rest = jnp.concatenate([low.astype(F32), jnp.zeros((8, LANES), F32)], axis=0).astype(BF16)
    me = lax.axis_index("dp")
    for s, ref in enumerate(out_refs):
        share = ref.shape[1] - LANES
        spot = lax.bitwise_xor(me, s) if by_distance else s
        ref[:span, :share] = up[:, pl.ds(pl.multiple_of(spot * share, share), share)]
        ref[:span, share:] = o_ref[...]
        ref[span:, :LANES] = parts
        ref[span:, LANES : 2 * LANES] = rest


def backward_inputs(rows, taps_a, first_ref, do_ref, ch, cl, pt_ref, bh_ref, bl_ref, q16, k_hbm, dq_ref, dk_ref, dv_ref, k_in, z, sem):
    keys, depth = k_in.shape
    rows_up = q16.shape[0]
    span = do_ref.shape[0]
    blocks = keys // LANES
    scale = 1.0 / math.sqrt(depth)
    first = first_ref[0]
    copy = pltpu.make_async_copy(k_hbm.at[0], k_in, sem.at[0])
    copy.start()
    dv_ref[0] = dot(pt_ref[HALF : HALF + keys], do_ref[...]).astype(BF16)
    depth_z = z.shape[0] // blocks
    for n in range(blocks):
        left_h = jnp.concatenate([ch[n * span : (n + 1) * span], ch[(n + 1) * span : (n + 2) * span]], axis=1)
        left_l = jnp.concatenate([cl[n * span : (n + 1) * span], cl[(n + 1) * span : (n + 2) * span]], axis=1)
        z[n * depth_z : n * depth_z + 8] = jnp.zeros((8, z.shape[1]), F32)
        z[n * depth_z + 8 + span : (n + 1) * depth_z] = jnp.zeros((depth_z - 8 - span, z.shape[1]), F32)
        for at in range(0, taps_a * LANES, 2 * LANES):
            cols = pl.ds(at, 2 * LANES)
            z[n * depth_z + 8 : n * depth_z + 8 + span, cols] = (
                dot(left_h, bh_ref[:, cols]) + dot(left_h, bl_ref[:, cols]) + dot(left_l, bh_ref[:, cols])
            )
    copy.wait()
    dq = jnp.zeros((rows_up, depth), F32)
    for n in range(blocks):
        total = None
        for a in range(taps_a):
            start = n * depth_z + 8 - (taps_a - 1) + a
            term = z[start : start + rows_up, a * LANES : (a + 1) * LANES]
            total = term if total is None else total + term
        key = n * LANES + iota(total.shape, 1)
        pos = first - (taps_a - 1) + iota(total.shape, 0)
        ds = jnp.where(key <= pos, total, 0.0)
        here = slice(n * LANES, (n + 1) * LANES)
        dq = dq + dot(ds.astype(BF16), k_in[here])
        dk_ref[0, here] = (scale * dot(ds.T.astype(BF16), q16[...])).astype(BF16)
    dq_ref[0] = (scale * dq)[:rows].astype(BF16)


def update(last, *refs):
    payload_refs, (w_ref, one_ref, two_ref, new_ref, one_new_ref, two_new_ref, taps_ref) = refs[:-7], refs[-7:]
    count = len(payload_refs)
    taps_a, _, taps_b = taps_ref.shape
    span = payload_refs[0].shape[0] - 16
    share = w_ref.shape[1]
    grad, taps = None, None
    for ref in payload_refs:
        term = dot(ref[:span, share:], ref[:span, :share], ((0,), (0,)))
        parts, rest = ref[span:, :LANES].astype(F32), ref[span:, LANES : 2 * LANES].astype(F32)
        tap = parts[:8] + (parts[8:] + rest[:8])
        grad, taps = (term, tap) if grad is None else (grad + term, taps + tap)
    grad = grad / float(count)
    taps = taps / float(count * span)
    lane = iota((8, LANES), 1)
    turned = jnp.zeros((8, LANES), F32)
    for b in range(taps_b):
        turned = jnp.where(lane == b, taps[:, last - b : last - b + 1], turned)
    for a in range(taps_a):
        taps_ref[a] = turned[a : a + 1, :taps_b]
    one = beta_one * one_ref[...] + (1.0 - beta_one) * grad
    two = beta_two * two_ref[...] + (1.0 - beta_two) * grad * grad
    one_new_ref[...] = one
    two_new_ref[...] = two
    old = w_ref[...]
    new_ref[...] = old - learn_rate * ((one / bias_one) / (jnp.sqrt(two / bias_two) + adam_eps) + decay_rate * old)


def swap(x, axis, shift):
    n = lax.axis_size(axis)
    return lax.ppermute(x, axis, [(i, i ^ shift) for i in range(n)])


def few(axis):
    n = lax.axis_size(axis)
    return n <= 8 and n & (n - 1) == 0


def gathered(x, axis):
    if few(axis):
        shifts = range(lax.axis_size(axis))
        return [x] + [swap(x, axis, s) for s in shifts[1:]], [(s, slice(None), s, None) for s in shifts]
    n = lax.axis_size(axis)
    return [lax.all_gather(x, axis)], [(0, i, None, i) for i in range(n)]


def gathered_by_pairs(x, axis):
    n = lax.axis_size(axis)
    if not few(axis) or n < 4:
        return gathered(x, axis)
    rows = x.shape[0]
    pair = jnp.concatenate([x, swap(x, axis, 1)], axis=0)
    arrays = [pair] + [swap(pair, axis, s) for s in range(2, n, 2)]
    return arrays, [(s // 2, slice(c * rows, (c + 1) * rows), s + c, None) for s in range(0, n, 2) for c in (0, 1)]


def shards(queries, keys, values, conv_kernel, span_start, out_grad, proj_weight, moment_one, moment_two):
    _, rows, depth = queries.shape
    key_count = keys.shape[1]
    _, taps_a, taps_b = conv_kernel.shape
    span = out_grad.shape[1]
    blocks = key_count // LANES
    rows_up = up_to(rows, 16)
    padded = key_count + LANES
    half = (taps_b - 1) // 2
    edge = up_to(HALF + half, 16)
    wide = key_count + 2 * edge
    group_count = lax.axis_size("dp")
    share = proj_weight.shape[1]
    columns = share * group_count
    vmem = pltpu.CompilerParams(vmem_limit_bytes=24 * 2**20)
    smem = pl.BlockSpec(memory_space=pltpu.SMEM)
    whole = pl.BlockSpec(memory_space=pltpu.VMEM)
    hbm = pl.BlockSpec(memory_space=pltpu.HBM)
    shape = jax.ShapeDtypeStruct

    up_arrays, up_places = gathered_by_pairs(out_grad[0], "tensor")
    w_arrays, w_places = gathered(proj_weight.astype(BF16), "dp")
    taps_by_row = conv_kernel.transpose(1, 0, 2)

    p, pt, attended, xth, xtl, bh, bl, vpad, q16 = pl.pallas_call(
        forward,
        out_shape=(
            shape((span, padded), F32),
            shape((padded, span), BF16),
            shape((span, depth), BF16),
            shape((wide, taps_a * span), BF16),
            shape((wide, taps_a * span), BF16),
            shape((2 * LANES, taps_a * LANES), BF16),
            shape((2 * LANES, taps_a * LANES), BF16),
            shape((padded, depth), BF16),
            shape((rows_up, depth), BF16),
        ),
        in_specs=[smem, smem, hbm, hbm, hbm],
        out_specs=(whole,) * 9,
        scratch_shapes=[
            pltpu.VMEM((rows, depth), BF16),
            pltpu.VMEM((key_count, depth), BF16),
            pltpu.VMEM((key_count, depth), BF16),
            pltpu.VMEM((rows_up, depth), F32),
            pltpu.VMEM((2 * LANES, taps_a * LANES), BF16),
            pltpu.VMEM((2 * LANES, taps_a * LANES), BF16),
            pltpu.VMEM(((blocks + 1) * rows_up, 2 * LANES), BF16),
            pltpu.VMEM(((blocks + 1) * rows_up, 2 * LANES), BF16),
            pltpu.VMEM(((blocks + 1) * rows_up, taps_a * LANES), F32),
            pltpu.VMEM((wide, depth), BF16),
            pltpu.SemaphoreType.DMA((3,)),
        ],
        compiler_params=vmem,
        cost_estimate=pl.CostEstimate(flops=5 * 10**9, bytes_accessed=10**6, transcendentals=span * padded),
        name="attention_forward",
    )(span_start, taps_by_row, queries, keys, values)

    payload = shape((span + 16, share + LANES), BF16)
    do, ch, cl, *payloads = pl.pallas_call(
        functools.partial(backward_scores, taps_b, up_places, w_places, group_count, few("dp")),
        out_shape=(
            shape((span, depth), BF16),
            shape(((blocks + 1) * span, LANES), BF16),
            shape(((blocks + 1) * span, LANES), BF16),
        ) + (payload,) * group_count,
        in_specs=[whole] * (len(up_arrays) + len(w_arrays) + 5),
        out_specs=(whole,) * (3 + group_count),
        scratch_shapes=[pltpu.VMEM((span, columns), BF16), pltpu.VMEM((depth, columns), BF16)],
        compiler_params=vmem,
        cost_estimate=pl.CostEstimate(flops=2 * 10**9, bytes_accessed=10**6, transcendentals=0),
        name="attention_backward_scores",
    )(*up_arrays, *w_arrays, p, vpad, xth, xtl, attended)

    if few("dp"):
        payloads = payloads[:1] + [swap(payloads[s], "dp", s) for s in range(1, group_count)]
    else:
        sent = lax.all_to_all(jnp.stack(payloads), "dp", 0, 0)
        payloads = [sent[s] for s in range(group_count)]

    query_grad, key_grad, value_grad = pl.pallas_call(
        functools.partial(backward_inputs, rows, taps_a),
        out_shape=(shape(queries.shape, BF16), shape(keys.shape, BF16), shape(values.shape, BF16)),
        in_specs=[smem] + [whole] * 7 + [hbm],
        out_specs=(whole,) * 3,
        scratch_shapes=[
            pltpu.VMEM((key_count, depth), BF16),
            pltpu.VMEM((blocks * (span + 32), taps_a * LANES), F32),
            pltpu.SemaphoreType.DMA((1,)),
        ],
        compiler_params=vmem,
        cost_estimate=pl.CostEstimate(flops=3 * 10**9, bytes_accessed=10**6, transcendentals=0),
        name="attention_backward_inputs",
    )(span_start, do, ch, cl, pt, bh, bl, q16, keys)

    last = up_to(LANES + edge - HALF + half, 16) - 1 - (edge - HALF - half) - LANES
    proj_new, moment_one_new, moment_two_new, kernel_total = pl.pallas_call(
        functools.partial(update, last),
        out_shape=(shape(proj_weight.shape, F32),) * 3 + (shape((taps_a, 1, taps_b), F32),),
        in_specs=[whole] * (group_count + 3),
        out_specs=(whole,) * 4,
        compiler_params=vmem,
        name="projection_update",
    )(*payloads, proj_weight, moment_one, moment_two)
    return (
        query_grad,
        key_grad,
        value_grad,
        kernel_total.transpose(1, 0, 2),
        proj_new,
        moment_one_new,
        moment_two_new,
    )


def solution(mesh):
    heads, rows_of, blocks_of = P("dp", None, "tensor"), P("tensor", None, None), P("tensor", "dp")
    return jax.shard_map(
        shards,
        mesh=mesh,
        in_specs=(heads, heads, heads, rows_of, P("dp"), heads, blocks_of, blocks_of, blocks_of),
        out_specs=(heads, heads, heads, rows_of, blocks_of, blocks_of, blocks_of),
        check_vma=False,
    )
```

time: 72.5 us -> 37.6 us (0.52)
  blocking collectives: 25.2 us -> 0 us
  waiting for transfers between devices: 15.9 us -> 4.6 us
  local copies, waits for them, and re-layouts: 9.89 us -> 3.36 us
  starting transfers between devices: 7.31 us -> 13.8 us
  Pallas kernels: 10.1 us -> 12.4 us
    all_gather x2 -> x0, blocking collectives: 25.2 us -> none  [the longest x1 14.2 us: shards(): lax.all_gather(proj_weight.astype(BF16), 'dp', axis=1, tiled=True)]
    ppermute x6 -> x10, waiting for transfers between devices: 15.9 us -> 4.6 us  [swap(): return lax.ppermute(x, axis, [(i, i ^ shift) for i in range(n)])]
    ppermute x6 -> x10, starting transfers between devices: 7.31 us -> 13.8 us  [swap(): return lax.ppermute(x, axis, [(i, i ^ shift) for i in range(n)])]
    unnamed x28 -> x16, local copies, waits for them, and re-layouts: 8.99 us -> 3.36 us
    pallas_call x2 -> x4, Pallas kernels: 10.1 us -> 12.4 us  [the longest x1 5.85 us: shards(): pl.pallas_call(forward, out_shape=(shape((span, padded), F32), shape((pad...]
    sub x1 -> x0, other arithmetic: 2.1 us -> none  [shards(): proj_weight - learn_rate * (first_hat / (jnp.sqrt(second_hat) + adam_eps)...]
    convert_element_type x0 -> x1, other arithmetic: none -> 0.91 us  [shards(): w_arrays, w_places = gathered(proj_weight.astype(BF16), 'dp')]
    concatenate x0 -> x1, other arithmetic: none -> 0.77 us  [gathered_by_pairs(): pair = jnp.concatenate([x, swap(x, axis, 1)], axis=0)]
  transfers between devices with their start and end apart: 6 -> 10, of which waited for: 6 -> 1; matrix products, arithmetic and copies ran while one was open for 0% -> 5% of each run, Pallas kernels for 0% -> 24%
where the time goes in v2:
time: 37.6 us; the launch traced here: 37.2 us
  starting transfers between devices  13.8 us (37%)
  Pallas kernels  12.4 us (33%)
  waiting for transfers between devices  4.6 us (12%)
  local copies, waits for them, and re-layouts  3.36 us (9%)
  other arithmetic  1.68 us (4%)
  between operations  1.39 us (4%)
    ppermute x10, starting transfers between devices, swap(): return lax.ppermute(x, axis, [(i, i ^ shift) for i in range(n)])  13.8 us
    pallas_call x1, Pallas kernels, shards(): pl.pallas_call(forward, out_shape=(shape((span, padded), F32), shape((pad...  5.85 us
    ppermute x10, waiting for transfers between devices, swap(): return lax.ppermute(x, axis, [(i, i ^ shift) for i in range(n)])  4.6 us
    unnamed x16, local copies, waits for them, and re-layouts  3.36 us
    pallas_call x1, Pallas kernels, shards(): pl.pallas_call(functools.partial(backward_inputs, rows, taps_a), out_shap...  3.13 us
    pallas_call x1, Pallas kernels, shards(): pl.pallas_call(functools.partial(backward_scores, taps_b, up_places, w_pl...  2.35 us
    pallas_call x1, Pallas kernels, shards(): pl.pallas_call(functools.partial(update, last), out_shape=(shape(proj_wei...  1.09 us
    convert_element_type x1, other arithmetic, shards(): w_arrays, w_places = gathered(proj_weight.astype(BF16), 'dp')  0.91 us
  transfers between devices with their start and end apart: 10, of which 1 were waited for; matrix products, arithmetic and copies ran while one was open for 5% of the time, Pallas kernels for 24%

profile of v2, /device:TPU:0, one launch (start us, length us, event | category | flops | bytes accessed | tf_op | source)
XLA Modules:
  0.0 37.2 jit_solution(1052635874615010799)
XLA Ops:
  0.6 0.5 %collective-permute-start = (bf16[128,128]{1,0:T(8,128)(2,1)}, bf16[128,128]{1,0:T(8,128)(2,1)S(1)}, u32[]{:S(2)}, u32[]{:S(2)}) collective-permute-start(bf16[128,128]{1,0:T(8,128)(2,1)} %bitcast.4), channel_id=1, source_target_pairs={{0,1},{1,0},{2,3},{3,2},{4,5},{5,4},{6,7},{7,6},{8,9},{9,8},{10,11... | collective-permute-start | bytes 98312 | tf_op jit(solution)/shard_map/ppermute | solution.py:266
  1.1 0.9 %convert_element_type.3.refs_4_ = bf16[128,256]{1,0:T(8,128)(2,1)S(1)} convert(f32[128,256]{1,0:T(8,128)} %refs_4_.1) | non-fusion elementwise | flops 32768 | bytes 196608 | tf_op jit(solution)/shard_map/convert_element_type | solution.py:313
  2.1 4.7 %collective-permute-start.6 = (bf16[128,256]{1,0:T(8,128)(2,1)S(1)}, bf16[128,256]{1,0:T(8,128)(2,1)S(1)}, u32[]{:S(2)}, u32[]{:S(2)}) collective-permute-start(bf16[128,256]{1,0:T(8,128)(2,1)S(1)} %convert_element_type.3.refs_4_), channel_id=1, source_target_pairs={{0,24},{8,16},{16,8},{24,0},{1,25},{9,17},{17,9},{25,1},{2,26},{10... | collective-permute-start | bytes 196616 | tf_op jit(solution)/shard_map/ppermute | solution.py:266
  6.7 0.0 collective-permute-start.5
  6.7 0.6 %collective-permute-start.4 = (bf16[128,256]{1,0:T(8,128)(2,1)S(1)}, bf16[128,256]{1,0:T(8,128)(2,1)S(1)}, u32[]{:S(2)}, u32[]{:S(2)}) collective-permute-start(bf16[128,256]{1,0:T(8,128)(2,1)S(1)} %convert_element_type.3.refs_4_), channel_id=1, source_target_pairs={{0,8},{8,0},{16,24},{24,16},{1,9},{9,1},{17,25},{25,17},{2,10},{10... | collective-permute-start | bytes 196616 | tf_op jit(solution)/shard_map/ppermute | solution.py:266
  8.0 0.0 collective-permute-done
  8.0 0.8 %pad_maximum_fusion.refs_0_ = bf16[256,128]{1,0:T(8,128)(2,1)S(1)} fusion(bf16[128,128]{1,0:T(8,128)(2,1)S(1)} %collective-permute-done, bf16[128,128]{1,0:T(8,128)(2,1)} %bitcast.5), kind=kLoop, calls=%fused_computation | loop fusion | flops 131072 | bytes 131072 | tf_op jit(solution)/shard_map/concatenate | solution.py:287
  8.8 2.6 %collective-permute-start.3 = (bf16[256,128]{1,0:T(8,128)(2,1)S(1)}, bf16[256,128]{1,0:T(8,128)(2,1)S(1)}, u32[]{:S(2)}, u32[]{:S(2)}) collective-permute-start(bf16[256,128]{1,0:T(8,128)(2,1)S(1)} %pad_maximum_fusion.refs_0_), channel_id=1, source_target_pairs={{0,6},{1,7},{2,4},{3,5},{4,2},{5,3},{6,0},{7,1},{8,14},{9,15},{10,... | collective-permute-start | bytes 196616 | tf_op jit(solution)/shard_map/ppermute | solution.py:266
  11.4 0.5 %collective-permute-start.2 = (bf16[256,128]{1,0:T(8,128)(2,1)S(1)}, bf16[256,128]{1,0:T(8,128)(2,1)S(1)}, u32[]{:S(2)}, u32[]{:S(2)}) collective-permute-start(bf16[256,128]{1,0:T(8,128)(2,1)S(1)} %pad_maximum_fusion.refs_0_), channel_id=1, source_target_pairs={{0,4},{1,5},{2,6},{3,7},{4,0},{5,1},{6,2},{7,3},{8,12},{9,13},{10,... | collective-permute-start | bytes 196616 | tf_op jit(solution)/shard_map/ppermute | solution.py:266
  11.9 0.0 collective-permute-done.6.refs_7_
  11.9 0.4 %collective-permute-start.1 = (bf16[256,128]{1,0:T(8,128)(2,1)S(1)}, bf16[256,128]{1,0:T(8,128)(2,1)S(1)}, u32[]{:S(2)}, u32[]{:S(2)}) collective-permute-start(bf16[256,128]{1,0:T(8,128)(2,1)S(1)} %pad_maximum_fusion.refs_0_), channel_id=1, source_target_pairs={{0,2},{1,3},{2,0},{3,1},{4,6},{5,7},{6,4},{7,5},{8,10},{9,11},{10,... | collective-permute-start | bytes 196616 | tf_op jit(solution)/shard_map/ppermute | solution.py:266
  12.3 0.0 copy-start.3
  12.3 0.9 %copy-done.3 = bf16[1,1024,128]{2,1,0:T(8,128)(2,1)S(1)} copy-done((bf16[1,1024,128]{2,1,0:T(8,128)(2,1)S(1)}, bf16[1,1024,128]{2,1,0:T(8,128)(2,1)}, u32[]{:S(2)}) %copy-start.3) | copy-done | bytes 262168
  13.3 0.0 copy-start.4
  13.3 0.9 %copy-done.4 = bf16[1,1024,128]{2,1,0:T(8,128)(2,1)S(1)} copy-done((bf16[1,1024,128]{2,1,0:T(8,128)(2,1)S(1)}, bf16[1,1024,128]{2,1,0:T(8,128)(2,1)}, u32[]{:S(2)}) %copy-start.4) | copy-done | bytes 262168
  14.2 0.0 copy-start.6
  14.2 0.8 %copy-done.6 = bf16[1,133,128]{2,1,0:T(8,128)(2,1)S(1)} copy-done((bf16[1,133,128]{2,1,0:T(8,128)(2,1)S(1)}, bf16[1,133,128]{2,1,0:T(8,128)(2,1)}, u32[]{:S(2)}) %copy-start.6) | copy-done | bytes 34072
  15.0 0.0 copy-start.7
  15.0 0.7 %copy-done.7 = f32[1,6,11]{2,0,1:T(1,128)S(1)} copy-done((f32[1,6,11]{2,0,1:T(1,128)S(1)}, f32[1,6,11]{2,0,1:T(1,128)}, u32[]{:S(2)}) %copy-start.7) | copy-done | bytes 288
  15.7 5.8 %attention_forward.1 = (f32[128,1152]{1,0:T(8,128)S(1)}, bf16[1152,128]{1,0:T(8,128)(2,1)S(1)}, bf16[128,128]{1,0:T(8,128)(2,1)S(1)}, bf16[1184,768]{1,0:T(8,128...) custom-call(s32[1]{0:T(128)S(6)} %copy.16.first_ref, ...), custom_call_target="tpu_custom_call" | custom-call | flops 5000000000 | bytes 1000000 | tf_op jit(solution)/shard_map/attention_forward/pallas_call | solution.py:316
  21.5 0.0 collective-permute-done.5.refs_6_
  21.5 0.0 collective-permute-done.4.refs_5_
  21.5 0.0 collective-permute-done.3.refs_3_
  21.5 0.0 collective-permute-done.2.refs_2_
  21.6 0.0 collective-permute-done.1.refs_1_
  21.6 0.0 copy-start.5
  21.6 2.3 %attention_backward_scores.1 = (bf16[128,128]{1,0:T(8,128)(2,1)S(1)}, bf16[1152,128]{1,0:T(8,128)(2,1)S(1)}, bf16[1152,128]{1,0:T(8,128)(2,1)S(1)}, bf16[144,384...) custom-call(bf16[256,128]{1,0:T(8,128)(2,1)S(1)} %pad_maximum_fusion, ...), custom_call_target="tpu_custom_call" | custom-call | flops 2000000000 | bytes 1000000 | tf_op jit(solution)/shard_map/attention_backward_scores/pallas_call | solution.py:350
  23.9 1.7 %collective-permute-start.7 = (bf16[144,384]{1,0:T(8,128)(2,1)S(1)}, bf16[144,384]{1,0:T(8,128)(2,1)S(1)}, u32[]{:S(2)}, u32[]{:S(2)}) collective-permute-start(bf16[144,384]{1,0:T(8,128)(2,1)S(1)} %get-tuple-element.46), channel_id=1, source_target_pairs={{0,8},{8,0},{16,24},{24,16},{1,9},{9,1},{17,25},{25,17},{2,10},{10... | collective-permute-start | bytes 331784 | tf_op jit(solution)/shard_map/ppermute | solution.py:266
  25.6 2.7 %collective-permute-start.8 = (bf16[144,384]{1,0:T(8,128)(2,1)S(1)}, bf16[144,384]{1,0:T(8,128)(2,1)S(1)}, u32[]{:S(2)}, u32[]{:S(2)}) collective-permute-start(bf16[144,384]{1,0:T(8,128)(2,1)S(1)} %get-tuple-element.47), channel_id=1, source_target_pairs={{0,16},{8,24},{16,0},{24,8},{1,17},{9,25},{17,1},{25,9},{2,18},{10... | collective-permute-start | bytes 331784 | tf_op jit(solution)/shard_map/ppermute | solution.py:266
  28.3 0.1 collective-permute-start.9
  28.4 0.0 copy-done.5
  28.4 0.0 copy-start
  28.4 0.0 copy-start.1
  28.4 0.0 copy-start.2
  28.4 3.1 %attention_backward_inputs.1 = (bf16[1,133,128]{2,1,0:T(8,128)(2,1)}, bf16[1,1024,128]{2,1,0:T(8,128)(2,1)}, bf16[1,1024,128]{2,1,0:T(8,128)(2,1)}) custom-call(s32[1]{0:T(128)S(6)} %copy.16.first_ref, bf16[128,128]{1,0:T(8,128)(2,1)S(1)} %get-tuple-element.35.do_ref, bf16[1152,128]{1,0:T(8,128)(2,1)S(1)} %get-tuple-element.36.ch, ...), custom_call_target="tpu_custom_call" | custom-call | flops 3000000000 | bytes 1000000 | tf_op jit(solution)/shard_map/attention_backward_inputs/pallas_call | solution.py:371
  31.5 0.0 collective-permute-done.7.refs_1_
  31.5 4.6 %collective-permute-done.8.refs_2_ = bf16[144,384]{1,0:T(8,128)(2,1)S(1)} collective-permute-done((bf16[144,384]{1,0:T(8,128)(2,1)S(1)}, bf16[144,384]{1,0:T(8,128)(2,1)S(1)}, u32[]{:S(2)}, u32[]{:S(2)}) %collective-permute-start.8) | collective-permute-done | bytes 110624 | tf_op jit(solution)/shard_map/ppermute | solution.py:266
  36.1 0.0 collective-permute-done.9.refs_3_
  36.1 0.0 copy-done
  36.1 0.0 copy-done.1
  36.1 0.0 copy-done.2
  36.1 1.1 %projection_update.1 = (f32[128,256]{1,0:T(8,128)}, f32[128,256]{1,0:T(8,128)}, f32[128,256]{1,0:T(8,128)}, f32[6,1,11]{2,1,0:T(1,128)}) custom-call(bf16[144,384]{1,0:T(8,128)(2,1)S(1)} %get-tuple-element.45.refs_0_, bf16[144,384]{1,0:T(8,128)(2,1)S(1)} %collective-permute-done.7.refs_1_, bf16[144,384]{1,0:T(8,128)(2,1)S(1)} %collective-permute-done.8.refs_2_, ...), custom_call_target="tpu_custom_call" | custom-call | tf_op jit(solution)/shard_map/projection_update/pallas_call | solution.py:387
Async XLA Ops:
  0.6 7.4 %collective-permute-start = (bf16[128,128]{1,0:T(8,128)(2,1)}, bf16[128,128]{1,0:T(8,128)(2,1)S(1)}, u32[]{:S(2)}, u32[]{:S(2)}) collective-permute-start(bf16[128,128]{1,0:T(8,128)(2,1)} %bitcast.4), channel_id=1, source_target_pairs={{0,1},{1,0},{2,3},{3,2},{4,5},{5,4},{6,7},{7,6},{8,9},{9,8},{10,11... | collective-permute-start | bytes 98312 | tf_op jit(solution)/shard_map/ppermute | solution.py:266
  2.1 9.8 %collective-permute-start.6 = (bf16[128,256]{1,0:T(8,128)(2,1)S(1)}, bf16[128,256]{1,0:T(8,128)(2,1)S(1)}, u32[]{:S(2)}, u32[]{:S(2)}) collective-permute-start(bf16[128,256]{1,0:T(8,128)(2,1)S(1)} %convert_element_type.3.refs_4_), channel_id=1, source_target_pairs={{0,24},{8,16},{16,8},{24,0},{1,25},{9,17},{17,9},{25,1},{2,26},{10... | collective-permute-start | bytes 196616 | tf_op jit(solution)/shard_map/ppermute | solution.py:266
  6.7 14.8 %collective-permute-start.5 = (bf16[128,256]{1,0:T(8,128)(2,1)S(1)}, bf16[128,256]{1,0:T(8,128)(2,1)S(1)}, u32[]{:S(2)}, u32[]{:S(2)}) collective-permute-start(bf16[128,256]{1,0:T(8,128)(2,1)S(1)} %convert_element_type.3.refs_4_), channel_id=1, source_target_pairs={{0,16},{8,24},{16,0},{24,8},{1,17},{9,25},{17,1},{25,9},{2,18},{10... | collective-permute-start | bytes 196616 | tf_op jit(solution)/shard_map/ppermute | solution.py:266
  6.7 14.8 %collective-permute-start.4 = (bf16[128,256]{1,0:T(8,128)(2,1)S(1)}, bf16[128,256]{1,0:T(8,128)(2,1)S(1)}, u32[]{:S(2)}, u32[]{:S(2)}) collective-permute-start(bf16[128,256]{1,0:T(8,128)(2,1)S(1)} %convert_element_type.3.refs_4_), channel_id=1, source_target_pairs={{0,8},{8,0},{16,24},{24,16},{1,9},{9,1},{17,25},{25,17},{2,10},{10... | collective-permute-start | bytes 196616 | tf_op jit(solution)/shard_map/ppermute | solution.py:266
  8.8 12.7 %collective-permute-start.3 = (bf16[256,128]{1,0:T(8,128)(2,1)S(1)}, bf16[256,128]{1,0:T(8,128)(2,1)S(1)}, u32[]{:S(2)}, u32[]{:S(2)}) collective-permute-start(bf16[256,128]{1,0:T(8,128)(2,1)S(1)} %pad_maximum_fusion.refs_0_), channel_id=1, source_target_pairs={{0,6},{1,7},{2,4},{3,5},{4,2},{5,3},{6,0},{7,1},{8,14},{9,15},{10,... | collective-permute-start | bytes 196616 | tf_op jit(solution)/shard_map/ppermute | solution.py:266
  11.4 10.1 %collective-permute-start.2 = (bf16[256,128]{1,0:T(8,128)(2,1)S(1)}, bf16[256,128]{1,0:T(8,128)(2,1)S(1)}, u32[]{:S(2)}, u32[]{:S(2)}) collective-permute-start(bf16[256,128]{1,0:T(8,128)(2,1)S(1)} %pad_maximum_fusion.refs_0_), channel_id=1, source_target_pairs={{0,4},{1,5},{2,6},{3,7},{4,0},{5,1},{6,2},{7,3},{8,12},{9,13},{10,... | collective-permute-start | bytes 196616 | tf_op jit(solution)/shard_map/ppermute | solution.py:266
  11.9 9.6 %collective-permute-start.1 = (bf16[256,128]{1,0:T(8,128)(2,1)S(1)}, bf16[256,128]{1,0:T(8,128)(2,1)S(1)}, u32[]{:S(2)}, u32[]{:S(2)}) collective-permute-start(bf16[256,128]{1,0:T(8,128)(2,1)S(1)} %pad_maximum_fusion.refs_0_), channel_id=1, source_target_pairs={{0,2},{1,3},{2,0},{3,1},{4,6},{5,7},{6,4},{7,5},{8,10},{9,11},{10,... | collective-permute-start | bytes 196616 | tf_op jit(solution)/shard_map/ppermute | solution.py:266
  12.3 0.9 %copy-start.3 = (bf16[1,1024,128]{2,1,0:T(8,128)(2,1)S(1)}, bf16[1,1024,128]{2,1,0:T(8,128)(2,1)}, u32[]{:S(2)}) copy-start(bf16[1,1024,128]{2,1,0:T(8,128)(2,1)} %v_hbm.1) | copy-start | bytes 786436
  13.3 0.9 %copy-start.4 = (bf16[1,1024,128]{2,1,0:T(8,128)(2,1)S(1)}, bf16[1,1024,128]{2,1,0:T(8,128)(2,1)}, u32[]{:S(2)}) copy-start(bf16[1,1024,128]{2,1,0:T(8,128)(2,1)} %k_hbm.3) | copy-start | bytes 786436
  14.2 0.8 %copy-start.6 = (bf16[1,133,128]{2,1,0:T(8,128)(2,1)S(1)}, bf16[1,133,128]{2,1,0:T(8,128)(2,1)}, u32[]{:S(2)}) copy-start(bf16[1,133,128]{2,1,0:T(8,128)(2,1)} %q_hbm.1) | copy-start | bytes 102148
  15.0 0.7 %copy-start.7 = (f32[1,6,11]{2,0,1:T(1,128)S(1)}, f32[1,6,11]{2,0,1:T(1,128)}, u32[]{:S(2)}) copy-start(f32[1,6,11]{2,0,1:T(1,128)} %param.12) | copy-start | bytes 796
  21.6 6.8 %copy-start.5 = (bf16[1,1024,128]{2,1,0:T(8,128)(2,1)S(1)}, bf16[1,1024,128]{2,1,0:T(8,128)(2,1)}, u32[]{:S(2)}) copy-start(bf16[1,1024,128]{2,1,0:T(8,128)(2,1)} %k_hbm.3) | copy-start | bytes 786436
  23.9 7.6 %collective-permute-start.7 = (bf16[144,384]{1,0:T(8,128)(2,1)S(1)}, bf16[144,384]{1,0:T(8,128)(2,1)S(1)}, u32[]{:S(2)}, u32[]{:S(2)}) collective-permute-start(bf16[144,384]{1,0:T(8,128)(2,1)S(1)} %get-tuple-element.46), channel_id=1, source_target_pairs={{0,8},{8,0},{16,24},{24,16},{1,9},{9,1},{17,25},{25,17},{2,10},{10... | collective-permute-start | bytes 331784 | tf_op jit(solution)/shard_map/ppermute | solution.py:266
  25.6 10.5 %collective-permute-start.8 = (bf16[144,384]{1,0:T(8,128)(2,1)S(1)}, bf16[144,384]{1,0:T(8,128)(2,1)S(1)}, u32[]{:S(2)}, u32[]{:S(2)}) collective-permute-start(bf16[144,384]{1,0:T(8,128)(2,1)S(1)} %get-tuple-element.47), channel_id=1, source_target_pairs={{0,16},{8,24},{16,0},{24,8},{1,17},{9,25},{17,1},{25,9},{2,18},{10... | collective-permute-start | bytes 331784 | tf_op jit(solution)/shard_map/ppermute | solution.py:266
  28.3 7.8 %collective-permute-start.9 = (bf16[144,384]{1,0:T(8,128)(2,1)S(1)}, bf16[144,384]{1,0:T(8,128)(2,1)S(1)}, u32[]{:S(2)}, u32[]{:S(2)}) collective-permute-start(bf16[144,384]{1,0:T(8,128)(2,1)S(1)} %get-tuple-element.48), channel_id=1, source_target_pairs={{0,24},{8,16},{16,8},{24,0},{1,25},{9,17},{17,9},{25,1},{2,26},{10... | collective-permute-start | bytes 331784 | tf_op jit(solution)/shard_map/ppermute | solution.py:266
  28.4 7.7 %copy-start = (f32[128,256]{1,0:T(8,128)S(1)}, f32[128,256]{1,0:T(8,128)}, u32[]{:S(2)}) copy-start(f32[128,256]{1,0:T(8,128)} %refs_4_.1) | copy-start | bytes 393220
  28.4 7.7 %copy-start.1 = (f32[128,256]{1,0:T(8,128)S(1)}, f32[128,256]{1,0:T(8,128)}, u32[]{:S(2)}) copy-start(f32[128,256]{1,0:T(8,128)} %refs_5_.1) | copy-start | bytes 393220
  28.4 7.7 %copy-start.2 = (f32[128,256]{1,0:T(8,128)S(1)}, f32[128,256]{1,0:T(8,128)}, u32[]{:S(2)}) copy-start(f32[128,256]{1,0:T(8,128)} %refs_6_.1) | copy-start | bytes 393220

commit v3 on v2

--- a/solution.py
+++ b/solution.py
@@ -39,47 +39,57 @@
     return lax.broadcasted_iota(jnp.int32, shape, axis)
 
 
-def bands(kernel_ref, flipped):
-    taps_a, _, taps_b = kernel_ref.shape
+def bands(taps_ref, flipped):
+    taps_a, _, taps_b = taps_ref.shape
     half = (taps_b - 1) // 2
     place = iota((2 * LANES, LANES), 0) - iota((2 * LANES, LANES), 1) - (HALF - half)
     out = [jnp.zeros((2 * LANES, LANES), F32) for _ in range(taps_a)]
     for b in range(taps_b):
         here = place == (taps_b - 1 - b if flipped else b)
         for a in range(taps_a):
-            out[a] = jnp.where(here, kernel_ref[a, 0, b], out[a])
+            out[a] = jnp.where(here, taps_ref[a, 0, b], out[a])
     return out
 
 
-def forward(
-    first_ref, kernel_ref, q_hbm, k_hbm, v_hbm,
-    p_ref, pt_ref, o_ref, xth_ref, xtl_ref, bh_ref, bl_ref, vpad, q16,
-    q_in, k_in, v_in, q32, fh, fl, xh, xl, y, kpad, sems,
-):
-    taps_a, _, taps_b = kernel_ref.shape
+def fetch(pairs, sems):
+    copies = [pltpu.make_async_copy(src, dst, sems.at[n]) for n, (src, dst) in enumerate(pairs)]
+    for copy in copies:
+        copy.start()
+    return copies
+
+
+def forward(pieces, *refs):
+    piece_refs, (first_ref, taps_hbm, q_hbm, k_hbm, v_hbm) = refs[:pieces], refs[pieces : pieces + 5]
+    p_ref, o_ref, vpad, q16, q32, pack_ref = refs[pieces + 5 : pieces + 11]
+    taps_ref, q_in, k_in, v_in, fh, fl, xh, xl, y, sems = refs[pieces + 11 :]
+    taps_a, _, _ = taps_ref.shape
     rows, depth = q_in.shape
     keys = k_in.shape[0]
     span = rows - taps_a + 1
     rows_up = q32.shape[0]
     blocks = keys // LANES
     scale = 1.0 / math.sqrt(depth)
-    first = first_ref[0]
-    copies = [
-        pltpu.make_async_copy(src.at[0], dst, sems.at[n])
-        for n, (src, dst) in enumerate(((q_hbm, q_in), (k_hbm, k_in), (v_hbm, v_in)))
-    ]
-    for copy in copies:
-        copy.start()
-
-    for a, (f, t) in enumerate(zip(bands(kernel_ref, False), bands(kernel_ref, True), strict=True)):
+    copies = fetch(
+        (
+            (taps_hbm, taps_ref),
+            (q_hbm.at[0], q_in),
+            (k_hbm.at[0], k_in),
+            (v_hbm.at[0], v_in),
+            (piece_refs[0].at[0], pack_ref.at[pl.ds(0, span)]),
+        ),
+        sems,
+    )
+    for n, ref in enumerate(piece_refs[1:]):
+        pack_ref[(n + 1) * span : (n + 2) * span] = ref[0]
+    q32[...] = jnp.zeros_like(q32)
+    vpad[...] = jnp.zeros_like(vpad)
+    copies[0].wait()
+    for a, f in enumerate(bands(taps_ref, False)):
         cols = pl.ds(a * LANES, LANES)
         fh[:, cols], fl[:, cols] = split(f)
-        bh_ref[:, cols], bl_ref[:, cols] = split(t)
-    q32[...] = jnp.zeros_like(q32)
-    vpad[...] = jnp.zeros_like(vpad)
-    kpad[...] = jnp.zeros_like(kpad)
-    for copy in copies:
+    for copy in copies[1:]:
         copy.wait()
+    first = first_ref[0]
     q32[:rows] = q_in[...].astype(F32)
     q_all = q32[...].astype(BF16)
     q16[...] = q_all
@@ -116,11 +126,21 @@
     terms = jnp.where(live, jnp.exp(c - top), 0.0)
     p = terms / jnp.sum(terms, axis=1, keepdims=True)
     p_ref[...] = p
-    pt_ref[...] = p.T.astype(BF16)
     o_ref[...] = dot(p.astype(BF16), vpad[...]).astype(BF16)
 
+
+def forward_turned(taps_a, first_ref, k_hbm, q32, xth_ref, xtl_ref, k_in, kpad, sems):
+    keys, depth = k_in.shape
+    span = xth_ref.shape[1] // taps_a
+    blocks = keys // LANES
+    scale = 1.0 / math.sqrt(depth)
+    copies = fetch(((k_hbm.at[0], k_in),), sems)
+    kpad[...] = jnp.zeros_like(kpad)
     edge = (kpad.shape[0] - keys) // 2
     flip = (iota((LANES, LANES), 0) + iota((LANES, LANES), 1) == LANES - 1).astype(F32).astype(BF16)
+    for copy in copies:
+        copy.wait()
+    first = first_ref[0]
     for n in range(blocks):
         kpad[edge + n * LANES : edge + (n + 1) * LANES] = dot(
             flip, k_in[keys - (n + 1) * LANES : keys - n * LANES]
@@ -137,8 +157,8 @@
 def backward_scores(taps_b, up_places, w_places, payloads, by_distance, *refs):
     n_up, n_w = len({p[0] for p in up_places}), len({p[0] for p in w_places})
     up_refs, w_refs, refs = refs[:n_up], refs[n_up : n_up + n_w], refs[n_up + n_w :]
-    p_ref, vpad, xth_ref, xtl_ref, o_ref, do_ref, ch, cl = refs[:8]
-    out_refs, (up, w) = refs[8 : 8 + payloads], refs[8 + payloads :]
+    p_ref, vpad, xth_ref, xtl_ref, o_ref, do_ref, ch, cl, own_ref, own_taps_ref = refs[:10]
+    out_refs, (up, w, grad) = refs[10 : 10 + payloads], refs[10 + payloads :]
     span = p_ref.shape[0]
     keys = vpad.shape[0] - LANES
     taps_a = xth_ref.shape[1] // span
@@ -152,9 +172,10 @@
             block = refs_in[n][part]
             width = block.shape[1]
             spot = at if shift is None else lax.bitwise_xor(me, shift)
-            whole[:, pl.ds(pl.multiple_of(spot * width, width), width)] = block
+            whole[:, pl.ds(pl.multiple_of(spot * width, width), width)] = block.astype(BF16)
     do = dot(up[...], w[...], ((1,), (1,))).astype(BF16)
     do_ref[...] = do
+    grad[...] = dot(o_ref[...], up[...], ((0,), (0,)))
     dp = dot(do, vpad[...], ((1,), (1,)))
     p = p_ref[...]
     high, low = split(p * (dp - jnp.sum(p * dp, axis=1, keepdims=True)))
@@ -185,26 +206,39 @@
     mid, low = low, (taps - high.astype(F32) - low.astype(F32)).astype(BF16)
     parts = jnp.concatenate([high.astype(F32), mid.astype(F32)], axis=0).astype(BF16)
     rest = jnp.concatenate([low.astype(F32), jnp.zeros((8, LANES), F32)], axis=0).astype(BF16)
+    own_taps_ref[...] = taps
+    depth, share = own_ref.shape
     me = lax.axis_index("dp")
-    for s, ref in enumerate(out_refs):
-        share = ref.shape[1] - LANES
-        spot = lax.bitwise_xor(me, s) if by_distance else s
-        ref[:span, :share] = up[:, pl.ds(pl.multiple_of(spot * share, share), share)]
-        ref[:span, share:] = o_ref[...]
-        ref[span:, :LANES] = parts
-        ref[span:, LANES : 2 * LANES] = rest
-
-
-def backward_inputs(rows, taps_a, first_ref, do_ref, ch, cl, pt_ref, bh_ref, bl_ref, q16, k_hbm, dq_ref, dk_ref, dv_ref, k_in, z, sem):
+
+    def owned(spot):
+        return grad[:, pl.ds(pl.multiple_of(spot * share, share), share)]
+
+    own_ref[...] = owned(me)
+    for n, ref in enumerate(out_refs):
+        ref[:depth, :share] = owned(lax.bitwise_xor(me, n + 1) if by_distance else n).astype(BF16)
+        ref[depth:, :LANES] = parts
+        ref[depth:, LANES : 2 * LANES] = rest
+
+
+def backward_inputs(
+    rows, first_ref, taps_hbm, k_hbm, do_ref, ch, cl, p_ref, q16,
+    dq_ref, dk_ref, dv_ref,
+    taps_ref, k_in, bh, bl, z, sems,
+):
+    taps_a = taps_ref.shape[0]
     keys, depth = k_in.shape
     rows_up = q16.shape[0]
     span = do_ref.shape[0]
     blocks = keys // LANES
     scale = 1.0 / math.sqrt(depth)
-    first = first_ref[0]
-    copy = pltpu.make_async_copy(k_hbm.at[0], k_in, sem.at[0])
-    copy.start()
-    dv_ref[0] = dot(pt_ref[HALF : HALF + keys], do_ref[...]).astype(BF16)
+    copies = fetch(((taps_hbm, taps_ref), (k_hbm.at[0], k_in)), sems)
+    do = do_ref[...]
+    turned = jnp.concatenate([p_ref[:, n * LANES : (n + 1) * LANES].T for n in range(blocks + 1)], axis=0).astype(BF16)
+    dv_ref[0] = dot(turned, do)[HALF : HALF + keys].astype(BF16)
+    copies[0].wait()
+    for a, f in enumerate(bands(taps_ref, True)):
+        cols = pl.ds(a * LANES, LANES)
+        bh[:, cols], bl[:, cols] = split(f)
     depth_z = z.shape[0] // blocks
     for n in range(blocks):
         left_h = jnp.concatenate([ch[n * span : (n + 1) * span], ch[(n + 1) * span : (n + 2) * span]], axis=1)
@@ -214,9 +248,11 @@
         for at in range(0, taps_a * LANES, 2 * LANES):
             cols = pl.ds(at, 2 * LANES)
             z[n * depth_z + 8 : n * depth_z + 8 + span, cols] = (
-                dot(left_h, bh_ref[:, cols]) + dot(left_h, bl_ref[:, cols]) + dot(left_l, bh_ref[:, cols])
+                dot(left_h, bh[:, cols]) + dot(left_h, bl[:, cols]) + dot(left_l, bh[:, cols])
             )
-    copy.wait()
+    for copy in copies[1:]:
+        copy.wait()
+    first = first_ref[0]
     dq = jnp.zeros((rows_up, depth), F32)
     for n in range(blocks):
         total = None
@@ -233,18 +269,16 @@
     dq_ref[0] = (scale * dq)[:rows].astype(BF16)
 
 
-def update(last, *refs):
-    payload_refs, (w_ref, one_ref, two_ref, new_ref, one_new_ref, two_new_ref, taps_ref) = refs[:-7], refs[-7:]
-    count = len(payload_refs)
+def update(last, count, span, *refs):
+    payload_refs, (own_ref, own_taps_ref, w_ref, one_ref, two_ref) = refs[:-9], refs[-9:-4]
+    new_ref, one_new_ref, two_new_ref, taps_ref = refs[-4:]
     taps_a, _, taps_b = taps_ref.shape
-    span = payload_refs[0].shape[0] - 16
-    share = w_ref.shape[1]
-    grad, taps = None, None
+    depth, share = own_ref.shape
+    grad, taps = own_ref[...], own_taps_ref[...]
     for ref in payload_refs:
-        term = dot(ref[:span, share:], ref[:span, :share], ((0,), (0,)))
-        parts, rest = ref[span:, :LANES].astype(F32), ref[span:, LANES : 2 * LANES].astype(F32)
-        tap = parts[:8] + (parts[8:] + rest[:8])
-        grad, taps = (term, tap) if grad is None else (grad + term, taps + tap)
+        grad = grad + ref[:depth, :share].astype(F32)
+        parts, rest = ref[depth:, :LANES].astype(F32), ref[depth:, LANES : 2 * LANES].astype(F32)
+        taps = taps + (parts[:8] + (parts[8:] + rest[:8]))
     grad = grad / float(count)
     taps = taps / float(count * span)
     lane = iota((8, LANES), 1)
@@ -277,16 +311,6 @@
         return [x] + [swap(x, axis, s) for s in shifts[1:]], [(s, slice(None), s, None) for s in shifts]
     n = lax.axis_size(axis)
     return [lax.all_gather(x, axis)], [(0, i, None, i) for i in range(n)]
-
-
-def gathered_by_pairs(x, axis):
-    n = lax.axis_size(axis)
-    if not few(axis) or n < 4:
-        return gathered(x, axis)
-    rows = x.shape[0]
-    pair = jnp.concatenate([x, swap(x, axis, 1)], axis=0)
-    arrays = [pair] + [swap(pair, axis, s) for s in range(2, n, 2)]
-    return arrays, [(s // 2, slice(c * rows, (c + 1) * rows), s + c, None) for s in range(0, n, 2) for c in (0, 1)]
 
 
 def shards(queries, keys, values, conv_kernel, span_start, out_grad, proj_weight, moment_one, moment_two):
@@ -304,94 +328,125 @@
     share = proj_weight.shape[1]
     columns = share * group_count
     vmem = pltpu.CompilerParams(vmem_limit_bytes=24 * 2**20)
-    smem = pl.BlockSpec(memory_space=pltpu.SMEM)
     whole = pl.BlockSpec(memory_space=pltpu.VMEM)
     hbm = pl.BlockSpec(memory_space=pltpu.HBM)
     shape = jax.ShapeDtypeStruct
-
-    up_arrays, up_places = gathered_by_pairs(out_grad[0], "tensor")
-    w_arrays, w_places = gathered(proj_weight.astype(BF16), "dp")
-    taps_by_row = conv_kernel.transpose(1, 0, 2)
-
-    p, pt, attended, xth, xtl, bh, bl, vpad, q16 = pl.pallas_call(
-        forward,
+    stay = lambda x: pltpu.with_memory_space_constraint(x, pltpu.HBM)
+    q_hbm, k_hbm, v_hbm = stay(queries), stay(keys), stay(values)
+    taps_hbm = stay(conv_kernel.transpose(1, 0, 2))
+    smem = pl.BlockSpec(memory_space=pltpu.SMEM)
+    taps_ref = pltpu.SMEM((taps_a, 1, taps_b), F32)
+    k_in = pltpu.VMEM((key_count, depth), BF16)
+
+    def cost(flops):
+        return pl.CostEstimate(flops=flops, bytes_accessed=10**6, transcendentals=0)
+
+    w_arrays, w_places = gathered(proj_weight, "dp")
+    cores_last = few("tensor") and lax.axis_size("tensor") > 2
+    pieces = [stay(out_grad)]
+    if cores_last:
+        pieces += [swap(out_grad, "tensor", s) for s in range(2, lax.axis_size("tensor"), 2)]
+    p, attended, vpad, q16, q32, pack = pl.pallas_call(
+        functools.partial(forward, len(pieces)),
         out_shape=(
             shape((span, padded), F32),
-            shape((padded, span), BF16),
             shape((span, depth), BF16),
-            shape((wide, taps_a * span), BF16),
-            shape((wide, taps_a * span), BF16),
-            shape((2 * LANES, taps_a * LANES), BF16),
-            shape((2 * LANES, taps_a * LANES), BF16),
             shape((padded, depth), BF16),
             shape((rows_up, depth), BF16),
+            shape((rows_up, depth), F32),
+            shape((len(pieces) * span, out_grad.shape[2]), BF16),
         ),
-        in_specs=[smem, smem, hbm, hbm, hbm],
-        out_specs=(whole,) * 9,
+        in_specs=[hbm] + [whole] * (len(pieces) - 1) + [smem] + [hbm] * 4,
+        out_specs=(whole,) * 6,
         scratch_shapes=[
+            taps_ref,
             pltpu.VMEM((rows, depth), BF16),
-            pltpu.VMEM((key_count, depth), BF16),
-            pltpu.VMEM((key_count, depth), BF16),
-            pltpu.VMEM((rows_up, depth), F32),
+            k_in,
+            k_in,
             pltpu.VMEM((2 * LANES, taps_a * LANES), BF16),
             pltpu.VMEM((2 * LANES, taps_a * LANES), BF16),
             pltpu.VMEM(((blocks + 1) * rows_up, 2 * LANES), BF16),
             pltpu.VMEM(((blocks + 1) * rows_up, 2 * LANES), BF16),
             pltpu.VMEM(((blocks + 1) * rows_up, taps_a * LANES), F32),
-            pltpu.VMEM((wide, depth), BF16),
-            pltpu.SemaphoreType.DMA((3,)),
+            pltpu.SemaphoreType.DMA((5,)),
         ],
         compiler_params=vmem,
-        cost_estimate=pl.CostEstimate(flops=5 * 10**9, bytes_accessed=10**6, transcendentals=span * padded),
+        cost_estimate=cost(5 * 10**9),
         name="attention_forward",
-    )(span_start, taps_by_row, queries, keys, values)
-
-    payload = shape((span + 16, share + LANES), BF16)
-    do, ch, cl, *payloads = pl.pallas_call(
-        functools.partial(backward_scores, taps_b, up_places, w_places, group_count, few("dp")),
+    )(*pieces, span_start, taps_hbm, q_hbm, k_hbm, v_hbm)
+    if cores_last:
+        up_arrays = [pack, swap(pack, "tensor", 1)]
+        up_places = [
+            (c, slice(n * span, (n + 1) * span), 2 * n + c, None) for n in range(len(pieces)) for c in (0, 1)
+        ]
+    else:
+        up_arrays, up_places = gathered(out_grad[0], "tensor")
+    xth, xtl = pl.pallas_call(
+        functools.partial(forward_turned, taps_a),
+        out_shape=(shape((wide, taps_a * span), BF16),) * 2,
+        in_specs=[smem, hbm, whole],
+        out_specs=(whole,) * 2,
+        scratch_shapes=[k_in, pltpu.VMEM((wide, depth), BF16), pltpu.SemaphoreType.DMA((1,))],
+        compiler_params=vmem,
+        cost_estimate=cost(2 * 10**9),
+        name="attention_forward_turned",
+    )(span_start, k_hbm, q32)
+
+    others = group_count - 1 if few("dp") else group_count
+    do, ch, cl, own, own_taps, *payloads = pl.pallas_call(
+        functools.partial(backward_scores, taps_b, up_places, w_places, others, few("dp")),
         out_shape=(
             shape((span, depth), BF16),
             shape(((blocks + 1) * span, LANES), BF16),
             shape(((blocks + 1) * span, LANES), BF16),
-        ) + (payload,) * group_count,
+            shape((depth, share), F32),
+            shape((8, LANES), F32),
+        ) + (shape((depth + 16, max(share, 2 * LANES)), BF16),) * others,
         in_specs=[whole] * (len(up_arrays) + len(w_arrays) + 5),
-        out_specs=(whole,) * (3 + group_count),
-        scratch_shapes=[pltpu.VMEM((span, columns), BF16), pltpu.VMEM((depth, columns), BF16)],
+        out_specs=(whole,) * (5 + others),
+        scratch_shapes=[
+            pltpu.VMEM((span, columns), BF16),
+            pltpu.VMEM((depth, columns), BF16),
+            pltpu.VMEM((depth, columns), F32),
+        ],
         compiler_params=vmem,
-        cost_estimate=pl.CostEstimate(flops=2 * 10**9, bytes_accessed=10**6, transcendentals=0),
+        cost_estimate=cost(2 * 10**9),
         name="attention_backward_scores",
     )(*up_arrays, *w_arrays, p, vpad, xth, xtl, attended)
 
     if few("dp"):
-        payloads = payloads[:1] + [swap(payloads[s], "dp", s) for s in range(1, group_count)]
+        payloads = [swap(payload, "dp", n + 1) for n, payload in enumerate(payloads)]
     else:
         sent = lax.all_to_all(jnp.stack(payloads), "dp", 0, 0)
-        payloads = [sent[s] for s in range(group_count)]
+        payloads = [jnp.where(lax.axis_index("dp") == n, jnp.zeros_like(sent[n]), sent[n]) for n in range(group_count)]
 
     query_grad, key_grad, value_grad = pl.pallas_call(
-        functools.partial(backward_inputs, rows, taps_a),
+        functools.partial(backward_inputs, rows),
         out_shape=(shape(queries.shape, BF16), shape(keys.shape, BF16), shape(values.shape, BF16)),
-        in_specs=[smem] + [whole] * 7 + [hbm],
+        in_specs=[smem, hbm, hbm] + [whole] * 5,
         out_specs=(whole,) * 3,
         scratch_shapes=[
-            pltpu.VMEM((key_count, depth), BF16),
+            taps_ref,
+            k_in,
+            pltpu.VMEM((2 * LANES, taps_a * LANES), BF16),
+            pltpu.VMEM((2 * LANES, taps_a * LANES), BF16),
             pltpu.VMEM((blocks * (span + 32), taps_a * LANES), F32),
-            pltpu.SemaphoreType.DMA((1,)),
+            pltpu.SemaphoreType.DMA((2,)),
         ],
         compiler_params=vmem,
-        cost_estimate=pl.CostEstimate(flops=3 * 10**9, bytes_accessed=10**6, transcendentals=0),
+        cost_estimate=cost(3 * 10**9),
         name="attention_backward_inputs",
-    )(span_start, do, ch, cl, pt, bh, bl, q16, keys)
+    )(span_start, taps_hbm, k_hbm, do, ch, cl, p, q16)
 
     last = up_to(LANES + edge - HALF + half, 16) - 1 - (edge - HALF - half) - LANES
     proj_new, moment_one_new, moment_two_new, kernel_total = pl.pallas_call(
-        functools.partial(update, last),
+        functools.partial(update, last, group_count, span),
         out_shape=(shape(proj_weight.shape, F32),) * 3 + (shape((taps_a, 1, taps_b), F32),),
-        in_specs=[whole] * (group_count + 3),
+        in_specs=[whole] * (len(payloads) + 5),
         out_specs=(whole,) * 4,
         compiler_params=vmem,
         name="projection_update",
-    )(*payloads, proj_weight, moment_one, moment_two)
+    )(*payloads, own, own_taps, proj_weight, moment_one, moment_two)
     return (
         query_grad,
         key_grad,

time: 37.6 us -> 32.5 us (0.86)
  local copies, waits for them, and re-layouts: 3.36 us -> 0.01 us
  other arithmetic: 1.68 us -> 0 us
  Pallas kernels: 12.4 us -> 13.8 us
  waiting for transfers between devices: 4.6 us -> 3.41 us
    unnamed x16 -> x6, local copies, waits for them, and re-layouts: 3.36 us -> 0.01 us
    pallas_call x3 -> x4, Pallas kernels: 10.1 us -> 11.4 us  [the longest x1 4.2 us: shards(): pl.pallas_call(functools.partial(backward_inputs, rows), out_shape=(shape...]
    ppermute x10, waiting for transfers between devices: 4.6 us -> 3.41 us  [swap(): return lax.ppermute(x, axis, [(i, i ^ shift) for i in range(n)])]
    convert_element_type x1 -> x0, other arithmetic: 0.91 us -> none  [shards(): w_arrays, w_places = gathered(proj_weight.astype(BF16), 'dp')]
    concatenate x1 -> x0, other arithmetic: 0.77 us -> none  [gathered_by_pairs(): pair = jnp.concatenate([x, swap(x, axis, 1)], axis=0)]
  transfers between devices with their start and end apart: 10 -> 10, of which waited for: 1 -> 2; matrix products, arithmetic and copies ran while one was open for 5% -> 0% of each run, Pallas kernels for 24% -> 33%
where the time goes in v3:
time: 32.5 us; the launch traced here: 32.3 us
  Pallas kernels  13.8 us (42%)
  starting transfers between devices  13.7 us (42%)
  waiting for transfers between devices  3.41 us (10%)
  between operations  1.38 us (4%)
    ppermute x10, starting transfers between devices, swap(): return lax.ppermute(x, axis, [(i, i ^ shift) for i in range(n)])  13.7 us
    pallas_call x1, Pallas kernels, shards(): pl.pallas_call(functools.partial(backward_inputs, rows), out_shape=(shape...  4.2 us
    pallas_call x1, Pallas kernels, shards(): pl.pallas_call(functools.partial(forward, len(pieces)), out_shape=(shape(...  4 us
    ppermute x10, waiting for transfers between devices, swap(): return lax.ppermute(x, axis, [(i, i ^ shift) for i in range(n)])  3.41 us
    pallas_call x1, Pallas kernels, shards(): pl.pallas_call(functools.partial(backward_scores, taps_b, up_places, w_pl...  2.39 us
    pallas_call x1, Pallas kernels, shards(): pl.pallas_call(functools.partial(forward_turned, taps_a), out_shape=(shap...  2.32 us
    pallas_call x1, Pallas kernels, shards(): pl.pallas_call(functools.partial(update, last, group_count, span), out_sh...  0.87 us
  transfers between devices with their start and end apart: 10, of which 2 were waited for; matrix products, arithmetic and copies ran while one was open for 0% of the time, Pallas kernels for 33%

profile of v3, /device:TPU:0, one launch (start us, length us, event | category | flops | bytes accessed | tf_op | source)
XLA Modules:
  0.0 32.3 jit_solution(13968142466410941151)
XLA Ops:
  0.6 3.0 %collective-permute-start.1 = (bf16[1,128,128]{2,1,0:T(8,128)(2,1)}, bf16[1,128,128]{2,1,0:T(8,128)(2,1)S(1)}, u32[]{:S(2)}, u32[]{:S(2)}) collective-permute-start(bf16[1,128,128]{2,1,0:T(8,128)(2,1)} %refs_0_.1), channel_id=1, source_target_pairs={{0,4},{1,5},{2,6},{3,7},{4,0},{5,1},{6,2},{7,3},{8,12},{9,13},{10,... | collective-permute-start | bytes 98312 | tf_op jit(solution)/shard_map/ppermute | solution.py:300
  3.7 1.5 %collective-permute-start = (bf16[1,128,128]{2,1,0:T(8,128)(2,1)}, bf16[1,128,128]{2,1,0:T(8,128)(2,1)S(1)}, u32[]{:S(2)}, u32[]{:S(2)}) collective-permute-start(bf16[1,128,128]{2,1,0:T(8,128)(2,1)} %refs_0_.1), channel_id=1, source_target_pairs={{0,2},{1,3},{2,0},{3,1},{4,6},{5,7},{6,4},{7,5},{8,10},{9,11},{10,... | collective-permute-start | bytes 98312 | tf_op jit(solution)/shard_map/ppermute | solution.py:300
  5.2 0.0 collective-permute-start.2
  5.2 4.0 %collective-permute-start.6 = (f32[128,256]{1,0:T(8,128)}, f32[128,256]{1,0:T(8,128)S(1)}, u32[]{:S(2)}, u32[]{:S(2)}) collective-permute-start(f32[128,256]{1,0:T(8,128)} %refs_5_.1), channel_id=1, source_target_pairs={{0,24},{8,16},{16,8},{24,0},{1,25},{9,17},{17,9},{25,1},{2,26},{10... | collective-permute-start | bytes 393224 | tf_op jit(solution)/shard_map/ppermute | solution.py:300
  9.2 0.0 collective-permute-start.5
  9.9 0.0 collective-permute-done.1.refs_2_
  9.9 0.6 %collective-permute-start.4 = (f32[128,256]{1,0:T(8,128)}, f32[128,256]{1,0:T(8,128)S(1)}, u32[]{:S(2)}, u32[]{:S(2)}) collective-permute-start(f32[128,256]{1,0:T(8,128)} %refs_5_.1), channel_id=1, source_target_pairs={{0,8},{8,0},{16,24},{24,16},{1,9},{9,1},{17,25},{25,17},{2,10},{10... | collective-permute-start | bytes 393224 | tf_op jit(solution)/shard_map/ppermute | solution.py:300
  10.5 0.0 collective-permute-done.refs_1_
  10.5 0.0 collective-permute-done.2.refs_3_
  10.5 4.0 %attention_forward.1 = (f32[128,1152]{1,0:T(8,128)S(1)}, bf16[128,128]{1,0:T(8,128)(2,1)S(1)}, bf16[1152,128]{1,0:T(8,128)(2,1)S(1)}, bf16[144,128]{1,0:T(8,128)...) custom-call(bf16[1,128,128]{2,1,0:T(8,128)(2,1)} %refs_0_.1, ...), custom_call_target="tpu_custom_call" | custom-call | flops 5000000000 | bytes 1000000 | tf_op jit(solution)/shard_map/attention_forward/pallas_call | solution.py:349
  14.5 0.1 collective-permute-start.3
  14.6 0.0 copy-start
  14.6 2.3 %attention_forward_turned.1 = (bf16[1184,768]{1,0:T(8,128)(2,1)S(1)}, bf16[1184,768]{1,0:T(8,128)(2,1)S(1)}) custom-call(s32[1]{0:T(128)S(6)} %copy.16.refs_4_.first_ref, bf16[1,1024,128]{2,1,0:T(8,128)(2,1)} %k_hbm.3, f32[144,128]{1,0:T(8,128)S(1)} %get-tuple-element.33.q32), custom_call_target="tpu_custom_call" | custom-call | flops 2000000000 | bytes 1000000 | tf_op jit(solution)/shard_map/attention_forward_turned/pallas_call | solution.py:384
  17.0 0.0 collective-permute-done.6.refs_5_
  17.0 2.7 %collective-permute-done.5.refs_4_ = f32[128,256]{1,0:T(8,128)S(1)} collective-permute-done((f32[128,256]{1,0:T(8,128)}, f32[128,256]{1,0:T(8,128)S(1)}, u32[]{:S(2)}, u32[]{:S(2)}) %collective-permute-start.5) | collective-permute-done | bytes 131104 | tf_op jit(solution)/shard_map/ppermute | solution.py:300
  19.7 0.0 collective-permute-done.4.refs_3_
  19.7 0.0 collective-permute-done.3.refs_1_
  19.7 0.0 copy-done
  19.7 2.4 %attention_backward_scores.1 = (bf16[128,128]{1,0:T(8,128)(2,1)S(1)}, bf16[1152,128]{1,0:T(8,128)(2,1)S(1)}, bf16[1152,128]{1,0:T(8,128)(2,1)S(1)}, f32[128,256]...) custom-call(bf16[512,128]{1,0:T(8,128)(2,1)S(1)} %get-tuple-element., ...), custom_call_target="tpu_custom_call" | custom-call | flops 2000000000 | bytes 1000000 | tf_op jit(solution)/shard_map/attention_backward_scores/pallas_call | solution.py:396
  22.1 0.1 collective-permute-start.7
  22.2 3.0 %collective-permute-start.8 = (bf16[144,256]{1,0:T(8,128)(2,1)S(1)}, bf16[144,256]{1,0:T(8,128)(2,1)S(1)}, u32[]{:S(2)}, u32[]{:S(2)}) collective-permute-start(bf16[144,256]{1,0:T(8,128)(2,1)S(1)} %get-tuple-element.45), channel_id=1, source_target_pairs={{0,16},{8,24},{16,0},{24,8},{1,17},{9,25},{17,1},{25,9},{2,18},{10... | collective-permute-start | bytes 221192 | tf_op jit(solution)/shard_map/ppermute | solution.py:300
  25.2 1.3 %collective-permute-start.9 = (bf16[144,256]{1,0:T(8,128)(2,1)S(1)}, bf16[144,256]{1,0:T(8,128)(2,1)S(1)}, u32[]{:S(2)}, u32[]{:S(2)}) collective-permute-start(bf16[144,256]{1,0:T(8,128)(2,1)S(1)} %get-tuple-element.46), channel_id=1, source_target_pairs={{0,24},{8,16},{16,8},{24,0},{1,25},{9,17},{17,9},{25,1},{2,26},{10... | collective-permute-start | bytes 221192 | tf_op jit(solution)/shard_map/ppermute | solution.py:300
  26.5 0.0 copy-start.1
  26.5 0.0 copy-start.2
  26.5 4.2 %attention_backward_inputs.1 = (bf16[1,133,128]{2,1,0:T(8,128)(2,1)}, bf16[1,1024,128]{2,1,0:T(8,128)(2,1)}, bf16[1,1024,128]{2,1,0:T(8,128)(2,1)}) custom-call(s32[1]{0:T(128)S(6)} %copy.16.refs_4_.first_ref, f32[6,1,11]{2,1,0:T(1,128)} %bitcast.3, bf16[1,1024,128]{2,1,0:T(8,128)(2,1)} %k_hbm.3, bf16[128,128]{1,0:T(8,128)(2,1)S(1)} %get-tuple-element.37.do_ref, ...), custom_call_target="tpu_custom_call" | custom-call | flops 3000000000 | bytes 1000000 | tf_op jit(solution)/shard_map/attention_backward_inputs/pallas_call | solution.py:423
  30.8 0.0 collective-permute-done.7.refs_0_
  30.8 0.0 collective-permute-done.8.refs_1_
  30.8 0.7 %collective-permute-done.9.refs_2_ = bf16[144,256]{1,0:T(8,128)(2,1)S(1)} collective-permute-done((bf16[144,256]{1,0:T(8,128)(2,1)S(1)}, bf16[144,256]{1,0:T(8,128)(2,1)S(1)}, u32[]{:S(2)}, u32[]{:S(2)}) %collective-permute-start.9) | collective-permute-done | bytes 73760 | tf_op jit(solution)/shard_map/ppermute | solution.py:300
  31.5 0.0 copy-done.1
  31.5 0.0 copy-done.2
  31.5 0.9 %projection_update.1 = (f32[128,256]{1,0:T(8,128)}, f32[128,256]{1,0:T(8,128)}, f32[128,256]{1,0:T(8,128)}, f32[6,1,11]{2,1,0:T(1,128)}) custom-call(bf16[144,256]{1,0:T(8,128)(2,1)S(1)} %collective-permute-done.7.refs_0_, bf16[144,256]{1,0:T(8,128)(2,1)S(1)} %collective-permute-done.8.refs_1_, bf16[144,256]{1,0:T(8,128)(2,1)S(1)} %collective-permute-done.9.refs_2_, ...), custom_call_target="tpu_custom_call" | custom-call | tf_op jit(solution)/shard_map/projection_update/pallas_call | solution.py:442
Async XLA Ops:
  0.6 9.3 %collective-permute-start.1 = (bf16[1,128,128]{2,1,0:T(8,128)(2,1)}, bf16[1,128,128]{2,1,0:T(8,128)(2,1)S(1)}, u32[]{:S(2)}, u32[]{:S(2)}) collective-permute-start(bf16[1,128,128]{2,1,0:T(8,128)(2,1)} %refs_0_.1), channel_id=1, source_target_pairs={{0,4},{1,5},{2,6},{3,7},{4,0},{5,1},{6,2},{7,3},{8,12},{9,13},{10,... | collective-permute-start | bytes 98312 | tf_op jit(solution)/shard_map/ppermute | solution.py:300
  3.7 6.9 %collective-permute-start = (bf16[1,128,128]{2,1,0:T(8,128)(2,1)}, bf16[1,128,128]{2,1,0:T(8,128)(2,1)S(1)}, u32[]{:S(2)}, u32[]{:S(2)}) collective-permute-start(bf16[1,128,128]{2,1,0:T(8,128)(2,1)} %refs_0_.1), channel_id=1, source_target_pairs={{0,2},{1,3},{2,0},{3,1},{4,6},{5,7},{6,4},{7,5},{8,10},{9,11},{10,... | collective-permute-start | bytes 98312 | tf_op jit(solution)/shard_map/ppermute | solution.py:300
  5.2 5.4 %collective-permute-start.2 = (bf16[1,128,128]{2,1,0:T(8,128)(2,1)}, bf16[1,128,128]{2,1,0:T(8,128)(2,1)S(1)}, u32[]{:S(2)}, u32[]{:S(2)}) collective-permute-start(bf16[1,128,128]{2,1,0:T(8,128)(2,1)} %refs_0_.1), channel_id=1, source_target_pairs={{0,6},{1,7},{2,4},{3,5},{4,2},{5,3},{6,0},{7,1},{8,14},{9,15},{10,... | collective-permute-start | bytes 98312 | tf_op jit(solution)/shard_map/ppermute | solution.py:300
  5.2 11.8 %collective-permute-start.6 = (f32[128,256]{1,0:T(8,128)}, f32[128,256]{1,0:T(8,128)S(1)}, u32[]{:S(2)}, u32[]{:S(2)}) collective-permute-start(f32[128,256]{1,0:T(8,128)} %refs_5_.1), channel_id=1, source_target_pairs={{0,24},{8,16},{16,8},{24,0},{1,25},{9,17},{17,9},{25,1},{2,26},{10... | collective-permute-start | bytes 393224 | tf_op jit(solution)/shard_map/ppermute | solution.py:300
  9.2 10.4 %collective-permute-start.5 = (f32[128,256]{1,0:T(8,128)}, f32[128,256]{1,0:T(8,128)S(1)}, u32[]{:S(2)}, u32[]{:S(2)}) collective-permute-start(f32[128,256]{1,0:T(8,128)} %refs_5_.1), channel_id=1, source_target_pairs={{0,16},{8,24},{16,0},{24,8},{1,17},{9,25},{17,1},{25,9},{2,18},{10... | collective-permute-start | bytes 393224 | tf_op jit(solution)/shard_map/ppermute | solution.py:300
  9.9 9.8 %collective-permute-start.4 = (f32[128,256]{1,0:T(8,128)}, f32[128,256]{1,0:T(8,128)S(1)}, u32[]{:S(2)}, u32[]{:S(2)}) collective-permute-start(f32[128,256]{1,0:T(8,128)} %refs_5_.1), channel_id=1, source_target_pairs={{0,8},{8,0},{16,24},{24,16},{1,9},{9,1},{17,25},{25,17},{2,10},{10... | collective-permute-start | bytes 393224 | tf_op jit(solution)/shard_map/ppermute | solution.py:300
  14.5 5.1 %collective-permute-start.3 = (bf16[512,128]{1,0:T(8,128)(2,1)S(1)}, bf16[512,128]{1,0:T(8,128)(2,1)S(1)}, u32[]{:S(2)}, u32[]{:S(2)}) collective-permute-start(bf16[512,128]{1,0:T(8,128)(2,1)S(1)} %get-tuple-element.30.refs_0_), channel_id=1, source_target_pairs={{0,1},{1,0},{2,3},{3,2},{4,5},{5,4},{6,7},{7,6},{8,9},{9,8},{10,11... | collective-permute-start | bytes 393224 | tf_op jit(solution)/shard_map/ppermute | solution.py:300
  14.6 5.1 %copy-start = (f32[128,256]{1,0:T(8,128)S(1)}, f32[128,256]{1,0:T(8,128)}, u32[]{:S(2)}) copy-start(f32[128,256]{1,0:T(8,128)} %refs_5_.1) | copy-start | bytes 393220
  22.1 8.7 %collective-permute-start.7 = (bf16[144,256]{1,0:T(8,128)(2,1)S(1)}, bf16[144,256]{1,0:T(8,128)(2,1)S(1)}, u32[]{:S(2)}, u32[]{:S(2)}) collective-permute-start(bf16[144,256]{1,0:T(8,128)(2,1)S(1)} %get-tuple-element.44), channel_id=1, source_target_pairs={{0,8},{8,0},{16,24},{24,16},{1,9},{9,1},{17,25},{25,17},{2,10},{10... | collective-permute-start | bytes 221192 | tf_op jit(solution)/shard_map/ppermute | solution.py:300
  22.2 8.6 %collective-permute-start.8 = (bf16[144,256]{1,0:T(8,128)(2,1)S(1)}, bf16[144,256]{1,0:T(8,128)(2,1)S(1)}, u32[]{:S(2)}, u32[]{:S(2)}) collective-permute-start(bf16[144,256]{1,0:T(8,128)(2,1)S(1)} %get-tuple-element.45), channel_id=1, source_target_pairs={{0,16},{8,24},{16,0},{24,8},{1,17},{9,25},{17,1},{25,9},{2,18},{10... | collective-permute-start | bytes 221192 | tf_op jit(solution)/shard_map/ppermute | solution.py:300
  25.2 6.3 %collective-permute-start.9 = (bf16[144,256]{1,0:T(8,128)(2,1)S(1)}, bf16[144,256]{1,0:T(8,128)(2,1)S(1)}, u32[]{:S(2)}, u32[]{:S(2)}) collective-permute-start(bf16[144,256]{1,0:T(8,128)(2,1)S(1)} %get-tuple-element.46), channel_id=1, source_target_pairs={{0,24},{8,16},{16,8},{24,0},{1,25},{9,17},{17,9},{25,1},{2,26},{10... | collective-permute-start | bytes 221192 | tf_op jit(solution)/shard_map/ppermute | solution.py:300
  26.5 4.9 %copy-start.1 = (f32[128,256]{1,0:T(8,128)S(1)}, f32[128,256]{1,0:T(8,128)}, u32[]{:S(2)}) copy-start(f32[128,256]{1,0:T(8,128)} %refs_6_.3) | copy-start | bytes 393220
  26.5 4.9 %copy-start.2 = (f32[128,256]{1,0:T(8,128)S(1)}, f32[128,256]{1,0:T(8,128)}, u32[]{:S(2)}) copy-start(f32[128,256]{1,0:T(8,128)} %refs_7_.3) | copy-start | bytes 393220

commit v4 on v3

--- a/solution.py
+++ b/solution.py
@@ -58,11 +58,20 @@
     return copies
 
 
-def forward(pieces, *refs):
-    piece_refs, (first_ref, taps_hbm, q_hbm, k_hbm, v_hbm) = refs[:pieces], refs[pieces : pieces + 5]
-    p_ref, o_ref, vpad, q16, q32, pack_ref = refs[pieces + 5 : pieces + 11]
-    taps_ref, q_in, k_in, v_in, fh, fl, xh, xl, y, sems = refs[pieces + 11 :]
-    taps_a, _, _ = taps_ref.shape
+def prepare(taps_hbm, w_hbm, w_ref, fh, fl, taps_ref, w_in, sems):
+    copies = fetch(((w_hbm, w_in), (taps_hbm, taps_ref)), sems)
+    copies[1].wait()
+    for a, f in enumerate(bands(taps_ref, False)):
+        cols = pl.ds(a * LANES, LANES)
+        fh[:, cols], fl[:, cols] = split(f)
+    copies[0].wait()
+    w_ref[...] = w_in[...].astype(BF16)
+
+
+def forward(pieces, taps_a, *refs):
+    piece_refs, (first_ref, fh, fl, q_hbm, k_hbm, v_hbm) = refs[:pieces], refs[pieces : pieces + 6]
+    p_ref, o_ref, vpad, q16, q32, pack_ref = refs[pieces + 6 : pieces + 12]
+    q_in, k_in, v_in, xh, xl, y, sems = refs[pieces + 12 :]
     rows, depth = q_in.shape
     keys = k_in.shape[0]
     span = rows - taps_a + 1
@@ -71,7 +80,6 @@
     scale = 1.0 / math.sqrt(depth)
     copies = fetch(
         (
-            (taps_hbm, taps_ref),
             (q_hbm.at[0], q_in),
             (k_hbm.at[0], k_in),
             (v_hbm.at[0], v_in),
@@ -83,11 +91,7 @@
         pack_ref[(n + 1) * span : (n + 2) * span] = ref[0]
     q32[...] = jnp.zeros_like(q32)
     vpad[...] = jnp.zeros_like(vpad)
-    copies[0].wait()
-    for a, f in enumerate(bands(taps_ref, False)):
-        cols = pl.ds(a * LANES, LANES)
-        fh[:, cols], fl[:, cols] = split(f)
-    for copy in copies[1:]:
+    for copy in copies:
         copy.wait()
     first = first_ref[0]
     q32[:rows] = q_in[...].astype(F32)
@@ -172,7 +176,7 @@
             block = refs_in[n][part]
             width = block.shape[1]
             spot = at if shift is None else lax.bitwise_xor(me, shift)
-            whole[:, pl.ds(pl.multiple_of(spot * width, width), width)] = block.astype(BF16)
+            whole[:, pl.ds(pl.multiple_of(spot * width, width), width)] = block
     do = dot(up[...], w[...], ((1,), (1,))).astype(BF16)
     do_ref[...] = do
     grad[...] = dot(o_ref[...], up[...], ((0,), (0,)))
@@ -341,13 +345,24 @@
     def cost(flops):
         return pl.CostEstimate(flops=flops, bytes_accessed=10**6, transcendentals=0)
 
-    w_arrays, w_places = gathered(proj_weight, "dp")
+    band = shape((2 * LANES, taps_a * LANES), BF16)
+    proj_bf, fh, fl = pl.pallas_call(
+        prepare,
+        out_shape=(shape(proj_weight.shape, BF16), band, band),
+        in_specs=[hbm, hbm],
+        out_specs=(whole,) * 3,
+        scratch_shapes=[taps_ref, pltpu.VMEM(proj_weight.shape, F32), pltpu.SemaphoreType.DMA((2,))],
+        compiler_params=vmem,
+        cost_estimate=cost(10**9),
+        name="prepare",
+    )(taps_hbm, stay(proj_weight))
+    w_arrays, w_places = gathered(proj_bf, "dp")
     cores_last = few("tensor") and lax.axis_size("tensor") > 2
     pieces = [stay(out_grad)]
     if cores_last:
         pieces += [swap(out_grad, "tensor", s) for s in range(2, lax.axis_size("tensor"), 2)]
     p, attended, vpad, q16, q32, pack = pl.pallas_call(
-        functools.partial(forward, len(pieces)),
+        functools.partial(forward, len(pieces), taps_a),
         out_shape=(
             shape((span, padded), F32),
             shape((span, depth), BF16),
@@ -356,24 +371,21 @@
             shape((rows_up, depth), F32),
             shape((len(pieces) * span, out_grad.shape[2]), BF16),
         ),
-        in_specs=[hbm] + [whole] * (len(pieces) - 1) + [smem] + [hbm] * 4,
+        in_specs=[hbm] + [whole] * (len(pieces) - 1) + [smem, whole, whole] + [hbm] * 3,
         out_specs=(whole,) * 6,
         scratch_shapes=[
-            taps_ref,
             pltpu.VMEM((rows, depth), BF16),
             k_in,
             k_in,
-            pltpu.VMEM((2 * LANES, taps_a * LANES), BF16),
-            pltpu.VMEM((2 * LANES, taps_a * LANES), BF16),
             pltpu.VMEM(((blocks + 1) * rows_up, 2 * LANES), BF16),
             pltpu.VMEM(((blocks + 1) * rows_up, 2 * LANES), BF16),
             pltpu.VMEM(((blocks + 1) * rows_up, taps_a * LANES), F32),
-            pltpu.SemaphoreType.DMA((5,)),
+            pltpu.SemaphoreType.DMA((4,)),
         ],
         compiler_params=vmem,
         cost_estimate=cost(5 * 10**9),
         name="attention_forward",
-    )(*pieces, span_start, taps_hbm, q_hbm, k_hbm, v_hbm)
+    )(*pieces, span_start, fh, fl, q_hbm, k_hbm, v_hbm)
     if cores_last:
         up_arrays = [pack, swap(pack, "tensor", 1)]
         up_places = [

time: 32.5 us -> 32.3 us (level)
  waiting for transfers between devices: 3.41 us -> 1.9 us
  Pallas kernels: 13.8 us -> 14.9 us
    ppermute x10, waiting for transfers between devices: 3.41 us -> 1.9 us  [swap(): return lax.ppermute(x, axis, [(i, i ^ shift) for i in range(n)])]
    pallas_call x1 -> x2, Pallas kernels: 4 us -> 5.18 us  [the longest x1 3.88 us: shards(): pl.pallas_call(functools.partial(forward, len(pieces), taps_a), out_shape...]
  transfers between devices with their start and end apart: 10 -> 10, of which waited for: 2 -> 1; matrix products, arithmetic and copies ran while one was open for 0% -> 0% of each run, Pallas kernels for 33% -> 36%
where the time goes in v4:
time: 32.3 us; the launch traced here: 32.1 us
  Pallas kernels  14.9 us (46%)
  starting transfers between devices  13.9 us (43%)
  waiting for transfers between devices  1.9 us (6%)
  between operations  1.39 us (4%)
    ppermute x10, starting transfers between devices, swap(): return lax.ppermute(x, axis, [(i, i ^ shift) for i in range(n)])  13.9 us
    pallas_call x1, Pallas kernels, shards(): pl.pallas_call(functools.partial(backward_inputs, rows), out_shape=(shape...  4.21 us
    pallas_call x1, Pallas kernels, shards(): pl.pallas_call(functools.partial(forward, len(pieces), taps_a), out_shape...  3.88 us
    pallas_call x1, Pallas kernels, shards(): pl.pallas_call(functools.partial(backward_scores, taps_b, up_places, w_pl...  2.38 us
    pallas_call x1, Pallas kernels, shards(): pl.pallas_call(functools.partial(forward_turned, taps_a), out_shape=(shap...  2.26 us
    ppermute x10, waiting for transfers between devices, swap(): return lax.ppermute(x, axis, [(i, i ^ shift) for i in range(n)])  1.9 us
    pallas_call x1, Pallas kernels, shards(): pl.pallas_call(prepare, out_shape=(shape(proj_weight.shape, BF16), band,...  1.3 us
    pallas_call x1, Pallas kernels, shards(): pl.pallas_call(functools.partial(update, last, group_count, span), out_sh...  0.88 us
  transfers between devices with their start and end apart: 10, of which 1 were waited for; matrix products, arithmetic and copies ran while one was open for 0% of the time, Pallas kernels for 36%

profile of v4, /device:TPU:0, one launch (start us, length us, event | category | flops | bytes accessed | tf_op | source)
XLA Modules:
  0.0 32.1 jit_solution(17511189715688101854)
XLA Ops:
  0.6 3.0 %collective-permute-start.1 = (bf16[1,128,128]{2,1,0:T(8,128)(2,1)}, bf16[1,128,128]{2,1,0:T(8,128)(2,1)S(1)}, u32[]{:S(2)}, u32[]{:S(2)}) collective-permute-start(bf16[1,128,128]{2,1,0:T(8,128)(2,1)} %refs_0_.1), channel_id=1, source_target_pairs={{0,4},{1,5},{2,6},{3,7},{4,0},{5,1},{6,2},{7,3},{8,12},{9,13},{10,... | collective-permute-start | bytes 98312 | tf_op jit(solution)/shard_map/ppermute | solution.py:304
  3.7 1.5 %collective-permute-start = (bf16[1,128,128]{2,1,0:T(8,128)(2,1)}, bf16[1,128,128]{2,1,0:T(8,128)(2,1)S(1)}, u32[]{:S(2)}, u32[]{:S(2)}) collective-permute-start(bf16[1,128,128]{2,1,0:T(8,128)(2,1)} %refs_0_.1), channel_id=1, source_target_pairs={{0,2},{1,3},{2,0},{3,1},{4,6},{5,7},{6,4},{7,5},{8,10},{9,11},{10,... | collective-permute-start | bytes 98312 | tf_op jit(solution)/shard_map/ppermute | solution.py:304
  5.2 0.1 collective-permute-start.2
  5.2 1.3 %prepare.1 = (bf16[128,256]{1,0:T(8,128)(2,1)S(1)}, bf16[256,768]{1,0:T(8,128)(2,1)S(1)}, bf16[256,768]{1,0:T(8,128)(2,1)S(1)}) custom-call(f32[6,1,11]{2,1,0:T(1,128)} %bitcast.2, f32[128,256]{1,0:T(8,128)} %refs_5_.1), custom_call_target="tpu_custom_call" | custom-call | flops 1000000000 | bytes 1000000 | tf_op jit(solution)/shard_map/prepare/pallas_call | solution.py:349
  6.5 4.1 %collective-permute-start.6 = (bf16[128,256]{1,0:T(8,128)(2,1)S(1)}, bf16[128,256]{1,0:T(8,128)(2,1)S(1)}, u32[]{:S(2)}, u32[]{:S(2)}) collective-permute-start(bf16[128,256]{1,0:T(8,128)(2,1)S(1)} %get-tuple-element.36.refs_2_), channel_id=1, source_target_pairs={{0,24},{8,16},{16,8},{24,0},{1,25},{9,17},{17,9},{25,1},{2,26},{10... | collective-permute-start | bytes 196616 | tf_op jit(solution)/shard_map/ppermute | solution.py:304
  10.6 0.0 collective-permute-start.5
  11.3 0.0 collective-permute-done.1.refs_2_
  11.3 0.7 %collective-permute-start.4 = (bf16[128,256]{1,0:T(8,128)(2,1)S(1)}, bf16[128,256]{1,0:T(8,128)(2,1)S(1)}, u32[]{:S(2)}, u32[]{:S(2)}) collective-permute-start(bf16[128,256]{1,0:T(8,128)(2,1)S(1)} %get-tuple-element.36.refs_2_), channel_id=1, source_target_pairs={{0,8},{8,0},{16,24},{24,16},{1,9},{9,1},{17,25},{25,17},{2,10},{10... | collective-permute-start | bytes 196616 | tf_op jit(solution)/shard_map/ppermute | solution.py:304
  12.0 0.0 collective-permute-done.refs_1_
  12.0 0.0 collective-permute-done.2.refs_3_
  12.0 3.9 %attention_forward.1 = (f32[128,1152]{1,0:T(8,128)S(1)}, bf16[128,128]{1,0:T(8,128)(2,1)S(1)}, bf16[1152,128]{1,0:T(8,128)(2,1)S(1)}, bf16[144,128]{1,0:T(8,128)...) custom-call(bf16[1,128,128]{2,1,0:T(8,128)(2,1)} %refs_0_.1, ...), custom_call_target="tpu_custom_call" | custom-call | flops 5000000000 | bytes 1000000 | tf_op jit(solution)/shard_map/attention_forward/pallas_call | solution.py:364
  15.9 0.1 collective-permute-start.3
  16.0 2.3 %attention_forward_turned.1 = (bf16[1184,768]{1,0:T(8,128)(2,1)S(1)}, bf16[1184,768]{1,0:T(8,128)(2,1)S(1)}) custom-call(s32[1]{0:T(128)S(6)} %copy.16.refs_4_.first_ref, bf16[1,1024,128]{2,1,0:T(8,128)(2,1)} %k_hbm.3, f32[144,128]{1,0:T(8,128)S(1)} %get-tuple-element.39.q32), custom_call_target="tpu_custom_call" | custom-call | flops 2000000000 | bytes 1000000 | tf_op jit(solution)/shard_map/attention_forward_turned/pallas_call | solution.py:396
  18.2 0.0 collective-permute-done.6.refs_5_
  18.2 0.0 collective-permute-done.5.refs_4_
  18.2 0.0 collective-permute-done.4.refs_3_
  18.2 0.0 collective-permute-done.3.refs_1_
  18.3 2.4 %attention_backward_scores.1 = (bf16[128,128]{1,0:T(8,128)(2,1)S(1)}, bf16[1152,128]{1,0:T(8,128)(2,1)S(1)}, bf16[1152,128]{1,0:T(8,128)(2,1)S(1)}, f32[128,256]...) custom-call(bf16[512,128]{1,0:T(8,128)(2,1)S(1)} %get-tuple-element., ...), custom_call_target="tpu_custom_call" | custom-call | flops 2000000000 | bytes 1000000 | tf_op jit(solution)/shard_map/attention_backward_scores/pallas_call | solution.py:408
  20.6 1.4 %collective-permute-start.7 = (bf16[144,256]{1,0:T(8,128)(2,1)S(1)}, bf16[144,256]{1,0:T(8,128)(2,1)S(1)}, u32[]{:S(2)}, u32[]{:S(2)}) collective-permute-start(bf16[144,256]{1,0:T(8,128)(2,1)S(1)} %get-tuple-element.50), channel_id=1, source_target_pairs={{0,8},{8,0},{16,24},{24,16},{1,9},{9,1},{17,25},{25,17},{2,10},{10... | collective-permute-start | bytes 221192 | tf_op jit(solution)/shard_map/ppermute | solution.py:304
  22.1 2.9 %collective-permute-start.8 = (bf16[144,256]{1,0:T(8,128)(2,1)S(1)}, bf16[144,256]{1,0:T(8,128)(2,1)S(1)}, u32[]{:S(2)}, u32[]{:S(2)}) collective-permute-start(bf16[144,256]{1,0:T(8,128)(2,1)S(1)} %get-tuple-element.51), channel_id=1, source_target_pairs={{0,16},{8,24},{16,0},{24,8},{1,17},{9,25},{17,1},{25,9},{2,18},{10... | collective-permute-start | bytes 221192 | tf_op jit(solution)/shard_map/ppermute | solution.py:304
  25.0 0.1 collective-permute-start.9
  25.1 0.0 copy-start
  25.1 0.0 copy-start.1
  25.1 0.0 copy-start.2
  25.1 4.2 %attention_backward_inputs.1 = (bf16[1,133,128]{2,1,0:T(8,128)(2,1)}, bf16[1,1024,128]{2,1,0:T(8,128)(2,1)}, bf16[1,1024,128]{2,1,0:T(8,128)(2,1)}) custom-call(s32[1]{0:T(128)S(6)} %copy.16.refs_4_.first_ref, f32[6,1,11]{2,1,0:T(1,128)} %bitcast.3, bf16[1,1024,128]{2,1,0:T(8,128)(2,1)} %k_hbm.3, bf16[128,128]{1,0:T(8,128)(2,1)S(1)} %get-tuple-element.43.do_ref, ...), custom_call_target="tpu_custom_call" | custom-call | flops 3000000000 | bytes 1000000 | tf_op jit(solution)/shard_map/attention_backward_inputs/pallas_call | solution.py:435
  29.3 0.0 collective-permute-done.7.refs_0_
  29.3 1.9 %collective-permute-done.8.refs_1_ = bf16[144,256]{1,0:T(8,128)(2,1)S(1)} collective-permute-done((bf16[144,256]{1,0:T(8,128)(2,1)S(1)}, bf16[144,256]{1,0:T(8,128)(2,1)S(1)}, u32[]{:S(2)}, u32[]{:S(2)}) %collective-permute-start.8) | collective-permute-done | bytes 73760 | tf_op jit(solution)/shard_map/ppermute | solution.py:304
  31.2 0.0 collective-permute-done.9.refs_2_
  31.2 0.0 copy-done
  31.2 0.0 copy-done.1
  31.2 0.0 copy-done.2
  31.2 0.9 %projection_update.1 = (f32[128,256]{1,0:T(8,128)}, f32[128,256]{1,0:T(8,128)}, f32[128,256]{1,0:T(8,128)}, f32[6,1,11]{2,1,0:T(1,128)}) custom-call(bf16[144,256]{1,0:T(8,128)(2,1)S(1)} %collective-permute-done.7.refs_0_, bf16[144,256]{1,0:T(8,128)(2,1)S(1)} %collective-permute-done.8.refs_1_, bf16[144,256]{1,0:T(8,128)(2,1)S(1)} %collective-permute-done.9.refs_2_, ...), custom_call_target="tpu_custom_call" | custom-call | tf_op jit(solution)/shard_map/projection_update/pallas_call | solution.py:454
Async XLA Ops:
  0.6 10.6 %collective-permute-start.1 = (bf16[1,128,128]{2,1,0:T(8,128)(2,1)}, bf16[1,128,128]{2,1,0:T(8,128)(2,1)S(1)}, u32[]{:S(2)}, u32[]{:S(2)}) collective-permute-start(bf16[1,128,128]{2,1,0:T(8,128)(2,1)} %refs_0_.1), channel_id=1, source_target_pairs={{0,4},{1,5},{2,6},{3,7},{4,0},{5,1},{6,2},{7,3},{8,12},{9,13},{10,... | collective-permute-start | bytes 98312 | tf_op jit(solution)/shard_map/ppermute | solution.py:304
  3.7 8.3 %collective-permute-start = (bf16[1,128,128]{2,1,0:T(8,128)(2,1)}, bf16[1,128,128]{2,1,0:T(8,128)(2,1)S(1)}, u32[]{:S(2)}, u32[]{:S(2)}) collective-permute-start(bf16[1,128,128]{2,1,0:T(8,128)(2,1)} %refs_0_.1), channel_id=1, source_target_pairs={{0,2},{1,3},{2,0},{3,1},{4,6},{5,7},{6,4},{7,5},{8,10},{9,11},{10,... | collective-permute-start | bytes 98312 | tf_op jit(solution)/shard_map/ppermute | solution.py:304
  5.2 6.8 %collective-permute-start.2 = (bf16[1,128,128]{2,1,0:T(8,128)(2,1)}, bf16[1,128,128]{2,1,0:T(8,128)(2,1)S(1)}, u32[]{:S(2)}, u32[]{:S(2)}) collective-permute-start(bf16[1,128,128]{2,1,0:T(8,128)(2,1)} %refs_0_.1), channel_id=1, source_target_pairs={{0,6},{1,7},{2,4},{3,5},{4,2},{5,3},{6,0},{7,1},{8,14},{9,15},{10,... | collective-permute-start | bytes 98312 | tf_op jit(solution)/shard_map/ppermute | solution.py:304
  6.5 11.7 %collective-permute-start.6 = (bf16[128,256]{1,0:T(8,128)(2,1)S(1)}, bf16[128,256]{1,0:T(8,128)(2,1)S(1)}, u32[]{:S(2)}, u32[]{:S(2)}) collective-permute-start(bf16[128,256]{1,0:T(8,128)(2,1)S(1)} %get-tuple-element.36.refs_2_), channel_id=1, source_target_pairs={{0,24},{8,16},{16,8},{24,0},{1,25},{9,17},{17,9},{25,1},{2,26},{10... | collective-permute-start | bytes 196616 | tf_op jit(solution)/shard_map/ppermute | solution.py:304
  10.6 7.6 %collective-permute-start.5 = (bf16[128,256]{1,0:T(8,128)(2,1)S(1)}, bf16[128,256]{1,0:T(8,128)(2,1)S(1)}, u32[]{:S(2)}, u32[]{:S(2)}) collective-permute-start(bf16[128,256]{1,0:T(8,128)(2,1)S(1)} %get-tuple-element.36.refs_2_), channel_id=1, source_target_pairs={{0,16},{8,24},{16,0},{24,8},{1,17},{9,25},{17,1},{25,9},{2,18},{10... | collective-permute-start | bytes 196616 | tf_op jit(solution)/shard_map/ppermute | solution.py:304
  11.3 7.0 %collective-permute-start.4 = (bf16[128,256]{1,0:T(8,128)(2,1)S(1)}, bf16[128,256]{1,0:T(8,128)(2,1)S(1)}, u32[]{:S(2)}, u32[]{:S(2)}) collective-permute-start(bf16[128,256]{1,0:T(8,128)(2,1)S(1)} %get-tuple-element.36.refs_2_), channel_id=1, source_target_pairs={{0,8},{8,0},{16,24},{24,16},{1,9},{9,1},{17,25},{25,17},{2,10},{10... | collective-permute-start | bytes 196616 | tf_op jit(solution)/shard_map/ppermute | solution.py:304
  15.9 2.4 %collective-permute-start.3 = (bf16[512,128]{1,0:T(8,128)(2,1)S(1)}, bf16[512,128]{1,0:T(8,128)(2,1)S(1)}, u32[]{:S(2)}, u32[]{:S(2)}) collective-permute-start(bf16[512,128]{1,0:T(8,128)(2,1)S(1)} %get-tuple-element.35.refs_0_), channel_id=1, source_target_pairs={{0,1},{1,0},{2,3},{3,2},{4,5},{5,4},{6,7},{7,6},{8,9},{9,8},{10,11... | collective-permute-start | bytes 393224 | tf_op jit(solution)/shard_map/ppermute | solution.py:304
  20.6 8.7 %collective-permute-start.7 = (bf16[144,256]{1,0:T(8,128)(2,1)S(1)}, bf16[144,256]{1,0:T(8,128)(2,1)S(1)}, u32[]{:S(2)}, u32[]{:S(2)}) collective-permute-start(bf16[144,256]{1,0:T(8,128)(2,1)S(1)} %get-tuple-element.50), channel_id=1, source_target_pairs={{0,8},{8,0},{16,24},{24,16},{1,9},{9,1},{17,25},{25,17},{2,10},{10... | collective-permute-start | bytes 221192 | tf_op jit(solution)/shard_map/ppermute | solution.py:304
  22.1 9.1 %collective-permute-start.8 = (bf16[144,256]{1,0:T(8,128)(2,1)S(1)}, bf16[144,256]{1,0:T(8,128)(2,1)S(1)}, u32[]{:S(2)}, u32[]{:S(2)}) collective-permute-start(bf16[144,256]{1,0:T(8,128)(2,1)S(1)} %get-tuple-element.51), channel_id=1, source_target_pairs={{0,16},{8,24},{16,0},{24,8},{1,17},{9,25},{17,1},{25,9},{2,18},{10... | collective-permute-start | bytes 221192 | tf_op jit(solution)/shard_map/ppermute | solution.py:304
  25.0 6.2 %collective-permute-start.9 = (bf16[144,256]{1,0:T(8,128)(2,1)S(1)}, bf16[144,256]{1,0:T(8,128)(2,1)S(1)}, u32[]{:S(2)}, u32[]{:S(2)}) collective-permute-start(bf16[144,256]{1,0:T(8,128)(2,1)S(1)} %get-tuple-element.52), channel_id=1, source_target_pairs={{0,24},{8,16},{16,8},{24,0},{1,25},{9,17},{17,9},{25,1},{2,26},{10... | collective-permute-start | bytes 221192 | tf_op jit(solution)/shard_map/ppermute | solution.py:304
  25.1 6.1 %copy-start = (f32[128,256]{1,0:T(8,128)S(1)}, f32[128,256]{1,0:T(8,128)}, u32[]{:S(2)}) copy-start(f32[128,256]{1,0:T(8,128)} %refs_5_.1) | copy-start | bytes 393220
  25.1 6.1 %copy-start.1 = (f32[128,256]{1,0:T(8,128)S(1)}, f32[128,256]{1,0:T(8,128)}, u32[]{:S(2)}) copy-start(f32[128,256]{1,0:T(8,128)} %refs_6_.1) | copy-start | bytes 393220
  25.1 6.1 %copy-start.2 = (f32[128,256]{1,0:T(8,128)S(1)}, f32[128,256]{1,0:T(8,128)}, u32[]{:S(2)}) copy-start(f32[128,256]{1,0:T(8,128)} %refs_7_.3) | copy-start | bytes 393220

commit v5 on v3

--- a/solution.py
+++ b/solution.py
@@ -58,49 +58,52 @@
     return copies
 
 
-def forward(pieces, *refs):
-    piece_refs, (first_ref, taps_hbm, q_hbm, k_hbm, v_hbm) = refs[:pieces], refs[pieces : pieces + 5]
-    p_ref, o_ref, vpad, q16, q32, pack_ref = refs[pieces + 5 : pieces + 11]
-    taps_ref, q_in, k_in, v_in, fh, fl, xh, xl, y, sems = refs[pieces + 11 :]
-    taps_a, _, _ = taps_ref.shape
-    rows, depth = q_in.shape
-    keys = k_in.shape[0]
-    span = rows - taps_a + 1
-    rows_up = q32.shape[0]
-    blocks = keys // LANES
-    scale = 1.0 / math.sqrt(depth)
+def prepare(taps_hbm, w_hbm, q_hbm, k_hbm, v_hbm, w_ref, fh, fl, q32, q16, k_ref, vpad, taps_ref, w_in, q_in, sems):
+    rows = q_in.shape[0]
+    keys = k_ref.shape[0]
     copies = fetch(
         (
             (taps_hbm, taps_ref),
+            (w_hbm, w_in),
             (q_hbm.at[0], q_in),
-            (k_hbm.at[0], k_in),
-            (v_hbm.at[0], v_in),
-            (piece_refs[0].at[0], pack_ref.at[pl.ds(0, span)]),
+            (k_hbm.at[0], k_ref),
+            (v_hbm.at[0], vpad.at[pl.ds(HALF, keys)]),
         ),
         sems,
     )
-    for n, ref in enumerate(piece_refs[1:]):
-        pack_ref[(n + 1) * span : (n + 2) * span] = ref[0]
     q32[...] = jnp.zeros_like(q32)
-    vpad[...] = jnp.zeros_like(vpad)
+    vpad[:HALF] = jnp.zeros((HALF, vpad.shape[1]), BF16)
+    vpad[HALF + keys :] = jnp.zeros((vpad.shape[0] - HALF - keys, vpad.shape[1]), BF16)
     copies[0].wait()
     for a, f in enumerate(bands(taps_ref, False)):
         cols = pl.ds(a * LANES, LANES)
         fh[:, cols], fl[:, cols] = split(f)
     for copy in copies[1:]:
         copy.wait()
+    w_ref[...] = w_in[...].astype(BF16)
+    q32[:rows] = q_in[...].astype(F32)
+    q16[...] = q32[...].astype(BF16)
+
+
+def forward(pieces, taps_a, *refs):
+    piece_refs, (first_ref, fh, fl, q16, k_ref, vpad) = refs[:pieces], refs[pieces : pieces + 6]
+    p_ref, o_ref, pack_ref, xh, xl, y = refs[pieces + 6 :]
+    keys, depth = k_ref.shape
+    span = p_ref.shape[0]
+    rows_up = q16.shape[0]
+    blocks = keys // LANES
+    scale = 1.0 / math.sqrt(depth)
     first = first_ref[0]
-    q32[:rows] = q_in[...].astype(F32)
-    q_all = q32[...].astype(BF16)
-    q16[...] = q_all
-    vpad[HALF : HALF + keys] = v_in[...]
+    for n, ref in enumerate(piece_refs):
+        pack_ref[n * span : (n + 1) * span] = ref[0]
+    q_all = q16[...]
 
     zero = jnp.zeros((rows_up, LANES), BF16)
     for ref in (xh, xl):
         ref[:rows_up, :LANES] = zero
         ref[blocks * rows_up :, LANES:] = zero
     for n in range(blocks):
-        x = dot(q_all, k_in[n * LANES : (n + 1) * LANES], ((1,), (1,))) * scale
+        x = dot(q_all, k_ref[n * LANES : (n + 1) * LANES], ((1,), (1,))) * scale
         key = n * LANES + iota(x.shape, 1)
         pos = first - (taps_a - 1) + iota(x.shape, 0)
         high, low = split(jnp.where(key <= pos, x, 0.0))
@@ -108,9 +111,10 @@
             ref[n * rows_up : (n + 1) * rows_up, LANES:] = part
             ref[(n + 1) * rows_up : (n + 2) * rows_up, :LANES] = part
 
+    left = jnp.concatenate([xh[...], xh[...], xl[...]], axis=1)
     for at in range(0, taps_a * LANES, 2 * LANES):
         cols = pl.ds(at, 2 * LANES)
-        y[:, cols] = dot(xh[...], fh[:, cols]) + dot(xh[...], fl[:, cols]) + dot(xl[...], fh[:, cols])
+        y[:, cols] = dot(left, jnp.concatenate([fh[:, cols], fl[:, cols], fh[:, cols]], axis=0))
     mixed = []
     for w in range(blocks + 1):
         total = None
@@ -129,21 +133,18 @@
     o_ref[...] = dot(p.astype(BF16), vpad[...]).astype(BF16)
 
 
-def forward_turned(taps_a, first_ref, k_hbm, q32, xth_ref, xtl_ref, k_in, kpad, sems):
-    keys, depth = k_in.shape
+def forward_turned(taps_a, first_ref, k_ref, q32, xth_ref, xtl_ref, kpad):
+    keys, depth = k_ref.shape
     span = xth_ref.shape[1] // taps_a
     blocks = keys // LANES
     scale = 1.0 / math.sqrt(depth)
-    copies = fetch(((k_hbm.at[0], k_in),), sems)
     kpad[...] = jnp.zeros_like(kpad)
     edge = (kpad.shape[0] - keys) // 2
     flip = (iota((LANES, LANES), 0) + iota((LANES, LANES), 1) == LANES - 1).astype(F32).astype(BF16)
-    for copy in copies:
-        copy.wait()
     first = first_ref[0]
     for n in range(blocks):
         kpad[edge + n * LANES : edge + (n + 1) * LANES] = dot(
-            flip, k_in[keys - (n + 1) * LANES : keys - n * LANES]
+            flip, k_ref[keys - (n + 1) * LANES : keys - n * LANES]
         ).astype(BF16)
     for a in range(taps_a):
         start = taps_a - 1 - a
@@ -172,7 +173,7 @@
             block = refs_in[n][part]
             width = block.shape[1]
             spot = at if shift is None else lax.bitwise_xor(me, shift)
-            whole[:, pl.ds(pl.multiple_of(spot * width, width), width)] = block.astype(BF16)
+            whole[:, pl.ds(pl.multiple_of(spot * width, width), width)] = block
     do = dot(up[...], w[...], ((1,), (1,))).astype(BF16)
     do_ref[...] = do
     grad[...] = dot(o_ref[...], up[...], ((0,), (0,)))
@@ -187,17 +188,21 @@
 
     window = up_to(LANES + edge - HALF + half, 16)
     right = jnp.concatenate([ch[...], cl[...]], axis=1)
+    right = jnp.concatenate([right, right], axis=0)
     spot = window - 1 - (edge - HALF - half) - iota((window, LANES), 0) - iota((window, LANES), 1)
     wanted = (spot >= 0) & (spot < taps_b)
     sums = []
     for a in range(taps_a):
-        total = None
-        for ref in (xth_ref, xtl_ref):
-            left = jnp.concatenate(
-                [ref[n * LANES : n * LANES + window, a * LANES : (a + 1) * LANES] for n in range(blocks, -1, -1)], axis=1
-            )
-            term = dot(left, right)
-            total = term if total is None else total + term
+        cols = slice(a * LANES, (a + 1) * LANES)
+        left = jnp.concatenate(
+            [
+                ref[n * LANES : n * LANES + window, cols]
+                for ref in (xth_ref, xtl_ref)
+                for n in range(blocks, -1, -1)
+            ],
+            axis=1,
+        )
+        total = dot(left, right)
         total = jnp.where(wanted, total[:, :LANES] + total[:, LANES:], 0.0)
         sums.append(jnp.sum(pltpu.roll(total, 0, 1, stride=1, stride_axis=0), axis=0, keepdims=True))
     taps = jnp.concatenate(sums + [jnp.zeros((8 - taps_a, LANES), F32)], axis=0)
@@ -243,12 +248,13 @@
     for n in range(blocks):
         left_h = jnp.concatenate([ch[n * span : (n + 1) * span], ch[(n + 1) * span : (n + 2) * span]], axis=1)
         left_l = jnp.concatenate([cl[n * span : (n + 1) * span], cl[(n + 1) * span : (n + 2) * span]], axis=1)
+        left = jnp.concatenate([left_h, left_h, left_l], axis=1)
         z[n * depth_z : n * depth_z + 8] = jnp.zeros((8, z.shape[1]), F32)
         z[n * depth_z + 8 + span : (n + 1) * depth_z] = jnp.zeros((depth_z - 8 - span, z.shape[1]), F32)
         for at in range(0, taps_a * LANES, 2 * LANES):
             cols = pl.ds(at, 2 * LANES)
-            z[n * depth_z + 8 : n * depth_z + 8 + span, cols] = (
-                dot(left_h, bh[:, cols]) + dot(left_h, bl[:, cols]) + dot(left_l, bh[:, cols])
+            z[n * depth_z + 8 : n * depth_z + 8 + span, cols] = dot(
+                left, jnp.concatenate([bh[:, cols], bl[:, cols], bh[:, cols]], axis=0)
             )
     for copy in copies[1:]:
         copy.wait()
@@ -341,39 +347,53 @@
     def cost(flops):
         return pl.CostEstimate(flops=flops, bytes_accessed=10**6, transcendentals=0)
 
-    w_arrays, w_places = gathered(proj_weight, "dp")
+    band = shape((2 * LANES, taps_a * LANES), BF16)
+    proj_bf, fh, fl, q32, q16, k, vpad = pl.pallas_call(
+        prepare,
+        out_shape=(
+            shape(proj_weight.shape, BF16),
+            band,
+            band,
+            shape((rows_up, depth), F32),
+            shape((rows_up, depth), BF16),
+            shape((key_count, depth), BF16),
+            shape((padded, depth), BF16),
+        ),
+        in_specs=[hbm] * 5,
+        out_specs=(whole,) * 7,
+        scratch_shapes=[
+            taps_ref,
+            pltpu.VMEM(proj_weight.shape, F32),
+            pltpu.VMEM((rows, depth), BF16),
+            pltpu.SemaphoreType.DMA((5,)),
+        ],
+        compiler_params=vmem,
+        cost_estimate=cost(10**9),
+        name="prepare",
+    )(taps_hbm, stay(proj_weight), q_hbm, k_hbm, v_hbm)
+    w_arrays, w_places = gathered(proj_bf, "dp")
     cores_last = few("tensor") and lax.axis_size("tensor") > 2
     pieces = [stay(out_grad)]
     if cores_last:
         pieces += [swap(out_grad, "tensor", s) for s in range(2, lax.axis_size("tensor"), 2)]
-    p, attended, vpad, q16, q32, pack = pl.pallas_call(
-        functools.partial(forward, len(pieces)),
+    p, attended, pack = pl.pallas_call(
+        functools.partial(forward, len(pieces), taps_a),
         out_shape=(
             shape((span, padded), F32),
             shape((span, depth), BF16),
-            shape((padded, depth), BF16),
-            shape((rows_up, depth), BF16),
-            shape((rows_up, depth), F32),
             shape((len(pieces) * span, out_grad.shape[2]), BF16),
         ),
-        in_specs=[hbm] + [whole] * (len(pieces) - 1) + [smem] + [hbm] * 4,
-        out_specs=(whole,) * 6,
+        in_specs=[whole] * len(pieces) + [smem] + [whole] * 5,
+        out_specs=(whole,) * 3,
         scratch_shapes=[
-            taps_ref,
-            pltpu.VMEM((rows, depth), BF16),
-            k_in,
-            k_in,
-            pltpu.VMEM((2 * LANES, taps_a * LANES), BF16),
-            pltpu.VMEM((2 * LANES, taps_a * LANES), BF16),
             pltpu.VMEM(((blocks + 1) * rows_up, 2 * LANES), BF16),
             pltpu.VMEM(((blocks + 1) * rows_up, 2 * LANES), BF16),
             pltpu.VMEM(((blocks + 1) * rows_up, taps_a * LANES), F32),
-            pltpu.SemaphoreType.DMA((5,)),
         ],
         compiler_params=vmem,
         cost_estimate=cost(5 * 10**9),
         name="attention_forward",
-    )(*pieces, span_start, taps_hbm, q_hbm, k_hbm, v_hbm)
+    )(*pieces, span_start, fh, fl, q16, k, vpad)
     if cores_last:
         up_arrays = [pack, swap(pack, "tensor", 1)]
         up_places = [
@@ -384,13 +404,13 @@
     xth, xtl = pl.pallas_call(
         functools.partial(forward_turned, taps_a),
         out_shape=(shape((wide, taps_a * span), BF16),) * 2,
-        in_specs=[smem, hbm, whole],
+        in_specs=[smem, whole, whole],
         out_specs=(whole,) * 2,
-        scratch_shapes=[k_in, pltpu.VMEM((wide, depth), BF16), pltpu.SemaphoreType.DMA((1,))],
+        scratch_shapes=[pltpu.VMEM((wide, depth), BF16)],
         compiler_params=vmem,
         cost_estimate=cost(2 * 10**9),
         name="attention_forward_turned",
-    )(span_start, k_hbm, q32)
+    )(span_start, k, q32)
 
     others = group_count - 1 if few("dp") else group_count
     do, ch, cl, own, own_taps, *payloads = pl.pallas_call(

time: 32.5 us -> 30.8 us (0.948)
  waiting for transfers between devices: 3.41 us -> 1.95 us
  Pallas kernels: 13.8 us -> 13.3 us
    ppermute x10, waiting for transfers between devices: 3.41 us -> 1.95 us  [swap(): return lax.ppermute(x, axis, [(i, i ^ shift) for i in range(n)])]
    pallas_call x1, Pallas kernels: 2.32 us -> 1.3 us  [shards(): pl.pallas_call(functools.partial(forward_turned, taps_a), out_shape=(shap...]
    pallas_call x1 -> x2, Pallas kernels: 4 us -> 4.65 us  [the longest x1 3.44 us: shards(): pl.pallas_call(functools.partial(forward, len(pieces), taps_a), out_shape...]
  transfers between devices with their start and end apart: 10 -> 10, of which waited for: 2 -> 1; matrix products, arithmetic and copies ran while one was open for 0% -> 0% of each run, Pallas kernels for 33% -> 33%
where the time goes in v5:
time: 30.8 us; the launch traced here: 30.5 us
  starting transfers between devices  13.9 us (45%)
  Pallas kernels  13.3 us (43%)
  waiting for transfers between devices  1.95 us (6%)
  between operations  1.39 us (5%)
    ppermute x10, starting transfers between devices, swap(): return lax.ppermute(x, axis, [(i, i ^ shift) for i in range(n)])  13.9 us
    pallas_call x1, Pallas kernels, shards(): pl.pallas_call(functools.partial(backward_inputs, rows), out_shape=(shape...  4.17 us
    pallas_call x1, Pallas kernels, shards(): pl.pallas_call(functools.partial(forward, len(pieces), taps_a), out_shape...  3.44 us
    pallas_call x1, Pallas kernels, shards(): pl.pallas_call(functools.partial(backward_scores, taps_b, up_places, w_pl...  2.27 us
    ppermute x10, waiting for transfers between devices, swap(): return lax.ppermute(x, axis, [(i, i ^ shift) for i in range(n)])  1.95 us
    pallas_call x1, Pallas kernels, shards(): pl.pallas_call(functools.partial(forward_turned, taps_a), out_shape=(shap...  1.3 us
    pallas_call x1, Pallas kernels, shards(): pl.pallas_call(prepare, out_shape=(shape(proj_weight.shape, BF16), band,...  1.22 us
    pallas_call x1, Pallas kernels, shards(): pl.pallas_call(functools.partial(update, last, group_count, span), out_sh...  0.88 us
  transfers between devices with their start and end apart: 10, of which 1 were waited for; matrix products, arithmetic and copies ran while one was open for 0% of the time, Pallas kernels for 33%

profile of v5, /device:TPU:0, one launch (start us, length us, event | category | flops | bytes accessed | tf_op | source)
XLA Modules:
  0.0 30.5 jit_solution(4415661320954477616)
XLA Ops:
  0.6 3.0 %collective-permute-start.1 = (bf16[1,128,128]{2,1,0:T(8,128)(2,1)}, bf16[1,128,128]{2,1,0:T(8,128)(2,1)S(1)}, u32[]{:S(2)}, u32[]{:S(2)}) collective-permute-start(bf16[1,128,128]{2,1,0:T(8,128)(2,1)} %refs_0_.1), channel_id=1, source_target_pairs={{0,4},{1,5},{2,6},{3,7},{4,0},{5,1},{6,2},{7,3},{8,12},{9,13},{10,... | collective-permute-start | bytes 98312 | tf_op jit(solution)/shard_map/ppermute | solution.py:306
  3.7 1.5 %collective-permute-start = (bf16[1,128,128]{2,1,0:T(8,128)(2,1)}, bf16[1,128,128]{2,1,0:T(8,128)(2,1)S(1)}, u32[]{:S(2)}, u32[]{:S(2)}) collective-permute-start(bf16[1,128,128]{2,1,0:T(8,128)(2,1)} %refs_0_.1), channel_id=1, source_target_pairs={{0,2},{1,3},{2,0},{3,1},{4,6},{5,7},{6,4},{7,5},{8,10},{9,11},{10,... | collective-permute-start | bytes 98312 | tf_op jit(solution)/shard_map/ppermute | solution.py:306
  5.2 0.1 collective-permute-start.2
  5.2 1.2 %prepare.1 = (bf16[128,256]{1,0:T(8,128)(2,1)S(1)}, bf16[256,768]{1,0:T(8,128)(2,1)S(1)}, bf16[256,768]{1,0:T(8,128)(2,1)S(1)}, f32[144,128]{1,0:T(8,128)S(1)}, ...) custom-call(f32[6,1,11]{2,1,0:T(1,128)} %bitcast.2, ...), custom_call_target="tpu_custom_call" | custom-call | flops 1000000000 | bytes 1000000 | tf_op jit(solution)/shard_map/prepare/pallas_call | solution.py:351
  6.4 4.1 %collective-permute-start.6 = (bf16[128,256]{1,0:T(8,128)(2,1)S(1)}, bf16[128,256]{1,0:T(8,128)(2,1)S(1)}, u32[]{:S(2)}, u32[]{:S(2)}) collective-permute-start(bf16[128,256]{1,0:T(8,128)(2,1)S(1)} %get-tuple-element.40.refs_2_), channel_id=1, source_target_pairs={{0,24},{8,16},{16,8},{24,0},{1,25},{9,17},{17,9},{25,1},{2,26},{10... | collective-permute-start | bytes 196616 | tf_op jit(solution)/shard_map/ppermute | solution.py:306
  10.5 0.0 collective-permute-start.5
  11.2 0.0 collective-permute-done.1.refs_2_
  11.2 0.7 %collective-permute-start.4 = (bf16[128,256]{1,0:T(8,128)(2,1)S(1)}, bf16[128,256]{1,0:T(8,128)(2,1)S(1)}, u32[]{:S(2)}, u32[]{:S(2)}) collective-permute-start(bf16[128,256]{1,0:T(8,128)(2,1)S(1)} %get-tuple-element.40.refs_2_), channel_id=1, source_target_pairs={{0,8},{8,0},{16,24},{24,16},{1,9},{9,1},{17,25},{25,17},{2,10},{10... | collective-permute-start | bytes 196616 | tf_op jit(solution)/shard_map/ppermute | solution.py:306
  11.9 0.0 collective-permute-done.refs_1_
  11.9 0.0 collective-permute-done.2.refs_3_
  11.9 3.4 %attention_forward.1 = (f32[128,1152]{1,0:T(8,128)S(1)}, bf16[128,128]{1,0:T(8,128)(2,1)S(1)}, bf16[512,128]{1,0:T(8,128)(2,1)S(1)}) custom-call(bf16[1,128,128]{2,1,0:T(8,128)(2,1)} %refs_0_.1, bf16[1,128,128]{2,1,0:T(8,128)(2,1)S(1)} %collective-permute-done.refs_1_, bf16[1,128,128]{2,1,0:T(8,128)(2,1)S(1)} %collective-permute-done.1.refs_2_, ...), custom_call_target="tpu_custom_call" | custom-call | flops 5000000000 | bytes 1000000 | tf_op jit(solution)/shard_map/attention_forward/pallas_call | solution.py:379
  15.3 0.1 collective-permute-start.3
  15.4 1.3 %attention_forward_turned.1 = (bf16[1184,768]{1,0:T(8,128)(2,1)S(1)}, bf16[1184,768]{1,0:T(8,128)(2,1)S(1)}) custom-call(s32[1]{0:T(128)S(6)} %copy.16.refs_4_.first_ref, bf16[1024,128]{1,0:T(8,128)(2,1)S(1)} %get-tuple-element.37.refs_8_.k_ref, f32[144,128]{1,0:T(8,128)S(1)} %get-tuple-element.42.q32), custom_call_target="tpu_custom_call" | custom-call | flops 2000000000 | bytes 1000000 | tf_op jit(solution)/shard_map/attention_forward_turned/pallas_call | solution.py:404
  16.7 0.0 collective-permute-done.6.refs_5_
  16.7 0.0 collective-permute-done.5.refs_4_
  16.8 0.0 collective-permute-done.4.refs_3_
  16.8 0.0 collective-permute-done.3.refs_1_
  16.8 2.3 %attention_backward_scores.1 = (bf16[128,128]{1,0:T(8,128)(2,1)S(1)}, bf16[1152,128]{1,0:T(8,128)(2,1)S(1)}, bf16[1152,128]{1,0:T(8,128)(2,1)S(1)}, f32[128,256]...) custom-call(bf16[512,128]{1,0:T(8,128)(2,1)S(1)} %get-tuple-element., ...), custom_call_target="tpu_custom_call" | custom-call | flops 2000000000 | bytes 1000000 | tf_op jit(solution)/shard_map/attention_backward_scores/pallas_call | solution.py:416
  19.0 1.5 %collective-permute-start.7 = (bf16[144,256]{1,0:T(8,128)(2,1)S(1)}, bf16[144,256]{1,0:T(8,128)(2,1)S(1)}, u32[]{:S(2)}, u32[]{:S(2)}) collective-permute-start(bf16[144,256]{1,0:T(8,128)(2,1)S(1)} %get-tuple-element.52), channel_id=1, source_target_pairs={{0,8},{8,0},{16,24},{24,16},{1,9},{9,1},{17,25},{25,17},{2,10},{10... | collective-permute-start | bytes 221192 | tf_op jit(solution)/shard_map/ppermute | solution.py:306
  20.5 2.9 %collective-permute-start.8 = (bf16[144,256]{1,0:T(8,128)(2,1)S(1)}, bf16[144,256]{1,0:T(8,128)(2,1)S(1)}, u32[]{:S(2)}, u32[]{:S(2)}) collective-permute-start(bf16[144,256]{1,0:T(8,128)(2,1)S(1)} %get-tuple-element.53), channel_id=1, source_target_pairs={{0,16},{8,24},{16,0},{24,8},{1,17},{9,25},{17,1},{25,9},{2,18},{10... | collective-permute-start | bytes 221192 | tf_op jit(solution)/shard_map/ppermute | solution.py:306
  23.4 0.1 collective-permute-start.9
  23.5 0.0 copy-start
  23.5 0.0 copy-start.1
  23.5 0.0 copy-start.2
  23.5 4.2 %attention_backward_inputs.1 = (bf16[1,133,128]{2,1,0:T(8,128)(2,1)}, bf16[1,1024,128]{2,1,0:T(8,128)(2,1)}, bf16[1,1024,128]{2,1,0:T(8,128)(2,1)}) custom-call(s32[1]{0:T(128)S(6)} %copy.16.refs_4_.first_ref, f32[6,1,11]{2,1,0:T(1,128)} %bitcast.3, bf16[1,1024,128]{2,1,0:T(8,128)(2,1)} %k_hbm.3, bf16[128,128]{1,0:T(8,128)(2,1)S(1)} %get-tuple-element.46.do_ref, ...), custom_call_target="tpu_custom_call" | custom-call | flops 3000000000 | bytes 1000000 | tf_op jit(solution)/shard_map/attention_backward_inputs/pallas_call | solution.py:443
  27.7 0.0 collective-permute-done.7.refs_0_
  27.7 1.9 %collective-permute-done.8.refs_1_ = bf16[144,256]{1,0:T(8,128)(2,1)S(1)} collective-permute-done((bf16[144,256]{1,0:T(8,128)(2,1)S(1)}, bf16[144,256]{1,0:T(8,128)(2,1)S(1)}, u32[]{:S(2)}, u32[]{:S(2)}) %collective-permute-start.8) | collective-permute-done | bytes 73760 | tf_op jit(solution)/shard_map/ppermute | solution.py:306
  29.6 0.0 collective-permute-done.9.refs_2_
  29.6 0.0 copy-done
  29.6 0.0 copy-done.1
  29.6 0.0 copy-done.2
  29.6 0.9 %projection_update.1 = (f32[128,256]{1,0:T(8,128)}, f32[128,256]{1,0:T(8,128)}, f32[128,256]{1,0:T(8,128)}, f32[6,1,11]{2,1,0:T(1,128)}) custom-call(bf16[144,256]{1,0:T(8,128)(2,1)S(1)} %collective-permute-done.7.refs_0_, bf16[144,256]{1,0:T(8,128)(2,1)S(1)} %collective-permute-done.8.refs_1_, bf16[144,256]{1,0:T(8,128)(2,1)S(1)} %collective-permute-done.9.refs_2_, ...), custom_call_target="tpu_custom_call" | custom-call | tf_op jit(solution)/shard_map/projection_update/pallas_call | solution.py:462
Async XLA Ops:
  0.6 10.6 %collective-permute-start.1 = (bf16[1,128,128]{2,1,0:T(8,128)(2,1)}, bf16[1,128,128]{2,1,0:T(8,128)(2,1)S(1)}, u32[]{:S(2)}, u32[]{:S(2)}) collective-permute-start(bf16[1,128,128]{2,1,0:T(8,128)(2,1)} %refs_0_.1), channel_id=1, source_target_pairs={{0,4},{1,5},{2,6},{3,7},{4,0},{5,1},{6,2},{7,3},{8,12},{9,13},{10,... | collective-permute-start | bytes 98312 | tf_op jit(solution)/shard_map/ppermute | solution.py:306
  3.7 8.2 %collective-permute-start = (bf16[1,128,128]{2,1,0:T(8,128)(2,1)}, bf16[1,128,128]{2,1,0:T(8,128)(2,1)S(1)}, u32[]{:S(2)}, u32[]{:S(2)}) collective-permute-start(bf16[1,128,128]{2,1,0:T(8,128)(2,1)} %refs_0_.1), channel_id=1, source_target_pairs={{0,2},{1,3},{2,0},{3,1},{4,6},{5,7},{6,4},{7,5},{8,10},{9,11},{10,... | collective-permute-start | bytes 98312 | tf_op jit(solution)/shard_map/ppermute | solution.py:306
  5.2 6.7 %collective-permute-start.2 = (bf16[1,128,128]{2,1,0:T(8,128)(2,1)}, bf16[1,128,128]{2,1,0:T(8,128)(2,1)S(1)}, u32[]{:S(2)}, u32[]{:S(2)}) collective-permute-start(bf16[1,128,128]{2,1,0:T(8,128)(2,1)} %refs_0_.1), channel_id=1, source_target_pairs={{0,6},{1,7},{2,4},{3,5},{4,2},{5,3},{6,0},{7,1},{8,14},{9,15},{10,... | collective-permute-start | bytes 98312 | tf_op jit(solution)/shard_map/ppermute | solution.py:306
  6.4 10.3 %collective-permute-start.6 = (bf16[128,256]{1,0:T(8,128)(2,1)S(1)}, bf16[128,256]{1,0:T(8,128)(2,1)S(1)}, u32[]{:S(2)}, u32[]{:S(2)}) collective-permute-start(bf16[128,256]{1,0:T(8,128)(2,1)S(1)} %get-tuple-element.40.refs_2_), channel_id=1, source_target_pairs={{0,24},{8,16},{16,8},{24,0},{1,25},{9,17},{17,9},{25,1},{2,26},{10... | collective-permute-start | bytes 196616 | tf_op jit(solution)/shard_map/ppermute | solution.py:306
  10.5 6.2 %collective-permute-start.5 = (bf16[128,256]{1,0:T(8,128)(2,1)S(1)}, bf16[128,256]{1,0:T(8,128)(2,1)S(1)}, u32[]{:S(2)}, u32[]{:S(2)}) collective-permute-start(bf16[128,256]{1,0:T(8,128)(2,1)S(1)} %get-tuple-element.40.refs_2_), channel_id=1, source_target_pairs={{0,16},{8,24},{16,0},{24,8},{1,17},{9,25},{17,1},{25,9},{2,18},{10... | collective-permute-start | bytes 196616 | tf_op jit(solution)/shard_map/ppermute | solution.py:306
  11.2 5.6 %collective-permute-start.4 = (bf16[128,256]{1,0:T(8,128)(2,1)S(1)}, bf16[128,256]{1,0:T(8,128)(2,1)S(1)}, u32[]{:S(2)}, u32[]{:S(2)}) collective-permute-start(bf16[128,256]{1,0:T(8,128)(2,1)S(1)} %get-tuple-element.40.refs_2_), channel_id=1, source_target_pairs={{0,8},{8,0},{16,24},{24,16},{1,9},{9,1},{17,25},{25,17},{2,10},{10... | collective-permute-start | bytes 196616 | tf_op jit(solution)/shard_map/ppermute | solution.py:306
  15.3 1.4 %collective-permute-start.3 = (bf16[512,128]{1,0:T(8,128)(2,1)S(1)}, bf16[512,128]{1,0:T(8,128)(2,1)S(1)}, u32[]{:S(2)}, u32[]{:S(2)}) collective-permute-start(bf16[512,128]{1,0:T(8,128)(2,1)S(1)} %get-tuple-element.39.refs_0_), channel_id=1, source_target_pairs={{0,1},{1,0},{2,3},{3,2},{4,5},{5,4},{6,7},{7,6},{8,9},{9,8},{10,11... | collective-permute-start | bytes 393224 | tf_op jit(solution)/shard_map/ppermute | solution.py:306
  19.0 8.6 %collective-permute-start.7 = (bf16[144,256]{1,0:T(8,128)(2,1)S(1)}, bf16[144,256]{1,0:T(8,128)(2,1)S(1)}, u32[]{:S(2)}, u32[]{:S(2)}) collective-permute-start(bf16[144,256]{1,0:T(8,128)(2,1)S(1)} %get-tuple-element.52), channel_id=1, source_target_pairs={{0,8},{8,0},{16,24},{24,16},{1,9},{9,1},{17,25},{25,17},{2,10},{10... | collective-permute-start | bytes 221192 | tf_op jit(solution)/shard_map/ppermute | solution.py:306
  20.5 9.1 %collective-permute-start.8 = (bf16[144,256]{1,0:T(8,128)(2,1)S(1)}, bf16[144,256]{1,0:T(8,128)(2,1)S(1)}, u32[]{:S(2)}, u32[]{:S(2)}) collective-permute-start(bf16[144,256]{1,0:T(8,128)(2,1)S(1)} %get-tuple-element.53), channel_id=1, source_target_pairs={{0,16},{8,24},{16,0},{24,8},{1,17},{9,25},{17,1},{25,9},{2,18},{10... | collective-permute-start | bytes 221192 | tf_op jit(solution)/shard_map/ppermute | solution.py:306
  23.4 6.2 %collective-permute-start.9 = (bf16[144,256]{1,0:T(8,128)(2,1)S(1)}, bf16[144,256]{1,0:T(8,128)(2,1)S(1)}, u32[]{:S(2)}, u32[]{:S(2)}) collective-permute-start(bf16[144,256]{1,0:T(8,128)(2,1)S(1)} %get-tuple-element.54), channel_id=1, source_target_pairs={{0,24},{8,16},{16,8},{24,0},{1,25},{9,17},{17,9},{25,1},{2,26},{10... | collective-permute-start | bytes 221192 | tf_op jit(solution)/shard_map/ppermute | solution.py:306
  23.5 6.1 %copy-start = (f32[128,256]{1,0:T(8,128)S(1)}, f32[128,256]{1,0:T(8,128)}, u32[]{:S(2)}) copy-start(f32[128,256]{1,0:T(8,128)} %refs_5_.1) | copy-start | bytes 393220
  23.5 6.1 %copy-start.1 = (f32[128,256]{1,0:T(8,128)S(1)}, f32[128,256]{1,0:T(8,128)}, u32[]{:S(2)}) copy-start(f32[128,256]{1,0:T(8,128)} %refs_6_.1) | copy-start | bytes 393220
  23.5 6.1 %copy-start.2 = (f32[128,256]{1,0:T(8,128)S(1)}, f32[128,256]{1,0:T(8,128)}, u32[]{:S(2)}) copy-start(f32[128,256]{1,0:T(8,128)} %refs_7_.1) | copy-start | bytes 393220

commit v6 on v5

v6 whole, which is shorter than its diff:
```python
import functools
import math

import jax
import jax.numpy as jnp
from jax import lax
from jax.experimental import pallas as pl
from jax.experimental.pallas import tpu as pltpu
from jax.sharding import PartitionSpec as P

beta_one = 0.9
beta_two = 0.95
learn_rate = 0.01
decay_rate = 0.1
adam_eps = 1e-08
bias_one = 1.0 - 0.9**10
bias_two = 1.0 - 0.95**10

LANES = 128
HALF = LANES // 2
F32 = jnp.float32
BF16 = jnp.bfloat16


def dot(left, right, dims=((1,), (0,))):
    return lax.dot_general(left, right, (dims, ((), ())), preferred_element_type=F32)


def split(x):
    high = x.astype(BF16)
    return high, (x - high.astype(F32)).astype(BF16)


def up_to(n, multiple):
    return -(-n // multiple) * multiple


def iota(shape, axis):
    return lax.broadcasted_iota(jnp.int32, shape, axis)


def bands(taps_ref, turned):
    taps_a, _, taps_b = taps_ref.shape
    place = iota((LANES, LANES), 0) - iota((LANES, LANES), 1)
    place = -place if turned else place
    out = [jnp.zeros((LANES, LANES), F32) for _ in range(taps_a)]
    for b in range(taps_b):
        here = place == b
        for a in range(taps_a):
            out[a] = jnp.where(here, taps_ref[a, 0, b], out[a])
    pairs = []
    for a in range(0, taps_a, 2):
        both = (out[a], out[a + 1]) if turned else (out[a + 1], out[a])
        pairs.append(jnp.concatenate(split(jnp.concatenate(both, axis=0)), axis=1))
    return pairs


def banded(high, low, bands_ref):
    pairs = bands_ref.shape[1] // (2 * LANES)
    tops = [bands_ref[:, 2 * n * LANES : (2 * n + 1) * LANES] for n in range(pairs)]
    rest = []
    for n in range(0, pairs, 2):
        term = dot(low, jnp.concatenate(tops[n : n + 2], axis=1))
        rest += [term[:, at : at + LANES] for at in range(0, term.shape[1], LANES)]
    out = []
    for n in range(pairs):
        term = dot(high, bands_ref[:, 2 * n * LANES : 2 * (n + 1) * LANES])
        out.append(term[:, :LANES] + term[:, LANES:] + rest[n])
    return out


def fetch(pairs, sems):
    copies = [pltpu.make_async_copy(src, dst, sems.at[n]) for n, (src, dst) in enumerate(pairs)]
    for copy in copies:
        copy.start()
    return copies


def prepare(
    half, taps_hbm, w_hbm, q_hbm, k_hbm, v_hbm,
    w_ref, bands_ref, q32, q16, kwin, vblk,
    taps_ref, w_in, q_in, k_in, v_in, rows32, sems,
):
    rows = q_in.shape[0]
    keys = k_in.shape[0]
    step = LANES - 2 * half
    copies = fetch(
        ((taps_hbm, taps_ref), (w_hbm, w_in), (q_hbm.at[0], q_in), (k_hbm.at[0], k_in), (v_hbm.at[0], v_in)), sems
    )
    q32[...] = jnp.zeros_like(q32)
    rows32[:8] = jnp.zeros((8, LANES), F32)
    rows32[8 + keys :] = jnp.zeros((rows32.shape[0] - 8 - keys, LANES), F32)
    copies[0].wait()
    for n, pair in enumerate(bands(taps_ref, False)):
        bands_ref[:, 2 * n * LANES : 2 * (n + 1) * LANES] = pair
    for copy in copies[1:]:
        copy.wait()
    w_ref[...] = w_in[...].astype(BF16)
    q32[:rows] = q_in[...].astype(F32)
    q16[...] = q32[...].astype(BF16)
    rows32[8 : 8 + keys] = k_in[...].astype(F32)
    for n in range(kwin.shape[0] // LANES):
        start = 8 - half + n * step
        kwin[n * LANES : (n + 1) * LANES] = rows32[start : start + LANES].astype(BF16)
    rows32[8 : 8 + keys] = v_in[...].astype(F32)
    for n in range(vblk.shape[0] // LANES):
        start = 8 + n * step
        block = rows32[start : start + LANES]
        vblk[n * LANES : (n + 1) * LANES] = jnp.where(iota(block.shape, 0) < step, block, 0.0).astype(BF16)


def forward(pieces, taps_a, half, *refs):
    piece_refs, (first_ref, bands_ref, q16, kwin, vblk) = refs[:pieces], refs[pieces : pieces + 5]
    p_ref, o_ref, pack_ref, x32, xh, xl, y = refs[pieces + 5 :]
    depth = kwin.shape[1]
    span = p_ref.shape[0]
    rows_up = q16.shape[0]
    windows = kwin.shape[0] // LANES
    step = LANES - 2 * half
    scale = 1.0 / math.sqrt(depth)
    first = first_ref[0]
    for n, ref in enumerate(piece_refs):
        pack_ref[n * span : (n + 1) * span] = ref[0]

    x32[rows_up:] = jnp.zeros((x32.shape[0] - rows_up, x32.shape[1]), F32)
    for n in range(windows):
        cols = slice(n * LANES, (n + 1) * LANES)
        here = slice(n * rows_up, (n + 1) * rows_up)
        x = dot(q16[...], kwin[cols], ((1,), (1,))) * scale
        key = n * step - half + iota(x.shape, 1)
        pos = first - (taps_a - 1) + iota(x.shape, 0)
        x = jnp.where(key <= pos, x, 0.0)
        x32[:rows_up, cols] = x
        xh[here, :LANES], xl[here, :LANES] = split(x)
        xh[here, LANES:], xl[here, LANES:] = split(x32[1 : 1 + rows_up, cols])

    for n, term in enumerate(banded(xh[...], xl[...], bands_ref)):
        y[:, n * LANES : (n + 1) * LANES] = term
    mixed = []
    for n in range(windows):
        total = None
        for pair in range(taps_a // 2):
            start = n * rows_up + taps_a - 2 - 2 * pair
            term = y[start : start + span, pair * LANES : (pair + 1) * LANES]
            total = term if total is None else total + term
        mixed.append(total)
    c = jnp.concatenate(mixed, axis=1)
    lane = iota((span, LANES), 1)
    row = iota((span, LANES), 0)
    live = jnp.concatenate([(lane < step) & (n * step + lane <= first + row) for n in range(windows)], axis=1)
    top = jnp.max(jnp.where(live, c, -jnp.inf), axis=1, keepdims=True)
    terms = jnp.where(live, jnp.exp(c - top), 0.0)
    p = terms / jnp.sum(terms, axis=1, keepdims=True)
    p_ref[...] = p
    o_ref[...] = dot(p.astype(BF16), vblk[...]).astype(BF16)


def forward_turned(taps_a, half, first_ref, kwin, q32, xth_ref, xtl_ref, kturn):
    depth = kwin.shape[1]
    span = xth_ref.shape[1] // taps_a
    windows = kwin.shape[0] // LANES
    step = LANES - 2 * half
    scale = 1.0 / math.sqrt(depth)
    first = first_ref[0]
    flip = (iota((LANES, LANES), 0) + iota((LANES, LANES), 1) == LANES - 1).astype(F32).astype(BF16)
    for n in range(windows):
        here = slice(n * LANES, (n + 1) * LANES)
        kturn[here] = dot(flip, kwin[here]).astype(BF16)
    lead = LANES - 1 - half - iota((LANES, span), 0) - iota((LANES, span), 1)
    lead = jnp.concatenate([lead + n * step for n in range(windows)], axis=0)
    for a in range(taps_a):
        start = taps_a - 1 - a
        xt = dot(kturn[...], q32[start : start + span].astype(BF16), ((1,), (1,))) * scale
        cols = pl.ds(a * span, span)
        xth_ref[:, cols], xtl_ref[:, cols] = split(jnp.where(lead <= first - a, xt, 0.0))


def backward_scores(up_places, w_places, payloads, by_distance, *refs):
    n_up, n_w = len({p[0] for p in up_places}), len({p[0] for p in w_places})
    up_refs, w_refs, refs = refs[:n_up], refs[n_up : n_up + n_w], refs[n_up + n_w :]
    p_ref, vblk, xth_ref, xtl_ref, o_ref, do_ref, dc_ref, own_ref, own_taps_ref = refs[:9]
    out_refs, (up, w, grad) = refs[9 : 9 + payloads], refs[9 + payloads :]
    span = p_ref.shape[0]
    taps_a = xth_ref.shape[1] // span
    windows = vblk.shape[0] // LANES

    for refs_in, places, axis, whole in ((up_refs, up_places, "tensor", up), (w_refs, w_places, "dp", w)):
        me = lax.axis_index(axis)
        for n, part, shift, at in places:
            block = refs_in[n][part]
            width = block.shape[1]
            spot = at if shift is None else lax.bitwise_xor(me, shift)
            whole[:, pl.ds(pl.multiple_of(spot * width, width), width)] = block
    do = dot(up[...], w[...], ((1,), (1,))).astype(BF16)
    do_ref[...] = do
    grad[...] = dot(o_ref[...], up[...], ((0,), (0,)))
    dp = dot(do, vblk[...], ((1,), (1,)))
    p = p_ref[...]
    dc = p * (dp - jnp.sum(p * dp, axis=1, keepdims=True))
    dc_ref[:8] = jnp.zeros((8, dc.shape[1]), F32)
    dc_ref[8 : 8 + span] = dc
    dc_ref[8 + span :] = jnp.zeros((dc_ref.shape[0] - 8 - span, dc.shape[1]), F32)

    right = jnp.concatenate(
        [jnp.concatenate(split(dc[:, n * LANES : (n + 1) * LANES]), axis=1) for n in range(windows)], axis=0
    )
    right = jnp.concatenate([right, right], axis=0)
    sums = []
    for a in range(taps_a):
        cols = slice(a * span, (a + 1) * span)
        left = jnp.concatenate(
            [ref[n * LANES : (n + 1) * LANES, cols] for ref in (xth_ref, xtl_ref) for n in range(windows)], axis=1
        )
        total = dot(left, right)
        turned = pltpu.roll(total[:, :LANES] + total[:, LANES:], 0, 1, stride=1, stride_axis=0)
        sums.append(jnp.sum(turned, axis=0, keepdims=True))
    taps = jnp.concatenate(sums + [jnp.zeros((8 - taps_a, LANES), F32)], axis=0)

    high, low = split(taps)
    mid, low = low, (taps - high.astype(F32) - low.astype(F32)).astype(BF16)
    parts = jnp.concatenate([high.astype(F32), mid.astype(F32)], axis=0).astype(BF16)
    rest = jnp.concatenate([low.astype(F32), jnp.zeros((8, LANES), F32)], axis=0).astype(BF16)
    own_taps_ref[...] = taps
    depth, share = own_ref.shape
    me = lax.axis_index("dp")

    def owned(spot):
        return grad[:, pl.ds(pl.multiple_of(spot * share, share), share)]

    own_ref[...] = owned(me)
    for n, ref in enumerate(out_refs):
        ref[:depth, :share] = owned(lax.bitwise_xor(me, payloads - n) if by_distance else n).astype(BF16)
        ref[depth:, :LANES] = parts
        ref[depth:, LANES : 2 * LANES] = rest


def backward_inputs(
    rows, keys, first_ref, taps_hbm, do_ref, dc_ref, p_ref, q16, kwin,
    dq_ref, dk_ref, dv_ref,
    taps_ref, bands_ref, left_h, left_l, z, sums, sems,
):
    taps_a, _, taps_b = taps_ref.shape
    half = (taps_b - 1) // 2
    step = LANES - 2 * half
    depth = kwin.shape[1]
    windows = kwin.shape[0] // LANES
    rows_up = q16.shape[0]
    scale = 1.0 / math.sqrt(depth)
    copies = fetch(((taps_hbm, taps_ref),), sems)
    first = first_ref[0]
    do = do_ref[...]
    for n in range(windows):
        cols = slice(n * LANES, (n + 1) * LANES)
        here = slice(n * rows_up, (n + 1) * rows_up)
        left_h[here, :LANES], left_l[here, :LANES] = split(dc_ref[:rows_up, cols])
        left_h[here, LANES:], left_l[here, LANES:] = split(dc_ref[1 : 1 + rows_up, cols])
        sums[n * step : n * step + LANES] = dot(p_ref[:, cols].T.astype(BF16), do)
    dv_ref[0] = sums[:keys].astype(BF16)
    copies[0].wait()
    for n, pair in enumerate(bands(taps_ref, True)):
        bands_ref[:, 2 * n * LANES : 2 * (n + 1) * LANES] = pair
    z[windows * rows_up :] = jnp.zeros((z.shape[0] - windows * rows_up, z.shape[1]), F32)
    for n, term in enumerate(banded(left_h[...], left_l[...], bands_ref)):
        z[: windows * rows_up, n * LANES : (n + 1) * LANES] = term

    sums[...] = jnp.zeros_like(sums)
    dq = jnp.zeros((rows_up, depth), F32)
    for n in range(windows):
        total = None
        for pair in range(taps_a // 2):
            start = n * rows_up + 8 - (taps_a - 1) + 2 * pair
            term = z[start : start + rows_up, pair * LANES : (pair + 1) * LANES]
            total = term if total is None else total + term
        key = n * step - half + iota(total.shape, 1)
        row = iota(total.shape, 0)
        ds = jnp.where((key <= first - (taps_a - 1) + row) & (row < rows), total, 0.0)
        dq = dq + dot(ds.astype(BF16), kwin[n * LANES : (n + 1) * LANES])
        sums[n * step : n * step + LANES] += dot(ds.T.astype(BF16), q16[...])
    dk_ref[0] = (scale * sums[half : half + keys]).astype(BF16)
    dq_ref[0] = (scale * dq)[:rows].astype(BF16)


def update(count, span, *refs):
    payload_refs, (own_ref, own_taps_ref, w_ref, one_ref, two_ref) = refs[:-9], refs[-9:-4]
    new_ref, one_new_ref, two_new_ref, taps_ref = refs[-4:]
    taps_a, _, taps_b = taps_ref.shape
    depth, share = own_ref.shape
    grad, taps = own_ref[...], own_taps_ref[...]
    for ref in payload_refs:
        grad = grad + ref[:depth, :share].astype(F32)
        parts, rest = ref[depth:, :LANES].astype(F32), ref[depth:, LANES : 2 * LANES].astype(F32)
        taps = taps + (parts[:8] + (parts[8:] + rest[:8]))
    grad = grad / float(count)
    taps = taps / float(count * span)
    lane = iota((8, LANES), 1)
    turned = jnp.zeros((8, LANES), F32)
    for b in range(taps_b):
        turned = jnp.where(lane == b, taps[:, LANES - 1 - b : LANES - b], turned)
    for a in range(taps_a):
        taps_ref[a] = turned[a : a + 1, :taps_b]
    one = beta_one * one_ref[...] + (1.0 - beta_one) * grad
    two = beta_two * two_ref[...] + (1.0 - beta_two) * grad * grad
    one_new_ref[...] = one
    two_new_ref[...] = two
    old = w_ref[...]
    new_ref[...] = old - learn_rate * ((one / bias_one) / (jnp.sqrt(two / bias_two) + adam_eps) + decay_rate * old)


def swap(x, axis, shift):
    n = lax.axis_size(axis)
    return lax.ppermute(x, axis, [(i, i ^ shift) for i in range(n)])


def few(axis):
    n = lax.axis_size(axis)
    return n <= 8 and n & (n - 1) == 0


def gathered(x, axis):
    if few(axis):
        shifts = range(lax.axis_size(axis))
        return [x] + [swap(x, axis, s) for s in shifts[1:]], [(s, slice(None), s, None) for s in shifts]
    n = lax.axis_size(axis)
    return [lax.all_gather(x, axis)], [(0, i, None, i) for i in range(n)]


def shards(queries, keys, values, conv_kernel, span_start, out_grad, proj_weight, moment_one, moment_two):
    _, rows, depth = queries.shape
    key_count = keys.shape[1]
    _, taps_a, taps_b = conv_kernel.shape
    span = out_grad.shape[1]
    half = (taps_b - 1) // 2
    step = LANES - 2 * half
    windows = -(-key_count // step)
    rows_up = up_to(rows, 16)
    wide = windows * LANES
    reach = up_to((windows - 1) * step + LANES, 8)
    pairs = taps_a // 2
    group_count = lax.axis_size("dp")
    share = proj_weight.shape[1]
    columns = share * group_count
    vmem = pltpu.CompilerParams(vmem_limit_bytes=24 * 2**20)
    whole = pl.BlockSpec(memory_space=pltpu.VMEM)
    hbm = pl.BlockSpec(memory_space=pltpu.HBM)
    shape = jax.ShapeDtypeStruct
    stay = lambda x: pltpu.with_memory_space_constraint(x, pltpu.HBM)
    q_hbm, k_hbm, v_hbm = stay(queries), stay(keys), stay(values)
    taps_hbm = stay(conv_kernel.transpose(1, 0, 2))
    smem = pl.BlockSpec(memory_space=pltpu.SMEM)
    taps_ref = pltpu.SMEM((taps_a, 1, taps_b), F32)
    k_in = pltpu.VMEM((key_count, depth), BF16)
    band = shape((2 * LANES, 2 * pairs * LANES), BF16)
    sides = pltpu.VMEM((windows * rows_up, 2 * LANES), BF16)

    def cost(flops):
        return pl.CostEstimate(flops=flops, bytes_accessed=10**6, transcendentals=0)

    proj_bf, band_rows, q32, q16, kwin, vblk = pl.pallas_call(
        functools.partial(prepare, half),
        out_shape=(
            shape(proj_weight.shape, BF16),
            band,
            shape((rows_up, depth), F32),
            shape((rows_up, depth), BF16),
            shape((wide, depth), BF16),
            shape((wide, depth), BF16),
        ),
        in_specs=[hbm] * 5,
        out_specs=(whole,) * 6,
        scratch_shapes=[
            taps_ref,
            pltpu.VMEM(proj_weight.shape, F32),
            pltpu.VMEM((rows, depth), BF16),
            k_in,
            k_in,
            pltpu.VMEM((reach + 8, depth), F32),
            pltpu.SemaphoreType.DMA((5,)),
        ],
        compiler_params=vmem,
        cost_estimate=cost(10**9),
        name="prepare",
    )(taps_hbm, stay(proj_weight), q_hbm, k_hbm, v_hbm)
    w_arrays, w_places = gathered(proj_bf, "dp")
    cores_last = few("tensor") and lax.axis_size("tensor") > 2
    pieces = [stay(out_grad)]
    if cores_last:
        pieces += [swap(out_grad, "tensor", s) for s in range(2, lax.axis_size("tensor"), 2)]
    p, attended, pack = pl.pallas_call(
        functools.partial(forward, len(pieces), taps_a, half),
        out_shape=(
            shape((span, wide), F32),
            shape((span, depth), BF16),
            shape((len(pieces) * span, out_grad.shape[2]), BF16),
        ),
        in_specs=[whole] * len(pieces) + [smem] + [whole] * 4,
        out_specs=(whole,) * 3,
        scratch_shapes=[
            pltpu.VMEM((rows_up + 8, wide), F32),
            sides,
            sides,
            pltpu.VMEM((windows * rows_up, pairs * LANES), F32),
        ],
        compiler_params=vmem,
        cost_estimate=cost(5 * 10**9),
        name="attention_forward",
    )(*pieces, span_start, band_rows, q16, kwin, vblk)
    if cores_last:
        up_arrays = [pack, swap(pack, "tensor", 1)]
        up_places = [
            (c, slice(n * span, (n + 1) * span), 2 * n + c, None) for n in range(len(pieces)) for c in (0, 1)
        ]
    else:
        up_arrays, up_places = gathered(out_grad[0], "tensor")
    xth, xtl = pl.pallas_call(
        functools.partial(forward_turned, taps_a, half),
        out_shape=(shape((wide, taps_a * span), BF16),) * 2,
        in_specs=[smem, whole, whole],
        out_specs=(whole,) * 2,
        scratch_shapes=[pltpu.VMEM((wide, depth), BF16)],
        compiler_params=vmem,
        cost_estimate=cost(2 * 10**9),
        name="attention_forward_turned",
    )(span_start, kwin, q32)

    others = group_count - 1 if few("dp") else group_count
    do, dc, own, own_taps, *payloads = pl.pallas_call(
        functools.partial(backward_scores, up_places, w_places, others, few("dp")),
        out_shape=(
            shape((span, depth), BF16),
            shape((rows_up + 8, wide), F32),
            shape((depth, share), F32),
            shape((8, LANES), F32),
        ) + (shape((depth + 16, max(share, 2 * LANES)), BF16),) * others,
        in_specs=[whole] * (len(up_arrays) + len(w_arrays) + 5),
        out_specs=(whole,) * (4 + others),
        scratch_shapes=[
            pltpu.VMEM((span, columns), BF16),
            pltpu.VMEM((depth, columns), BF16),
            pltpu.VMEM((depth, columns), F32),
        ],
        compiler_params=vmem,
        cost_estimate=cost(2 * 10**9),
        name="attention_backward_scores",
    )(*up_arrays, *w_arrays, p, vblk, xth, xtl, attended)

    if few("dp"):
        payloads = [swap(payload, "dp", others - n) for n, payload in enumerate(payloads)]
    else:
        sent = lax.all_to_all(jnp.stack(payloads), "dp", 0, 0)
        payloads = [jnp.where(lax.axis_index("dp") == n, jnp.zeros_like(sent[n]), sent[n]) for n in range(group_count)]

    query_grad, key_grad, value_grad = pl.pallas_call(
        functools.partial(backward_inputs, rows, key_count),
        out_shape=(shape(queries.shape, BF16), shape(keys.shape, BF16), shape(values.shape, BF16)),
        in_specs=[smem, hbm] + [whole] * 5,
        out_specs=(whole,) * 3,
        scratch_shapes=[
            taps_ref,
            pltpu.VMEM(band.shape, BF16),
            sides,
            sides,
            pltpu.VMEM((windows * rows_up + 8, pairs * LANES), F32),
            pltpu.VMEM((reach, depth), F32),
            pltpu.SemaphoreType.DMA((1,)),
        ],
        compiler_params=vmem,
        cost_estimate=cost(3 * 10**9),
        name="attention_backward_inputs",
    )(span_start, taps_hbm, do, dc, p, q16, kwin)

    proj_new, moment_one_new, moment_two_new, kernel_total = pl.pallas_call(
        functools.partial(update, group_count, span),
        out_shape=(shape(proj_weight.shape, F32),) * 3 + (shape((taps_a, 1, taps_b), F32),),
        in_specs=[whole] * (len(payloads) + 5),
        out_specs=(whole,) * 4,
        compiler_params=vmem,
        name="projection_update",
    )(*payloads, own, own_taps, proj_weight, moment_one, moment_two)
    return (
        query_grad,
        key_grad,
        value_grad,
        kernel_total.transpose(1, 0, 2),
        proj_new,
        moment_one_new,
        moment_two_new,
    )


def solution(mesh):
    heads, rows_of, blocks_of = P("dp", None, "tensor"), P("tensor", None, None), P("tensor", "dp")
    return jax.shard_map(
        shards,
        mesh=mesh,
        in_specs=(heads, heads, heads, rows_of, P("dp"), heads, blocks_of, blocks_of, blocks_of),
        out_specs=(heads, heads, heads, rows_of, blocks_of, blocks_of, blocks_of),
        check_vma=False,
    )
```

time: 30.8 us -> 29.9 us (0.971)
  Pallas kernels: 13.3 us -> 12.6 us
    pallas_call x6, Pallas kernels: 13.3 us -> 12.6 us  [the longest x1 4.13 us: shards(): pl.pallas_call(functools.partial(backward_inputs, rows, key_count), out_s...]
  transfers between devices with their start and end apart: 10 -> 10, of which waited for: 1 -> 2; matrix products, arithmetic and copies ran while one was open for 0% -> 0% of each run, Pallas kernels for 33% -> 33%
where the time goes in v6:
time: 29.9 us; the launch traced here: 29.6 us
  starting transfers between devices  13.9 us (46%)
  Pallas kernels  12.6 us (42%)
  waiting for transfers between devices  1.72 us (6%)
  between operations  1.38 us (5%)
    ppermute x10, starting transfers between devices, swap(): return lax.ppermute(x, axis, [(i, i ^ shift) for i in range(n)])  13.9 us
    pallas_call x1, Pallas kernels, shards(): pl.pallas_call(functools.partial(backward_inputs, rows, key_count), out_s...  4.13 us
    pallas_call x1, Pallas kernels, shards(): pl.pallas_call(functools.partial(forward, len(pieces), taps_a, half), out...  3 us
    pallas_call x1, Pallas kernels, shards(): pl.pallas_call(functools.partial(backward_scores, up_places, w_places, ot...  2.04 us
    ppermute x10, waiting for transfers between devices, swap(): return lax.ppermute(x, axis, [(i, i ^ shift) for i in range(n)])  1.72 us
    pallas_call x1, Pallas kernels, shards(): pl.pallas_call(functools.partial(forward_turned, taps_a, half), out_shape...  1.31 us
    pallas_call x1, Pallas kernels, shards(): pl.pallas_call(functools.partial(prepare, half), out_shape=(shape(proj_we...  1.29 us
    pallas_call x1, Pallas kernels, shards(): pl.pallas_call(functools.partial(update, group_count, span), out_shape=(s...  0.87 us
  transfers between devices with their start and end apart: 10, of which 2 were waited for; matrix products, arithmetic and copies ran while one was open for 0% of the time, Pallas kernels for 33%

profile of v6, /device:TPU:0, one launch (start us, length us, event | category | flops | bytes accessed | tf_op | source)
XLA Modules:
  0.0 29.6 jit_solution(1248949580668863052)
XLA Ops:
  0.6 3.0 %collective-permute-start.1 = (bf16[1,128,128]{2,1,0:T(8,128)(2,1)}, bf16[1,128,128]{2,1,0:T(8,128)(2,1)S(1)}, u32[]{:S(2)}, u32[]{:S(2)}) collective-permute-start(bf16[1,128,128]{2,1,0:T(8,128)(2,1)} %refs_0_.1), channel_id=1, source_target_pairs={{0,4},{1,5},{2,6},{3,7},{4,0},{5,1},{6,2},{7,3},{8,12},{9,13},{10,... | collective-permute-start | bytes 98312 | tf_op jit(solution)/shard_map/ppermute | solution.py:311
  3.7 1.5 %collective-permute-start = (bf16[1,128,128]{2,1,0:T(8,128)(2,1)}, bf16[1,128,128]{2,1,0:T(8,128)(2,1)S(1)}, u32[]{:S(2)}, u32[]{:S(2)}) collective-permute-start(bf16[1,128,128]{2,1,0:T(8,128)(2,1)} %refs_0_.1), channel_id=1, source_target_pairs={{0,2},{1,3},{2,0},{3,1},{4,6},{5,7},{6,4},{7,5},{8,10},{9,11},{10,... | collective-permute-start | bytes 98312 | tf_op jit(solution)/shard_map/ppermute | solution.py:311
  5.2 0.1 collective-permute-start.2
  5.2 1.3 %prepare.1 = (bf16[128,256]{1,0:T(8,128)(2,1)S(1)}, bf16[256,768]{1,0:T(8,128)(2,1)S(1)}, f32[144,128]{1,0:T(8,128)S(1)}, bf16[144,128]{1,0:T(8,128)(2,1)S(1)}, ...) custom-call(f32[6,1,11]{2,1,0:T(1,128)} %bitcast.2, f32[128,256]{1,0:T(8,128)} %refs_5_.1, ...), custom_call_target="tpu_custom_call" | custom-call | flops 1000000000 | bytes 1000000 | tf_op jit(solution)/shard_map/prepare/pallas_call | solution.py:358
  6.5 4.1 %collective-permute-start.6 = (bf16[128,256]{1,0:T(8,128)(2,1)S(1)}, bf16[128,256]{1,0:T(8,128)(2,1)S(1)}, u32[]{:S(2)}, u32[]{:S(2)}) collective-permute-start(bf16[128,256]{1,0:T(8,128)(2,1)S(1)} %get-tuple-element.37.refs_2_), channel_id=1, source_target_pairs={{0,24},{8,16},{16,8},{24,0},{1,25},{9,17},{17,9},{25,1},{2,26},{10... | collective-permute-start | bytes 196616 | tf_op jit(solution)/shard_map/ppermute | solution.py:311
  10.6 0.0 collective-permute-start.5
  11.3 0.0 collective-permute-done.1.refs_2_
  11.3 0.7 %collective-permute-start.4 = (bf16[128,256]{1,0:T(8,128)(2,1)S(1)}, bf16[128,256]{1,0:T(8,128)(2,1)S(1)}, u32[]{:S(2)}, u32[]{:S(2)}) collective-permute-start(bf16[128,256]{1,0:T(8,128)(2,1)S(1)} %get-tuple-element.37.refs_2_), channel_id=1, source_target_pairs={{0,8},{8,0},{16,24},{24,16},{1,9},{9,1},{17,25},{25,17},{2,10},{10... | collective-permute-start | bytes 196616 | tf_op jit(solution)/shard_map/ppermute | solution.py:311
  12.0 0.0 collective-permute-done.refs_1_
  12.0 0.0 collective-permute-done.2.refs_3_
  12.0 3.0 %attention_forward.1 = (f32[128,1152]{1,0:T(8,128)S(1)}, bf16[128,128]{1,0:T(8,128)(2,1)S(1)}, bf16[512,128]{1,0:T(8,128)(2,1)S(1)}) custom-call(bf16[1,128,128]{2,1,0:T(8,128)(2,1)} %refs_0_.1, bf16[1,128,128]{2,1,0:T(8,128)(2,1)S(1)} %collective-permute-done.refs_1_, bf16[1,128,128]{2,1,0:T(8,128)(2,1)S(1)} %collective-permute-done.1.refs_2_, ...), custom_call_target="tpu_custom_call" | custom-call | flops 5000000000 | bytes 1000000 | tf_op jit(solution)/shard_map/attention_forward/pallas_call | solution.py:388
  15.0 0.1 collective-permute-start.3
  15.1 1.3 %attention_forward_turned.1 = (bf16[1152,768]{1,0:T(8,128)(2,1)S(1)}, bf16[1152,768]{1,0:T(8,128)(2,1)S(1)}) custom-call(s32[1]{0:T(128)S(6)} %copy.16.refs_4_.first_ref, bf16[1152,128]{1,0:T(8,128)(2,1)S(1)} %get-tuple-element.34.refs_7_.kwin, f32[144,128]{1,0:T(8,128)S(1)} %get-tuple-element.39.q32), custom_call_target="tpu_custom_call" | custom-call | flops 2000000000 | bytes 1000000 | tf_op jit(solution)/shard_map/attention_forward_turned/pallas_call | solution.py:414
  16.4 0.0 collective-permute-done.6.refs_5_
  16.4 0.0 collective-permute-done.5.refs_4_
  16.4 0.1 collective-permute-done.4.refs_3_
  16.5 0.0 collective-permute-done.3.refs_1_
  16.5 2.0 %attention_backward_scores.1 = (bf16[128,128]{1,0:T(8,128)(2,1)S(1)}, f32[152,1152]{1,0:T(8,128)S(1)}, f32[128,256]{1,0:T(8,128)S(1)}, f32[8,128]{1,0:T(8,128)S(...) custom-call(bf16[512,128]{1,0:T(8,128)(2,1)S(1)} %get-tuple-element.36.refs_0_, ...), custom_call_target="tpu_custom_call" | custom-call | flops 2000000000 | bytes 1000000 | tf_op jit(solution)/shard_map/attention_backward_scores/pallas_call | solution.py:426
  18.5 3.7 %collective-permute-start.7 = (bf16[144,256]{1,0:T(8,128)(2,1)S(1)}, bf16[144,256]{1,0:T(8,128)(2,1)S(1)}, u32[]{:S(2)}, u32[]{:S(2)}) collective-permute-start(bf16[144,256]{1,0:T(8,128)(2,1)S(1)} %get-tuple-element.48), channel_id=1, source_target_pairs={{0,24},{8,16},{16,8},{24,0},{1,25},{9,17},{17,9},{25,1},{2,26},{10... | collective-permute-start | bytes 221192 | tf_op jit(solution)/shard_map/ppermute | solution.py:311
  22.2 0.0 collective-permute-start.8
  22.2 0.7 %collective-permute-start.9 = (bf16[144,256]{1,0:T(8,128)(2,1)S(1)}, bf16[144,256]{1,0:T(8,128)(2,1)S(1)}, u32[]{:S(2)}, u32[]{:S(2)}) collective-permute-start(bf16[144,256]{1,0:T(8,128)(2,1)S(1)} %get-tuple-element.50), channel_id=1, source_target_pairs={{0,8},{8,0},{16,24},{24,16},{1,9},{9,1},{17,25},{25,17},{2,10},{10... | collective-permute-start | bytes 221192 | tf_op jit(solution)/shard_map/ppermute | solution.py:311
  23.0 0.0 copy-start
  23.0 0.0 copy-start.1
  23.0 0.0 copy-start.2
  23.0 4.1 %attention_backward_inputs.1 = (bf16[1,133,128]{2,1,0:T(8,128)(2,1)}, bf16[1,1024,128]{2,1,0:T(8,128)(2,1)}, bf16[1,1024,128]{2,1,0:T(8,128)(2,1)}) custom-call(s32[1]{0:T(128)S(6)} %copy.16.refs_4_.first_ref, f32[6,1,11]{2,1,0:T(1,128)} %bitcast.3, bf16[128,128]{1,0:T(8,128)(2,1)S(1)} %get-tuple-element.43.do_ref, ...), custom_call_target="tpu_custom_call" | custom-call | flops 3000000000 | bytes 1000000 | tf_op jit(solution)/shard_map/attention_backward_inputs/pallas_call | solution.py:452
  27.1 0.0 collective-permute-done.7.refs_0_
  27.1 1.6 %collective-permute-done.8.refs_1_ = bf16[144,256]{1,0:T(8,128)(2,1)S(1)} collective-permute-done((bf16[144,256]{1,0:T(8,128)(2,1)S(1)}, bf16[144,256]{1,0:T(8,128)(2,1)S(1)}, u32[]{:S(2)}, u32[]{:S(2)}) %collective-permute-start.8) | collective-permute-done | bytes 73760 | tf_op jit(solution)/shard_map/ppermute | solution.py:311
  28.7 0.0 collective-permute-done.9.refs_2_
  28.8 0.0 copy-done
  28.8 0.0 copy-done.1
  28.8 0.0 copy-done.2
  28.8 0.9 %projection_update.1 = (f32[128,256]{1,0:T(8,128)}, f32[128,256]{1,0:T(8,128)}, f32[128,256]{1,0:T(8,128)}, f32[6,1,11]{2,1,0:T(1,128)}) custom-call(bf16[144,256]{1,0:T(8,128)(2,1)S(1)} %collective-permute-done.7.refs_0_, bf16[144,256]{1,0:T(8,128)(2,1)S(1)} %collective-permute-done.8.refs_1_, bf16[144,256]{1,0:T(8,128)(2,1)S(1)} %collective-permute-done.9.refs_2_, ...), custom_call_target="tpu_custom_call" | custom-call | tf_op jit(solution)/shard_map/projection_update/pallas_call | solution.py:471
Async XLA Ops:
  0.6 10.6 %collective-permute-start.1 = (bf16[1,128,128]{2,1,0:T(8,128)(2,1)}, bf16[1,128,128]{2,1,0:T(8,128)(2,1)S(1)}, u32[]{:S(2)}, u32[]{:S(2)}) collective-permute-start(bf16[1,128,128]{2,1,0:T(8,128)(2,1)} %refs_0_.1), channel_id=1, source_target_pairs={{0,4},{1,5},{2,6},{3,7},{4,0},{5,1},{6,2},{7,3},{8,12},{9,13},{10,... | collective-permute-start | bytes 98312 | tf_op jit(solution)/shard_map/ppermute | solution.py:311
  3.7 8.3 %collective-permute-start = (bf16[1,128,128]{2,1,0:T(8,128)(2,1)}, bf16[1,128,128]{2,1,0:T(8,128)(2,1)S(1)}, u32[]{:S(2)}, u32[]{:S(2)}) collective-permute-start(bf16[1,128,128]{2,1,0:T(8,128)(2,1)} %refs_0_.1), channel_id=1, source_target_pairs={{0,2},{1,3},{2,0},{3,1},{4,6},{5,7},{6,4},{7,5},{8,10},{9,11},{10,... | collective-permute-start | bytes 98312 | tf_op jit(solution)/shard_map/ppermute | solution.py:311
  5.2 6.8 %collective-permute-start.2 = (bf16[1,128,128]{2,1,0:T(8,128)(2,1)}, bf16[1,128,128]{2,1,0:T(8,128)(2,1)S(1)}, u32[]{:S(2)}, u32[]{:S(2)}) collective-permute-start(bf16[1,128,128]{2,1,0:T(8,128)(2,1)} %refs_0_.1), channel_id=1, source_target_pairs={{0,6},{1,7},{2,4},{3,5},{4,2},{5,3},{6,0},{7,1},{8,14},{9,15},{10,... | collective-permute-start | bytes 98312 | tf_op jit(solution)/shard_map/ppermute | solution.py:311
  6.5 9.9 %collective-permute-start.6 = (bf16[128,256]{1,0:T(8,128)(2,1)S(1)}, bf16[128,256]{1,0:T(8,128)(2,1)S(1)}, u32[]{:S(2)}, u32[]{:S(2)}) collective-permute-start(bf16[128,256]{1,0:T(8,128)(2,1)S(1)} %get-tuple-element.37.refs_2_), channel_id=1, source_target_pairs={{0,24},{8,16},{16,8},{24,0},{1,25},{9,17},{17,9},{25,1},{2,26},{10... | collective-permute-start | bytes 196616 | tf_op jit(solution)/shard_map/ppermute | solution.py:311
  10.6 5.8 %collective-permute-start.5 = (bf16[128,256]{1,0:T(8,128)(2,1)S(1)}, bf16[128,256]{1,0:T(8,128)(2,1)S(1)}, u32[]{:S(2)}, u32[]{:S(2)}) collective-permute-start(bf16[128,256]{1,0:T(8,128)(2,1)S(1)} %get-tuple-element.37.refs_2_), channel_id=1, source_target_pairs={{0,16},{8,24},{16,0},{24,8},{1,17},{9,25},{17,1},{25,9},{2,18},{10... | collective-permute-start | bytes 196616 | tf_op jit(solution)/shard_map/ppermute | solution.py:311
  11.3 5.2 %collective-permute-start.4 = (bf16[128,256]{1,0:T(8,128)(2,1)S(1)}, bf16[128,256]{1,0:T(8,128)(2,1)S(1)}, u32[]{:S(2)}, u32[]{:S(2)}) collective-permute-start(bf16[128,256]{1,0:T(8,128)(2,1)S(1)} %get-tuple-element.37.refs_2_), channel_id=1, source_target_pairs={{0,8},{8,0},{16,24},{24,16},{1,9},{9,1},{17,25},{25,17},{2,10},{10... | collective-permute-start | bytes 196616 | tf_op jit(solution)/shard_map/ppermute | solution.py:311
  15.0 1.5 %collective-permute-start.3 = (bf16[512,128]{1,0:T(8,128)(2,1)S(1)}, bf16[512,128]{1,0:T(8,128)(2,1)S(1)}, u32[]{:S(2)}, u32[]{:S(2)}) collective-permute-start(bf16[512,128]{1,0:T(8,128)(2,1)S(1)} %get-tuple-element.36.refs_0_), channel_id=1, source_target_pairs={{0,1},{1,0},{2,3},{3,2},{4,5},{5,4},{6,7},{7,6},{8,9},{9,8},{10,11... | collective-permute-start | bytes 393224 | tf_op jit(solution)/shard_map/ppermute | solution.py:311
  18.5 8.6 %collective-permute-start.7 = (bf16[144,256]{1,0:T(8,128)(2,1)S(1)}, bf16[144,256]{1,0:T(8,128)(2,1)S(1)}, u32[]{:S(2)}, u32[]{:S(2)}) collective-permute-start(bf16[144,256]{1,0:T(8,128)(2,1)S(1)} %get-tuple-element.48), channel_id=1, source_target_pairs={{0,24},{8,16},{16,8},{24,0},{1,25},{9,17},{17,9},{25,1},{2,26},{10... | collective-permute-start | bytes 221192 | tf_op jit(solution)/shard_map/ppermute | solution.py:311
  22.2 6.5 %collective-permute-start.8 = (bf16[144,256]{1,0:T(8,128)(2,1)S(1)}, bf16[144,256]{1,0:T(8,128)(2,1)S(1)}, u32[]{:S(2)}, u32[]{:S(2)}) collective-permute-start(bf16[144,256]{1,0:T(8,128)(2,1)S(1)} %get-tuple-element.49), channel_id=1, source_target_pairs={{0,16},{8,24},{16,0},{24,8},{1,17},{9,25},{17,1},{25,9},{2,18},{10... | collective-permute-start | bytes 221192 | tf_op jit(solution)/shard_map/ppermute | solution.py:311
  22.2 6.5 %collective-permute-start.9 = (bf16[144,256]{1,0:T(8,128)(2,1)S(1)}, bf16[144,256]{1,0:T(8,128)(2,1)S(1)}, u32[]{:S(2)}, u32[]{:S(2)}) collective-permute-start(bf16[144,256]{1,0:T(8,128)(2,1)S(1)} %get-tuple-element.50), channel_id=1, source_target_pairs={{0,8},{8,0},{16,24},{24,16},{1,9},{9,1},{17,25},{25,17},{2,10},{10... | collective-permute-start | bytes 221192 | tf_op jit(solution)/shard_map/ppermute | solution.py:311
  23.0 5.8 %copy-start = (f32[128,256]{1,0:T(8,128)S(1)}, f32[128,256]{1,0:T(8,128)}, u32[]{:S(2)}) copy-start(f32[128,256]{1,0:T(8,128)} %refs_5_.1) | copy-start | bytes 393220
  23.0 5.8 %copy-start.1 = (f32[128,256]{1,0:T(8,128)S(1)}, f32[128,256]{1,0:T(8,128)}, u32[]{:S(2)}) copy-start(f32[128,256]{1,0:T(8,128)} %refs_6_.1) | copy-start | bytes 393220
  23.0 5.8 %copy-start.2 = (f32[128,256]{1,0:T(8,128)S(1)}, f32[128,256]{1,0:T(8,128)}, u32[]{:S(2)}) copy-start(f32[128,256]{1,0:T(8,128)} %refs_7_.1) | copy-start | bytes 393220

commit v7 on v6

--- a/solution.py
+++ b/solution.py
@@ -17,7 +17,6 @@
 bias_two = 1.0 - 0.95**10
 
 LANES = 128
-HALF = LANES // 2
 F32 = jnp.float32
 BF16 = jnp.bfloat16
 
@@ -39,34 +38,30 @@
     return lax.broadcasted_iota(jnp.int32, shape, axis)
 
 
-def bands(taps_ref, turned):
+def hold_bands(taps_ref, bands_ref):
     taps_a, _, taps_b = taps_ref.shape
     place = iota((LANES, LANES), 0) - iota((LANES, LANES), 1)
-    place = -place if turned else place
     out = [jnp.zeros((LANES, LANES), F32) for _ in range(taps_a)]
     for b in range(taps_b):
         here = place == b
         for a in range(taps_a):
             out[a] = jnp.where(here, taps_ref[a, 0, b], out[a])
-    pairs = []
     for a in range(0, taps_a, 2):
-        both = (out[a], out[a + 1]) if turned else (out[a + 1], out[a])
-        pairs.append(jnp.concatenate(split(jnp.concatenate(both, axis=0)), axis=1))
-    return pairs
-
-
-def banded(high, low, bands_ref):
-    pairs = bands_ref.shape[1] // (2 * LANES)
-    tops = [bands_ref[:, 2 * n * LANES : (2 * n + 1) * LANES] for n in range(pairs)]
-    rest = []
-    for n in range(0, pairs, 2):
-        term = dot(low, jnp.concatenate(tops[n : n + 2], axis=1))
-        rest += [term[:, at : at + LANES] for at in range(0, term.shape[1], LANES)]
-    out = []
+        cols = slice(a // 2 * LANES, (a // 2 + 1) * LANES)
+        high, low = split(jnp.concatenate((out[a + 1], out[a]), axis=0))
+        bands_ref[: 2 * LANES, cols] = high
+        bands_ref[2 * LANES : 4 * LANES, cols] = low
+        bands_ref[4 * LANES :, cols] = high
+
+
+def turned_bands(bands_ref):
+    pairs = bands_ref.shape[1] // LANES
+    rows = []
     for n in range(pairs):
-        term = dot(high, bands_ref[:, 2 * n * LANES : 2 * (n + 1) * LANES])
-        out.append(term[:, :LANES] + term[:, LANES:] + rest[n])
-    return out
+        cols = slice(n * LANES, (n + 1) * LANES)
+        parts = [bands_ref[at * LANES : (at + 1) * LANES, cols] for at in (1, 0, 3, 2, 1, 0)]
+        rows.append(jnp.concatenate(parts, axis=1))
+    return jnp.concatenate(rows, axis=0)
 
 
 def fetch(pairs, sems):
@@ -91,8 +86,7 @@
     rows32[:8] = jnp.zeros((8, LANES), F32)
     rows32[8 + keys :] = jnp.zeros((rows32.shape[0] - 8 - keys, LANES), F32)
     copies[0].wait()
-    for n, pair in enumerate(bands(taps_ref, False)):
-        bands_ref[:, 2 * n * LANES : 2 * (n + 1) * LANES] = pair
+    hold_bands(taps_ref, bands_ref)
     for copy in copies[1:]:
         copy.wait()
     w_ref[...] = w_in[...].astype(BF16)
@@ -112,21 +106,20 @@
 def forward(pieces, taps_a, half, *refs):
     piece_refs, (first_ref, bands_ref, q16, kwin, vblk) = refs[:pieces], refs[pieces : pieces + 5]
     p_ref, o_ref, pack_ref, x32, xh, xl, y = refs[pieces + 5 :]
-    depth = kwin.shape[1]
     span = p_ref.shape[0]
     rows_up = q16.shape[0]
     windows = kwin.shape[0] // LANES
     step = LANES - 2 * half
-    scale = 1.0 / math.sqrt(depth)
     first = first_ref[0]
     for n, ref in enumerate(piece_refs):
         pack_ref[n * span : (n + 1) * span] = ref[0]
 
     x32[rows_up:] = jnp.zeros((x32.shape[0] - rows_up, x32.shape[1]), F32)
+    scores = dot(q16[...], kwin[...], ((1,), (1,))) * (1.0 / math.sqrt(kwin.shape[1]))
     for n in range(windows):
         cols = slice(n * LANES, (n + 1) * LANES)
         here = slice(n * rows_up, (n + 1) * rows_up)
-        x = dot(q16[...], kwin[cols], ((1,), (1,))) * scale
+        x = scores[:, cols]
         key = n * step - half + iota(x.shape, 1)
         pos = first - (taps_a - 1) + iota(x.shape, 0)
         x = jnp.where(key <= pos, x, 0.0)
@@ -134,8 +127,7 @@
         xh[here, :LANES], xl[here, :LANES] = split(x)
         xh[here, LANES:], xl[here, LANES:] = split(x32[1 : 1 + rows_up, cols])
 
-    for n, term in enumerate(banded(xh[...], xl[...], bands_ref)):
-        y[:, n * LANES : (n + 1) * LANES] = term
+    y[...] = dot(jnp.concatenate([xh[...], xh[...], xl[...]], axis=1), bands_ref[...])
     mixed = []
     for n in range(windows):
         total = None
@@ -150,17 +142,15 @@
     live = jnp.concatenate([(lane < step) & (n * step + lane <= first + row) for n in range(windows)], axis=1)
     top = jnp.max(jnp.where(live, c, -jnp.inf), axis=1, keepdims=True)
     terms = jnp.where(live, jnp.exp(c - top), 0.0)
-    p = terms / jnp.sum(terms, axis=1, keepdims=True)
+    p = terms * (1.0 / jnp.sum(terms, axis=1, keepdims=True))
     p_ref[...] = p
     o_ref[...] = dot(p.astype(BF16), vblk[...]).astype(BF16)
 
 
 def forward_turned(taps_a, half, first_ref, kwin, q32, xth_ref, xtl_ref, kturn):
-    depth = kwin.shape[1]
     span = xth_ref.shape[1] // taps_a
     windows = kwin.shape[0] // LANES
     step = LANES - 2 * half
-    scale = 1.0 / math.sqrt(depth)
     first = first_ref[0]
     flip = (iota((LANES, LANES), 0) + iota((LANES, LANES), 1) == LANES - 1).astype(F32).astype(BF16)
     for n in range(windows):
@@ -168,18 +158,18 @@
         kturn[here] = dot(flip, kwin[here]).astype(BF16)
     lead = LANES - 1 - half - iota((LANES, span), 0) - iota((LANES, span), 1)
     lead = jnp.concatenate([lead + n * step for n in range(windows)], axis=0)
+    shifted = jnp.concatenate([q32[taps_a - 1 - a : taps_a - 1 - a + span].astype(BF16) for a in range(taps_a)], axis=0)
+    xt = dot(kturn[...], shifted, ((1,), (1,)))
     for a in range(taps_a):
-        start = taps_a - 1 - a
-        xt = dot(kturn[...], q32[start : start + span].astype(BF16), ((1,), (1,))) * scale
-        cols = pl.ds(a * span, span)
-        xth_ref[:, cols], xtl_ref[:, cols] = split(jnp.where(lead <= first - a, xt, 0.0))
-
-
-def backward_scores(up_places, w_places, payloads, by_distance, *refs):
+        cols = slice(a * span, (a + 1) * span)
+        xth_ref[:, cols], xtl_ref[:, cols] = split(jnp.where(lead <= first - a, xt[:, cols], 0.0))
+
+
+def backward_scores(up_places, w_places, owners, by_distance, *refs):
     n_up, n_w = len({p[0] for p in up_places}), len({p[0] for p in w_places})
     up_refs, w_refs, refs = refs[:n_up], refs[n_up : n_up + n_w], refs[n_up + n_w :]
     p_ref, vblk, xth_ref, xtl_ref, o_ref, do_ref, dc_ref, own_ref, own_taps_ref = refs[:9]
-    out_refs, (up, w, grad) = refs[9 : 9 + payloads], refs[9 + payloads :]
+    out_refs, (up, w, grad) = refs[9 : 9 + len(owners)], refs[9 + len(owners) :]
     span = p_ref.shape[0]
     taps_a = xth_ref.shape[1] // span
     windows = vblk.shape[0] // LANES
@@ -218,8 +208,9 @@
 
     high, low = split(taps)
     mid, low = low, (taps - high.astype(F32) - low.astype(F32)).astype(BF16)
-    parts = jnp.concatenate([high.astype(F32), mid.astype(F32)], axis=0).astype(BF16)
-    rest = jnp.concatenate([low.astype(F32), jnp.zeros((8, LANES), F32)], axis=0).astype(BF16)
+    aside = pltpu.roll(low.astype(F32), LANES // 2, 1)
+    first = jnp.where(iota(aside.shape, 1) < LANES // 2, aside, high.astype(F32))
+    parts = jnp.concatenate([first, mid.astype(F32)], axis=0).astype(BF16)
     own_taps_ref[...] = taps
     depth, share = own_ref.shape
     me = lax.axis_index("dp")
@@ -228,25 +219,23 @@
         return grad[:, pl.ds(pl.multiple_of(spot * share, share), share)]
 
     own_ref[...] = owned(me)
-    for n, ref in enumerate(out_refs):
-        ref[:depth, :share] = owned(lax.bitwise_xor(me, payloads - n) if by_distance else n).astype(BF16)
-        ref[depth:, :LANES] = parts
-        ref[depth:, LANES : 2 * LANES] = rest
+    for owner, ref in zip(owners, out_refs, strict=True):
+        piece = owned(lax.bitwise_xor(me, owner) if by_distance else owner).astype(BF16)
+        for n in range(share // LANES):
+            ref[n * depth : (n + 1) * depth] = piece[:, n * LANES : (n + 1) * LANES]
+        ref[ref.shape[0] - 16 :] = parts
 
 
 def backward_inputs(
-    rows, keys, first_ref, taps_hbm, do_ref, dc_ref, p_ref, q16, kwin,
+    rows, keys, taps_a, half, first_ref, bands_ref, do_ref, dc_ref, p_ref, q16, kwin,
     dq_ref, dk_ref, dv_ref,
-    taps_ref, bands_ref, left_h, left_l, z, sums, sems,
+    left_h, left_l, z, sums,
 ):
-    taps_a, _, taps_b = taps_ref.shape
-    half = (taps_b - 1) // 2
     step = LANES - 2 * half
     depth = kwin.shape[1]
     windows = kwin.shape[0] // LANES
     rows_up = q16.shape[0]
     scale = 1.0 / math.sqrt(depth)
-    copies = fetch(((taps_hbm, taps_ref),), sems)
     first = first_ref[0]
     do = do_ref[...]
     for n in range(windows):
@@ -254,28 +243,31 @@
         here = slice(n * rows_up, (n + 1) * rows_up)
         left_h[here, :LANES], left_l[here, :LANES] = split(dc_ref[:rows_up, cols])
         left_h[here, LANES:], left_l[here, LANES:] = split(dc_ref[1 : 1 + rows_up, cols])
-        sums[n * step : n * step + LANES] = dot(p_ref[:, cols].T.astype(BF16), do)
+        sums[n * step : n * step + LANES] = dot(p_ref[:, cols].astype(BF16).T, do)
     dv_ref[0] = sums[:keys].astype(BF16)
-    copies[0].wait()
-    for n, pair in enumerate(bands(taps_ref, True)):
-        bands_ref[:, 2 * n * LANES : 2 * (n + 1) * LANES] = pair
     z[windows * rows_up :] = jnp.zeros((z.shape[0] - windows * rows_up, z.shape[1]), F32)
-    for n, term in enumerate(banded(left_h[...], left_l[...], bands_ref)):
-        z[: windows * rows_up, n * LANES : (n + 1) * LANES] = term
-
-    sums[...] = jnp.zeros_like(sums)
-    dq = jnp.zeros((rows_up, depth), F32)
+    left = jnp.concatenate([left_h[...], left_h[...], left_l[...]], axis=1)
+    z[: windows * rows_up] = dot(left, turned_bands(bands_ref), ((1,), (1,)))
+
+    lane = iota((rows_up, LANES), 1)
+    row = iota((rows_up, LANES), 0)
+    scores = []
     for n in range(windows):
         total = None
         for pair in range(taps_a // 2):
             start = n * rows_up + 8 - (taps_a - 1) + 2 * pair
             term = z[start : start + rows_up, pair * LANES : (pair + 1) * LANES]
             total = term if total is None else total + term
-        key = n * step - half + iota(total.shape, 1)
-        row = iota(total.shape, 0)
-        ds = jnp.where((key <= first - (taps_a - 1) + row) & (row < rows), total, 0.0)
+        scores.append(total)
+    sums[...] = jnp.zeros_like(sums)
+    dq = jnp.zeros((rows_up, depth), F32)
+    for n, total in enumerate(scores):
+        if n + 1 < windows:
+            total = jnp.where(lane < step, total, total + pltpu.roll(scores[n + 1], step, 1))
+        live = (n * step - half + lane <= first - (taps_a - 1) + row) & (row < rows)
+        ds = jnp.where(live & (lane >= 2 * half) if n else live, total, 0.0)
         dq = dq + dot(ds.astype(BF16), kwin[n * LANES : (n + 1) * LANES])
-        sums[n * step : n * step + LANES] += dot(ds.T.astype(BF16), q16[...])
+        sums[n * step : n * step + LANES] += dot(ds.astype(BF16).T, q16[...])
     dk_ref[0] = (scale * sums[half : half + keys]).astype(BF16)
     dq_ref[0] = (scale * dq)[:rows].astype(BF16)
 
@@ -287,11 +279,12 @@
     depth, share = own_ref.shape
     grad, taps = own_ref[...], own_taps_ref[...]
     for ref in payload_refs:
-        grad = grad + ref[:depth, :share].astype(F32)
-        parts, rest = ref[depth:, :LANES].astype(F32), ref[depth:, LANES : 2 * LANES].astype(F32)
-        taps = taps + (parts[:8] + (parts[8:] + rest[:8]))
-    grad = grad / float(count)
-    taps = taps / float(count * span)
+        piece = [ref[n * depth : (n + 1) * depth] for n in range(share // LANES)]
+        grad = grad + jnp.concatenate(piece, axis=1).astype(F32)
+        parts = ref[ref.shape[0] - 16 :].astype(F32)
+        taps = taps + (parts[:8] + (parts[8:] + pltpu.roll(parts[:8], LANES // 2, 1)))
+    grad = grad * (1.0 / count)
+    taps = taps * (1.0 / (math.sqrt(depth) * count * span))
     lane = iota((8, LANES), 1)
     turned = jnp.zeros((8, LANES), F32)
     for b in range(taps_b):
@@ -303,7 +296,7 @@
     one_new_ref[...] = one
     two_new_ref[...] = two
     old = w_ref[...]
-    new_ref[...] = old - learn_rate * ((one / bias_one) / (jnp.sqrt(two / bias_two) + adam_eps) + decay_rate * old)
+    new_ref[...] = old - learn_rate * ((one * (1.0 / bias_one)) / (jnp.sqrt(two * (1.0 / bias_two)) + adam_eps) + decay_rate * old)
 
 
 def swap(x, axis, shift):
@@ -311,6 +304,10 @@
     return lax.ppermute(x, axis, [(i, i ^ shift) for i in range(n)])
 
 
+def turns(n):
+    return list(range(n // 2, n)) + list(range(n // 2 - 1, 0, -1))
+
+
 def few(axis):
     n = lax.axis_size(axis)
     return n <= 8 and n & (n - 1) == 0
@@ -318,8 +315,9 @@
 
 def gathered(x, axis):
     if few(axis):
-        shifts = range(lax.axis_size(axis))
-        return [x] + [swap(x, axis, s) for s in shifts[1:]], [(s, slice(None), s, None) for s in shifts]
+        shifts = turns(lax.axis_size(axis))[::-1]
+        arrays = [x] + [swap(x, axis, s) for s in shifts]
+        return arrays, [(n, slice(None), s, None) for n, s in enumerate([0, *shifts])]
     n = lax.axis_size(axis)
     return [lax.all_gather(x, axis)], [(0, i, None, i) for i in range(n)]
 
@@ -349,7 +347,7 @@
     smem = pl.BlockSpec(memory_space=pltpu.SMEM)
     taps_ref = pltpu.SMEM((taps_a, 1, taps_b), F32)
     k_in = pltpu.VMEM((key_count, depth), BF16)
-    band = shape((2 * LANES, 2 * pairs * LANES), BF16)
+    band = shape((6 * LANES, pairs * LANES), BF16)
     sides = pltpu.VMEM((windows * rows_up, 2 * LANES), BF16)
 
     def cost(flops):
@@ -422,15 +420,16 @@
         name="attention_forward_turned",
     )(span_start, kwin, q32)
 
-    others = group_count - 1 if few("dp") else group_count
+    owners = turns(group_count) if few("dp") else list(range(group_count))
+    others = len(owners)
     do, dc, own, own_taps, *payloads = pl.pallas_call(
-        functools.partial(backward_scores, up_places, w_places, others, few("dp")),
+        functools.partial(backward_scores, up_places, w_places, owners, few("dp")),
         out_shape=(
             shape((span, depth), BF16),
             shape((rows_up + 8, wide), F32),
             shape((depth, share), F32),
             shape((8, LANES), F32),
-        ) + (shape((depth + 16, max(share, 2 * LANES)), BF16),) * others,
+        ) + (shape((depth * (share // LANES) + 16, LANES), BF16),) * others,
         in_specs=[whole] * (len(up_arrays) + len(w_arrays) + 5),
         out_specs=(whole,) * (4 + others),
         scratch_shapes=[
@@ -444,29 +443,26 @@
     )(*up_arrays, *w_arrays, p, vblk, xth, xtl, attended)
 
     if few("dp"):
-        payloads = [swap(payload, "dp", others - n) for n, payload in enumerate(payloads)]
+        payloads = [swap(payload, "dp", owner) for owner, payload in zip(owners, payloads, strict=True)]
     else:
         sent = lax.all_to_all(jnp.stack(payloads), "dp", 0, 0)
         payloads = [jnp.where(lax.axis_index("dp") == n, jnp.zeros_like(sent[n]), sent[n]) for n in range(group_count)]
 
     query_grad, key_grad, value_grad = pl.pallas_call(
-        functools.partial(backward_inputs, rows, key_count),
+        functools.partial(backward_inputs, rows, key_count, taps_a, half),
         out_shape=(shape(queries.shape, BF16), shape(keys.shape, BF16), shape(values.shape, BF16)),
-        in_specs=[smem, hbm] + [whole] * 5,
+        in_specs=[smem] + [whole] * 6,
         out_specs=(whole,) * 3,
         scratch_shapes=[
-            taps_ref,
-            pltpu.VMEM(band.shape, BF16),
             sides,
             sides,
             pltpu.VMEM((windows * rows_up + 8, pairs * LANES), F32),
             pltpu.VMEM((reach, depth), F32),
-            pltpu.SemaphoreType.DMA((1,)),
         ],
         compiler_params=vmem,
         cost_estimate=cost(3 * 10**9),
         name="attention_backward_inputs",
-    )(span_start, taps_hbm, do, dc, p, q16, kwin)
+    )(span_start, band_rows, do, dc, p, q16, kwin)
 
     proj_new, moment_one_new, moment_two_new, kernel_total = pl.pallas_call(
         functools.partial(update, group_count, span),

time: 29.9 us -> 29.5 us (0.987)
  waiting for transfers between devices: 1.72 us -> 2.9 us
  Pallas kernels: 12.6 us -> 11.5 us
  starting transfers between devices: 13.9 us -> 13.5 us
    ppermute x10, waiting for transfers between devices: 1.72 us -> 2.9 us  [swap(): return lax.ppermute(x, axis, [(i, i ^ shift) for i in range(n)])]
    pallas_call x2, Pallas kernels: 6.17 us -> 5.03 us  [the longest x1 2.95 us: shards(): pl.pallas_call(functools.partial(backward_inputs, rows, key_count, taps_a...]
    ppermute x10, starting transfers between devices: 13.9 us -> 13.5 us  [swap(): return lax.ppermute(x, axis, [(i, i ^ shift) for i in range(n)])]
  transfers between devices with their start and end apart: 10 -> 10, of which waited for: 2 -> 4; matrix products, arithmetic and copies ran while one was open for 0% -> 0% of each run, Pallas kernels for 33% -> 29%
where the time goes in v7:
time: 29.5 us; the launch traced here: 29.3 us
  starting transfers between devices  13.5 us (46%)
  Pallas kernels  11.5 us (39%)
  waiting for transfers between devices  2.9 us (10%)
  between operations  1.36 us (5%)
    ppermute x10, starting transfers between devices, swap(): return lax.ppermute(x, axis, [(i, i ^ shift) for i in range(n)])  13.5 us
    pallas_call x1, Pallas kernels, shards(): pl.pallas_call(functools.partial(forward, len(pieces), taps_a, half), out...  3.06 us
    pallas_call x1, Pallas kernels, shards(): pl.pallas_call(functools.partial(backward_inputs, rows, key_count, taps_a...  2.95 us
    ppermute x10, waiting for transfers between devices, swap(): return lax.ppermute(x, axis, [(i, i ^ shift) for i in range(n)])  2.9 us
    pallas_call x1, Pallas kernels, shards(): pl.pallas_call(functools.partial(backward_scores, up_places, w_places, ow...  2.09 us
    pallas_call x1, Pallas kernels, shards(): pl.pallas_call(functools.partial(prepare, half), out_shape=(shape(proj_we...  1.29 us
    pallas_call x1, Pallas kernels, shards(): pl.pallas_call(functools.partial(forward_turned, taps_a, half), out_shape...  1.15 us
    pallas_call x1, Pallas kernels, shards(): pl.pallas_call(functools.partial(update, group_count, span), out_shape=(s...  0.94 us
  transfers between devices with their start and end apart: 10, of which 4 were waited for; matrix products, arithmetic and copies ran while one was open for 0% of the time, Pallas kernels for 29%

profile of v7, /device:TPU:0, one launch (start us, length us, event | category | flops | bytes accessed | tf_op | source)
XLA Modules:
  0.0 29.3 jit_solution(10064779532705529760)
XLA Ops:
  0.6 3.0 %collective-permute-start.1 = (bf16[1,128,128]{2,1,0:T(8,128)(2,1)}, bf16[1,128,128]{2,1,0:T(8,128)(2,1)S(1)}, u32[]{:S(2)}, u32[]{:S(2)}) collective-permute-start(bf16[1,128,128]{2,1,0:T(8,128)(2,1)} %refs_0_.1), channel_id=1, source_target_pairs={{0,4},{1,5},{2,6},{3,7},{4,0},{5,1},{6,2},{7,3},{8,12},{9,13},{10,... | collective-permute-start | bytes 98312 | tf_op jit(solution)/shard_map/ppermute | solution.py:304
  3.7 1.5 %collective-permute-start = (bf16[1,128,128]{2,1,0:T(8,128)(2,1)}, bf16[1,128,128]{2,1,0:T(8,128)(2,1)S(1)}, u32[]{:S(2)}, u32[]{:S(2)}) collective-permute-start(bf16[1,128,128]{2,1,0:T(8,128)(2,1)} %refs_0_.1), channel_id=1, source_target_pairs={{0,2},{1,3},{2,0},{3,1},{4,6},{5,7},{6,4},{7,5},{8,10},{9,11},{10,... | collective-permute-start | bytes 98312 | tf_op jit(solution)/shard_map/ppermute | solution.py:304
  5.2 0.1 collective-permute-start.2
  5.2 1.3 %prepare.1 = (bf16[128,256]{1,0:T(8,128)(2,1)S(1)}, bf16[768,384]{1,0:T(8,128)(2,1)S(1)}, f32[144,128]{1,0:T(8,128)S(1)}, bf16[144,128]{1,0:T(8,128)(2,1)S(1)}, ...) custom-call(f32[6,1,11]{2,1,0:T(1,128)} %bitcast.2, f32[128,256]{1,0:T(8,128)} %refs_5_.1, ...), custom_call_target="tpu_custom_call" | custom-call | flops 1000000000 | bytes 1000000 | tf_op jit(solution)/shard_map/prepare/pallas_call | solution.py:356
  6.5 3.1 %collective-permute-start.6 = (bf16[128,256]{1,0:T(8,128)(2,1)S(1)}, bf16[128,256]{1,0:T(8,128)(2,1)S(1)}, u32[]{:S(2)}, u32[]{:S(2)}) collective-permute-start(bf16[128,256]{1,0:T(8,128)(2,1)S(1)} %get-tuple-element.37.refs_2_), channel_id=1, source_target_pairs={{0,16},{8,24},{16,0},{24,8},{1,17},{9,25},{17,1},{25,9},{2,18},{10... | collective-permute-start | bytes 196616 | tf_op jit(solution)/shard_map/ppermute | solution.py:304
  9.6 1.3 %collective-permute-start.5 = (bf16[128,256]{1,0:T(8,128)(2,1)S(1)}, bf16[128,256]{1,0:T(8,128)(2,1)S(1)}, u32[]{:S(2)}, u32[]{:S(2)}) collective-permute-start(bf16[128,256]{1,0:T(8,128)(2,1)S(1)} %get-tuple-element.37.refs_2_), channel_id=1, source_target_pairs={{0,24},{8,16},{16,8},{24,0},{1,25},{9,17},{17,9},{25,1},{2,26},{10... | collective-permute-start | bytes 196616 | tf_op jit(solution)/shard_map/ppermute | solution.py:304
  11.6 0.0 collective-permute-done.1.refs_2_
  11.6 0.3 %collective-permute-start.4 = (bf16[128,256]{1,0:T(8,128)(2,1)S(1)}, bf16[128,256]{1,0:T(8,128)(2,1)S(1)}, u32[]{:S(2)}, u32[]{:S(2)}) collective-permute-start(bf16[128,256]{1,0:T(8,128)(2,1)S(1)} %get-tuple-element.37.refs_2_), channel_id=1, source_target_pairs={{0,8},{8,0},{16,24},{24,16},{1,9},{9,1},{17,25},{25,17},{2,10},{10... | collective-permute-start | bytes 196616 | tf_op jit(solution)/shard_map/ppermute | solution.py:304
  11.9 0.0 collective-permute-done.refs_1_
  11.9 0.0 collective-permute-done.2.refs_3_
  11.9 3.1 %attention_forward.1 = (f32[128,1152]{1,0:T(8,128)S(1)}, bf16[128,128]{1,0:T(8,128)(2,1)S(1)}, bf16[512,128]{1,0:T(8,128)(2,1)S(1)}) custom-call(bf16[1,128,128]{2,1,0:T(8,128)(2,1)} %refs_0_.1, bf16[1,128,128]{2,1,0:T(8,128)(2,1)S(1)} %collective-permute-done.refs_1_, bf16[1,128,128]{2,1,0:T(8,128)(2,1)S(1)} %collective-permute-done.1.refs_2_, ...), custom_call_target="tpu_custom_call" | custom-call | flops 5000000000 | bytes 1000000 | tf_op jit(solution)/shard_map/attention_forward/pallas_call | solution.py:386
  15.0 0.1 collective-permute-start.3
  15.0 1.1 %attention_forward_turned.1 = (bf16[1152,768]{1,0:T(8,128)(2,1)S(1)}, bf16[1152,768]{1,0:T(8,128)(2,1)S(1)}) custom-call(s32[1]{0:T(128)S(6)} %copy.16.refs_4_.first_ref, bf16[1152,128]{1,0:T(8,128)(2,1)S(1)} %get-tuple-element.34.refs_7_.kwin, f32[144,128]{1,0:T(8,128)S(1)} %get-tuple-element.39.q32), custom_call_target="tpu_custom_call" | custom-call | flops 2000000000 | bytes 1000000 | tf_op jit(solution)/shard_map/attention_forward_turned/pallas_call | solution.py:412
  16.2 0.0 collective-permute-done.6.refs_5_
  16.2 0.0 collective-permute-done.5.refs_4_
  16.2 0.1 collective-permute-done.4.refs_3_
  16.4 0.0 collective-permute-done.3.refs_1_
  16.4 2.1 %attention_backward_scores.1 = (bf16[128,128]{1,0:T(8,128)(2,1)S(1)}, f32[152,1152]{1,0:T(8,128)S(1)}, f32[128,256]{1,0:T(8,128)S(1)}, f32[8,128]{1,0:T(8,128)S(...) custom-call(bf16[512,128]{1,0:T(8,128)(2,1)S(1)} %get-tuple-element.36.refs_0_, ...), custom_call_target="tpu_custom_call" | custom-call | flops 2000000000 | bytes 1000000 | tf_op jit(solution)/shard_map/attention_backward_scores/pallas_call | solution.py:425
  18.5 2.8 %collective-permute-start.7 = (bf16[272,128]{1,0:T(8,128)(2,1)S(1)}, bf16[272,128]{1,0:T(8,128)(2,1)S(1)}, u32[]{:S(2)}, u32[]{:S(2)}) collective-permute-start(bf16[272,128]{1,0:T(8,128)(2,1)S(1)} %get-tuple-element.48), channel_id=1, source_target_pairs={{0,16},{8,24},{16,0},{24,8},{1,17},{9,25},{17,1},{25,9},{2,18},{10... | collective-permute-start | bytes 208904 | tf_op jit(solution)/shard_map/ppermute | solution.py:304
  21.3 1.4 %collective-permute-start.8 = (bf16[272,128]{1,0:T(8,128)(2,1)S(1)}, bf16[272,128]{1,0:T(8,128)(2,1)S(1)}, u32[]{:S(2)}, u32[]{:S(2)}) collective-permute-start(bf16[272,128]{1,0:T(8,128)(2,1)S(1)} %get-tuple-element.49), channel_id=1, source_target_pairs={{0,24},{8,16},{16,8},{24,0},{1,25},{9,17},{17,9},{25,1},{2,26},{10... | collective-permute-start | bytes 208904 | tf_op jit(solution)/shard_map/ppermute | solution.py:304
  22.6 0.0 collective-permute-start.9
  22.6 0.0 copy-start
  22.6 0.0 copy-start.1
  22.6 0.0 copy-start.2
  22.6 2.9 %attention_backward_inputs.1 = (bf16[1,133,128]{2,1,0:T(8,128)(2,1)}, bf16[1,1024,128]{2,1,0:T(8,128)(2,1)}, bf16[1,1024,128]{2,1,0:T(8,128)(2,1)}) custom-call(s32[1]{0:T(128)S(6)} %copy.16.refs_4_.first_ref, bf16[768,384]{1,0:T(8,128)(2,1)S(1)} %get-tuple-element.32.refs_5_.bands_ref, bf16[128,128]{1,0:T(8,128)(2,1)S(1)} %get-tuple-element.43.do_ref, ...), custom_call_target="tpu_custom_call" | custom-call | flops 3000000000 | bytes 1000000 | tf_op jit(solution)/shard_map/attention_backward_inputs/pallas_call | solution.py:451
  25.6 0.2 collective-permute-done.7.refs_0_
  25.8 2.2 %collective-permute-done.8.refs_1_ = bf16[272,128]{1,0:T(8,128)(2,1)S(1)} collective-permute-done((bf16[272,128]{1,0:T(8,128)(2,1)S(1)}, bf16[272,128]{1,0:T(8,128)(2,1)S(1)}, u32[]{:S(2)}, u32[]{:S(2)}) %collective-permute-start.8) | collective-permute-done | bytes 69664 | tf_op jit(solution)/shard_map/ppermute | solution.py:304
  28.0 0.3 %collective-permute-done.9.refs_2_ = bf16[272,128]{1,0:T(8,128)(2,1)S(1)} collective-permute-done((bf16[272,128]{1,0:T(8,128)(2,1)S(1)}, bf16[272,128]{1,0:T(8,128)(2,1)S(1)}, u32[]{:S(2)}, u32[]{:S(2)}) %collective-permute-start.9) | collective-permute-done | bytes 69664 | tf_op jit(solution)/shard_map/ppermute | solution.py:304
  28.3 0.0 copy-done
  28.3 0.0 copy-done.1
  28.3 0.0 copy-done.2
  28.3 0.9 %projection_update.1 = (f32[128,256]{1,0:T(8,128)}, f32[128,256]{1,0:T(8,128)}, f32[128,256]{1,0:T(8,128)}, f32[6,1,11]{2,1,0:T(1,128)}) custom-call(bf16[272,128]{1,0:T(8,128)(2,1)S(1)} %collective-permute-done.7.refs_0_, bf16[272,128]{1,0:T(8,128)(2,1)S(1)} %collective-permute-done.8.refs_1_, bf16[272,128]{1,0:T(8,128)(2,1)S(1)} %collective-permute-done.9.refs_2_, ...), custom_call_target="tpu_custom_call" | custom-call | tf_op jit(solution)/shard_map/projection_update/pallas_call | solution.py:467
Async XLA Ops:
  0.6 11.0 %collective-permute-start.1 = (bf16[1,128,128]{2,1,0:T(8,128)(2,1)}, bf16[1,128,128]{2,1,0:T(8,128)(2,1)S(1)}, u32[]{:S(2)}, u32[]{:S(2)}) collective-permute-start(bf16[1,128,128]{2,1,0:T(8,128)(2,1)} %refs_0_.1), channel_id=1, source_target_pairs={{0,4},{1,5},{2,6},{3,7},{4,0},{5,1},{6,2},{7,3},{8,12},{9,13},{10,... | collective-permute-start | bytes 98312 | tf_op jit(solution)/shard_map/ppermute | solution.py:304
  3.7 8.2 %collective-permute-start = (bf16[1,128,128]{2,1,0:T(8,128)(2,1)}, bf16[1,128,128]{2,1,0:T(8,128)(2,1)S(1)}, u32[]{:S(2)}, u32[]{:S(2)}) collective-permute-start(bf16[1,128,128]{2,1,0:T(8,128)(2,1)} %refs_0_.1), channel_id=1, source_target_pairs={{0,2},{1,3},{2,0},{3,1},{4,6},{5,7},{6,4},{7,5},{8,10},{9,11},{10,... | collective-permute-start | bytes 98312 | tf_op jit(solution)/shard_map/ppermute | solution.py:304
  5.2 6.7 %collective-permute-start.2 = (bf16[1,128,128]{2,1,0:T(8,128)(2,1)}, bf16[1,128,128]{2,1,0:T(8,128)(2,1)S(1)}, u32[]{:S(2)}, u32[]{:S(2)}) collective-permute-start(bf16[1,128,128]{2,1,0:T(8,128)(2,1)} %refs_0_.1), channel_id=1, source_target_pairs={{0,6},{1,7},{2,4},{3,5},{4,2},{5,3},{6,0},{7,1},{8,14},{9,15},{10,... | collective-permute-start | bytes 98312 | tf_op jit(solution)/shard_map/ppermute | solution.py:304
  6.5 9.7 %collective-permute-start.6 = (bf16[128,256]{1,0:T(8,128)(2,1)S(1)}, bf16[128,256]{1,0:T(8,128)(2,1)S(1)}, u32[]{:S(2)}, u32[]{:S(2)}) collective-permute-start(bf16[128,256]{1,0:T(8,128)(2,1)S(1)} %get-tuple-element.37.refs_2_), channel_id=1, source_target_pairs={{0,16},{8,24},{16,0},{24,8},{1,17},{9,25},{17,1},{25,9},{2,18},{10... | collective-permute-start | bytes 196616 | tf_op jit(solution)/shard_map/ppermute | solution.py:304
  9.6 6.6 %collective-permute-start.5 = (bf16[128,256]{1,0:T(8,128)(2,1)S(1)}, bf16[128,256]{1,0:T(8,128)(2,1)S(1)}, u32[]{:S(2)}, u32[]{:S(2)}) collective-permute-start(bf16[128,256]{1,0:T(8,128)(2,1)S(1)} %get-tuple-element.37.refs_2_), channel_id=1, source_target_pairs={{0,24},{8,16},{16,8},{24,0},{1,25},{9,17},{17,9},{25,1},{2,26},{10... | collective-permute-start | bytes 196616 | tf_op jit(solution)/shard_map/ppermute | solution.py:304
  11.6 4.8 %collective-permute-start.4 = (bf16[128,256]{1,0:T(8,128)(2,1)S(1)}, bf16[128,256]{1,0:T(8,128)(2,1)S(1)}, u32[]{:S(2)}, u32[]{:S(2)}) collective-permute-start(bf16[128,256]{1,0:T(8,128)(2,1)S(1)} %get-tuple-element.37.refs_2_), channel_id=1, source_target_pairs={{0,8},{8,0},{16,24},{24,16},{1,9},{9,1},{17,25},{25,17},{2,10},{10... | collective-permute-start | bytes 196616 | tf_op jit(solution)/shard_map/ppermute | solution.py:304
  15.0 1.4 %collective-permute-start.3 = (bf16[512,128]{1,0:T(8,128)(2,1)S(1)}, bf16[512,128]{1,0:T(8,128)(2,1)S(1)}, u32[]{:S(2)}, u32[]{:S(2)}) collective-permute-start(bf16[512,128]{1,0:T(8,128)(2,1)S(1)} %get-tuple-element.36.refs_0_), channel_id=1, source_target_pairs={{0,1},{1,0},{2,3},{3,2},{4,5},{5,4},{6,7},{7,6},{8,9},{9,8},{10,11... | collective-permute-start | bytes 393224 | tf_op jit(solution)/shard_map/ppermute | solution.py:304
  18.5 7.3 %collective-permute-start.7 = (bf16[272,128]{1,0:T(8,128)(2,1)S(1)}, bf16[272,128]{1,0:T(8,128)(2,1)S(1)}, u32[]{:S(2)}, u32[]{:S(2)}) collective-permute-start(bf16[272,128]{1,0:T(8,128)(2,1)S(1)} %get-tuple-element.48), channel_id=1, source_target_pairs={{0,16},{8,24},{16,0},{24,8},{1,17},{9,25},{17,1},{25,9},{2,18},{10... | collective-permute-start | bytes 208904 | tf_op jit(solution)/shard_map/ppermute | solution.py:304
  21.3 6.7 %collective-permute-start.8 = (bf16[272,128]{1,0:T(8,128)(2,1)S(1)}, bf16[272,128]{1,0:T(8,128)(2,1)S(1)}, u32[]{:S(2)}, u32[]{:S(2)}) collective-permute-start(bf16[272,128]{1,0:T(8,128)(2,1)S(1)} %get-tuple-element.49), channel_id=1, source_target_pairs={{0,24},{8,16},{16,8},{24,0},{1,25},{9,17},{17,9},{25,1},{2,26},{10... | collective-permute-start | bytes 208904 | tf_op jit(solution)/shard_map/ppermute | solution.py:304
  22.6 5.7 %collective-permute-start.9 = (bf16[272,128]{1,0:T(8,128)(2,1)S(1)}, bf16[272,128]{1,0:T(8,128)(2,1)S(1)}, u32[]{:S(2)}, u32[]{:S(2)}) collective-permute-start(bf16[272,128]{1,0:T(8,128)(2,1)S(1)} %get-tuple-element.50), channel_id=1, source_target_pairs={{0,8},{8,0},{16,24},{24,16},{1,9},{9,1},{17,25},{25,17},{2,10},{10... | collective-permute-start | bytes 208904 | tf_op jit(solution)/shard_map/ppermute | solution.py:304
  22.6 5.7 %copy-start = (f32[128,256]{1,0:T(8,128)S(1)}, f32[128,256]{1,0:T(8,128)}, u32[]{:S(2)}) copy-start(f32[128,256]{1,0:T(8,128)} %refs_5_.1) | copy-start | bytes 393220
  22.6 5.7 %copy-start.1 = (f32[128,256]{1,0:T(8,128)S(1)}, f32[128,256]{1,0:T(8,128)}, u32[]{:S(2)}) copy-start(f32[128,256]{1,0:T(8,128)} %refs_6_.1) | copy-start | bytes 393220
  22.6 5.7 %copy-start.2 = (f32[128,256]{1,0:T(8,128)S(1)}, f32[128,256]{1,0:T(8,128)}, u32[]{:S(2)}) copy-start(f32[128,256]{1,0:T(8,128)} %refs_7_.1) | copy-start | bytes 393220

commit v8 on v7

--- a/solution.py
+++ b/solution.py
@@ -87,15 +87,17 @@
     rows32[8 + keys :] = jnp.zeros((rows32.shape[0] - 8 - keys, LANES), F32)
     copies[0].wait()
     hold_bands(taps_ref, bands_ref)
-    for copy in copies[1:]:
-        copy.wait()
-    w_ref[...] = w_in[...].astype(BF16)
-    q32[:rows] = q_in[...].astype(F32)
-    q16[...] = q32[...].astype(BF16)
+    copies[3].wait()
     rows32[8 : 8 + keys] = k_in[...].astype(F32)
     for n in range(kwin.shape[0] // LANES):
         start = 8 - half + n * step
         kwin[n * LANES : (n + 1) * LANES] = rows32[start : start + LANES].astype(BF16)
+    copies[1].wait()
+    w_ref[...] = w_in[...].astype(BF16)
+    copies[2].wait()
+    q32[:rows] = q_in[...].astype(F32)
+    q16[...] = q32[...].astype(BF16)
+    copies[4].wait()
     rows32[8 : 8 + keys] = v_in[...].astype(F32)
     for n in range(vblk.shape[0] // LANES):
         start = 8 + n * step
@@ -420,7 +422,9 @@
         name="attention_forward_turned",
     )(span_start, kwin, q32)
 
-    owners = turns(group_count) if few("dp") else list(range(group_count))
+    owners = list(range(group_count))
+    if few("dp"):
+        owners = owners[group_count // 2 : 0 : -1] + owners[group_count // 2 + 1 :]
     others = len(owners)
     do, dc, own, own_taps, *payloads = pl.pallas_call(
         functools.partial(backward_scores, up_places, w_places, owners, few("dp")),

time: 29.5 us -> 29.2 us (0.990)
  waiting for transfers between devices: 2.9 us -> 2.48 us
  starting transfers between devices: 13.5 us -> 13.8 us
    ppermute x10, waiting for transfers between devices: 2.9 us -> 2.48 us  [swap(): return lax.ppermute(x, axis, [(i, i ^ shift) for i in range(n)])]
  transfers between devices with their start and end apart: 10 -> 10, of which waited for: 4 -> 2; matrix products, arithmetic and copies ran while one was open for 0% -> 0% of each run, Pallas kernels for 29% -> 29%
where the time goes in v8:
time: 29.2 us; the launch traced here: 29 us
  starting transfers between devices  13.8 us (47%)
  Pallas kernels  11.4 us (39%)
  waiting for transfers between devices  2.48 us (8%)
  between operations  1.35 us (5%)
    ppermute x10, starting transfers between devices, swap(): return lax.ppermute(x, axis, [(i, i ^ shift) for i in range(n)])  13.8 us
    pallas_call x1, Pallas kernels, shards(): pl.pallas_call(functools.partial(forward, len(pieces), taps_a, half), out...  3.06 us
    pallas_call x1, Pallas kernels, shards(): pl.pallas_call(functools.partial(backward_inputs, rows, key_count, taps_a...  2.94 us
    ppermute x10, waiting for transfers between devices, swap(): return lax.ppermute(x, axis, [(i, i ^ shift) for i in range(n)])  2.48 us
    pallas_call x1, Pallas kernels, shards(): pl.pallas_call(functools.partial(backward_scores, up_places, w_places, ow...  2.09 us
    pallas_call x1, Pallas kernels, shards(): pl.pallas_call(functools.partial(prepare, half), out_shape=(shape(proj_we...  1.23 us
    pallas_call x1, Pallas kernels, shards(): pl.pallas_call(functools.partial(forward_turned, taps_a, half), out_shape...  1.15 us
    pallas_call x1, Pallas kernels, shards(): pl.pallas_call(functools.partial(update, group_count, span), out_shape=(s...  0.94 us
  transfers between devices with their start and end apart: 10, of which 2 were waited for; matrix products, arithmetic and copies ran while one was open for 0% of the time, Pallas kernels for 29%

profile of v8, /device:TPU:0, one launch (start us, length us, event | category | flops | bytes accessed | tf_op | source)
XLA Modules:
  0.0 29.0 jit_solution(15672884223729117506)
XLA Ops:
  0.6 3.0 %collective-permute-start.1 = (bf16[1,128,128]{2,1,0:T(8,128)(2,1)}, bf16[1,128,128]{2,1,0:T(8,128)(2,1)S(1)}, u32[]{:S(2)}, u32[]{:S(2)}) collective-permute-start(bf16[1,128,128]{2,1,0:T(8,128)(2,1)} %refs_0_.1), channel_id=1, source_target_pairs={{0,4},{1,5},{2,6},{3,7},{4,0},{5,1},{6,2},{7,3},{8,12},{9,13},{10,... | collective-permute-start | bytes 98312 | tf_op jit(solution)/shard_map/ppermute | solution.py:306
  3.7 1.5 %collective-permute-start = (bf16[1,128,128]{2,1,0:T(8,128)(2,1)}, bf16[1,128,128]{2,1,0:T(8,128)(2,1)S(1)}, u32[]{:S(2)}, u32[]{:S(2)}) collective-permute-start(bf16[1,128,128]{2,1,0:T(8,128)(2,1)} %refs_0_.1), channel_id=1, source_target_pairs={{0,2},{1,3},{2,0},{3,1},{4,6},{5,7},{6,4},{7,5},{8,10},{9,11},{10,... | collective-permute-start | bytes 98312 | tf_op jit(solution)/shard_map/ppermute | solution.py:306
  5.2 0.1 collective-permute-start.2
  5.2 1.2 %prepare.1 = (bf16[128,256]{1,0:T(8,128)(2,1)S(1)}, bf16[768,384]{1,0:T(8,128)(2,1)S(1)}, f32[144,128]{1,0:T(8,128)S(1)}, bf16[144,128]{1,0:T(8,128)(2,1)S(1)}, ...) custom-call(f32[6,1,11]{2,1,0:T(1,128)} %bitcast.2, f32[128,256]{1,0:T(8,128)} %refs_5_.1, ...), custom_call_target="tpu_custom_call" | custom-call | flops 1000000000 | bytes 1000000 | tf_op jit(solution)/shard_map/prepare/pallas_call | solution.py:358
  6.4 3.1 %collective-permute-start.6 = (bf16[128,256]{1,0:T(8,128)(2,1)S(1)}, bf16[128,256]{1,0:T(8,128)(2,1)S(1)}, u32[]{:S(2)}, u32[]{:S(2)}) collective-permute-start(bf16[128,256]{1,0:T(8,128)(2,1)S(1)} %get-tuple-element.37.refs_2_), channel_id=1, source_target_pairs={{0,16},{8,24},{16,0},{24,8},{1,17},{9,25},{17,1},{25,9},{2,18},{10... | collective-permute-start | bytes 196616 | tf_op jit(solution)/shard_map/ppermute | solution.py:306
  9.5 1.3 %collective-permute-start.5 = (bf16[128,256]{1,0:T(8,128)(2,1)S(1)}, bf16[128,256]{1,0:T(8,128)(2,1)S(1)}, u32[]{:S(2)}, u32[]{:S(2)}) collective-permute-start(bf16[128,256]{1,0:T(8,128)(2,1)S(1)} %get-tuple-element.37.refs_2_), channel_id=1, source_target_pairs={{0,24},{8,16},{16,8},{24,0},{1,25},{9,17},{17,9},{25,1},{2,26},{10... | collective-permute-start | bytes 196616 | tf_op jit(solution)/shard_map/ppermute | solution.py:306
  11.5 0.0 collective-permute-done.1.refs_2_
  11.5 0.3 %collective-permute-start.4 = (bf16[128,256]{1,0:T(8,128)(2,1)S(1)}, bf16[128,256]{1,0:T(8,128)(2,1)S(1)}, u32[]{:S(2)}, u32[]{:S(2)}) collective-permute-start(bf16[128,256]{1,0:T(8,128)(2,1)S(1)} %get-tuple-element.37.refs_2_), channel_id=1, source_target_pairs={{0,8},{8,0},{16,24},{24,16},{1,9},{9,1},{17,25},{25,17},{2,10},{10... | collective-permute-start | bytes 196616 | tf_op jit(solution)/shard_map/ppermute | solution.py:306
  11.8 0.0 collective-permute-done.refs_1_
  11.8 0.0 collective-permute-done.2.refs_3_
  11.8 3.1 %attention_forward.1 = (f32[128,1152]{1,0:T(8,128)S(1)}, bf16[128,128]{1,0:T(8,128)(2,1)S(1)}, bf16[512,128]{1,0:T(8,128)(2,1)S(1)}) custom-call(bf16[1,128,128]{2,1,0:T(8,128)(2,1)} %refs_0_.1, bf16[1,128,128]{2,1,0:T(8,128)(2,1)S(1)} %collective-permute-done.refs_1_, bf16[1,128,128]{2,1,0:T(8,128)(2,1)S(1)} %collective-permute-done.1.refs_2_, ...), custom_call_target="tpu_custom_call" | custom-call | flops 5000000000 | bytes 1000000 | tf_op jit(solution)/shard_map/attention_forward/pallas_call | solution.py:388
  14.9 0.1 collective-permute-start.3
  15.0 1.1 %attention_forward_turned.1 = (bf16[1152,768]{1,0:T(8,128)(2,1)S(1)}, bf16[1152,768]{1,0:T(8,128)(2,1)S(1)}) custom-call(s32[1]{0:T(128)S(6)} %copy.16.refs_4_.first_ref, bf16[1152,128]{1,0:T(8,128)(2,1)S(1)} %get-tuple-element.34.refs_7_.kwin, f32[144,128]{1,0:T(8,128)S(1)} %get-tuple-element.39.q32), custom_call_target="tpu_custom_call" | custom-call | flops 2000000000 | bytes 1000000 | tf_op jit(solution)/shard_map/attention_forward_turned/pallas_call | solution.py:414
  16.1 0.0 collective-permute-done.6.refs_5_
  16.1 0.0 collective-permute-done.5.refs_4_
  16.2 0.1 collective-permute-done.4.refs_3_
  16.3 0.0 collective-permute-done.3.refs_1_
  16.3 2.1 %attention_backward_scores.1 = (bf16[128,128]{1,0:T(8,128)(2,1)S(1)}, f32[152,1152]{1,0:T(8,128)S(1)}, f32[128,256]{1,0:T(8,128)S(1)}, f32[8,128]{1,0:T(8,128)S(...) custom-call(bf16[512,128]{1,0:T(8,128)(2,1)S(1)} %get-tuple-element.36.refs_0_, ...), custom_call_target="tpu_custom_call" | custom-call | flops 2000000000 | bytes 1000000 | tf_op jit(solution)/shard_map/attention_backward_scores/pallas_call | solution.py:429
  18.4 2.8 %collective-permute-start.7 = (bf16[272,128]{1,0:T(8,128)(2,1)S(1)}, bf16[272,128]{1,0:T(8,128)(2,1)S(1)}, u32[]{:S(2)}, u32[]{:S(2)}) collective-permute-start(bf16[272,128]{1,0:T(8,128)(2,1)S(1)} %get-tuple-element.48), channel_id=1, source_target_pairs={{0,16},{8,24},{16,0},{24,8},{1,17},{9,25},{17,1},{25,9},{2,18},{10... | collective-permute-start | bytes 208904 | tf_op jit(solution)/shard_map/ppermute | solution.py:306
  21.2 0.7 %collective-permute-start.8 = (bf16[272,128]{1,0:T(8,128)(2,1)S(1)}, bf16[272,128]{1,0:T(8,128)(2,1)S(1)}, u32[]{:S(2)}, u32[]{:S(2)}) collective-permute-start(bf16[272,128]{1,0:T(8,128)(2,1)S(1)} %get-tuple-element.49), channel_id=1, source_target_pairs={{0,8},{8,0},{16,24},{24,16},{1,9},{9,1},{17,25},{25,17},{2,10},{10... | collective-permute-start | bytes 208904 | tf_op jit(solution)/shard_map/ppermute | solution.py:306
  21.9 0.9 %collective-permute-start.9 = (bf16[272,128]{1,0:T(8,128)(2,1)S(1)}, bf16[272,128]{1,0:T(8,128)(2,1)S(1)}, u32[]{:S(2)}, u32[]{:S(2)}) collective-permute-start(bf16[272,128]{1,0:T(8,128)(2,1)S(1)} %get-tuple-element.50), channel_id=1, source_target_pairs={{0,24},{8,16},{16,8},{24,0},{1,25},{9,17},{17,9},{25,1},{2,26},{10... | collective-permute-start | bytes 208904 | tf_op jit(solution)/shard_map/ppermute | solution.py:306
  22.8 0.0 copy-start
  22.8 0.0 copy-start.1
  22.8 0.0 copy-start.2
  22.8 2.9 %attention_backward_inputs.1 = (bf16[1,133,128]{2,1,0:T(8,128)(2,1)}, bf16[1,1024,128]{2,1,0:T(8,128)(2,1)}, bf16[1,1024,128]{2,1,0:T(8,128)(2,1)}) custom-call(s32[1]{0:T(128)S(6)} %copy.16.refs_4_.first_ref, bf16[768,384]{1,0:T(8,128)(2,1)S(1)} %get-tuple-element.32.refs_5_.bands_ref, bf16[128,128]{1,0:T(8,128)(2,1)S(1)} %get-tuple-element.43.do_ref, ...), custom_call_target="tpu_custom_call" | custom-call | flops 3000000000 | bytes 1000000 | tf_op jit(solution)/shard_map/attention_backward_inputs/pallas_call | solution.py:455
  25.8 0.0 collective-permute-done.7.refs_0_
  25.8 0.0 collective-permute-done.8.refs_1_
  25.8 2.3 %collective-permute-done.9.refs_2_ = bf16[272,128]{1,0:T(8,128)(2,1)S(1)} collective-permute-done((bf16[272,128]{1,0:T(8,128)(2,1)S(1)}, bf16[272,128]{1,0:T(8,128)(2,1)S(1)}, u32[]{:S(2)}, u32[]{:S(2)}) %collective-permute-start.9) | collective-permute-done | bytes 69664 | tf_op jit(solution)/shard_map/ppermute | solution.py:306
  28.1 0.0 copy-done
  28.1 0.0 copy-done.1
  28.1 0.0 copy-done.2
  28.1 0.9 %projection_update.1 = (f32[128,256]{1,0:T(8,128)}, f32[128,256]{1,0:T(8,128)}, f32[128,256]{1,0:T(8,128)}, f32[6,1,11]{2,1,0:T(1,128)}) custom-call(bf16[272,128]{1,0:T(8,128)(2,1)S(1)} %collective-permute-done.7.refs_0_, bf16[272,128]{1,0:T(8,128)(2,1)S(1)} %collective-permute-done.8.refs_1_, bf16[272,128]{1,0:T(8,128)(2,1)S(1)} %collective-permute-done.9.refs_2_, ...), custom_call_target="tpu_custom_call" | custom-call | tf_op jit(solution)/shard_map/projection_update/pallas_call | solution.py:471
Async XLA Ops:
  0.6 10.9 %collective-permute-start.1 = (bf16[1,128,128]{2,1,0:T(8,128)(2,1)}, bf16[1,128,128]{2,1,0:T(8,128)(2,1)S(1)}, u32[]{:S(2)}, u32[]{:S(2)}) collective-permute-start(bf16[1,128,128]{2,1,0:T(8,128)(2,1)} %refs_0_.1), channel_id=1, source_target_pairs={{0,4},{1,5},{2,6},{3,7},{4,0},{5,1},{6,2},{7,3},{8,12},{9,13},{10,... | collective-permute-start | bytes 98312 | tf_op jit(solution)/shard_map/ppermute | solution.py:306
  3.7 8.2 %collective-permute-start = (bf16[1,128,128]{2,1,0:T(8,128)(2,1)}, bf16[1,128,128]{2,1,0:T(8,128)(2,1)S(1)}, u32[]{:S(2)}, u32[]{:S(2)}) collective-permute-start(bf16[1,128,128]{2,1,0:T(8,128)(2,1)} %refs_0_.1), channel_id=1, source_target_pairs={{0,2},{1,3},{2,0},{3,1},{4,6},{5,7},{6,4},{7,5},{8,10},{9,11},{10,... | collective-permute-start | bytes 98312 | tf_op jit(solution)/shard_map/ppermute | solution.py:306
  5.2 6.7 %collective-permute-start.2 = (bf16[1,128,128]{2,1,0:T(8,128)(2,1)}, bf16[1,128,128]{2,1,0:T(8,128)(2,1)S(1)}, u32[]{:S(2)}, u32[]{:S(2)}) collective-permute-start(bf16[1,128,128]{2,1,0:T(8,128)(2,1)} %refs_0_.1), channel_id=1, source_target_pairs={{0,6},{1,7},{2,4},{3,5},{4,2},{5,3},{6,0},{7,1},{8,14},{9,15},{10,... | collective-permute-start | bytes 98312 | tf_op jit(solution)/shard_map/ppermute | solution.py:306
  6.4 9.7 %collective-permute-start.6 = (bf16[128,256]{1,0:T(8,128)(2,1)S(1)}, bf16[128,256]{1,0:T(8,128)(2,1)S(1)}, u32[]{:S(2)}, u32[]{:S(2)}) collective-permute-start(bf16[128,256]{1,0:T(8,128)(2,1)S(1)} %get-tuple-element.37.refs_2_), channel_id=1, source_target_pairs={{0,16},{8,24},{16,0},{24,8},{1,17},{9,25},{17,1},{25,9},{2,18},{10... | collective-permute-start | bytes 196616 | tf_op jit(solution)/shard_map/ppermute | solution.py:306
  9.5 6.6 %collective-permute-start.5 = (bf16[128,256]{1,0:T(8,128)(2,1)S(1)}, bf16[128,256]{1,0:T(8,128)(2,1)S(1)}, u32[]{:S(2)}, u32[]{:S(2)}) collective-permute-start(bf16[128,256]{1,0:T(8,128)(2,1)S(1)} %get-tuple-element.37.refs_2_), channel_id=1, source_target_pairs={{0,24},{8,16},{16,8},{24,0},{1,25},{9,17},{17,9},{25,1},{2,26},{10... | collective-permute-start | bytes 196616 | tf_op jit(solution)/shard_map/ppermute | solution.py:306
  11.5 4.8 %collective-permute-start.4 = (bf16[128,256]{1,0:T(8,128)(2,1)S(1)}, bf16[128,256]{1,0:T(8,128)(2,1)S(1)}, u32[]{:S(2)}, u32[]{:S(2)}) collective-permute-start(bf16[128,256]{1,0:T(8,128)(2,1)S(1)} %get-tuple-element.37.refs_2_), channel_id=1, source_target_pairs={{0,8},{8,0},{16,24},{24,16},{1,9},{9,1},{17,25},{25,17},{2,10},{10... | collective-permute-start | bytes 196616 | tf_op jit(solution)/shard_map/ppermute | solution.py:306
  14.9 1.4 %collective-permute-start.3 = (bf16[512,128]{1,0:T(8,128)(2,1)S(1)}, bf16[512,128]{1,0:T(8,128)(2,1)S(1)}, u32[]{:S(2)}, u32[]{:S(2)}) collective-permute-start(bf16[512,128]{1,0:T(8,128)(2,1)S(1)} %get-tuple-element.36.refs_0_), channel_id=1, source_target_pairs={{0,1},{1,0},{2,3},{3,2},{4,5},{5,4},{6,7},{7,6},{8,9},{9,8},{10,11... | collective-permute-start | bytes 393224 | tf_op jit(solution)/shard_map/ppermute | solution.py:306
  18.4 7.3 %collective-permute-start.7 = (bf16[272,128]{1,0:T(8,128)(2,1)S(1)}, bf16[272,128]{1,0:T(8,128)(2,1)S(1)}, u32[]{:S(2)}, u32[]{:S(2)}) collective-permute-start(bf16[272,128]{1,0:T(8,128)(2,1)S(1)} %get-tuple-element.48), channel_id=1, source_target_pairs={{0,16},{8,24},{16,0},{24,8},{1,17},{9,25},{17,1},{25,9},{2,18},{10... | collective-permute-start | bytes 208904 | tf_op jit(solution)/shard_map/ppermute | solution.py:306
  21.2 4.5 %collective-permute-start.8 = (bf16[272,128]{1,0:T(8,128)(2,1)S(1)}, bf16[272,128]{1,0:T(8,128)(2,1)S(1)}, u32[]{:S(2)}, u32[]{:S(2)}) collective-permute-start(bf16[272,128]{1,0:T(8,128)(2,1)S(1)} %get-tuple-element.49), channel_id=1, source_target_pairs={{0,8},{8,0},{16,24},{24,16},{1,9},{9,1},{17,25},{25,17},{2,10},{10... | collective-permute-start | bytes 208904 | tf_op jit(solution)/shard_map/ppermute | solution.py:306
  21.9 6.2 %collective-permute-start.9 = (bf16[272,128]{1,0:T(8,128)(2,1)S(1)}, bf16[272,128]{1,0:T(8,128)(2,1)S(1)}, u32[]{:S(2)}, u32[]{:S(2)}) collective-permute-start(bf16[272,128]{1,0:T(8,128)(2,1)S(1)} %get-tuple-element.50), channel_id=1, source_target_pairs={{0,24},{8,16},{16,8},{24,0},{1,25},{9,17},{17,9},{25,1},{2,26},{10... | collective-permute-start | bytes 208904 | tf_op jit(solution)/shard_map/ppermute | solution.py:306
  22.8 5.3 %copy-start = (f32[128,256]{1,0:T(8,128)S(1)}, f32[128,256]{1,0:T(8,128)}, u32[]{:S(2)}) copy-start(f32[128,256]{1,0:T(8,128)} %refs_5_.1) | copy-start | bytes 393220
  22.8 5.3 %copy-start.1 = (f32[128,256]{1,0:T(8,128)S(1)}, f32[128,256]{1,0:T(8,128)}, u32[]{:S(2)}) copy-start(f32[128,256]{1,0:T(8,128)} %refs_6_.1) | copy-start | bytes 393220
  22.8 5.3 %copy-start.2 = (f32[128,256]{1,0:T(8,128)S(1)}, f32[128,256]{1,0:T(8,128)}, u32[]{:S(2)}) copy-start(f32[128,256]{1,0:T(8,128)} %refs_7_.1) | copy-start | bytes 393220

commit v9 on v8

v9 whole, which is shorter than its diff:
```python
import functools
import math

import jax
import jax.numpy as jnp
from jax import lax
from jax.experimental import pallas as pl
from jax.experimental.pallas import tpu as pltpu
from jax.sharding import PartitionSpec as P

beta_one = 0.9
beta_two = 0.95
learn_rate = 0.01
decay_rate = 0.1
adam_eps = 1e-08
bias_one = 1.0 - 0.9**10
bias_two = 1.0 - 0.95**10

LANES = 128
GROUP = 2
F32 = jnp.float32
BF16 = jnp.bfloat16


def dot(left, right, dims=((1,), (0,))):
    return lax.dot_general(left, right, (dims, ((), ())), preferred_element_type=F32)


def split(x):
    high = x.astype(BF16)
    return high, (x - high.astype(F32)).astype(BF16)


def up_to(n, multiple):
    return -(-n // multiple) * multiple


def iota(shape, axis):
    return lax.broadcasted_iota(jnp.int32, shape, axis)


def hold_bands(taps_ref, scale, bands_ref):
    taps_a, _, taps_b = taps_ref.shape
    lane = iota((1, LANES), 1)
    out = []
    for a in range(taps_a):
        row = jnp.zeros((1, LANES), F32)
        for b in range(taps_b):
            row = jnp.where(lane == (LANES - b) % LANES, taps_ref[a, 0, b], row)
        out.append(pltpu.roll(jnp.broadcast_to(row, (LANES, LANES)), 0, 1, stride=1, stride_axis=0))
    height = GROUP * LANES
    for n in range(taps_a // GROUP):
        cols = slice(n * LANES, (n + 1) * LANES)
        high, low = split(jnp.concatenate(out[n * GROUP : (n + 1) * GROUP][::-1], axis=0) * scale)
        bands_ref[:height, cols] = high
        bands_ref[height : 2 * height, cols] = low
        bands_ref[2 * height :, cols] = high


def turned_bands(bands_ref):
    spots = [part * GROUP + at for part in range(3) for at in range(GROUP - 1, -1, -1)]
    rows = []
    for n in range(bands_ref.shape[1] // LANES):
        cols = slice(n * LANES, (n + 1) * LANES)
        rows.append(jnp.concatenate([bands_ref[at * LANES : (at + 1) * LANES, cols] for at in spots], axis=1))
    return jnp.concatenate(rows, axis=0)


def fetch(pairs, sems):
    copies = [pltpu.make_async_copy(src, dst, sems.at[n]) for n, (src, dst) in enumerate(pairs)]
    for copy in copies:
        copy.start()
    return copies


def prepare(
    taps_hbm, w_hbm, q_hbm,
    w_ref, bands_ref, q32, q16,
    taps_ref, w_in, q_in, sems,
):
    rows = q_in.shape[0]
    copies = fetch(((taps_hbm, taps_ref), (w_hbm, w_in), (q_hbm.at[0], q_in)), sems)
    q32[...] = jnp.zeros_like(q32)
    copies[0].wait()
    hold_bands(taps_ref, 1.0 / math.sqrt(q_in.shape[1]), bands_ref)
    copies[1].wait()
    w_ref[...] = w_in[...].astype(BF16)
    copies[2].wait()
    q32[:rows] = q_in[...].astype(F32)
    rows_up = q16.shape[0] // GROUP
    for n in range(GROUP):
        q16[n * rows_up : (n + 1) * rows_up] = q32[n : n + rows_up].astype(BF16)


def by_blocks(rows_ref, out, rows32, start, live):
    rows = rows_ref.shape[1]
    rows32[:8] = jnp.zeros((8, LANES), F32)
    rows32[8 : 8 + rows] = rows_ref[0].astype(F32)
    rows32[8 + rows :] = jnp.zeros((rows32.shape[0] - 8 - rows, LANES), F32)
    count = out.shape[0] // LANES
    step = (rows32.shape[0] - 8 - LANES) // (count - 1)
    for n in range(count):
        block = rows32[8 + start + n * step : 8 + start + n * step + LANES]
        if live < LANES:
            block = jnp.where(iota(block.shape, 0) < live, block, 0.0)
        out[n * LANES : (n + 1) * LANES] = block.astype(BF16)


def forward(pieces, taps_a, half, *refs):
    piece_refs, (first_ref, bands_ref, q16, k_ref) = refs[:pieces], refs[pieces : pieces + 4]
    p_ref, kwin, pack_ref, rows32, xh, xl, y = refs[pieces + 4 :]
    span = p_ref.shape[0]
    rows_up = q16.shape[0] // GROUP
    windows = kwin.shape[0] // LANES
    step = LANES - 2 * half
    first = first_ref[0]
    for n, ref in enumerate(piece_refs):
        pack_ref[n * span : (n + 1) * span] = ref[0]

    by_blocks(k_ref, kwin, rows32, -half, LANES)

    scores = dot(q16[...], kwin[...], ((1,), (1,)))
    pos = first - (taps_a - 1) + iota((rows_up, LANES), 0) - iota((rows_up, LANES), 1)
    for n in range(windows):
        here = slice(n * rows_up, (n + 1) * rows_up)
        for at in range(GROUP):
            x = scores[at * rows_up : (at + 1) * rows_up, n * LANES : (n + 1) * LANES]
            cols = slice(at * LANES, (at + 1) * LANES)
            xh[here, cols], xl[here, cols] = split(jnp.where(pos >= n * step - half - at, x, 0.0))

    y[...] = dot(jnp.concatenate([xh[...], xh[...], xl[...]], axis=1), bands_ref[...])
    mixed = []
    for n in range(windows):
        total = None
        for group in range(taps_a // GROUP):
            start = n * rows_up + taps_a - GROUP * (group + 1)
            term = y[start : start + span, group * LANES : (group + 1) * LANES]
            total = term if total is None else total + term
        mixed.append(total)
    c = jnp.concatenate(mixed, axis=1)
    lane = iota((span, LANES), 1)
    row = iota((span, LANES), 0)
    live = jnp.concatenate([(lane < step) & (n * step + lane <= first + row) for n in range(windows)], axis=1)
    c = jnp.where(live, c, -jnp.inf)
    terms = jnp.exp(c - jnp.max(c, axis=1, keepdims=True))
    p = terms * (1.0 / jnp.sum(terms, axis=1, keepdims=True))
    p_ref[...] = p


def forward_turned(taps_a, half, first_ref, kwin, q32, p_ref, v_ref, xth_ref, xtl_ref, vblk, o_ref, kturn, rows32):
    span = xth_ref.shape[1] // taps_a
    windows = kwin.shape[0] // LANES
    step = LANES - 2 * half
    first = first_ref[0]
    by_blocks(v_ref, vblk, rows32, 0, step)
    o_ref[...] = dot(p_ref[...].astype(BF16), vblk[...]).astype(BF16)
    flip = (iota((LANES, LANES), 0) + iota((LANES, LANES), 1) == LANES - 1).astype(F32).astype(BF16)
    for n in range(windows):
        here = slice(n * LANES, (n + 1) * LANES)
        kturn[here] = dot(flip, kwin[here]).astype(BF16)
    lead = LANES - 1 - half - iota((LANES, span), 0) - iota((LANES, span), 1)
    lead = jnp.concatenate([lead + n * step for n in range(windows)], axis=0)
    shifted = jnp.concatenate([q32[taps_a - 1 - a : taps_a - 1 - a + span].astype(BF16) for a in range(taps_a)], axis=0)
    xt = dot(kturn[...], shifted, ((1,), (1,)))
    for a in range(taps_a):
        cols = slice(a * span, (a + 1) * span)
        xth_ref[:, cols], xtl_ref[:, cols] = split(jnp.where(lead <= first - a, xt[:, cols], 0.0))


def backward_scores(up_places, w_places, owners, by_distance, *refs):
    n_up, n_w = len({p[0] for p in up_places}), len({p[0] for p in w_places})
    up_refs, w_refs, refs = refs[:n_up], refs[n_up : n_up + n_w], refs[n_up + n_w :]
    p_ref, vblk, xth_ref, xtl_ref, o_ref, do_ref, own_ref, own_taps_ref = refs[:8]
    out_refs, (up, grad) = refs[8 : 8 + len(owners)], refs[8 + len(owners) :]
    span = p_ref.shape[0]
    taps_a = xth_ref.shape[1] // span
    windows = vblk.shape[0] // LANES

    def columns(places, axis):
        me = lax.axis_index(axis)
        return [(n, part, at if shift is None else lax.bitwise_xor(me, shift)) for n, part, shift, at in places]

    for n, part, spot in columns(up_places, "tensor"):
        block = up_refs[n][part]
        width = block.shape[1]
        up[:, pl.ds(pl.multiple_of(spot * width, width), width)] = block
    do = None
    for n, part, spot in columns(w_places, "dp"):
        block = w_refs[n][part]
        width = block.shape[1]
        term = dot(up[:, pl.ds(pl.multiple_of(spot * width, width), width)], block, ((1,), (1,)))
        do = term if do is None else do + term
    do = do.astype(BF16)
    do_ref[...] = do
    grad[...] = dot(o_ref[...], up[...], ((0,), (0,)))
    dc = scores_grad(p_ref[...], do, vblk[...])

    right = jnp.concatenate(
        [jnp.concatenate(split(dc[:, n * LANES : (n + 1) * LANES]), axis=1) for n in range(windows)], axis=0
    )
    right = jnp.concatenate([right, right], axis=0)
    sums = []
    for a in range(taps_a):
        cols = slice(a * span, (a + 1) * span)
        left = jnp.concatenate(
            [ref[n * LANES : (n + 1) * LANES, cols] for ref in (xth_ref, xtl_ref) for n in range(windows)], axis=1
        )
        total = dot(left, right)
        turned = pltpu.roll(total[:, :LANES] + total[:, LANES:], 0, 1, stride=1, stride_axis=0)
        sums.append(jnp.sum(turned, axis=0, keepdims=True))
    taps = jnp.concatenate(sums + [jnp.zeros((8 - taps_a, LANES), F32)], axis=0)

    high, low = split(taps)
    mid, low = low, (taps - high.astype(F32) - low.astype(F32)).astype(BF16)
    aside = pltpu.roll(low.astype(F32), LANES // 2, 1)
    first = jnp.where(iota(aside.shape, 1) < LANES // 2, aside, high.astype(F32))
    parts = jnp.concatenate([first, mid.astype(F32)], axis=0).astype(BF16)
    own_taps_ref[...] = taps
    depth, share = own_ref.shape
    me = lax.axis_index("dp")

    def owned(spot):
        return grad[:, pl.ds(pl.multiple_of(spot * share, share), share)]

    own_ref[...] = owned(me)
    for owner, ref in zip(owners, out_refs, strict=True):
        piece = owned(lax.bitwise_xor(me, owner) if by_distance else owner).astype(BF16)
        for n in range(share // LANES):
            ref[n * depth : (n + 1) * depth] = piece[:, n * LANES : (n + 1) * LANES]
        ref[ref.shape[0] - 16 :] = parts


def scores_grad(p, do, vblk):
    dp = dot(do, vblk, ((1,), (1,)))
    return p * (dp - jnp.sum(p * dp, axis=1, keepdims=True))


def backward_inputs(
    rows, keys, taps_a, half, first_ref, bands_ref, do_ref, p_ref, vblk, q16, kwin,
    dq_ref, dk_ref, dv_ref,
    dc_ref, left_h, left_l, z, sums,
):
    step = LANES - 2 * half
    depth = kwin.shape[1]
    windows = kwin.shape[0] // LANES
    rows_up = q16.shape[0] // GROUP
    scale = 1.0 / math.sqrt(depth)
    first = first_ref[0]
    do = do_ref[...]
    span = do.shape[0]
    dc_ref[:8] = jnp.zeros((8, dc_ref.shape[1]), F32)
    dc_ref[8 : 8 + span] = scores_grad(p_ref[...], do, vblk[...])
    dc_ref[8 + span :] = jnp.zeros((dc_ref.shape[0] - 8 - span, dc_ref.shape[1]), F32)
    for n in range(windows):
        cols = slice(n * LANES, (n + 1) * LANES)
        here = slice(n * rows_up, (n + 1) * rows_up)
        for at in range(GROUP):
            there = slice(at * LANES, (at + 1) * LANES)
            left_h[here, there], left_l[here, there] = split(dc_ref[at : at + rows_up, cols])
        sums[n * step : n * step + LANES] = dot(p_ref[:, cols].astype(BF16).T, do)
    dv_ref[0] = sums[:keys].astype(BF16)
    z[windows * rows_up :] = jnp.zeros((z.shape[0] - windows * rows_up, z.shape[1]), F32)
    left = jnp.concatenate([left_h[...], left_h[...], left_l[...]], axis=1)
    z[: windows * rows_up] = dot(left, turned_bands(bands_ref), ((1,), (1,)))

    lane = iota((rows_up, LANES), 1)
    row = iota((rows_up, LANES), 0)
    scores = []
    for n in range(windows):
        total = None
        for group in range(taps_a // GROUP):
            start = n * rows_up + 8 - (taps_a - 1) + GROUP * group
            term = z[start : start + rows_up, group * LANES : (group + 1) * LANES]
            total = term if total is None else total + term
        scores.append(total)
    sums[...] = jnp.zeros_like(sums)
    dq = jnp.zeros((rows_up, depth), F32)
    for n, total in enumerate(scores):
        if n + 1 < windows:
            total = jnp.where(lane < step, total, total + pltpu.roll(scores[n + 1], step, 1))
        live = (n * step - half + lane <= first - (taps_a - 1) + row) & (row < rows)
        ds = jnp.where(live & (lane >= 2 * half) if n else live, total * (1.0 / scale), 0.0)
        dq = dq + dot(ds.astype(BF16), kwin[n * LANES : (n + 1) * LANES])
        sums[n * step : n * step + LANES] += dot(ds.astype(BF16).T, q16[:rows_up])
    dk_ref[0] = (scale * sums[half : half + keys]).astype(BF16)
    dq_ref[0] = (scale * dq)[:rows].astype(BF16)


def update(count, span, *refs):
    payload_refs, (own_ref, own_taps_ref, w_ref, one_ref, two_ref) = refs[:-9], refs[-9:-4]
    new_ref, one_new_ref, two_new_ref, taps_ref = refs[-4:]
    taps_a, _, taps_b = taps_ref.shape
    depth, share = own_ref.shape
    grad, taps = own_ref[...], own_taps_ref[...]
    for ref in payload_refs:
        piece = [ref[n * depth : (n + 1) * depth] for n in range(share // LANES)]
        grad = grad + jnp.concatenate(piece, axis=1).astype(F32)
        parts = ref[ref.shape[0] - 16 :].astype(F32)
        taps = taps + (parts[:8] + (parts[8:] + pltpu.roll(parts[:8], LANES // 2, 1)))
    grad = grad * (1.0 / count)
    taps = taps * (1.0 / (math.sqrt(depth) * count * span))
    lane = iota((8, LANES), 1)
    turned = jnp.zeros((8, LANES), F32)
    for b in range(taps_b):
        turned = jnp.where(lane == b, taps[:, LANES - 1 - b : LANES - b], turned)
    for a in range(taps_a):
        taps_ref[a] = turned[a : a + 1, :taps_b]
    one = beta_one * one_ref[...] + (1.0 - beta_one) * grad
    two = beta_two * two_ref[...] + (1.0 - beta_two) * grad * grad
    one_new_ref[...] = one
    two_new_ref[...] = two
    old = w_ref[...]
    new_ref[...] = old - learn_rate * ((one * (1.0 / bias_one)) / (jnp.sqrt(two * (1.0 / bias_two)) + adam_eps) + decay_rate * old)


def swap(x, axis, shift):
    n = lax.axis_size(axis)
    return lax.ppermute(x, axis, [(i, i ^ shift) for i in range(n)])


def turns(n):
    return list(range(n // 2, n)) + list(range(n // 2 - 1, 0, -1))


def few(axis):
    n = lax.axis_size(axis)
    return n <= 8 and n & (n - 1) == 0


def gathered(x, axis):
    if few(axis):
        order = turns(lax.axis_size(axis))
        shifts = (order[1:] + order[:1])[::-1]
        arrays = [x] + [swap(x, axis, s) for s in shifts]
        return arrays, [(n, slice(None), s, None) for n, s in enumerate([0, *shifts])]
    n = lax.axis_size(axis)
    return [lax.all_gather(x, axis)], [(0, i, None, i) for i in range(n)]


def shards(queries, keys, values, conv_kernel, span_start, out_grad, proj_weight, moment_one, moment_two):
    _, rows, depth = queries.shape
    key_count = keys.shape[1]
    _, taps_a, taps_b = conv_kernel.shape
    span = out_grad.shape[1]
    half = (taps_b - 1) // 2
    step = LANES - 2 * half
    windows = -(-key_count // step)
    rows_up = up_to(rows, 16)
    wide = windows * LANES
    reach = up_to((windows - 1) * step + LANES, 8)
    groups = taps_a // GROUP
    group_count = lax.axis_size("dp")
    share = proj_weight.shape[1]
    columns = share * group_count
    vmem = pltpu.CompilerParams(vmem_limit_bytes=24 * 2**20)
    whole = pl.BlockSpec(memory_space=pltpu.VMEM)
    hbm = pl.BlockSpec(memory_space=pltpu.HBM)
    shape = jax.ShapeDtypeStruct
    stay = lambda x: pltpu.with_memory_space_constraint(x, pltpu.HBM)
    q_hbm = stay(queries)
    taps_hbm = stay(conv_kernel.transpose(1, 0, 2))
    smem = pl.BlockSpec(memory_space=pltpu.SMEM)
    taps_ref = pltpu.SMEM((taps_a, 1, taps_b), F32)
    rows32 = pltpu.VMEM(((windows - 1) * step + LANES + 8, depth), F32)
    band = shape((3 * GROUP * LANES, groups * LANES), BF16)
    sides = pltpu.VMEM((windows * rows_up, GROUP * LANES), BF16)

    def cost(flops):
        return pl.CostEstimate(flops=flops, bytes_accessed=10**6, transcendentals=0)

    proj_bf, band_rows, q32, q16 = pl.pallas_call(
        prepare,
        out_shape=(
            shape(proj_weight.shape, BF16),
            band,
            shape((rows_up + 8, depth), F32),
            shape((GROUP * rows_up, depth), BF16),
        ),
        in_specs=[hbm] * 3,
        out_specs=(whole,) * 4,
        scratch_shapes=[
            taps_ref,
            pltpu.VMEM(proj_weight.shape, F32),
            pltpu.VMEM((rows, depth), BF16),
            pltpu.SemaphoreType.DMA((3,)),
        ],
        compiler_params=vmem,
        cost_estimate=cost(5 * 10**9),
        name="prepare",
    )(taps_hbm, stay(proj_weight), q_hbm)
    w_arrays, w_places = gathered(proj_bf, "dp")
    cores_last = few("tensor") and lax.axis_size("tensor") > 2
    pieces = [stay(out_grad)]
    if cores_last:
        pieces += [swap(out_grad, "tensor", s) for s in range(2, lax.axis_size("tensor"), 2)]
    p, kwin, pack = pl.pallas_call(
        functools.partial(forward, len(pieces), taps_a, half),
        out_shape=(
            shape((span, wide), F32),
            shape((wide, depth), BF16),
            shape((len(pieces) * span, out_grad.shape[2]), BF16),
        ),
        in_specs=[whole] * len(pieces) + [smem] + [whole] * 3,
        out_specs=(whole,) * 3,
        scratch_shapes=[
            rows32,
            sides,
            sides,
            pltpu.VMEM((windows * rows_up, groups * LANES), F32),
        ],
        compiler_params=vmem,
        cost_estimate=cost(5 * 10**9),
        name="attention_forward",
    )(*pieces, span_start, band_rows, q16, keys)
    if cores_last:
        up_arrays = [pack, swap(pack, "tensor", 1)]
        up_places = [
            (c, slice(n * span, (n + 1) * span), 2 * n + c, None) for n in range(len(pieces)) for c in (0, 1)
        ]
    else:
        up_arrays, up_places = gathered(out_grad[0], "tensor")
    xth, xtl, vblk, attended = pl.pallas_call(
        functools.partial(forward_turned, taps_a, half),
        out_shape=(shape((wide, taps_a * span), BF16),) * 2 + (shape((wide, depth), BF16), shape((span, depth), BF16)),
        in_specs=[smem] + [whole] * 4,
        out_specs=(whole,) * 4,
        scratch_shapes=[pltpu.VMEM((wide, depth), BF16), rows32],
        compiler_params=vmem,
        cost_estimate=cost(2 * 10**9),
        name="attention_forward_turned",
    )(span_start, kwin, q32, p, values)

    owners = turns(group_count) if few("dp") else list(range(group_count))
    others = len(owners)
    do, own, own_taps, *payloads = pl.pallas_call(
        functools.partial(backward_scores, up_places, w_places, owners, few("dp")),
        out_shape=(
            shape((span, depth), BF16),
            shape((depth, share), F32),
            shape((8, LANES), F32),
        ) + (shape((depth * (share // LANES) + 16, LANES), BF16),) * others,
        in_specs=[whole] * (len(up_arrays) + len(w_arrays) + 5),
        out_specs=(whole,) * (3 + others),
        scratch_shapes=[
            pltpu.VMEM((span, columns), BF16),
            pltpu.VMEM((depth, columns), F32),
        ],
        compiler_params=vmem,
        cost_estimate=cost(2 * 10**9),
        name="attention_backward_scores",
    )(*up_arrays, *w_arrays, p, vblk, xth, xtl, attended)

    if few("dp"):
        payloads = [swap(payload, "dp", owner) for owner, payload in zip(owners, payloads, strict=True)]
    else:
        sent = lax.all_to_all(jnp.stack(payloads), "dp", 0, 0)
        payloads = [jnp.where(lax.axis_index("dp") == n, jnp.zeros_like(sent[n]), sent[n]) for n in range(group_count)]

    query_grad, key_grad, value_grad = pl.pallas_call(
        functools.partial(backward_inputs, rows, key_count, taps_a, half),
        out_shape=(shape(queries.shape, BF16), shape(keys.shape, BF16), shape(values.shape, BF16)),
        in_specs=[smem] + [whole] * 6,
        out_specs=(whole,) * 3,
        scratch_shapes=[
            pltpu.VMEM((rows_up + 8, wide), F32),
            sides,
            sides,
            pltpu.VMEM((windows * rows_up + 8, groups * LANES), F32),
            pltpu.VMEM((reach, depth), F32),
        ],
        compiler_params=vmem,
        cost_estimate=cost(3 * 10**9),
        name="attention_backward_inputs",
    )(span_start, band_rows, do, p, vblk, q16, kwin)

    proj_new, moment_one_new, moment_two_new, kernel_total = pl.pallas_call(
        functools.partial(update, group_count, span),
        out_shape=(shape(proj_weight.shape, F32),) * 3 + (shape((taps_a, 1, taps_b), F32),),
        in_specs=[whole] * (len(payloads) + 5),
        out_specs=(whole,) * 4,
        compiler_params=vmem,
        name="projection_update",
    )(*payloads, own, own_taps, proj_weight, moment_one, moment_two)
    return (
        query_grad,
        key_grad,
        value_grad,
        kernel_total.transpose(1, 0, 2),
        proj_new,
        moment_one_new,
        moment_two_new,
    )


def solution(mesh):
    heads, rows_of, blocks_of = P("dp", None, "tensor"), P("tensor", None, None), P("tensor", "dp")
    return jax.shard_map(
        shards,
        mesh=mesh,
        in_specs=(heads, heads, heads, rows_of, P("dp"), heads, blocks_of, blocks_of, blocks_of),
        out_specs=(heads, heads, heads, rows_of, blocks_of, blocks_of, blocks_of),
        check_vma=False,
    )
```

time: 29.2 us -> 28.6 us (0.979)
  Pallas kernels: 11.4 us -> 11 us
    pallas_call x1, Pallas kernels: 3.06 us -> 2.59 us  [shards(): pl.pallas_call(functools.partial(forward, len(pieces), taps_a, half), out...]
  transfers between devices with their start and end apart: 10 -> 10, of which waited for: 2 -> 4; matrix products, arithmetic and copies ran while one was open for 0% -> 0% of each run, Pallas kernels for 29% -> 28%
where the time goes in v9:
time: 28.6 us; the launch traced here: 28.4 us
  starting transfers between devices  13.8 us (48%)
  Pallas kernels  11 us (38%)
  waiting for transfers between devices  2.23 us (8%)
  between operations  1.38 us (5%)
    ppermute x10, starting transfers between devices, swap(): return lax.ppermute(x, axis, [(i, i ^ shift) for i in range(n)])  13.8 us
    pallas_call x1, Pallas kernels, shards(): pl.pallas_call(functools.partial(backward_inputs, rows, key_count, taps_a...  3.05 us
    pallas_call x1, Pallas kernels, shards(): pl.pallas_call(functools.partial(forward, len(pieces), taps_a, half), out...  2.59 us
    ppermute x10, waiting for transfers between devices, swap(): return lax.ppermute(x, axis, [(i, i ^ shift) for i in range(n)])  2.23 us
    pallas_call x1, Pallas kernels, shards(): pl.pallas_call(functools.partial(backward_scores, up_places, w_places, ow...  2 us
    pallas_call x1, Pallas kernels, shards(): pl.pallas_call(functools.partial(forward_turned, taps_a, half), out_shape...  1.3 us
    pallas_call x1, Pallas kernels, shards(): pl.pallas_call(prepare, out_shape=(shape(proj_weight.shape, BF16), band,...  1.07 us
    pallas_call x1, Pallas kernels, shards(): pl.pallas_call(functools.partial(update, group_count, span), out_shape=(s...  0.94 us
  transfers between devices with their start and end apart: 10, of which 4 were waited for; matrix products, arithmetic and copies ran while one was open for 0% of the time, Pallas kernels for 28%

profile of v9, /device:TPU:0, one launch (start us, length us, event | category | flops | bytes accessed | tf_op | source)
XLA Modules:
  0.0 28.4 jit_solution(14998989205866368444)
XLA Ops:
  0.6 3.0 %collective-permute-start.1 = (bf16[1,128,128]{2,1,0:T(8,128)(2,1)}, bf16[1,128,128]{2,1,0:T(8,128)(2,1)S(1)}, u32[]{:S(2)}, u32[]{:S(2)}) collective-permute-start(bf16[1,128,128]{2,1,0:T(8,128)(2,1)} %refs_0_.1), channel_id=1, source_target_pairs={{0,4},{1,5},{2,6},{3,7},{4,0},{5,1},{6,2},{7,3},{8,12},{9,13},{10,... | collective-permute-start | bytes 98312 | tf_op jit(solution)/shard_map/ppermute | solution.py:318
  3.7 1.5 %collective-permute-start = (bf16[1,128,128]{2,1,0:T(8,128)(2,1)}, bf16[1,128,128]{2,1,0:T(8,128)(2,1)S(1)}, u32[]{:S(2)}, u32[]{:S(2)}) collective-permute-start(bf16[1,128,128]{2,1,0:T(8,128)(2,1)} %refs_0_.1), channel_id=1, source_target_pairs={{0,2},{1,3},{2,0},{3,1},{4,6},{5,7},{6,4},{7,5},{8,10},{9,11},{10,... | collective-permute-start | bytes 98312 | tf_op jit(solution)/shard_map/ppermute | solution.py:318
  5.2 0.1 collective-permute-start.2
  5.2 0.0 copy-start.3
  5.2 1.1 %prepare.1 = (bf16[128,256]{1,0:T(8,128)(2,1)S(1)}, bf16[768,384]{1,0:T(8,128)(2,1)S(1)}, f32[152,128]{1,0:T(8,128)S(1)}, bf16[288,128]{1,0:T(8,128)(2,1)S(1)}) custom-call(f32[6,1,11]{2,1,0:T(1,128)} %bitcast.2, f32[128,256]{1,0:T(8,128)} %refs_5_.1, bf16[1,133,128]{2,1,0:T(8,128)(2,1)} %q_hbm.1), custom_call_target="tpu_custom_call" | custom-call | flops 5000000000 | bytes 1000000 | tf_op jit(solution)/shard_map/prepare/pallas_call | solution.py:371
  6.3 4.1 %collective-permute-start.6 = (bf16[128,256]{1,0:T(8,128)(2,1)S(1)}, bf16[128,256]{1,0:T(8,128)(2,1)S(1)}, u32[]{:S(2)}, u32[]{:S(2)}) collective-permute-start(bf16[128,256]{1,0:T(8,128)(2,1)S(1)} %get-tuple-element.34.refs_2_), channel_id=1, source_target_pairs={{0,24},{8,16},{16,8},{24,0},{1,25},{9,17},{17,9},{25,1},{2,26},{10... | collective-permute-start | bytes 196616 | tf_op jit(solution)/shard_map/ppermute | solution.py:318
  10.4 0.0 collective-permute-start.5
  11.0 0.0 collective-permute-done.1.refs_2_
  11.0 0.7 %collective-permute-start.4 = (bf16[128,256]{1,0:T(8,128)(2,1)S(1)}, bf16[128,256]{1,0:T(8,128)(2,1)S(1)}, u32[]{:S(2)}, u32[]{:S(2)}) collective-permute-start(bf16[128,256]{1,0:T(8,128)(2,1)S(1)} %get-tuple-element.34.refs_2_), channel_id=1, source_target_pairs={{0,16},{8,24},{16,0},{24,8},{1,17},{9,25},{17,1},{25,9},{2,18},{10... | collective-permute-start | bytes 196616 | tf_op jit(solution)/shard_map/ppermute | solution.py:318
  11.8 0.0 collective-permute-done.refs_1_
  11.8 0.0 collective-permute-done.2.refs_3_
  11.8 0.0 copy-done.3
  11.8 0.0 copy-start.4
  11.8 2.6 %attention_forward.1 = (f32[128,1152]{1,0:T(8,128)S(1)}, bf16[1152,128]{1,0:T(8,128)(2,1)S(1)}, bf16[512,128]{1,0:T(8,128)(2,1)S(1)}) custom-call(bf16[1,128,128]{2,1,0:T(8,128)(2,1)} %refs_0_.1, bf16[1,128,128]{2,1,0:T(8,128)(2,1)S(1)} %collective-permute-done.refs_1_, bf16[1,128,128]{2,1,0:T(8,128)(2,1)S(1)} %collective-permute-done.1.refs_2_, ...), custom_call_target="tpu_custom_call" | custom-call | flops 5000000000 | bytes 1000000 | tf_op jit(solution)/shard_map/attention_forward/pallas_call | solution.py:396
  14.4 0.1 collective-permute-start.3
  14.5 0.0 copy-done.4
  14.5 1.3 %attention_forward_turned.1 = (bf16[1152,768]{1,0:T(8,128)(2,1)S(1)}, bf16[1152,768]{1,0:T(8,128)(2,1)S(1)}, bf16[1152,128]{1,0:T(8,128)(2,1)S(1)}, bf16[128,128]{1,0:T(8,128)(2,1)S(1)}) custom-call(s32[1]{0:T(128)S(6)} %copy.16.refs_4_.first_ref, bf16[1152,128]{1,0:T(8,128)(2,1)S(1)} %get-tuple-element.36.kwin, f32[152,128]{1,0:T(8,128)S(1)} %get-tuple-element.37.q32, ...), custom_call_target="tpu_custom_call" | custom-call | flops 2000000000 | bytes 1000000 | tf_op jit(solution)/shard_map/attention_forward_turned/pallas_call | solution.py:422
  15.8 0.0 collective-permute-done.6.refs_5_
  15.8 0.0 collective-permute-done.5.refs_4_
  15.8 0.5 %collective-permute-done.4.refs_3_ = bf16[128,256]{1,0:T(8,128)(2,1)S(1)} collective-permute-done((bf16[128,256]{1,0:T(8,128)(2,1)S(1)}, bf16[128,256]{1,0:T(8,128)(2,1)S(1)}, u32[]{:S(2)}, u32[]{:S(2)}) %collective-permute-start.4) | collective-permute-done | bytes 65568 | tf_op jit(solution)/shard_map/ppermute | solution.py:318
  16.3 0.0 collective-permute-done.3.refs_1_
  16.3 2.0 %attention_backward_scores.1 = (bf16[128,128]{1,0:T(8,128)(2,1)S(1)}, f32[128,256]{1,0:T(8,128)S(1)}, f32[8,128]{1,0:T(8,128)S(1)}, bf16[272,128]{1,0:T(8,128)(2...) custom-call(bf16[512,128]{1,0:T(8,128)(2,1)S(1)} %get-tuple-element.33.refs_0_, ...), custom_call_target="tpu_custom_call" | custom-call | flops 2000000000 | bytes 1000000 | tf_op jit(solution)/shard_map/attention_backward_scores/pallas_call | solution.py:435
  18.3 1.8 %collective-permute-start.7 = (bf16[272,128]{1,0:T(8,128)(2,1)S(1)}, bf16[272,128]{1,0:T(8,128)(2,1)S(1)}, u32[]{:S(2)}, u32[]{:S(2)}) collective-permute-start(bf16[272,128]{1,0:T(8,128)(2,1)S(1)} %get-tuple-element.46), channel_id=1, source_target_pairs={{0,16},{8,24},{16,0},{24,8},{1,17},{9,25},{17,1},{25,9},{2,18},{10... | collective-permute-start | bytes 208904 | tf_op jit(solution)/shard_map/ppermute | solution.py:318
  20.1 2.6 %collective-permute-start.8 = (bf16[272,128]{1,0:T(8,128)(2,1)S(1)}, bf16[272,128]{1,0:T(8,128)(2,1)S(1)}, u32[]{:S(2)}, u32[]{:S(2)}) collective-permute-start(bf16[272,128]{1,0:T(8,128)(2,1)S(1)} %get-tuple-element.47), channel_id=1, source_target_pairs={{0,24},{8,16},{16,8},{24,0},{1,25},{9,17},{17,9},{25,1},{2,26},{10... | collective-permute-start | bytes 208904 | tf_op jit(solution)/shard_map/ppermute | solution.py:318
  22.7 0.0 collective-permute-start.9
  22.7 0.0 copy-start
  22.7 0.0 copy-start.1
  22.7 0.0 copy-start.2
  22.7 3.0 %attention_backward_inputs.1 = (bf16[1,133,128]{2,1,0:T(8,128)(2,1)}, bf16[1,1024,128]{2,1,0:T(8,128)(2,1)}, bf16[1,1024,128]{2,1,0:T(8,128)(2,1)}) custom-call(s32[1]{0:T(128)S(6)} %copy.16.refs_4_.first_ref, bf16[768,384]{1,0:T(8,128)(2,1)S(1)} %get-tuple-element.31.refs_5_.bands_ref, bf16[128,128]{1,0:T(8,128)(2,1)S(1)} %get-tuple-element.42.do_ref, ...), custom_call_target="tpu_custom_call" | custom-call | flops 3000000000 | bytes 1000000 | tf_op jit(solution)/shard_map/attention_backward_inputs/pallas_call | solution.py:459
  25.7 0.3 %collective-permute-done.7.refs_0_ = bf16[272,128]{1,0:T(8,128)(2,1)S(1)} collective-permute-done((bf16[272,128]{1,0:T(8,128)(2,1)S(1)}, bf16[272,128]{1,0:T(8,128)(2,1)S(1)}, u32[]{:S(2)}, u32[]{:S(2)}) %collective-permute-start.7) | collective-permute-done | bytes 69664 | tf_op jit(solution)/shard_map/ppermute | solution.py:318
  26.1 0.9 %collective-permute-done.8.refs_1_ = bf16[272,128]{1,0:T(8,128)(2,1)S(1)} collective-permute-done((bf16[272,128]{1,0:T(8,128)(2,1)S(1)}, bf16[272,128]{1,0:T(8,128)(2,1)S(1)}, u32[]{:S(2)}, u32[]{:S(2)}) %collective-permute-start.8) | collective-permute-done | bytes 69664 | tf_op jit(solution)/shard_map/ppermute | solution.py:318
  26.9 0.5 %collective-permute-done.9.refs_2_ = bf16[272,128]{1,0:T(8,128)(2,1)S(1)} collective-permute-done((bf16[272,128]{1,0:T(8,128)(2,1)S(1)}, bf16[272,128]{1,0:T(8,128)(2,1)S(1)}, u32[]{:S(2)}, u32[]{:S(2)}) %collective-permute-start.9) | collective-permute-done | bytes 69664 | tf_op jit(solution)/shard_map/ppermute | solution.py:318
  27.5 0.0 copy-done
  27.5 0.0 copy-done.1
  27.5 0.0 copy-done.2
  27.5 0.9 %projection_update.1 = (f32[128,256]{1,0:T(8,128)}, f32[128,256]{1,0:T(8,128)}, f32[128,256]{1,0:T(8,128)}, f32[6,1,11]{2,1,0:T(1,128)}) custom-call(bf16[272,128]{1,0:T(8,128)(2,1)S(1)} %collective-permute-done.7.refs_0_, bf16[272,128]{1,0:T(8,128)(2,1)S(1)} %collective-permute-done.8.refs_1_, bf16[272,128]{1,0:T(8,128)(2,1)S(1)} %collective-permute-done.9.refs_2_, ...), custom_call_target="tpu_custom_call" | custom-call | tf_op jit(solution)/shard_map/projection_update/pallas_call | solution.py:476
Async XLA Ops:
  0.6 10.4 %collective-permute-start.1 = (bf16[1,128,128]{2,1,0:T(8,128)(2,1)}, bf16[1,128,128]{2,1,0:T(8,128)(2,1)S(1)}, u32[]{:S(2)}, u32[]{:S(2)}) collective-permute-start(bf16[1,128,128]{2,1,0:T(8,128)(2,1)} %refs_0_.1), channel_id=1, source_target_pairs={{0,4},{1,5},{2,6},{3,7},{4,0},{5,1},{6,2},{7,3},{8,12},{9,13},{10,... | collective-permute-start | bytes 98312 | tf_op jit(solution)/shard_map/ppermute | solution.py:318
  3.7 8.1 %collective-permute-start = (bf16[1,128,128]{2,1,0:T(8,128)(2,1)}, bf16[1,128,128]{2,1,0:T(8,128)(2,1)S(1)}, u32[]{:S(2)}, u32[]{:S(2)}) collective-permute-start(bf16[1,128,128]{2,1,0:T(8,128)(2,1)} %refs_0_.1), channel_id=1, source_target_pairs={{0,2},{1,3},{2,0},{3,1},{4,6},{5,7},{6,4},{7,5},{8,10},{9,11},{10,... | collective-permute-start | bytes 98312 | tf_op jit(solution)/shard_map/ppermute | solution.py:318
  5.2 6.6 %collective-permute-start.2 = (bf16[1,128,128]{2,1,0:T(8,128)(2,1)}, bf16[1,128,128]{2,1,0:T(8,128)(2,1)S(1)}, u32[]{:S(2)}, u32[]{:S(2)}) collective-permute-start(bf16[1,128,128]{2,1,0:T(8,128)(2,1)} %refs_0_.1), channel_id=1, source_target_pairs={{0,6},{1,7},{2,4},{3,5},{4,2},{5,3},{6,0},{7,1},{8,14},{9,15},{10,... | collective-permute-start | bytes 98312 | tf_op jit(solution)/shard_map/ppermute | solution.py:318
  5.2 6.6 %copy-start.3 = (bf16[1,1024,128]{2,1,0:T(8,128)(2,1)S(1)}, bf16[1,1024,128]{2,1,0:T(8,128)(2,1)}, u32[]{:S(2)}) copy-start(bf16[1,1024,128]{2,1,0:T(8,128)(2,1)} %refs_7_.2) | copy-start | bytes 786436
  6.3 9.5 %collective-permute-start.6 = (bf16[128,256]{1,0:T(8,128)(2,1)S(1)}, bf16[128,256]{1,0:T(8,128)(2,1)S(1)}, u32[]{:S(2)}, u32[]{:S(2)}) collective-permute-start(bf16[128,256]{1,0:T(8,128)(2,1)S(1)} %get-tuple-element.34.refs_2_), channel_id=1, source_target_pairs={{0,24},{8,16},{16,8},{24,0},{1,25},{9,17},{17,9},{25,1},{2,26},{10... | collective-permute-start | bytes 196616 | tf_op jit(solution)/shard_map/ppermute | solution.py:318
  10.4 5.4 %collective-permute-start.5 = (bf16[128,256]{1,0:T(8,128)(2,1)S(1)}, bf16[128,256]{1,0:T(8,128)(2,1)S(1)}, u32[]{:S(2)}, u32[]{:S(2)}) collective-permute-start(bf16[128,256]{1,0:T(8,128)(2,1)S(1)} %get-tuple-element.34.refs_2_), channel_id=1, source_target_pairs={{0,8},{8,0},{16,24},{24,16},{1,9},{9,1},{17,25},{25,17},{2,10},{10... | collective-permute-start | bytes 196616 | tf_op jit(solution)/shard_map/ppermute | solution.py:318
  11.0 5.2 %collective-permute-start.4 = (bf16[128,256]{1,0:T(8,128)(2,1)S(1)}, bf16[128,256]{1,0:T(8,128)(2,1)S(1)}, u32[]{:S(2)}, u32[]{:S(2)}) collective-permute-start(bf16[128,256]{1,0:T(8,128)(2,1)S(1)} %get-tuple-element.34.refs_2_), channel_id=1, source_target_pairs={{0,16},{8,24},{16,0},{24,8},{1,17},{9,25},{17,1},{25,9},{2,18},{10... | collective-permute-start | bytes 196616 | tf_op jit(solution)/shard_map/ppermute | solution.py:318
  11.8 2.7 %copy-start.4 = (bf16[1,1024,128]{2,1,0:T(8,128)(2,1)S(1)}, bf16[1,1024,128]{2,1,0:T(8,128)(2,1)}, u32[]{:S(2)}) copy-start(bf16[1,1024,128]{2,1,0:T(8,128)(2,1)} %v_ref.1) | copy-start | bytes 786436
  14.4 1.9 %collective-permute-start.3 = (bf16[512,128]{1,0:T(8,128)(2,1)S(1)}, bf16[512,128]{1,0:T(8,128)(2,1)S(1)}, u32[]{:S(2)}, u32[]{:S(2)}) collective-permute-start(bf16[512,128]{1,0:T(8,128)(2,1)S(1)} %get-tuple-element.33.refs_0_), channel_id=1, source_target_pairs={{0,1},{1,0},{2,3},{3,2},{4,5},{5,4},{6,7},{7,6},{8,9},{9,8},{10,11... | collective-permute-start | bytes 393224 | tf_op jit(solution)/shard_map/ppermute | solution.py:318
  18.3 7.8 %collective-permute-start.7 = (bf16[272,128]{1,0:T(8,128)(2,1)S(1)}, bf16[272,128]{1,0:T(8,128)(2,1)S(1)}, u32[]{:S(2)}, u32[]{:S(2)}) collective-permute-start(bf16[272,128]{1,0:T(8,128)(2,1)S(1)} %get-tuple-element.46), channel_id=1, source_target_pairs={{0,16},{8,24},{16,0},{24,8},{1,17},{9,25},{17,1},{25,9},{2,18},{10... | collective-permute-start | bytes 208904 | tf_op jit(solution)/shard_map/ppermute | solution.py:318
  20.1 6.8 %collective-permute-start.8 = (bf16[272,128]{1,0:T(8,128)(2,1)S(1)}, bf16[272,128]{1,0:T(8,128)(2,1)S(1)}, u32[]{:S(2)}, u32[]{:S(2)}) collective-permute-start(bf16[272,128]{1,0:T(8,128)(2,1)S(1)} %get-tuple-element.47), channel_id=1, source_target_pairs={{0,24},{8,16},{16,8},{24,0},{1,25},{9,17},{17,9},{25,1},{2,26},{10... | collective-permute-start | bytes 208904 | tf_op jit(solution)/shard_map/ppermute | solution.py:318
  22.7 4.8 %collective-permute-start.9 = (bf16[272,128]{1,0:T(8,128)(2,1)S(1)}, bf16[272,128]{1,0:T(8,128)(2,1)S(1)}, u32[]{:S(2)}, u32[]{:S(2)}) collective-permute-start(bf16[272,128]{1,0:T(8,128)(2,1)S(1)} %get-tuple-element.48), channel_id=1, source_target_pairs={{0,8},{8,0},{16,24},{24,16},{1,9},{9,1},{17,25},{25,17},{2,10},{10... | collective-permute-start | bytes 208904 | tf_op jit(solution)/shard_map/ppermute | solution.py:318
  22.7 4.8 %copy-start = (f32[128,256]{1,0:T(8,128)S(1)}, f32[128,256]{1,0:T(8,128)}, u32[]{:S(2)}) copy-start(f32[128,256]{1,0:T(8,128)} %refs_5_.1) | copy-start | bytes 393220
  22.7 4.8 %copy-start.1 = (f32[128,256]{1,0:T(8,128)S(1)}, f32[128,256]{1,0:T(8,128)}, u32[]{:S(2)}) copy-start(f32[128,256]{1,0:T(8,128)} %refs_6_.1) | copy-start | bytes 393220
  22.7 4.8 %copy-start.2 = (f32[128,256]{1,0:T(8,128)S(1)}, f32[128,256]{1,0:T(8,128)}, u32[]{:S(2)}) copy-start(f32[128,256]{1,0:T(8,128)} %refs_7_.3) | copy-start | bytes 393220

commit v10 on v9

--- a/solution.py
+++ b/solution.py
@@ -74,12 +74,12 @@
 
 
 def prepare(
-    taps_hbm, w_hbm, q_hbm,
-    w_ref, bands_ref, q32, q16,
+    taps_hbm, w_hbm, q_hbm, grad_hbm,
+    w_ref, bands_ref, q32, q16, grad_ref,
     taps_ref, w_in, q_in, sems,
 ):
     rows = q_in.shape[0]
-    copies = fetch(((taps_hbm, taps_ref), (w_hbm, w_in), (q_hbm.at[0], q_in)), sems)
+    copies = fetch(((taps_hbm, taps_ref), (w_hbm, w_in), (q_hbm.at[0], q_in), (grad_hbm, grad_ref)), sems)
     q32[...] = jnp.zeros_like(q32)
     copies[0].wait()
     hold_bands(taps_ref, 1.0 / math.sqrt(q_in.shape[1]), bands_ref)
@@ -90,6 +90,7 @@
     rows_up = q16.shape[0] // GROUP
     for n in range(GROUP):
         q16[n * rows_up : (n + 1) * rows_up] = q32[n : n + rows_up].astype(BF16)
+    copies[3].wait()
 
 
 def by_blocks(rows_ref, out, rows32, start, live):
@@ -329,8 +330,7 @@
 
 def gathered(x, axis):
     if few(axis):
-        order = turns(lax.axis_size(axis))
-        shifts = (order[1:] + order[:1])[::-1]
+        shifts = turns(lax.axis_size(axis))[::-1]
         arrays = [x] + [swap(x, axis, s) for s in shifts]
         return arrays, [(n, slice(None), s, None) for n, s in enumerate([0, *shifts])]
     n = lax.axis_size(axis)
@@ -368,29 +368,30 @@
     def cost(flops):
         return pl.CostEstimate(flops=flops, bytes_accessed=10**6, transcendentals=0)
 
-    proj_bf, band_rows, q32, q16 = pl.pallas_call(
+    proj_bf, band_rows, q32, q16, local_grad = pl.pallas_call(
         prepare,
         out_shape=(
             shape(proj_weight.shape, BF16),
             band,
             shape((rows_up + 8, depth), F32),
             shape((GROUP * rows_up, depth), BF16),
+            shape(out_grad.shape, BF16),
         ),
-        in_specs=[hbm] * 3,
-        out_specs=(whole,) * 4,
+        in_specs=[hbm] * 4,
+        out_specs=(whole,) * 5,
         scratch_shapes=[
             taps_ref,
             pltpu.VMEM(proj_weight.shape, F32),
             pltpu.VMEM((rows, depth), BF16),
-            pltpu.SemaphoreType.DMA((3,)),
+            pltpu.SemaphoreType.DMA((4,)),
         ],
         compiler_params=vmem,
         cost_estimate=cost(5 * 10**9),
         name="prepare",
-    )(taps_hbm, stay(proj_weight), q_hbm)
+    )(taps_hbm, stay(proj_weight), q_hbm, stay(out_grad))
     w_arrays, w_places = gathered(proj_bf, "dp")
     cores_last = few("tensor") and lax.axis_size("tensor") > 2
-    pieces = [stay(out_grad)]
+    pieces = [local_grad]
     if cores_last:
         pieces += [swap(out_grad, "tensor", s) for s in range(2, lax.axis_size("tensor"), 2)]
     p, kwin, pack = pl.pallas_call(
@@ -430,7 +431,9 @@
         name="attention_forward_turned",
     )(span_start, kwin, q32, p, values)
 
-    owners = turns(group_count) if few("dp") else list(range(group_count))
+    owners = list(range(group_count))
+    if few("dp"):
+        owners = owners[group_count // 2 : 0 : -1] + owners[group_count // 2 + 1 :]
     others = len(owners)
     do, own, own_taps, *payloads = pl.pallas_call(
         functools.partial(backward_scores, up_places, w_places, owners, few("dp")),

time: 28.6 us -> 28.1 us (0.983)
  Pallas kernels: 11 us -> 10.2 us
  waiting for transfers between devices: 2.23 us -> 2.67 us
    pallas_call x1, Pallas kernels: 2.59 us -> 1.79 us  [shards(): pl.pallas_call(functools.partial(forward, len(pieces), taps_a, half), out...]
    ppermute x10, waiting for transfers between devices: 2.23 us -> 2.67 us  [swap(): return lax.ppermute(x, axis, [(i, i ^ shift) for i in range(n)])]
  transfers between devices with their start and end apart: 10 -> 10, of which waited for: 4 -> 3; matrix products, arithmetic and copies ran while one was open for 0% -> 0% of each run, Pallas kernels for 28% -> 26%
where the time goes in v10:
time: 28.1 us; the launch traced here: 28 us
  starting transfers between devices  13.8 us (49%)
  Pallas kernels  10.2 us (36%)
  waiting for transfers between devices  2.67 us (10%)
  between operations  1.37 us (5%)
    ppermute x10, starting transfers between devices, swap(): return lax.ppermute(x, axis, [(i, i ^ shift) for i in range(n)])  13.8 us
    pallas_call x1, Pallas kernels, shards(): pl.pallas_call(functools.partial(backward_inputs, rows, key_count, taps_a...  3.05 us
    ppermute x10, waiting for transfers between devices, swap(): return lax.ppermute(x, axis, [(i, i ^ shift) for i in range(n)])  2.67 us
    pallas_call x1, Pallas kernels, shards(): pl.pallas_call(functools.partial(backward_scores, up_places, w_places, ow...  2 us
    pallas_call x1, Pallas kernels, shards(): pl.pallas_call(functools.partial(forward, len(pieces), taps_a, half), out...  1.79 us
    pallas_call x1, Pallas kernels, shards(): pl.pallas_call(functools.partial(forward_turned, taps_a, half), out_shape...  1.3 us
    pallas_call x1, Pallas kernels, shards(): pl.pallas_call(prepare, out_shape=(shape(proj_weight.shape, BF16), band,...  1.08 us
    pallas_call x1, Pallas kernels, shards(): pl.pallas_call(functools.partial(update, group_count, span), out_shape=(s...  0.94 us
  transfers between devices with their start and end apart: 10, of which 3 were waited for; matrix products, arithmetic and copies ran while one was open for 0% of the time, Pallas kernels for 26%

profile of v10, /device:TPU:0, one launch (start us, length us, event | category | flops | bytes accessed | tf_op | source)
XLA Modules:
  0.0 28.0 jit_solution(11416624951905169831)
XLA Ops:
  0.6 3.0 %collective-permute-start = (bf16[1,128,128]{2,1,0:T(8,128)(2,1)}, bf16[1,128,128]{2,1,0:T(8,128)(2,1)S(1)}, u32[]{:S(2)}, u32[]{:S(2)}) collective-permute-start(bf16[1,128,128]{2,1,0:T(8,128)(2,1)} %grad_hbm.1), channel_id=1, source_target_pairs={{0,2},{1,3},{2,0},{3,1},{4,6},{5,7},{6,4},{7,5},{8,10},{9,11},{10,... | collective-permute-start | bytes 98312 | tf_op jit(solution)/shard_map/ppermute | solution.py:319
  3.6 1.5 %collective-permute-start.2 = (bf16[1,128,128]{2,1,0:T(8,128)(2,1)}, bf16[1,128,128]{2,1,0:T(8,128)(2,1)S(1)}, u32[]{:S(2)}, u32[]{:S(2)}) collective-permute-start(bf16[1,128,128]{2,1,0:T(8,128)(2,1)} %grad_hbm.1), channel_id=1, source_target_pairs={{0,6},{1,7},{2,4},{3,5},{4,2},{5,3},{6,0},{7,1},{8,14},{9,15},{10,... | collective-permute-start | bytes 98312 | tf_op jit(solution)/shard_map/ppermute | solution.py:319
  5.1 0.0 collective-permute-start.1
  5.2 0.0 copy-start.3
  5.2 1.1 %prepare.1 = (bf16[128,256]{1,0:T(8,128)(2,1)S(1)}, bf16[768,384]{1,0:T(8,128)(2,1)S(1)}, f32[152,128]{1,0:T(8,128)S(1)}, bf16[288,128]{1,0:T(8,128)(2,1)S(1)}, bf16[1,128,128]{2,1,0:T(8,128)(2,1)S(1)}) custom-call(f32[6,1,11]{2,1,0:T(1,128)} %bitcast.2, f32[128,256]{1,0:T(8,128)} %refs_5_.1, bf16[1,133,128]{2,1,0:T(8,128)(2,1)} %q_hbm.1, ...), custom_call_target="tpu_custom_call" | custom-call | flops 5000000000 | bytes 1000000 | tf_op jit(solution)/shard_map/prepare/pallas_call | solution.py:371
  6.3 3.1 %collective-permute-start.6 = (bf16[128,256]{1,0:T(8,128)(2,1)S(1)}, bf16[128,256]{1,0:T(8,128)(2,1)S(1)}, u32[]{:S(2)}, u32[]{:S(2)}) collective-permute-start(bf16[128,256]{1,0:T(8,128)(2,1)S(1)} %get-tuple-element.36.refs_2_), channel_id=1, source_target_pairs={{0,16},{8,24},{16,0},{24,8},{1,17},{9,25},{17,1},{25,9},{2,18},{10... | collective-permute-start | bytes 196616 | tf_op jit(solution)/shard_map/ppermute | solution.py:319
  9.4 1.3 %collective-permute-start.5 = (bf16[128,256]{1,0:T(8,128)(2,1)S(1)}, bf16[128,256]{1,0:T(8,128)(2,1)S(1)}, u32[]{:S(2)}, u32[]{:S(2)}) collective-permute-start(bf16[128,256]{1,0:T(8,128)(2,1)S(1)} %get-tuple-element.36.refs_2_), channel_id=1, source_target_pairs={{0,24},{8,16},{16,8},{24,0},{1,25},{9,17},{17,9},{25,1},{2,26},{10... | collective-permute-start | bytes 196616 | tf_op jit(solution)/shard_map/ppermute | solution.py:319
  11.4 0.0 collective-permute-done.refs_1_
  11.4 0.3 %collective-permute-start.4 = (bf16[128,256]{1,0:T(8,128)(2,1)S(1)}, bf16[128,256]{1,0:T(8,128)(2,1)S(1)}, u32[]{:S(2)}, u32[]{:S(2)}) collective-permute-start(bf16[128,256]{1,0:T(8,128)(2,1)S(1)} %get-tuple-element.36.refs_2_), channel_id=1, source_target_pairs={{0,8},{8,0},{16,24},{24,16},{1,9},{9,1},{17,25},{25,17},{2,10},{10... | collective-permute-start | bytes 196616 | tf_op jit(solution)/shard_map/ppermute | solution.py:319
  11.7 0.0 collective-permute-done.2.refs_3_
  11.7 0.0 collective-permute-done.1.refs_2_
  11.7 0.0 copy-done.3
  11.7 0.0 copy-start.4
  11.7 1.8 %attention_forward.1 = (f32[128,1152]{1,0:T(8,128)S(1)}, bf16[1152,128]{1,0:T(8,128)(2,1)S(1)}, bf16[512,128]{1,0:T(8,128)(2,1)S(1)}) custom-call(bf16[1,128,128]{2,1,0:T(8,128)(2,1)S(1)} %get-tuple-element.33.refs_0_, bf16[1,128,128]{2,1,0:T(8,128)(2,1)S(1)} %collective-permute-done.refs_1_, bf16[1,128,128]{2,1,0:T(8,128)(2,1)S(1)} %collective-permute-done.1.refs_2_, ...), custom_call_target="tpu_custom_call" | custom-call | flops 5000000000 | bytes 1000000 | tf_op jit(solution)/shard_map/attention_forward/pallas_call | solution.py:397
  13.5 0.1 collective-permute-start.3
  13.6 0.0 copy-done.4
  13.6 1.3 %attention_forward_turned.1 = (bf16[1152,768]{1,0:T(8,128)(2,1)S(1)}, bf16[1152,768]{1,0:T(8,128)(2,1)S(1)}, bf16[1152,128]{1,0:T(8,128)(2,1)S(1)}, bf16[128,128]{1,0:T(8,128)(2,1)S(1)}) custom-call(s32[1]{0:T(128)S(6)} %copy.16.refs_4_.first_ref, bf16[1152,128]{1,0:T(8,128)(2,1)S(1)} %get-tuple-element.38.kwin, f32[152,128]{1,0:T(8,128)S(1)} %get-tuple-element.39.q32, ...), custom_call_target="tpu_custom_call" | custom-call | flops 2000000000 | bytes 1000000 | tf_op jit(solution)/shard_map/attention_forward_turned/pallas_call | solution.py:423
  14.9 0.0 collective-permute-done.6.refs_5_
  14.9 0.6 %collective-permute-done.5.refs_4_ = bf16[128,256]{1,0:T(8,128)(2,1)S(1)} collective-permute-done((bf16[128,256]{1,0:T(8,128)(2,1)S(1)}, bf16[128,256]{1,0:T(8,128)(2,1)S(1)}, u32[]{:S(2)}, u32[]{:S(2)}) %collective-permute-start.5) | collective-permute-done | bytes 65568 | tf_op jit(solution)/shard_map/ppermute | solution.py:319
  15.5 0.7 %collective-permute-done.4.refs_3_ = bf16[128,256]{1,0:T(8,128)(2,1)S(1)} collective-permute-done((bf16[128,256]{1,0:T(8,128)(2,1)S(1)}, bf16[128,256]{1,0:T(8,128)(2,1)S(1)}, u32[]{:S(2)}, u32[]{:S(2)}) %collective-permute-start.4) | collective-permute-done | bytes 65568 | tf_op jit(solution)/shard_map/ppermute | solution.py:319
  16.1 0.0 collective-permute-done.3.refs_1_
  16.2 2.0 %attention_backward_scores.1 = (bf16[128,128]{1,0:T(8,128)(2,1)S(1)}, f32[128,256]{1,0:T(8,128)S(1)}, f32[8,128]{1,0:T(8,128)S(1)}, bf16[272,128]{1,0:T(8,128)(2...) custom-call(bf16[512,128]{1,0:T(8,128)(2,1)S(1)} %get-tuple-element.35.refs_0_, ...), custom_call_target="tpu_custom_call" | custom-call | flops 2000000000 | bytes 1000000 | tf_op jit(solution)/shard_map/attention_backward_scores/pallas_call | solution.py:438
  18.1 1.6 %collective-permute-start.7 = (bf16[272,128]{1,0:T(8,128)(2,1)S(1)}, bf16[272,128]{1,0:T(8,128)(2,1)S(1)}, u32[]{:S(2)}, u32[]{:S(2)}) collective-permute-start(bf16[272,128]{1,0:T(8,128)(2,1)S(1)} %get-tuple-element.48), channel_id=1, source_target_pairs={{0,16},{8,24},{16,0},{24,8},{1,17},{9,25},{17,1},{25,9},{2,18},{10... | collective-permute-start | bytes 208904 | tf_op jit(solution)/shard_map/ppermute | solution.py:319
  19.8 1.1 %collective-permute-start.8 = (bf16[272,128]{1,0:T(8,128)(2,1)S(1)}, bf16[272,128]{1,0:T(8,128)(2,1)S(1)}, u32[]{:S(2)}, u32[]{:S(2)}) collective-permute-start(bf16[272,128]{1,0:T(8,128)(2,1)S(1)} %get-tuple-element.49), channel_id=1, source_target_pairs={{0,8},{8,0},{16,24},{24,16},{1,9},{9,1},{17,25},{25,17},{2,10},{10... | collective-permute-start | bytes 208904 | tf_op jit(solution)/shard_map/ppermute | solution.py:319
  20.9 1.7 %collective-permute-start.9 = (bf16[272,128]{1,0:T(8,128)(2,1)S(1)}, bf16[272,128]{1,0:T(8,128)(2,1)S(1)}, u32[]{:S(2)}, u32[]{:S(2)}) collective-permute-start(bf16[272,128]{1,0:T(8,128)(2,1)S(1)} %get-tuple-element.50), channel_id=1, source_target_pairs={{0,24},{8,16},{16,8},{24,0},{1,25},{9,17},{17,9},{25,1},{2,26},{10... | collective-permute-start | bytes 208904 | tf_op jit(solution)/shard_map/ppermute | solution.py:319
  22.5 0.0 copy-start
  22.5 0.0 copy-start.1
  22.5 0.0 copy-start.2
  22.5 3.1 %attention_backward_inputs.1 = (bf16[1,133,128]{2,1,0:T(8,128)(2,1)}, bf16[1,1024,128]{2,1,0:T(8,128)(2,1)}, bf16[1,1024,128]{2,1,0:T(8,128)(2,1)}) custom-call(s32[1]{0:T(128)S(6)} %copy.16.refs_4_.first_ref, bf16[768,384]{1,0:T(8,128)(2,1)S(1)} %get-tuple-element.32.refs_5_.bands_ref, bf16[128,128]{1,0:T(8,128)(2,1)S(1)} %get-tuple-element.44.do_ref, ...), custom_call_target="tpu_custom_call" | custom-call | flops 3000000000 | bytes 1000000 | tf_op jit(solution)/shard_map/attention_backward_inputs/pallas_call | solution.py:462
  25.6 0.0 collective-permute-done.7.refs_0_
  25.6 0.0 collective-permute-done.8.refs_1_
  25.6 1.4 %collective-permute-done.9.refs_2_ = bf16[272,128]{1,0:T(8,128)(2,1)S(1)} collective-permute-done((bf16[272,128]{1,0:T(8,128)(2,1)S(1)}, bf16[272,128]{1,0:T(8,128)(2,1)S(1)}, u32[]{:S(2)}, u32[]{:S(2)}) %collective-permute-start.9) | collective-permute-done | bytes 69664 | tf_op jit(solution)/shard_map/ppermute | solution.py:319
  27.0 0.0 copy-done
  27.0 0.0 copy-done.1
  27.0 0.0 copy-done.2
  27.0 0.9 %projection_update.1 = (f32[128,256]{1,0:T(8,128)}, f32[128,256]{1,0:T(8,128)}, f32[128,256]{1,0:T(8,128)}, f32[6,1,11]{2,1,0:T(1,128)}) custom-call(bf16[272,128]{1,0:T(8,128)(2,1)S(1)} %collective-permute-done.7.refs_0_, bf16[272,128]{1,0:T(8,128)(2,1)S(1)} %collective-permute-done.8.refs_1_, bf16[272,128]{1,0:T(8,128)(2,1)S(1)} %collective-permute-done.9.refs_2_, ...), custom_call_target="tpu_custom_call" | custom-call | tf_op jit(solution)/shard_map/projection_update/pallas_call | solution.py:479
Async XLA Ops:
  0.6 10.8 %collective-permute-start = (bf16[1,128,128]{2,1,0:T(8,128)(2,1)}, bf16[1,128,128]{2,1,0:T(8,128)(2,1)S(1)}, u32[]{:S(2)}, u32[]{:S(2)}) collective-permute-start(bf16[1,128,128]{2,1,0:T(8,128)(2,1)} %grad_hbm.1), channel_id=1, source_target_pairs={{0,2},{1,3},{2,0},{3,1},{4,6},{5,7},{6,4},{7,5},{8,10},{9,11},{10,... | collective-permute-start | bytes 98312 | tf_op jit(solution)/shard_map/ppermute | solution.py:319
  3.6 8.1 %collective-permute-start.2 = (bf16[1,128,128]{2,1,0:T(8,128)(2,1)}, bf16[1,128,128]{2,1,0:T(8,128)(2,1)S(1)}, u32[]{:S(2)}, u32[]{:S(2)}) collective-permute-start(bf16[1,128,128]{2,1,0:T(8,128)(2,1)} %grad_hbm.1), channel_id=1, source_target_pairs={{0,6},{1,7},{2,4},{3,5},{4,2},{5,3},{6,0},{7,1},{8,14},{9,15},{10,... | collective-permute-start | bytes 98312 | tf_op jit(solution)/shard_map/ppermute | solution.py:319
  5.1 6.6 %collective-permute-start.1 = (bf16[1,128,128]{2,1,0:T(8,128)(2,1)}, bf16[1,128,128]{2,1,0:T(8,128)(2,1)S(1)}, u32[]{:S(2)}, u32[]{:S(2)}) collective-permute-start(bf16[1,128,128]{2,1,0:T(8,128)(2,1)} %grad_hbm.1), channel_id=1, source_target_pairs={{0,4},{1,5},{2,6},{3,7},{4,0},{5,1},{6,2},{7,3},{8,12},{9,13},{10,... | collective-permute-start | bytes 98312 | tf_op jit(solution)/shard_map/ppermute | solution.py:319
  5.2 6.5 %copy-start.3 = (bf16[1,1024,128]{2,1,0:T(8,128)(2,1)S(1)}, bf16[1,1024,128]{2,1,0:T(8,128)(2,1)}, u32[]{:S(2)}) copy-start(bf16[1,1024,128]{2,1,0:T(8,128)(2,1)} %refs_7_.2) | copy-start | bytes 786436
  6.3 8.6 %collective-permute-start.6 = (bf16[128,256]{1,0:T(8,128)(2,1)S(1)}, bf16[128,256]{1,0:T(8,128)(2,1)S(1)}, u32[]{:S(2)}, u32[]{:S(2)}) collective-permute-start(bf16[128,256]{1,0:T(8,128)(2,1)S(1)} %get-tuple-element.36.refs_2_), channel_id=1, source_target_pairs={{0,16},{8,24},{16,0},{24,8},{1,17},{9,25},{17,1},{25,9},{2,18},{10... | collective-permute-start | bytes 196616 | tf_op jit(solution)/shard_map/ppermute | solution.py:319
  9.4 6.1 %collective-permute-start.5 = (bf16[128,256]{1,0:T(8,128)(2,1)S(1)}, bf16[128,256]{1,0:T(8,128)(2,1)S(1)}, u32[]{:S(2)}, u32[]{:S(2)}) collective-permute-start(bf16[128,256]{1,0:T(8,128)(2,1)S(1)} %get-tuple-element.36.refs_2_), channel_id=1, source_target_pairs={{0,24},{8,16},{16,8},{24,0},{1,25},{9,17},{17,9},{25,1},{2,26},{10... | collective-permute-start | bytes 196616 | tf_op jit(solution)/shard_map/ppermute | solution.py:319
  11.4 4.8 %collective-permute-start.4 = (bf16[128,256]{1,0:T(8,128)(2,1)S(1)}, bf16[128,256]{1,0:T(8,128)(2,1)S(1)}, u32[]{:S(2)}, u32[]{:S(2)}) collective-permute-start(bf16[128,256]{1,0:T(8,128)(2,1)S(1)} %get-tuple-element.36.refs_2_), channel_id=1, source_target_pairs={{0,8},{8,0},{16,24},{24,16},{1,9},{9,1},{17,25},{25,17},{2,10},{10... | collective-permute-start | bytes 196616 | tf_op jit(solution)/shard_map/ppermute | solution.py:319
  11.7 1.9 %copy-start.4 = (bf16[1,1024,128]{2,1,0:T(8,128)(2,1)S(1)}, bf16[1,1024,128]{2,1,0:T(8,128)(2,1)}, u32[]{:S(2)}) copy-start(bf16[1,1024,128]{2,1,0:T(8,128)(2,1)} %v_ref.1) | copy-start | bytes 786436
  13.5 2.6 %collective-permute-start.3 = (bf16[512,128]{1,0:T(8,128)(2,1)S(1)}, bf16[512,128]{1,0:T(8,128)(2,1)S(1)}, u32[]{:S(2)}, u32[]{:S(2)}) collective-permute-start(bf16[512,128]{1,0:T(8,128)(2,1)S(1)} %get-tuple-element.35.refs_0_), channel_id=1, source_target_pairs={{0,1},{1,0},{2,3},{3,2},{4,5},{5,4},{6,7},{7,6},{8,9},{9,8},{10,11... | collective-permute-start | bytes 393224 | tf_op jit(solution)/shard_map/ppermute | solution.py:319
  18.1 7.5 %collective-permute-start.7 = (bf16[272,128]{1,0:T(8,128)(2,1)S(1)}, bf16[272,128]{1,0:T(8,128)(2,1)S(1)}, u32[]{:S(2)}, u32[]{:S(2)}) collective-permute-start(bf16[272,128]{1,0:T(8,128)(2,1)S(1)} %get-tuple-element.48), channel_id=1, source_target_pairs={{0,16},{8,24},{16,0},{24,8},{1,17},{9,25},{17,1},{25,9},{2,18},{10... | collective-permute-start | bytes 208904 | tf_op jit(solution)/shard_map/ppermute | solution.py:319
  19.8 5.8 %collective-permute-start.8 = (bf16[272,128]{1,0:T(8,128)(2,1)S(1)}, bf16[272,128]{1,0:T(8,128)(2,1)S(1)}, u32[]{:S(2)}, u32[]{:S(2)}) collective-permute-start(bf16[272,128]{1,0:T(8,128)(2,1)S(1)} %get-tuple-element.49), channel_id=1, source_target_pairs={{0,8},{8,0},{16,24},{24,16},{1,9},{9,1},{17,25},{25,17},{2,10},{10... | collective-permute-start | bytes 208904 | tf_op jit(solution)/shard_map/ppermute | solution.py:319
  20.9 6.2 %collective-permute-start.9 = (bf16[272,128]{1,0:T(8,128)(2,1)S(1)}, bf16[272,128]{1,0:T(8,128)(2,1)S(1)}, u32[]{:S(2)}, u32[]{:S(2)}) collective-permute-start(bf16[272,128]{1,0:T(8,128)(2,1)S(1)} %get-tuple-element.50), channel_id=1, source_target_pairs={{0,24},{8,16},{16,8},{24,0},{1,25},{9,17},{17,9},{25,1},{2,26},{10... | collective-permute-start | bytes 208904 | tf_op jit(solution)/shard_map/ppermute | solution.py:319
  22.5 4.5 %copy-start = (f32[128,256]{1,0:T(8,128)S(1)}, f32[128,256]{1,0:T(8,128)}, u32[]{:S(2)}) copy-start(f32[128,256]{1,0:T(8,128)} %refs_5_.1) | copy-start | bytes 393220
  22.5 4.5 %copy-start.1 = (f32[128,256]{1,0:T(8,128)S(1)}, f32[128,256]{1,0:T(8,128)}, u32[]{:S(2)}) copy-start(f32[128,256]{1,0:T(8,128)} %refs_6_.1) | copy-start | bytes 393220
  22.5 4.5 %copy-start.2 = (f32[128,256]{1,0:T(8,128)S(1)}, f32[128,256]{1,0:T(8,128)}, u32[]{:S(2)}) copy-start(f32[128,256]{1,0:T(8,128)} %refs_7_.3) | copy-start | bytes 393220

commit v11 on v10

--- a/solution.py
+++ b/solution.py
@@ -168,32 +168,36 @@
         xth_ref[:, cols], xtl_ref[:, cols] = split(jnp.where(lead <= first - a, xt[:, cols], 0.0))
 
 
-def backward_scores(up_places, w_places, owners, by_distance, *refs):
-    n_up, n_w = len({p[0] for p in up_places}), len({p[0] for p in w_places})
-    up_refs, w_refs, refs = refs[:n_up], refs[n_up : n_up + n_w], refs[n_up + n_w :]
-    p_ref, vblk, xth_ref, xtl_ref, o_ref, do_ref, own_ref, own_taps_ref = refs[:8]
-    out_refs, (up, grad) = refs[8 : 8 + len(owners)], refs[8 + len(owners) :]
+def spots(places, axis):
+    me = lax.axis_index(axis)
+    return [(n, part, at if shift is None else lax.bitwise_xor(me, shift)) for n, part, shift, at in places]
+
+
+def backward_columns(places, *refs):
+    *up_refs, o_ref, up, grad = refs
+    for n, part, spot in spots(places, "tensor"):
+        block = up_refs[n][part]
+        width = block.shape[1]
+        up[:, pl.ds(pl.multiple_of(spot * width, width), width)] = block
+    grad[...] = dot(o_ref[...], up[...], ((0,), (0,)))
+
+
+def backward_scores(places, owners, by_distance, *refs):
+    n_w = len({p[0] for p in places})
+    w_refs, refs = refs[:n_w], refs[n_w:]
+    up, grad, p_ref, vblk, xth_ref, xtl_ref, do_ref, own_ref, own_taps_ref, *out_refs = refs
     span = p_ref.shape[0]
     taps_a = xth_ref.shape[1] // span
     windows = vblk.shape[0] // LANES
 
-    def columns(places, axis):
-        me = lax.axis_index(axis)
-        return [(n, part, at if shift is None else lax.bitwise_xor(me, shift)) for n, part, shift, at in places]
-
-    for n, part, spot in columns(up_places, "tensor"):
-        block = up_refs[n][part]
-        width = block.shape[1]
-        up[:, pl.ds(pl.multiple_of(spot * width, width), width)] = block
     do = None
-    for n, part, spot in columns(w_places, "dp"):
+    for n, part, spot in spots(places, "dp"):
         block = w_refs[n][part]
         width = block.shape[1]
         term = dot(up[:, pl.ds(pl.multiple_of(spot * width, width), width)], block, ((1,), (1,)))
         do = term if do is None else do + term
     do = do.astype(BF16)
     do_ref[...] = do
-    grad[...] = dot(o_ref[...], up[...], ((0,), (0,)))
     dc = scores_grad(p_ref[...], do, vblk[...])
 
     right = jnp.concatenate(
@@ -435,23 +439,28 @@
     if few("dp"):
         owners = owners[group_count // 2 : 0 : -1] + owners[group_count // 2 + 1 :]
     others = len(owners)
+    up, grad = pl.pallas_call(
+        functools.partial(backward_columns, up_places),
+        out_shape=(shape((span, columns), BF16), shape((depth, columns), F32)),
+        in_specs=[whole] * (len(up_arrays) + 1),
+        out_specs=(whole,) * 2,
+        compiler_params=vmem,
+        cost_estimate=cost(10**9),
+        name="attention_backward_columns",
+    )(*up_arrays, attended)
     do, own, own_taps, *payloads = pl.pallas_call(
-        functools.partial(backward_scores, up_places, w_places, owners, few("dp")),
+        functools.partial(backward_scores, w_places, owners, few("dp")),
         out_shape=(
             shape((span, depth), BF16),
             shape((depth, share), F32),
             shape((8, LANES), F32),
         ) + (shape((depth * (share // LANES) + 16, LANES), BF16),) * others,
-        in_specs=[whole] * (len(up_arrays) + len(w_arrays) + 5),
+        in_specs=[whole] * (len(w_arrays) + 6),
         out_specs=(whole,) * (3 + others),
-        scratch_shapes=[
-            pltpu.VMEM((span, columns), BF16),
-            pltpu.VMEM((depth, columns), F32),
-        ],
         compiler_params=vmem,
         cost_estimate=cost(2 * 10**9),
         name="attention_backward_scores",
-    )(*up_arrays, *w_arrays, p, vblk, xth, xtl, attended)
+    )(*w_arrays, up, grad, p, vblk, xth, xtl)
 
     if few("dp"):
         payloads = [swap(payload, "dp", owner) for owner, payload in zip(owners, payloads, strict=True)]

time: 28.1 us -> 28 us (level)
    pallas_call x1 -> x2, Pallas kernels: 2 us -> 2.18 us  [the longest x1 1.91 us: shards(): pl.pallas_call(functools.partial(backward_scores, w_places, owners, few('...]
  transfers between devices with their start and end apart: 10 -> 10, of which waited for: 3 -> 3; matrix products, arithmetic and copies ran while one was open for 0% -> 0% of each run, Pallas kernels for 26% -> 27%
where the time goes in v11:
time: 28 us; the launch traced here: 27.9 us
  starting transfers between devices  13.8 us (49%)
  Pallas kernels  10.3 us (37%)
  waiting for transfers between devices  2.43 us (9%)
  between operations  1.37 us (5%)
    ppermute x10, starting transfers between devices, swap(): return lax.ppermute(x, axis, [(i, i ^ shift) for i in range(n)])  13.8 us
    pallas_call x1, Pallas kernels, shards(): pl.pallas_call(functools.partial(backward_inputs, rows, key_count, taps_a...  3.01 us
    ppermute x10, waiting for transfers between devices, swap(): return lax.ppermute(x, axis, [(i, i ^ shift) for i in range(n)])  2.43 us
    pallas_call x1, Pallas kernels, shards(): pl.pallas_call(functools.partial(backward_scores, w_places, owners, few('...  1.91 us
    pallas_call x1, Pallas kernels, shards(): pl.pallas_call(functools.partial(forward, len(pieces), taps_a, half), out...  1.78 us
    pallas_call x1, Pallas kernels, shards(): pl.pallas_call(functools.partial(forward_turned, taps_a, half), out_shape...  1.3 us
    pallas_call x1, Pallas kernels, shards(): pl.pallas_call(prepare, out_shape=(shape(proj_weight.shape, BF16), band,...  1.08 us
    pallas_call x1, Pallas kernels, shards(): pl.pallas_call(functools.partial(update, group_count, span), out_shape=(s...  0.94 us
  transfers between devices with their start and end apart: 10, of which 3 were waited for; matrix products, arithmetic and copies ran while one was open for 0% of the time, Pallas kernels for 27%

profile of v11, /device:TPU:0, one launch (start us, length us, event | category | flops | bytes accessed | tf_op | source)
XLA Modules:
  0.0 27.9 jit_solution(3549761069575216159)
XLA Ops:
  0.6 3.0 %collective-permute-start.3 = (bf16[1,128,128]{2,1,0:T(8,128)(2,1)}, bf16[1,128,128]{2,1,0:T(8,128)(2,1)S(1)}, u32[]{:S(2)}, u32[]{:S(2)}) collective-permute-start(bf16[1,128,128]{2,1,0:T(8,128)(2,1)} %grad_hbm.1), channel_id=1, source_target_pairs={{0,2},{1,3},{2,0},{3,1},{4,6},{5,7},{6,4},{7,5},{8,10},{9,11},{10,... | collective-permute-start | bytes 98312 | tf_op jit(solution)/shard_map/ppermute | solution.py:323
  3.6 1.5 %collective-permute-start.5 = (bf16[1,128,128]{2,1,0:T(8,128)(2,1)}, bf16[1,128,128]{2,1,0:T(8,128)(2,1)S(1)}, u32[]{:S(2)}, u32[]{:S(2)}) collective-permute-start(bf16[1,128,128]{2,1,0:T(8,128)(2,1)} %grad_hbm.1), channel_id=1, source_target_pairs={{0,6},{1,7},{2,4},{3,5},{4,2},{5,3},{6,0},{7,1},{8,14},{9,15},{10,... | collective-permute-start | bytes 98312 | tf_op jit(solution)/shard_map/ppermute | solution.py:323
  5.1 0.0 collective-permute-start.4
  5.2 0.0 copy-start.3
  5.2 1.1 %prepare.1 = (bf16[128,256]{1,0:T(8,128)(2,1)S(1)}, bf16[768,384]{1,0:T(8,128)(2,1)S(1)}, f32[152,128]{1,0:T(8,128)S(1)}, bf16[288,128]{1,0:T(8,128)(2,1)S(1)}, bf16[1,128,128]{2,1,0:T(8,128)(2,1)S(1)}) custom-call(f32[6,1,11]{2,1,0:T(1,128)} %bitcast.2, f32[128,256]{1,0:T(8,128)} %refs_5_.1, bf16[1,133,128]{2,1,0:T(8,128)(2,1)} %q_hbm.1, ...), custom_call_target="tpu_custom_call" | custom-call | flops 5000000000 | bytes 1000000 | tf_op jit(solution)/shard_map/prepare/pallas_call | solution.py:375
  6.3 3.1 %collective-permute-start.2 = (bf16[128,256]{1,0:T(8,128)(2,1)S(1)}, bf16[128,256]{1,0:T(8,128)(2,1)S(1)}, u32[]{:S(2)}, u32[]{:S(2)}) collective-permute-start(bf16[128,256]{1,0:T(8,128)(2,1)S(1)} %get-tuple-element.35.refs_0_), channel_id=1, source_target_pairs={{0,16},{8,24},{16,0},{24,8},{1,17},{9,25},{17,1},{25,9},{2,18},{10... | collective-permute-start | bytes 196616 | tf_op jit(solution)/shard_map/ppermute | solution.py:323
  9.4 1.3 %collective-permute-start.1 = (bf16[128,256]{1,0:T(8,128)(2,1)S(1)}, bf16[128,256]{1,0:T(8,128)(2,1)S(1)}, u32[]{:S(2)}, u32[]{:S(2)}) collective-permute-start(bf16[128,256]{1,0:T(8,128)(2,1)S(1)} %get-tuple-element.35.refs_0_), channel_id=1, source_target_pairs={{0,24},{8,16},{16,8},{24,0},{1,25},{9,17},{17,9},{25,1},{2,26},{10... | collective-permute-start | bytes 196616 | tf_op jit(solution)/shard_map/ppermute | solution.py:323
  11.4 0.0 collective-permute-done.3.refs_1_
  11.4 0.3 %collective-permute-start = (bf16[128,256]{1,0:T(8,128)(2,1)S(1)}, bf16[128,256]{1,0:T(8,128)(2,1)S(1)}, u32[]{:S(2)}, u32[]{:S(2)}) collective-permute-start(bf16[128,256]{1,0:T(8,128)(2,1)S(1)} %get-tuple-element.35.refs_0_), channel_id=1, source_target_pairs={{0,8},{8,0},{16,24},{24,16},{1,9},{9,1},{17,25},{25,17},{2,10},{10... | collective-permute-start | bytes 196616 | tf_op jit(solution)/shard_map/ppermute | solution.py:323
  11.7 0.0 collective-permute-done.5.refs_3_
  11.7 0.0 collective-permute-done.4.refs_2_
  11.7 0.0 copy-done.3
  11.7 0.0 copy-start.4
  11.7 1.8 %attention_forward.1 = (f32[128,1152]{1,0:T(8,128)S(1)}, bf16[1152,128]{1,0:T(8,128)(2,1)S(1)}, bf16[512,128]{1,0:T(8,128)(2,1)S(1)}) custom-call(bf16[1,128,128]{2,1,0:T(8,128)(2,1)S(1)} %get-tuple-element.36.refs_0_, bf16[1,128,128]{2,1,0:T(8,128)(2,1)S(1)} %collective-permute-done.3.refs_1_, bf16[1,128,128]{2,1,0:T(8,128)(2,1)S(1)} %collective-permute-done.4.refs_2_, ...), custom_call_target="tpu_custom_call" | custom-call | flops 5000000000 | bytes 1000000 | tf_op jit(solution)/shard_map/attention_forward/pallas_call | solution.py:401
  13.5 0.1 collective-permute-start.6
  13.6 0.0 copy-done.4
  13.6 1.3 %attention_forward_turned.1 = (bf16[1152,768]{1,0:T(8,128)(2,1)S(1)}, bf16[1152,768]{1,0:T(8,128)(2,1)S(1)}, bf16[1152,128]{1,0:T(8,128)(2,1)S(1)}, bf16[128,128]{1,0:T(8,128)(2,1)S(1)}) custom-call(s32[1]{0:T(128)S(6)} %copy.16.refs_4_.first_ref, bf16[1152,128]{1,0:T(8,128)(2,1)S(1)} %get-tuple-element.39.kwin, f32[152,128]{1,0:T(8,128)S(1)} %get-tuple-element.40.q32, ...), custom_call_target="tpu_custom_call" | custom-call | flops 2000000000 | bytes 1000000 | tf_op jit(solution)/shard_map/attention_forward_turned/pallas_call | solution.py:427
  14.9 0.0 collective-permute-done.6.refs_1_
  14.9 0.3 attention_backward_columns.1
  15.2 0.0 collective-permute-done.2.refs_3_
  15.2 0.3 %collective-permute-done.1.refs_2_ = bf16[128,256]{1,0:T(8,128)(2,1)S(1)} collective-permute-done((bf16[128,256]{1,0:T(8,128)(2,1)S(1)}, bf16[128,256]{1,0:T(8,128)(2,1)S(1)}, u32[]{:S(2)}, u32[]{:S(2)}) %collective-permute-start.1) | collective-permute-done | bytes 65568 | tf_op jit(solution)/shard_map/ppermute | solution.py:323
  15.5 0.7 %collective-permute-done.refs_1_ = bf16[128,256]{1,0:T(8,128)(2,1)S(1)} collective-permute-done((bf16[128,256]{1,0:T(8,128)(2,1)S(1)}, bf16[128,256]{1,0:T(8,128)(2,1)S(1)}, u32[]{:S(2)}, u32[]{:S(2)}) %collective-permute-start) | collective-permute-done | bytes 65568 | tf_op jit(solution)/shard_map/ppermute | solution.py:323
  16.1 1.9 %attention_backward_scores.1 = (bf16[128,128]{1,0:T(8,128)(2,1)S(1)}, f32[128,256]{1,0:T(8,128)S(1)}, f32[8,128]{1,0:T(8,128)S(1)}, bf16[272,128]{1,0:T(8,128)(2...) custom-call(bf16[128,256]{1,0:T(8,128)(2,1)S(1)} %get-tuple-element.35.refs_0_, ...), custom_call_target="tpu_custom_call" | custom-call | flops 2000000000 | bytes 1000000 | tf_op jit(solution)/shard_map/attention_backward_scores/pallas_call | solution.py:451
  18.1 1.9 %collective-permute-start.7 = (bf16[272,128]{1,0:T(8,128)(2,1)S(1)}, bf16[272,128]{1,0:T(8,128)(2,1)S(1)}, u32[]{:S(2)}, u32[]{:S(2)}) collective-permute-start(bf16[272,128]{1,0:T(8,128)(2,1)S(1)} %get-tuple-element.52), channel_id=1, source_target_pairs={{0,16},{8,24},{16,0},{24,8},{1,17},{9,25},{17,1},{25,9},{2,18},{10... | collective-permute-start | bytes 208904 | tf_op jit(solution)/shard_map/ppermute | solution.py:323
  20.0 0.8 %collective-permute-start.8 = (bf16[272,128]{1,0:T(8,128)(2,1)S(1)}, bf16[272,128]{1,0:T(8,128)(2,1)S(1)}, u32[]{:S(2)}, u32[]{:S(2)}) collective-permute-start(bf16[272,128]{1,0:T(8,128)(2,1)S(1)} %get-tuple-element.53), channel_id=1, source_target_pairs={{0,8},{8,0},{16,24},{24,16},{1,9},{9,1},{17,25},{25,17},{2,10},{10... | collective-permute-start | bytes 208904 | tf_op jit(solution)/shard_map/ppermute | solution.py:323
  20.8 1.7 %collective-permute-start.9 = (bf16[272,128]{1,0:T(8,128)(2,1)S(1)}, bf16[272,128]{1,0:T(8,128)(2,1)S(1)}, u32[]{:S(2)}, u32[]{:S(2)}) collective-permute-start(bf16[272,128]{1,0:T(8,128)(2,1)S(1)} %get-tuple-element.54), channel_id=1, source_target_pairs={{0,24},{8,16},{16,8},{24,0},{1,25},{9,17},{17,9},{25,1},{2,26},{10... | collective-permute-start | bytes 208904 | tf_op jit(solution)/shard_map/ppermute | solution.py:323
  22.4 0.0 copy-start
  22.5 0.0 copy-start.1
  22.5 0.0 copy-start.2
  22.5 3.0 %attention_backward_inputs.1 = (bf16[1,133,128]{2,1,0:T(8,128)(2,1)}, bf16[1,1024,128]{2,1,0:T(8,128)(2,1)}, bf16[1,1024,128]{2,1,0:T(8,128)(2,1)}) custom-call(s32[1]{0:T(128)S(6)} %copy.16.refs_4_.first_ref, bf16[768,384]{1,0:T(8,128)(2,1)S(1)} %get-tuple-element.34.refs_5_.bands_ref, bf16[128,128]{1,0:T(8,128)(2,1)S(1)} %get-tuple-element.48.do_ref, ...), custom_call_target="tpu_custom_call" | custom-call | flops 3000000000 | bytes 1000000 | tf_op jit(solution)/shard_map/attention_backward_inputs/pallas_call | solution.py:471
  25.5 0.0 collective-permute-done.7.refs_0_
  25.5 0.0 collective-permute-done.8.refs_1_
  25.5 1.4 %collective-permute-done.9.refs_2_ = bf16[272,128]{1,0:T(8,128)(2,1)S(1)} collective-permute-done((bf16[272,128]{1,0:T(8,128)(2,1)S(1)}, bf16[272,128]{1,0:T(8,128)(2,1)S(1)}, u32[]{:S(2)}, u32[]{:S(2)}) %collective-permute-start.9) | collective-permute-done | bytes 69664 | tf_op jit(solution)/shard_map/ppermute | solution.py:323
  26.9 0.0 copy-done
  26.9 0.0 copy-done.1
  26.9 0.0 copy-done.2
  26.9 0.9 %projection_update.1 = (f32[128,256]{1,0:T(8,128)}, f32[128,256]{1,0:T(8,128)}, f32[128,256]{1,0:T(8,128)}, f32[6,1,11]{2,1,0:T(1,128)}) custom-call(bf16[272,128]{1,0:T(8,128)(2,1)S(1)} %collective-permute-done.7.refs_0_, bf16[272,128]{1,0:T(8,128)(2,1)S(1)} %collective-permute-done.8.refs_1_, bf16[272,128]{1,0:T(8,128)(2,1)S(1)} %collective-permute-done.9.refs_2_, ...), custom_call_target="tpu_custom_call" | custom-call | tf_op jit(solution)/shard_map/projection_update/pallas_call | solution.py:488
Async XLA Ops:
  0.6 10.8 %collective-permute-start.3 = (bf16[1,128,128]{2,1,0:T(8,128)(2,1)}, bf16[1,128,128]{2,1,0:T(8,128)(2,1)S(1)}, u32[]{:S(2)}, u32[]{:S(2)}) collective-permute-start(bf16[1,128,128]{2,1,0:T(8,128)(2,1)} %grad_hbm.1), channel_id=1, source_target_pairs={{0,2},{1,3},{2,0},{3,1},{4,6},{5,7},{6,4},{7,5},{8,10},{9,11},{10,... | collective-permute-start | bytes 98312 | tf_op jit(solution)/shard_map/ppermute | solution.py:323
  3.6 8.1 %collective-permute-start.5 = (bf16[1,128,128]{2,1,0:T(8,128)(2,1)}, bf16[1,128,128]{2,1,0:T(8,128)(2,1)S(1)}, u32[]{:S(2)}, u32[]{:S(2)}) collective-permute-start(bf16[1,128,128]{2,1,0:T(8,128)(2,1)} %grad_hbm.1), channel_id=1, source_target_pairs={{0,6},{1,7},{2,4},{3,5},{4,2},{5,3},{6,0},{7,1},{8,14},{9,15},{10,... | collective-permute-start | bytes 98312 | tf_op jit(solution)/shard_map/ppermute | solution.py:323
  5.1 6.6 %collective-permute-start.4 = (bf16[1,128,128]{2,1,0:T(8,128)(2,1)}, bf16[1,128,128]{2,1,0:T(8,128)(2,1)S(1)}, u32[]{:S(2)}, u32[]{:S(2)}) collective-permute-start(bf16[1,128,128]{2,1,0:T(8,128)(2,1)} %grad_hbm.1), channel_id=1, source_target_pairs={{0,4},{1,5},{2,6},{3,7},{4,0},{5,1},{6,2},{7,3},{8,12},{9,13},{10,... | collective-permute-start | bytes 98312 | tf_op jit(solution)/shard_map/ppermute | solution.py:323
  5.2 6.5 %copy-start.3 = (bf16[1,1024,128]{2,1,0:T(8,128)(2,1)S(1)}, bf16[1,1024,128]{2,1,0:T(8,128)(2,1)}, u32[]{:S(2)}) copy-start(bf16[1,1024,128]{2,1,0:T(8,128)(2,1)} %refs_7_.2) | copy-start | bytes 786436
  6.3 8.9 %collective-permute-start.2 = (bf16[128,256]{1,0:T(8,128)(2,1)S(1)}, bf16[128,256]{1,0:T(8,128)(2,1)S(1)}, u32[]{:S(2)}, u32[]{:S(2)}) collective-permute-start(bf16[128,256]{1,0:T(8,128)(2,1)S(1)} %get-tuple-element.35.refs_0_), channel_id=1, source_target_pairs={{0,16},{8,24},{16,0},{24,8},{1,17},{9,25},{17,1},{25,9},{2,18},{10... | collective-permute-start | bytes 196616 | tf_op jit(solution)/shard_map/ppermute | solution.py:323
  9.4 6.1 %collective-permute-start.1 = (bf16[128,256]{1,0:T(8,128)(2,1)S(1)}, bf16[128,256]{1,0:T(8,128)(2,1)S(1)}, u32[]{:S(2)}, u32[]{:S(2)}) collective-permute-start(bf16[128,256]{1,0:T(8,128)(2,1)S(1)} %get-tuple-element.35.refs_0_), channel_id=1, source_target_pairs={{0,24},{8,16},{16,8},{24,0},{1,25},{9,17},{17,9},{25,1},{2,26},{10... | collective-permute-start | bytes 196616 | tf_op jit(solution)/shard_map/ppermute | solution.py:323
  11.4 4.8 %collective-permute-start = (bf16[128,256]{1,0:T(8,128)(2,1)S(1)}, bf16[128,256]{1,0:T(8,128)(2,1)S(1)}, u32[]{:S(2)}, u32[]{:S(2)}) collective-permute-start(bf16[128,256]{1,0:T(8,128)(2,1)S(1)} %get-tuple-element.35.refs_0_), channel_id=1, source_target_pairs={{0,8},{8,0},{16,24},{24,16},{1,9},{9,1},{17,25},{25,17},{2,10},{10... | collective-permute-start | bytes 196616 | tf_op jit(solution)/shard_map/ppermute | solution.py:323
  11.7 1.9 %copy-start.4 = (bf16[1,1024,128]{2,1,0:T(8,128)(2,1)S(1)}, bf16[1,1024,128]{2,1,0:T(8,128)(2,1)}, u32[]{:S(2)}) copy-start(bf16[1,1024,128]{2,1,0:T(8,128)(2,1)} %v_ref.1) | copy-start | bytes 786436
  13.5 1.4 %collective-permute-start.6 = (bf16[512,128]{1,0:T(8,128)(2,1)S(1)}, bf16[512,128]{1,0:T(8,128)(2,1)S(1)}, u32[]{:S(2)}, u32[]{:S(2)}) collective-permute-start(bf16[512,128]{1,0:T(8,128)(2,1)S(1)} %get-tuple-element.38.refs_0_), channel_id=1, source_target_pairs={{0,1},{1,0},{2,3},{3,2},{4,5},{5,4},{6,7},{7,6},{8,9},{9,8},{10,11... | collective-permute-start | bytes 393224 | tf_op jit(solution)/shard_map/ppermute | solution.py:323
  18.1 7.4 %collective-permute-start.7 = (bf16[272,128]{1,0:T(8,128)(2,1)S(1)}, bf16[272,128]{1,0:T(8,128)(2,1)S(1)}, u32[]{:S(2)}, u32[]{:S(2)}) collective-permute-start(bf16[272,128]{1,0:T(8,128)(2,1)S(1)} %get-tuple-element.52), channel_id=1, source_target_pairs={{0,16},{8,24},{16,0},{24,8},{1,17},{9,25},{17,1},{25,9},{2,18},{10... | collective-permute-start | bytes 208904 | tf_op jit(solution)/shard_map/ppermute | solution.py:323
  20.0 5.5 %collective-permute-start.8 = (bf16[272,128]{1,0:T(8,128)(2,1)S(1)}, bf16[272,128]{1,0:T(8,128)(2,1)S(1)}, u32[]{:S(2)}, u32[]{:S(2)}) collective-permute-start(bf16[272,128]{1,0:T(8,128)(2,1)S(1)} %get-tuple-element.53), channel_id=1, source_target_pairs={{0,8},{8,0},{16,24},{24,16},{1,9},{9,1},{17,25},{25,17},{2,10},{10... | collective-permute-start | bytes 208904 | tf_op jit(solution)/shard_map/ppermute | solution.py:323
  20.8 6.2 %collective-permute-start.9 = (bf16[272,128]{1,0:T(8,128)(2,1)S(1)}, bf16[272,128]{1,0:T(8,128)(2,1)S(1)}, u32[]{:S(2)}, u32[]{:S(2)}) collective-permute-start(bf16[272,128]{1,0:T(8,128)(2,1)S(1)} %get-tuple-element.54), channel_id=1, source_target_pairs={{0,24},{8,16},{16,8},{24,0},{1,25},{9,17},{17,9},{25,1},{2,26},{10... | collective-permute-start | bytes 208904 | tf_op jit(solution)/shard_map/ppermute | solution.py:323
  22.4 4.5 %copy-start = (f32[128,256]{1,0:T(8,128)S(1)}, f32[128,256]{1,0:T(8,128)}, u32[]{:S(2)}) copy-start(f32[128,256]{1,0:T(8,128)} %refs_5_.1) | copy-start | bytes 393220
  22.5 4.5 %copy-start.1 = (f32[128,256]{1,0:T(8,128)S(1)}, f32[128,256]{1,0:T(8,128)}, u32[]{:S(2)}) copy-start(f32[128,256]{1,0:T(8,128)} %refs_6_.1) | copy-start | bytes 393220
  22.5 4.5 %copy-start.2 = (f32[128,256]{1,0:T(8,128)S(1)}, f32[128,256]{1,0:T(8,128)}, u32[]{:S(2)}) copy-start(f32[128,256]{1,0:T(8,128)} %refs_7_.3) | copy-start | bytes 393220

commit v12 on v11

--- a/solution.py
+++ b/solution.py
@@ -141,7 +141,8 @@
     c = jnp.concatenate(mixed, axis=1)
     lane = iota((span, LANES), 1)
     row = iota((span, LANES), 0)
-    live = jnp.concatenate([(lane < step) & (n * step + lane <= first + row) for n in range(windows)], axis=1)
+    ahead = jnp.where(lane < step, lane - row, windows * LANES + span)
+    live = jnp.concatenate([ahead <= first - n * step for n in range(windows)], axis=1)
     c = jnp.where(live, c, -jnp.inf)
     terms = jnp.exp(c - jnp.max(c, axis=1, keepdims=True))
     p = terms * (1.0 / jnp.sum(terms, axis=1, keepdims=True))

time: 28 us -> 28 us (level)
  no operation moved by 1% of the time
where the time goes in v12:
time: 28 us; the launch traced here: 27.9 us
  starting transfers between devices  13.8 us (49%)
  Pallas kernels  10.3 us (37%)
  waiting for transfers between devices  2.46 us (9%)
  between operations  1.37 us (5%)
    ppermute x10, starting transfers between devices, swap(): return lax.ppermute(x, axis, [(i, i ^ shift) for i in range(n)])  13.8 us
    pallas_call x1, Pallas kernels, shards(): pl.pallas_call(functools.partial(backward_inputs, rows, key_count, taps_a...  3.01 us
    ppermute x10, waiting for transfers between devices, swap(): return lax.ppermute(x, axis, [(i, i ^ shift) for i in range(n)])  2.46 us
    pallas_call x1, Pallas kernels, shards(): pl.pallas_call(functools.partial(backward_scores, w_places, owners, few('...  1.91 us
    pallas_call x1, Pallas kernels, shards(): pl.pallas_call(functools.partial(forward, len(pieces), taps_a, half), out...  1.74 us
    pallas_call x1, Pallas kernels, shards(): pl.pallas_call(functools.partial(forward_turned, taps_a, half), out_shape...  1.3 us
    pallas_call x1, Pallas kernels, shards(): pl.pallas_call(prepare, out_shape=(shape(proj_weight.shape, BF16), band,...  1.08 us
    pallas_call x1, Pallas kernels, shards(): pl.pallas_call(functools.partial(update, group_count, span), out_shape=(s...  0.94 us
  transfers between devices with their start and end apart: 10, of which 3 were waited for; matrix products, arithmetic and copies ran while one was open for 0% of the time, Pallas kernels for 27%

profile of v12, /device:TPU:0, one launch (start us, length us, event | category | flops | bytes accessed | tf_op | source)
XLA Modules:
  0.0 27.9 jit_solution(9248307035430333894)
XLA Ops:
  0.6 3.0 %collective-permute-start.3 = (bf16[1,128,128]{2,1,0:T(8,128)(2,1)}, bf16[1,128,128]{2,1,0:T(8,128)(2,1)S(1)}, u32[]{:S(2)}, u32[]{:S(2)}) collective-permute-start(bf16[1,128,128]{2,1,0:T(8,128)(2,1)} %grad_hbm.1), channel_id=1, source_target_pairs={{0,2},{1,3},{2,0},{3,1},{4,6},{5,7},{6,4},{7,5},{8,10},{9,11},{10,... | collective-permute-start | bytes 98312 | tf_op jit(solution)/shard_map/ppermute | solution.py:324
  3.6 1.5 %collective-permute-start.5 = (bf16[1,128,128]{2,1,0:T(8,128)(2,1)}, bf16[1,128,128]{2,1,0:T(8,128)(2,1)S(1)}, u32[]{:S(2)}, u32[]{:S(2)}) collective-permute-start(bf16[1,128,128]{2,1,0:T(8,128)(2,1)} %grad_hbm.1), channel_id=1, source_target_pairs={{0,6},{1,7},{2,4},{3,5},{4,2},{5,3},{6,0},{7,1},{8,14},{9,15},{10,... | collective-permute-start | bytes 98312 | tf_op jit(solution)/shard_map/ppermute | solution.py:324
  5.1 0.0 collective-permute-start.4
  5.2 0.0 copy-start.3
  5.2 1.1 %prepare.1 = (bf16[128,256]{1,0:T(8,128)(2,1)S(1)}, bf16[768,384]{1,0:T(8,128)(2,1)S(1)}, f32[152,128]{1,0:T(8,128)S(1)}, bf16[288,128]{1,0:T(8,128)(2,1)S(1)}, bf16[1,128,128]{2,1,0:T(8,128)(2,1)S(1)}) custom-call(f32[6,1,11]{2,1,0:T(1,128)} %bitcast.2, f32[128,256]{1,0:T(8,128)} %refs_5_.1, bf16[1,133,128]{2,1,0:T(8,128)(2,1)} %q_hbm.1, ...), custom_call_target="tpu_custom_call" | custom-call | flops 5000000000 | bytes 1000000 | tf_op jit(solution)/shard_map/prepare/pallas_call | solution.py:376
  6.3 3.1 %collective-permute-start.2 = (bf16[128,256]{1,0:T(8,128)(2,1)S(1)}, bf16[128,256]{1,0:T(8,128)(2,1)S(1)}, u32[]{:S(2)}, u32[]{:S(2)}) collective-permute-start(bf16[128,256]{1,0:T(8,128)(2,1)S(1)} %get-tuple-element.35.refs_0_), channel_id=1, source_target_pairs={{0,16},{8,24},{16,0},{24,8},{1,17},{9,25},{17,1},{25,9},{2,18},{10... | collective-permute-start | bytes 196616 | tf_op jit(solution)/shard_map/ppermute | solution.py:324
  9.4 1.3 %collective-permute-start.1 = (bf16[128,256]{1,0:T(8,128)(2,1)S(1)}, bf16[128,256]{1,0:T(8,128)(2,1)S(1)}, u32[]{:S(2)}, u32[]{:S(2)}) collective-permute-start(bf16[128,256]{1,0:T(8,128)(2,1)S(1)} %get-tuple-element.35.refs_0_), channel_id=1, source_target_pairs={{0,24},{8,16},{16,8},{24,0},{1,25},{9,17},{17,9},{25,1},{2,26},{10... | collective-permute-start | bytes 196616 | tf_op jit(solution)/shard_map/ppermute | solution.py:324
  11.4 0.0 collective-permute-done.3.refs_1_
  11.4 0.3 %collective-permute-start = (bf16[128,256]{1,0:T(8,128)(2,1)S(1)}, bf16[128,256]{1,0:T(8,128)(2,1)S(1)}, u32[]{:S(2)}, u32[]{:S(2)}) collective-permute-start(bf16[128,256]{1,0:T(8,128)(2,1)S(1)} %get-tuple-element.35.refs_0_), channel_id=1, source_target_pairs={{0,8},{8,0},{16,24},{24,16},{1,9},{9,1},{17,25},{25,17},{2,10},{10... | collective-permute-start | bytes 196616 | tf_op jit(solution)/shard_map/ppermute | solution.py:324
  11.7 0.0 collective-permute-done.5.refs_3_
  11.7 0.0 collective-permute-done.4.refs_2_
  11.7 0.0 copy-done.3
  11.7 0.0 copy-start.4
  11.7 1.7 %attention_forward.1 = (f32[128,1152]{1,0:T(8,128)S(1)}, bf16[1152,128]{1,0:T(8,128)(2,1)S(1)}, bf16[512,128]{1,0:T(8,128)(2,1)S(1)}) custom-call(bf16[1,128,128]{2,1,0:T(8,128)(2,1)S(1)} %get-tuple-element.36.refs_0_, bf16[1,128,128]{2,1,0:T(8,128)(2,1)S(1)} %collective-permute-done.3.refs_1_, bf16[1,128,128]{2,1,0:T(8,128)(2,1)S(1)} %collective-permute-done.4.refs_2_, ...), custom_call_target="tpu_custom_call" | custom-call | flops 5000000000 | bytes 1000000 | tf_op jit(solution)/shard_map/attention_forward/pallas_call | solution.py:402
  13.5 0.1 collective-permute-start.6
  13.5 0.0 copy-done.4
  13.6 1.3 %attention_forward_turned.1 = (bf16[1152,768]{1,0:T(8,128)(2,1)S(1)}, bf16[1152,768]{1,0:T(8,128)(2,1)S(1)}, bf16[1152,128]{1,0:T(8,128)(2,1)S(1)}, bf16[128,128]{1,0:T(8,128)(2,1)S(1)}) custom-call(s32[1]{0:T(128)S(6)} %copy.16.refs_4_.first_ref, bf16[1152,128]{1,0:T(8,128)(2,1)S(1)} %get-tuple-element.39.kwin, f32[152,128]{1,0:T(8,128)S(1)} %get-tuple-element.40.q32, ...), custom_call_target="tpu_custom_call" | custom-call | flops 2000000000 | bytes 1000000 | tf_op jit(solution)/shard_map/attention_forward_turned/pallas_call | solution.py:428
  14.9 0.0 collective-permute-done.6.refs_1_
  14.9 0.3 attention_backward_columns.1
  15.2 0.0 collective-permute-done.2.refs_3_
  15.2 0.3 %collective-permute-done.1.refs_2_ = bf16[128,256]{1,0:T(8,128)(2,1)S(1)} collective-permute-done((bf16[128,256]{1,0:T(8,128)(2,1)S(1)}, bf16[128,256]{1,0:T(8,128)(2,1)S(1)}, u32[]{:S(2)}, u32[]{:S(2)}) %collective-permute-start.1) | collective-permute-done | bytes 65568 | tf_op jit(solution)/shard_map/ppermute | solution.py:324
  15.5 0.7 %collective-permute-done.refs_1_ = bf16[128,256]{1,0:T(8,128)(2,1)S(1)} collective-permute-done((bf16[128,256]{1,0:T(8,128)(2,1)S(1)}, bf16[128,256]{1,0:T(8,128)(2,1)S(1)}, u32[]{:S(2)}, u32[]{:S(2)}) %collective-permute-start) | collective-permute-done | bytes 65568 | tf_op jit(solution)/shard_map/ppermute | solution.py:324
  16.1 1.9 %attention_backward_scores.1 = (bf16[128,128]{1,0:T(8,128)(2,1)S(1)}, f32[128,256]{1,0:T(8,128)S(1)}, f32[8,128]{1,0:T(8,128)S(1)}, bf16[272,128]{1,0:T(8,128)(2...) custom-call(bf16[128,256]{1,0:T(8,128)(2,1)S(1)} %get-tuple-element.35.refs_0_, ...), custom_call_target="tpu_custom_call" | custom-call | flops 2000000000 | bytes 1000000 | tf_op jit(solution)/shard_map/attention_backward_scores/pallas_call | solution.py:452
  18.1 1.9 %collective-permute-start.7 = (bf16[272,128]{1,0:T(8,128)(2,1)S(1)}, bf16[272,128]{1,0:T(8,128)(2,1)S(1)}, u32[]{:S(2)}, u32[]{:S(2)}) collective-permute-start(bf16[272,128]{1,0:T(8,128)(2,1)S(1)} %get-tuple-element.52), channel_id=1, source_target_pairs={{0,16},{8,24},{16,0},{24,8},{1,17},{9,25},{17,1},{25,9},{2,18},{10... | collective-permute-start | bytes 208904 | tf_op jit(solution)/shard_map/ppermute | solution.py:324
  19.9 0.8 %collective-permute-start.8 = (bf16[272,128]{1,0:T(8,128)(2,1)S(1)}, bf16[272,128]{1,0:T(8,128)(2,1)S(1)}, u32[]{:S(2)}, u32[]{:S(2)}) collective-permute-start(bf16[272,128]{1,0:T(8,128)(2,1)S(1)} %get-tuple-element.53), channel_id=1, source_target_pairs={{0,8},{8,0},{16,24},{24,16},{1,9},{9,1},{17,25},{25,17},{2,10},{10... | collective-permute-start | bytes 208904 | tf_op jit(solution)/shard_map/ppermute | solution.py:324
  20.8 1.7 %collective-permute-start.9 = (bf16[272,128]{1,0:T(8,128)(2,1)S(1)}, bf16[272,128]{1,0:T(8,128)(2,1)S(1)}, u32[]{:S(2)}, u32[]{:S(2)}) collective-permute-start(bf16[272,128]{1,0:T(8,128)(2,1)S(1)} %get-tuple-element.54), channel_id=1, source_target_pairs={{0,24},{8,16},{16,8},{24,0},{1,25},{9,17},{17,9},{25,1},{2,26},{10... | collective-permute-start | bytes 208904 | tf_op jit(solution)/shard_map/ppermute | solution.py:324
  22.4 0.0 copy-start
  22.5 0.0 copy-start.1
  22.5 0.0 copy-start.2
  22.5 3.0 %attention_backward_inputs.1 = (bf16[1,133,128]{2,1,0:T(8,128)(2,1)}, bf16[1,1024,128]{2,1,0:T(8,128)(2,1)}, bf16[1,1024,128]{2,1,0:T(8,128)(2,1)}) custom-call(s32[1]{0:T(128)S(6)} %copy.16.refs_4_.first_ref, bf16[768,384]{1,0:T(8,128)(2,1)S(1)} %get-tuple-element.34.refs_5_.bands_ref, bf16[128,128]{1,0:T(8,128)(2,1)S(1)} %get-tuple-element.48.do_ref, ...), custom_call_target="tpu_custom_call" | custom-call | flops 3000000000 | bytes 1000000 | tf_op jit(solution)/shard_map/attention_backward_inputs/pallas_call | solution.py:472
  25.5 0.0 collective-permute-done.7.refs_0_
  25.5 0.0 collective-permute-done.8.refs_1_
  25.5 1.4 %collective-permute-done.9.refs_2_ = bf16[272,128]{1,0:T(8,128)(2,1)S(1)} collective-permute-done((bf16[272,128]{1,0:T(8,128)(2,1)S(1)}, bf16[272,128]{1,0:T(8,128)(2,1)S(1)}, u32[]{:S(2)}, u32[]{:S(2)}) %collective-permute-start.9) | collective-permute-done | bytes 69664 | tf_op jit(solution)/shard_map/ppermute | solution.py:324
  26.9 0.0 copy-done
  26.9 0.0 copy-done.1
  26.9 0.0 copy-done.2
  26.9 0.9 %projection_update.1 = (f32[128,256]{1,0:T(8,128)}, f32[128,256]{1,0:T(8,128)}, f32[128,256]{1,0:T(8,128)}, f32[6,1,11]{2,1,0:T(1,128)}) custom-call(bf16[272,128]{1,0:T(8,128)(2,1)S(1)} %collective-permute-done.7.refs_0_, bf16[272,128]{1,0:T(8,128)(2,1)S(1)} %collective-permute-done.8.refs_1_, bf16[272,128]{1,0:T(8,128)(2,1)S(1)} %collective-permute-done.9.refs_2_, ...), custom_call_target="tpu_custom_call" | custom-call | tf_op jit(solution)/shard_map/projection_update/pallas_call | solution.py:489
Async XLA Ops:
  0.6 10.8 %collective-permute-start.3 = (bf16[1,128,128]{2,1,0:T(8,128)(2,1)}, bf16[1,128,128]{2,1,0:T(8,128)(2,1)S(1)}, u32[]{:S(2)}, u32[]{:S(2)}) collective-permute-start(bf16[1,128,128]{2,1,0:T(8,128)(2,1)} %grad_hbm.1), channel_id=1, source_target_pairs={{0,2},{1,3},{2,0},{3,1},{4,6},{5,7},{6,4},{7,5},{8,10},{9,11},{10,... | collective-permute-start | bytes 98312 | tf_op jit(solution)/shard_map/ppermute | solution.py:324
  3.6 8.1 %collective-permute-start.5 = (bf16[1,128,128]{2,1,0:T(8,128)(2,1)}, bf16[1,128,128]{2,1,0:T(8,128)(2,1)S(1)}, u32[]{:S(2)}, u32[]{:S(2)}) collective-permute-start(bf16[1,128,128]{2,1,0:T(8,128)(2,1)} %grad_hbm.1), channel_id=1, source_target_pairs={{0,6},{1,7},{2,4},{3,5},{4,2},{5,3},{6,0},{7,1},{8,14},{9,15},{10,... | collective-permute-start | bytes 98312 | tf_op jit(solution)/shard_map/ppermute | solution.py:324
  5.1 6.6 %collective-permute-start.4 = (bf16[1,128,128]{2,1,0:T(8,128)(2,1)}, bf16[1,128,128]{2,1,0:T(8,128)(2,1)S(1)}, u32[]{:S(2)}, u32[]{:S(2)}) collective-permute-start(bf16[1,128,128]{2,1,0:T(8,128)(2,1)} %grad_hbm.1), channel_id=1, source_target_pairs={{0,4},{1,5},{2,6},{3,7},{4,0},{5,1},{6,2},{7,3},{8,12},{9,13},{10,... | collective-permute-start | bytes 98312 | tf_op jit(solution)/shard_map/ppermute | solution.py:324
  5.2 6.5 %copy-start.3 = (bf16[1,1024,128]{2,1,0:T(8,128)(2,1)S(1)}, bf16[1,1024,128]{2,1,0:T(8,128)(2,1)}, u32[]{:S(2)}) copy-start(bf16[1,1024,128]{2,1,0:T(8,128)(2,1)} %refs_7_.2) | copy-start | bytes 786436
  6.3 8.9 %collective-permute-start.2 = (bf16[128,256]{1,0:T(8,128)(2,1)S(1)}, bf16[128,256]{1,0:T(8,128)(2,1)S(1)}, u32[]{:S(2)}, u32[]{:S(2)}) collective-permute-start(bf16[128,256]{1,0:T(8,128)(2,1)S(1)} %get-tuple-element.35.refs_0_), channel_id=1, source_target_pairs={{0,16},{8,24},{16,0},{24,8},{1,17},{9,25},{17,1},{25,9},{2,18},{10... | collective-permute-start | bytes 196616 | tf_op jit(solution)/shard_map/ppermute | solution.py:324
  9.4 6.1 %collective-permute-start.1 = (bf16[128,256]{1,0:T(8,128)(2,1)S(1)}, bf16[128,256]{1,0:T(8,128)(2,1)S(1)}, u32[]{:S(2)}, u32[]{:S(2)}) collective-permute-start(bf16[128,256]{1,0:T(8,128)(2,1)S(1)} %get-tuple-element.35.refs_0_), channel_id=1, source_target_pairs={{0,24},{8,16},{16,8},{24,0},{1,25},{9,17},{17,9},{25,1},{2,26},{10... | collective-permute-start | bytes 196616 | tf_op jit(solution)/shard_map/ppermute | solution.py:324
  11.4 4.8 %collective-permute-start = (bf16[128,256]{1,0:T(8,128)(2,1)S(1)}, bf16[128,256]{1,0:T(8,128)(2,1)S(1)}, u32[]{:S(2)}, u32[]{:S(2)}) collective-permute-start(bf16[128,256]{1,0:T(8,128)(2,1)S(1)} %get-tuple-element.35.refs_0_), channel_id=1, source_target_pairs={{0,8},{8,0},{16,24},{24,16},{1,9},{9,1},{17,25},{25,17},{2,10},{10... | collective-permute-start | bytes 196616 | tf_op jit(solution)/shard_map/ppermute | solution.py:324
  11.7 1.8 %copy-start.4 = (bf16[1,1024,128]{2,1,0:T(8,128)(2,1)S(1)}, bf16[1,1024,128]{2,1,0:T(8,128)(2,1)}, u32[]{:S(2)}) copy-start(bf16[1,1024,128]{2,1,0:T(8,128)(2,1)} %v_ref.1) | copy-start | bytes 786436
  13.5 1.4 %collective-permute-start.6 = (bf16[512,128]{1,0:T(8,128)(2,1)S(1)}, bf16[512,128]{1,0:T(8,128)(2,1)S(1)}, u32[]{:S(2)}, u32[]{:S(2)}) collective-permute-start(bf16[512,128]{1,0:T(8,128)(2,1)S(1)} %get-tuple-element.38.refs_0_), channel_id=1, source_target_pairs={{0,1},{1,0},{2,3},{3,2},{4,5},{5,4},{6,7},{7,6},{8,9},{9,8},{10,11... | collective-permute-start | bytes 393224 | tf_op jit(solution)/shard_map/ppermute | solution.py:324
  18.1 7.4 %collective-permute-start.7 = (bf16[272,128]{1,0:T(8,128)(2,1)S(1)}, bf16[272,128]{1,0:T(8,128)(2,1)S(1)}, u32[]{:S(2)}, u32[]{:S(2)}) collective-permute-start(bf16[272,128]{1,0:T(8,128)(2,1)S(1)} %get-tuple-element.52), channel_id=1, source_target_pairs={{0,16},{8,24},{16,0},{24,8},{1,17},{9,25},{17,1},{25,9},{2,18},{10... | collective-permute-start | bytes 208904 | tf_op jit(solution)/shard_map/ppermute | solution.py:324
  19.9 5.6 %collective-permute-start.8 = (bf16[272,128]{1,0:T(8,128)(2,1)S(1)}, bf16[272,128]{1,0:T(8,128)(2,1)S(1)}, u32[]{:S(2)}, u32[]{:S(2)}) collective-permute-start(bf16[272,128]{1,0:T(8,128)(2,1)S(1)} %get-tuple-element.53), channel_id=1, source_target_pairs={{0,8},{8,0},{16,24},{24,16},{1,9},{9,1},{17,25},{25,17},{2,10},{10... | collective-permute-start | bytes 208904 | tf_op jit(solution)/shard_map/ppermute | solution.py:324
  20.8 6.2 %collective-permute-start.9 = (bf16[272,128]{1,0:T(8,128)(2,1)S(1)}, bf16[272,128]{1,0:T(8,128)(2,1)S(1)}, u32[]{:S(2)}, u32[]{:S(2)}) collective-permute-start(bf16[272,128]{1,0:T(8,128)(2,1)S(1)} %get-tuple-element.54), channel_id=1, source_target_pairs={{0,24},{8,16},{16,8},{24,0},{1,25},{9,17},{17,9},{25,1},{2,26},{10... | collective-permute-start | bytes 208904 | tf_op jit(solution)/shard_map/ppermute | solution.py:324
  22.4 4.5 %copy-start = (f32[128,256]{1,0:T(8,128)S(1)}, f32[128,256]{1,0:T(8,128)}, u32[]{:S(2)}) copy-start(f32[128,256]{1,0:T(8,128)} %refs_5_.1) | copy-start | bytes 393220
  22.5 4.5 %copy-start.1 = (f32[128,256]{1,0:T(8,128)S(1)}, f32[128,256]{1,0:T(8,128)}, u32[]{:S(2)}) copy-start(f32[128,256]{1,0:T(8,128)} %refs_6_.1) | copy-start | bytes 393220
  22.5 4.5 %copy-start.2 = (f32[128,256]{1,0:T(8,128)S(1)}, f32[128,256]{1,0:T(8,128)}, u32[]{:S(2)}) copy-start(f32[128,256]{1,0:T(8,128)} %refs_7_.3) | copy-start | bytes 393220
